TPU v7x, 32 devices: a whole 2x2x4 slice. The times are simulated.
32 devices in a mesh: row: 16 (over z, y, x), col: 2 (over core).
Axes of the slice: x: 2, y: 2, z: 4, core: 2. Of those that a mesh axis runs over, the one named last changes fastest.
Arguments:
- inverse_block: bfloat16 [1280, 1280], P('row', 'col')
- factor_cols: bfloat16 [3, 1280, 512], P(None, 'col', 'row'), may hold values from -6 to 6
- occupancy: int32 [3, 10], replicated, may hold values 0 or 1
- row_block: int32 [3, 10], replicated, may hold values from 0 to 9, each once within a row
- coupling: bfloat16 [2, 512, 512], replicated, may hold values from -0.25 to 0.25
- diag_inverse: float32 [3, 512, 512], P(None, None, 'col'), may hold values from -6 to 6
Outputs:
- columns: float32 [3, 1280, 512], P(None, ('row', 'col'))
- diagonals: float32 [3, 512, 512], P(None, None, 'col')
Inputs may be any that keep to these rules, and one draw needn't show every extreme that they name: `row_block`: each row names every one of the 10 row blocks exactly once.
All inputs are finite; a program needn't handle non-finite values.
Results may differ from a plain program's by a relative error of at most 0.0003.
Values may be sent and summed in bfloat16 or wider, within the bound.
No kernel may reach another device: no remote copies, remote signals or barrier semaphores. Data moves between devices by JAX's collectives and lax.ppermute only.
A program may use at most 64 MiB of HBM per device.

v0:
```python
import jax
import jax.numpy as jnp
from jax import lax
from jax.sharding import PartitionSpec as P

highest = lax.Precision.HIGHEST


def routed(gathered, occupancy, row_block, nblocks):
    count = gathered.shape[0]
    width_part = gathered.shape[1] // (nblocks * 128)
    blocks = gathered.reshape(count, nblocks, 128, width_part)
    levels = lax.broadcasted_iota(jnp.int32, (count, nblocks, nblocks), 1)
    picks = ((row_block[:, None, :] == levels) & (occupancy[:, None, :] > 0)).astype(jnp.bfloat16)
    placed = jnp.einsum("kqb,kbtx->kxqt", picks, blocks, preferred_element_type=jnp.float32)
    return placed.astype(jnp.bfloat16).reshape(count, width_part, nblocks * 128)


def split_rows(placed, column, row_parts, col_parts, tile):
    count, width_part, total = placed.shape
    span = total // col_parts
    column_part = lax.dynamic_slice_in_dim(placed, column * span, span, 2)
    grid = placed.reshape(count, width_part, row_parts, col_parts, tile)
    mine = lax.dynamic_index_in_dim(grid, column, 3, keepdims=False)
    return (column_part, jnp.transpose(mine, (0, 2, 1, 3)))


def make_term(inverse_block, column_full):
    return lax.dot_general(
        inverse_block, column_full, (((1,), (2,)), ((), ())), preferred_element_type=jnp.float32
    )


def local_step(summed, own_rows, previous, link, diag_part, column, row_first, rows_total):
    if link is None:
        coupled = jnp.zeros_like(summed)
    else:
        coupled = jnp.dot(previous, link.astype(jnp.float32), precision=highest)
    current = -(summed + coupled)
    own = own_rows.astype(jnp.float32)
    inner = jnp.dot(own, current, precision=highest) - jnp.dot(coupled.T, own.T, precision=highest)
    width = summed.shape[1]
    diag_cols = diag_part.shape[1]
    embedded = lax.dynamic_update_slice(
        jnp.zeros((width, width), jnp.float32), diag_part, (0, column * diag_cols)
    )
    return (current, row_first * embedded - inner / rows_total)


def chain_diag(total, chain_prev, link):
    if link is None:
        return total
    link_wide = link.astype(jnp.float32)
    return total + jnp.dot(
        link_wide.T, jnp.dot(chain_prev, link_wide, precision=highest), precision=highest
    )


def per_device(inverse_block, factor_cols, occupancy, row_block, coupling, diag_inverse):
    column = lax.axis_index("col")
    row_first = (lax.axis_index("row") == 0).astype(jnp.float32)
    row_parts = lax.axis_size("row")
    col_parts = lax.axis_size("col")
    local_rows = inverse_block.shape[0]
    rows_total = local_rows * row_parts
    supers, span, width_part = factor_cols.shape
    width = width_part * row_parts
    tile = local_rows // col_parts
    nblocks = occupancy.shape[1]
    diag_cols = diag_inverse.shape[2]
    flat = factor_cols.reshape(supers, span * width_part)
    column_list = []
    partial_list = []
    previous = None
    gathered = lax.all_gather(flat, "col", axis=1, tiled=True)
    placed = routed(gathered, occupancy, row_block, nblocks)
    column_part, outgoing = split_rows(placed, column, row_parts, col_parts, tile)
    column_full = lax.all_gather(column_part, "row", axis=1, tiled=True)
    arrived = lax.all_to_all(outgoing, "row", split_axis=1, concat_axis=1, tiled=True)
    own_all = arrived.reshape(supers, width, tile)
    summed = lax.psum_scatter(
        make_term(inverse_block, column_full), "col", scatter_dimension=0, tiled=True
    )
    for position in range(supers):
        link = None if position == 0 else coupling[position - 1]
        current, partial_value = local_step(
            summed[:, position, :],
            own_all[position],
            previous,
            link,
            diag_inverse[position],
            column,
            row_first,
            rows_total,
        )
        column_list.append(current)
        partial_list.append(partial_value)
        previous = current
    diag_list = []
    totals = lax.psum(jnp.stack(partial_list), ("row", "col"))
    chain_prev = None
    for position in range(supers):
        link = None if position == 0 else coupling[position - 1]
        diag_now = chain_diag(totals[position], chain_prev, link)
        diag_list.append(lax.dynamic_slice_in_dim(diag_now, column * diag_cols, diag_cols, 1))
        chain_prev = diag_now
    diagonals = jnp.stack(diag_list)
    return (jnp.stack(column_list), diagonals)


def solution(mesh):
    in_specs = (P("row", "col"), P(None, "col", "row"), P(), P(), P(), P(None, None, "col"))
    out_specs = (P(None, ("row", "col"), None), P(None, None, "col"))
    return jax.shard_map(
        per_device, mesh=mesh, in_specs=in_specs, out_specs=out_specs, check_vma=False
    )
```

profile of v0, /device:TPU:0, one launch (start us, length us, event | category | flops | bytes accessed | tf_op | source)
XLA Modules:
  0.0 250.0 jit_solution(13069497747625728933)
XLA Ops:
  7.2 0.7 broadcast_compare_fusion
  7.9 1.2 copy.17
  9.1 0.5 reshape.38
  9.6 2.1 all_gather.6
  11.8 0.6 reshape.39
  12.3 0.6 copy.18
  13.0 0.2 fusion.10
  13.2 0.2 reshape.40
  13.4 0.7 constant_dynamic-slice_fusion.2
  14.1 1.5 reshape_reshape.3
  15.5 0.8 constant_dynamic-slice_fusion.1
  16.4 0.3 copy.36
  16.6 1.2 reshape.43
  17.8 8.2 %all-to-all-start = ((bf16[16,2,1920]{2,1,0:T(2,128)(2,1)}), bf16[16,2,1920]{2,1,0:T(2,128)(2,1)S(1)}, u32[]{:S(2)}, u32[]{:S(2)}) async-start(bf16[16,2,1920]{2,1,0:T(2,128)(2,1)} %reshape.43), calls=%async_computation.1 | async-start | bytes 245760 | tf_op jit(solution)/shard_map/all_to_all | solution.py:79
  26.1 0.0 reduce-scatter.2.cloned.1.call-start
  26.1 1.1 broadcast.16.clone.1
  27.3 0.9 bitcast_dynamic-update-slice_fusion.1
  28.1 48.8 %all-gather.2.cloned.1.call-done = bf16[3,512,640]{2,1,0:T(8,128)(2,1)} async-done(((bf16[3,32,640]{2,1,0:T(8,128)(2,1)}), bf16[3,512,640]{2,1,0:T(8,128)(2,1)}) %all-gather.2.cloned.1.call-update) | async-done | bytes 1966096 | tf_op jit(solution)/shard_map/all_gather | solution.py:78
  76.9 3.1 %convolution_bitcast_fusion.2 = f32[80,3,512]{2,0,1:T(8,128)} fusion(bf16[3,512,640]{2,1,0:T(8,128)(2,1)} %all-gather.2.cloned.1.call-done, bf16[80,640]{1,0:T(8,128)(2,1)S(1)} %copy-done), kind=kOutput, calls=%fused_computation.18 | convolution fusion | flops 157286400 | bytes 2560000 | tf_op jit(solution)/shard_map/dot_general | solution.py:29
  80.0 0.2 all-reduce.2.cloned.1.call-start
  80.2 0.1 broadcast.16.clone
  80.4 0.1 bitcast_dynamic-update-slice_fusion
  80.4 1.0 copy-done.3
  81.4 0.1 broadcast.16.clone.2
  81.5 1.2 bitcast_dynamic-update-slice_fusion.2
  82.8 0.6 reshape.44
  83.3 0.7 fusion.54
  84.1 0.6 fusion.29
  84.6 2.2 reduce-scatter.2.cloned.1.call-done
  86.9 1.3 fusion.21
  88.2 1.5 fusion.48
  89.7 2.1 fusion.5
  91.8 0.4 fusion.17
  92.2 0.6 fusion.39
  92.8 0.8 fusion.8
  93.6 0.7 fusion.2
  94.3 2.0 pad_maximum_fusion
  96.3 0.9 copy-done.6
  97.3 0.7 pad_maximum_fusion.2
  98.0 137.3 %all-reduce.2.cloned.1.call-done = f32[3,512,512]{2,1,0:T(8,128)} async-done(((f32[3,512,512]{2,1,0:T(8,128)}), f32[3,512,512]{2,1,0:T(8,128)}) %all-reduce.2.cloned.1.call-update) | async-done | bytes 3145744 | tf_op jit(solution)/shard_map/psum | solution.py:100
  235.3 1.9 fusion.53
  237.2 0.6 copy-done.2
  237.8 1.0 fusion.11
  238.8 1.1 fusion.9
  239.9 1.0 fusion.15
  240.9 1.1 convolution_bitcast_fusion
  242.0 0.2 fusion.13
  242.2 1.2 pad_maximum_fusion.1
  (27 shorter events, 0.2 us)
Async XLA Ops:
  7.2 69.8 %copy-start = (bf16[80,640]{1,0:T(8,128)(2,1)S(1)}, bf16[80,640]{1,0:T(8,128)(2,1)}, u32[]{:S(2)}) copy-start(bf16[80,640]{1,0:T(8,128)(2,1)} %param.6) | copy-start | bytes 307204
  7.2 69.7 %all-gather.2.cloned.1.call-start = ((), (), s32[]{:S(2)}) async-start(), calls=%async_computation.2 | async-start | bytes 2088960 | tf_op jit(solution)/shard_map/all_gather | solution.py:78
  9.1 3.9 %copy-start.10 = (s32[3,10]{1,0:T(4,128)S(1)}, s32[3,10]{1,0:T(4,128)}, u32[]{:S(2)}) copy-start(s32[3,10]{1,0:T(4,128)} %param.9) | copy-start | bytes 364
  15.5 11.7 %copy-start.7 = (f32[3,512,256]{2,1,0:T(8,128)S(1)}, f32[3,512,256]{2,1,0:T(8,128)}, u32[]{:S(2)}) copy-start(f32[3,512,256]{2,1,0:T(8,128)} %param.11) | copy-start | bytes 4718596
  17.8 64.9 %all-to-all-start = ((bf16[16,2,1920]{2,1,0:T(2,128)(2,1)}), bf16[16,2,1920]{2,1,0:T(2,128)(2,1)S(1)}, u32[]{:S(2)}, u32[]{:S(2)}) async-start(bf16[16,2,1920]{2,1,0:T(2,128)(2,1)} %reshape.43), calls=%async_computation.1 | async-start | bytes 245760 | tf_op jit(solution)/shard_map/all_to_all | solution.py:79
  26.1 60.8 %reduce-scatter.2.cloned.1.call-start = ((), (), s32[]{:S(2)}) async-start(), calls=%async_computation.3 | async-start | bytes 737280 | tf_op jit(solution)/shard_map/reduce_scatter | solution.py:81
  80.0 155.3 %all-reduce.2.cloned.1.call-start = ((), (), s32[]{:S(2)}) async-start(), calls=%async_computation.4 | async-start | bytes 6291456 | tf_op jit(solution)/shard_map/psum | solution.py:100
  80.4 1.0 copy-start.3
  81.5 5.3 %copy-start.1 = (bf16[2,512,512]{2,1,0:T(8,128)(2,1)S(1)}, bf16[2,512,512]{2,1,0:T(8,128)(2,1)}, u32[]{:S(2)}) copy-start(bf16[2,512,512]{2,1,0:T(8,128)(2,1)} %param.10) | copy-start | bytes 3145732
  86.9 2.8 %copy-start.9 = (bf16[1,16,32,40]{3,2,0,1:T(8,128)(2,1)S(1)}, bf16[1,16,32,40]{3,2,0,1:T(8,128)(2,1)}, u32[]{:S(2)}) copy-start(bf16[1,16,32,40]{3,2,0,1:T(8,128)(2,1)} %get-tuple-element.6) | copy-start | bytes 122884
  89.7 2.1 copy-start.5
  89.7 2.5 %copy-start.8 = (bf16[1,16,32,40]{3,2,0,1:T(8,128)(2,1)S(1)}, bf16[1,16,32,40]{3,2,0,1:T(8,128)(2,1)}, u32[]{:S(2)}) copy-start(bf16[1,16,32,40]{3,2,0,1:T(8,128)(2,1)} %get-tuple-element.5) | copy-start | bytes 122884
  89.7 3.1 %copy-start.4 = (f32[512,512]{1,0:T(8,128)S(1)}, f32[512,512]{1,0:T(8,128)}, u32[]{:S(2)}) copy-start(f32[512,512]{1,0:T(8,128)} %copy-done.3) | copy-start | bytes 3145732
  96.3 0.9 copy-start.6
  235.3 2.5 %copy-start.2 = (f32[3,512,512]{2,1,0:T(8,128)S(1)}, f32[3,512,512]{2,1,0:T(8,128)}, u32[]{:S(2)}) copy-start(f32[3,512,512]{2,1,0:T(8,128)} %all-reduce.2.cloned.1.call-done) | copy-start | bytes 9437188
Sparse Core Ops, SparseCore 0:
  14.2 62.6 all-gather.1
  80.1 6.6 reduce-scatter.1
  96.5 138.7 all-reduce.1
where the time goes:
time: 250 us
  waiting for transfers between devices  188 us (75%)
  local copies, waits for them, and re-layouts  16.7 us (7%)
  matrix products  15.4 us (6%)
  between operations  14.1 us (6%)
  starting transfers between devices  8.53 us (3%)
  other arithmetic  4.87 us (2%)
    psum x1, waiting for transfers between devices, per_device(): totals = lax.psum(jnp.stack(partial_list), ('row', 'col'))  137 us
    all_gather x1, waiting for transfers between devices, per_device(): column_full = lax.all_gather(column_part, 'row', axis=1, tiled=True)  48.8 us
    all_to_all x1, starting transfers between devices, per_device(): lax.all_to_all(outgoing, 'row', split_axis=1, concat_axis=1, tiled=True)  8.23 us
    unnamed x25, local copies, waits for them, and re-layouts  5.5 us
  transfers between devices with their start and end apart: 4, of which 3 were waited for; matrix products, arithmetic and copies ran while one was open for 5% of the time, Pallas kernels for 0%

commit v1 on v0

--- a/solution.py
+++ b/solution.py
@@ -1,9 +1,17 @@
+import functools
+
 import jax
 import jax.numpy as jnp
 from jax import lax
+from jax.experimental import pallas as pl
+from jax.experimental.pallas import tpu as pltpu
 from jax.sharding import PartitionSpec as P
 
 highest = lax.Precision.HIGHEST
+f32 = jnp.float32
+bf16 = jnp.bfloat16
+
+REPLICATE_BYTES = 12 * 2**20
 
 
 def routed(gathered, occupancy, row_block, nblocks):
@@ -56,7 +64,7 @@
     )
 
 
-def per_device(inverse_block, factor_cols, occupancy, row_block, coupling, diag_inverse):
+def grid_plan(inverse_block, factor_cols, occupancy, row_block, coupling, diag_inverse):
     column = lax.axis_index("col")
     row_first = (lax.axis_index("row") == 0).astype(jnp.float32)
     row_parts = lax.axis_size("row")
@@ -108,9 +116,192 @@
     return (jnp.stack(column_list), diagonals)
 
 
+def swap(value, axis, bit, parts):
+    return lax.ppermute(value, axis, [(i, i ^ bit) for i in range(parts)])
+
+
+def spread(own, row_parts):
+    outer = row_parts // 4
+    line = jnp.stack([own] + [swap(own, "row", 4 * k, row_parts) for k in range(1, outer)])
+    over_x = swap(line, "row", 1, row_parts)
+    over_y = swap(line, "row", 2, row_parts)
+    half = outer // 2
+    far_a = swap(over_y[:half], "row", 1, row_parts)
+    far_b = swap(over_x[half:], "row", 2, row_parts)
+    return [(0, 0, line), (1, 0, over_x), (2, 0, over_y), (3, 0, far_a), (3, half, far_b)]
+
+
+def split2(value):
+    high = value.astype(bf16)
+    return high, (value - high.astype(f32)).astype(bf16)
+
+
+def nn(a, b):
+    return lax.dot_general(a, b, (((1,), (0,)), ((), ())), preferred_element_type=f32)
+
+
+def nt(a, b):
+    return lax.dot_general(a, b, (((1,), (1,)), ((), ())), preferred_element_type=f32)
+
+
+def nn2(pair, b):
+    return nn(pair[0], b) + nn(pair[1], b)
+
+
+def nn2r(a, pair):
+    return nn(a, pair[0]) + nn(a, pair[1])
+
+
+def local_kernel(groups, dims, *refs):
+    supers, width, rows, span, chunk = dims
+    n = len(groups)
+    place_ref, occ_ref, block_ref = refs[:3]
+    f_refs = refs[3 : 3 + 2 * n]
+    z_refs = refs[3 + 2 * n : 3 + 4 * n]
+    link_ref, link_t_ref, diag_ref, diag_other_ref = refs[3 + 4 * n : 7 + 4 * n]
+    col_out, diag_out = refs[7 + 4 * n : 9 + 4 * n]
+    (f_all, z_all, pt, c0h, c0l, c1h, c1l, p1h, p1l, c2h, c2l, tmp, f_sem, z_sem) = refs[9 + 4 * n :]
+    row = place_ref[0]
+    col = place_ref[1]
+    local_rows = z_refs[0].shape[1]
+    part = f_refs[0].shape[3]
+    half_w = width // 2
+    f_copies, z_copies = [], []
+    for side in range(2):
+        target = col if side == 0 else 1 - col
+        for g, (plane, first, count) in enumerate(groups):
+            for k in range(count):
+                owner = row ^ (4 * (first + k) + plane)
+                f_copies.append(pltpu.make_async_copy(f_refs[side * n + g].at[k], f_all.at[target, owner], f_sem))
+                z_copies.append(
+                    pltpu.make_async_copy(
+                        z_refs[side * n + g].at[k],
+                        z_all.at[
+                            pl.ds(pl.multiple_of(owner * local_rows, local_rows), local_rows),
+                            pl.ds(pl.multiple_of(target * span, span), span),
+                        ],
+                        z_sem,
+                    )
+                )
+    for copy in f_copies + z_copies:
+        copy.start()
+    for copy in f_copies:
+        copy.wait()
+    per_side = span // 128
+    for s in range(supers):
+        for b in range(2 * per_side):
+            lane = (b % per_side) * 128
+            blk = f_all[b // per_side, :, s, :, lane : lane + 128].reshape(width, 128)
+            keep = jnp.where(occ_ref[s * 2 * per_side + b] > 0, blk, jnp.zeros_like(blk))
+            pt[s, :, pl.ds(pl.multiple_of(block_ref[s * 2 * per_side + b] * 128, 128), 128)] = keep
+    for copy in z_copies:
+        copy.wait()
+    c_rows = pl.ds(pl.multiple_of(col * half_w, half_w), half_w)
+
+    def step(m, carry):
+        at = pl.ds(pl.multiple_of(m * chunk, chunk), chunk)
+        zm = z_all[at, :]
+        cols0 = split2(-nt(zm, pt[0]))
+        c0h[at, :], c0l[at, :] = cols0
+        tmp[...] = nn2(cols0, link_ref[0])
+        p1h[at, :], p1l[at, :] = split2(tmp[...])
+        tmp[...] += nt(zm, pt[1])
+        cols1 = split2(-tmp[...])
+        c1h[at, :], c1l[at, :] = cols1
+        cols2 = -(nt(zm, pt[2, c_rows, :]) + nn2(cols1, link_ref[1, :, c_rows]))
+        c2h[at, :], c2l[at, :] = split2(cols2)
+        return carry
+
+    lax.fori_loop(0, rows // chunk, step, 0)
+
+    own = pl.ds(pl.multiple_of(row * local_rows, local_rows), local_rows)
+    tile = local_rows // 2
+    o1 = (c1h[own, :], c1l[own, :])
+    mine = [
+        c0h[own, :].astype(f32) + c0l[own, :].astype(f32),
+        o1[0].astype(f32) + o1[1].astype(f32),
+        -(nt(z_all[own, :], pt[2]) + nn2(o1, link_ref[1])),
+    ]
+    for s in range(supers):
+        col_out[s] = jnp.where(col == 0, mine[s][:tile], mine[s][tile:])
+
+    scale = 1.0 / rows
+    whole = lambda s: (
+        jnp.where(col == 0, diag_ref[s], diag_other_ref[s]),
+        jnp.where(col == 0, diag_other_ref[s], diag_ref[s]),
+    )
+    d0 = jnp.concatenate(whole(0), axis=1) - nn2r(pt[0], (c0h[...], c0l[...])) * scale
+    u1 = nn2r(pt[1], (p1h[...], p1l[...]))
+    i1 = nn2r(pt[1], (c1h[...], c1l[...])) - u1.T
+    d1 = jnp.concatenate(whole(1), axis=1) - i1 * scale + nn2r(link_t_ref[0], split2(nn2(split2(d0), link_ref[0])))
+    n2 = nn2r(pt[2, c_rows, :], (c1h[...], c1l[...]))
+    i2 = nn2r(pt[2], (c2h[...], c2l[...])) - nn2(split2(n2), link_ref[1]).T
+    d2 = diag_ref[2] - i2 * scale + nn2r(link_t_ref[1], split2(nn2(split2(d1), link_ref[1, :, c_rows])))
+    diag_out[0] = jnp.where(col == 0, d0[:, :half_w], d0[:, half_w:])
+    diag_out[1] = jnp.where(col == 0, d1[:, :half_w], d1[:, half_w:])
+    diag_out[2] = d2
+
+
+def replicated_plan(inverse_block, factor_cols, occupancy, row_block, coupling, diag_inverse):
+    row_parts = lax.axis_size("row")
+    row = lax.axis_index("row")
+    col = lax.axis_index("col")
+    supers, span, part = factor_cols.shape
+    width = part * row_parts
+    local_rows = inverse_block.shape[0]
+    rows = local_rows * row_parts
+    f_groups = spread(jnp.transpose(factor_cols, (0, 2, 1)), row_parts)
+    z_groups = spread(inverse_block, row_parts)
+    across = lambda value: lax.ppermute(value, "col", [(0, 1), (1, 0)])
+    diag_other = across(diag_inverse[: supers - 1])
+    f_values = [v for _, _, v in f_groups]
+    z_values = [v for _, _, v in z_groups]
+    f_values = f_values + [across(v) for v in f_values]
+    z_values = z_values + [across(v) for v in z_values]
+    groups = tuple((plane, first, v.shape[0]) for plane, first, v in f_groups)
+    chunk = 256
+    any_spec = pl.BlockSpec(memory_space=pl.ANY)
+    smem = pl.BlockSpec(memory_space=pltpu.SMEM)
+    vmem = pl.BlockSpec(memory_space=pltpu.VMEM)
+    wide = lambda cols: pltpu.VMEM((rows, cols), bf16)
+    return pl.pallas_call(
+        functools.partial(local_kernel, groups, (supers, width, rows, span, chunk)),
+        out_shape=(
+            jax.ShapeDtypeStruct((supers, local_rows // 2, width), f32),
+            jax.ShapeDtypeStruct((supers, width, width // 2), f32),
+        ),
+        in_specs=[smem] * 3 + [any_spec] * (4 * len(groups)) + [vmem] * 4,
+        out_specs=(vmem, vmem),
+        scratch_shapes=[
+            pltpu.VMEM((2, row_parts, supers, part, span), bf16),
+            pltpu.VMEM((rows, 2 * span), bf16),
+            pltpu.VMEM((supers, width, rows), bf16),
+            wide(width), wide(width), wide(width), wide(width), wide(width), wide(width),
+            wide(width // 2), wide(width // 2),
+            pltpu.VMEM((chunk, width), f32),
+            pltpu.SemaphoreType.DMA,
+            pltpu.SemaphoreType.DMA,
+        ],
+        compiler_params=pltpu.CompilerParams(vmem_limit_bytes=56 * 2**20),
+        name="selected_inverse",
+    )(
+        jnp.stack([row, col]).astype(jnp.int32), occupancy.reshape(-1), row_block.reshape(-1),
+        *f_values, *z_values,
+        coupling, jnp.transpose(coupling, (0, 2, 1)), diag_inverse, diag_other,
+    )
+
+
 def solution(mesh):
+    row_parts, col_parts = mesh.shape["row"], mesh.shape["col"]
     in_specs = (P("row", "col"), P(None, "col", "row"), P(), P(), P(), P(None, None, "col"))
     out_specs = (P(None, ("row", "col"), None), P(None, None, "col"))
+
+    def per_device(inverse_block, factor_cols, *rest):
+        held = (inverse_block.size + factor_cols.size) * 2 * row_parts * col_parts
+        fits = held <= REPLICATE_BYTES and col_parts == 2 and row_parts in (8, 16, 32)
+        plan = replicated_plan if fits else grid_plan
+        return plan(inverse_block, factor_cols, *rest)
+
     return jax.shard_map(
         per_device, mesh=mesh, in_specs=in_specs, out_specs=out_specs, check_vma=False
     )

time: 250 us -> 92.2 us (0.37)
  waiting for transfers between devices: 188 us -> 33.1 us
  Pallas kernels: 0 us -> 26.5 us
  matrix products: 15.4 us -> 0 us
  between operations: 14.1 us -> 0.82 us
  starting transfers between devices: 8.53 us -> 20.9 us
  local copies, waits for them, and re-layouts: 16.7 us -> 7.21 us
    psum x1 -> x0, waiting for transfers between devices: 137 us -> none  [per_device(): totals = lax.psum(jnp.stack(partial_list), ('row', 'col'))]
    all_gather x1 -> x0, waiting for transfers between devices: 48.8 us -> none  [per_device(): column_full = lax.all_gather(column_part, 'row', axis=1, tiled=True)]
    ppermute x0 -> x25, waiting for transfers between devices: none -> 33.1 us  [the longest x14 31.2 us: swap(): return lax.ppermute(value, axis, [(i, i ^ bit) for i in range(parts)])]
    pallas_call x0 -> x1, Pallas kernels: none -> 26.5 us  [replicated_plan(): pl.pallas_call(functools.partial(local_kernel, groups, (supers, width, ro...]
    ppermute x0 -> x25, starting transfers between devices: none -> 20.9 us  [the longest x14 19.3 us: swap(): return lax.ppermute(value, axis, [(i, i ^ bit) for i in range(parts)])]
    dot_general x14 -> x0, matrix products: 15.4 us -> none  [the longest x3 3.44 us: local_step(): jnp.dot(coupled.T, own.T, precision=highest)]
    all_to_all x1 -> x0, starting transfers between devices: 8.23 us -> none  [per_device(): lax.all_to_all(outgoing, 'row', split_axis=1, concat_axis=1, tiled=True)]
    another operation x4 -> x0, local copies, waits for them, and re-layouts: 2.8 us -> none  [the longest x1 1.46 us: split_rows(): grid = placed.reshape(count, width_part, row_parts, col_parts, tile)]
  transfers between devices with their start and end apart: 4 -> 25, of which waited for: 3 -> 9; matrix products, arithmetic and copies ran while one was open for 5% -> 8% of each run, Pallas kernels for 0% -> 0%
where the time goes in v1:
time: 92.2 us; the launch traced here: 91.2 us
  waiting for transfers between devices  33.1 us (36%)
  Pallas kernels  26.5 us (29%)
  starting transfers between devices  20.9 us (23%)
  local copies, waits for them, and re-layouts  7.21 us (8%)
  other arithmetic  2.59 us (3%)
    ppermute x14, waiting for transfers between devices, swap(): return lax.ppermute(value, axis, [(i, i ^ bit) for i in range(parts)])  31.2 us
    pallas_call x1, Pallas kernels, replicated_plan(): pl.pallas_call(functools.partial(local_kernel, groups, (supers, width, ro...  26.5 us
    ppermute x14, starting transfers between devices, swap(): return lax.ppermute(value, axis, [(i, i ^ bit) for i in range(parts)])  19.3 us
    unnamed x37, local copies, waits for them, and re-layouts  2.99 us
    another operation x2, other arithmetic, spread(): jnp.stack([own] + [swap(own, 'row', 4 * k, row_parts) for k in range(1, o...  1.94 us
    ppermute x11, waiting for transfers between devices, replicated_plan(): across = lambda value: lax.ppermute(value, 'col', [(0, 1), (1, 0)])  1.87 us
  transfers between devices with their start and end apart: 25, of which 9 were waited for; matrix products, arithmetic and copies ran while one was open for 8% of the time, Pallas kernels for 0%

profile of v1, /device:TPU:0, one launch (start us, length us, event | category | flops | bytes accessed | tf_op | source)
XLA Modules:
  0.0 91.2 jit_solution(1618160162931997179)
XLA Ops:
  0.6 0.0 copy-start
  0.6 3.1 %collective-permute-start.12 = (bf16[80,640]{1,0:T(8,128)(2,1)}, bf16[80,640]{1,0:T(8,128)(2,1)S(1)}, u32[]{:S(2)}, u32[]{:S(2)}) collective-permute-start(bf16[80,640]{1,0:T(8,128)(2,1)} %param.6), channel_id=1, source_target_pairs={{0,8},{2,10},{4,12},{6,14},{8,0},{10,2},{12,4},{14,6},{16,24},{18,... | collective-permute-start | bytes 307208 | tf_op jit(solution)/shard_map/ppermute | solution.py:120
  3.7 2.5 %collective-permute-start.14 = (bf16[80,640]{1,0:T(8,128)(2,1)}, bf16[80,640]{1,0:T(8,128)(2,1)S(1)}, u32[]{:S(2)}, u32[]{:S(2)}) collective-permute-start(bf16[80,640]{1,0:T(8,128)(2,1)} %param.6), channel_id=1, source_target_pairs={{0,24},{2,26},{4,28},{6,30},{8,16},{10,18},{12,20},{14,22},{16,8},... | collective-permute-start | bytes 307208 | tf_op jit(solution)/shard_map/ppermute | solution.py:120
  6.2 0.1 collective-permute-start.13
  6.3 0.5 collective-permute-done.12
  6.8 5.5 %collective-permute-done.14 = bf16[80,640]{1,0:T(8,128)(2,1)S(1)} collective-permute-done((bf16[80,640]{1,0:T(8,128)(2,1)}, bf16[80,640]{1,0:T(8,128)(2,1)S(1)}, u32[]{:S(2)}, u32[]{:S(2)}) %collective-permute-start.14) | collective-permute-done | bytes 102432 | tf_op jit(solution)/shard_map/ppermute | solution.py:120
  12.3 3.4 %collective-permute-done.13 = bf16[80,640]{1,0:T(8,128)(2,1)S(1)} collective-permute-done((bf16[80,640]{1,0:T(8,128)(2,1)}, bf16[80,640]{1,0:T(8,128)(2,1)S(1)}, u32[]{:S(2)}, u32[]{:S(2)}) %collective-permute-start.13) | collective-permute-done | bytes 102432 | tf_op jit(solution)/shard_map/ppermute | solution.py:120
  15.7 1.0 %pad_maximum_fusion.1.refs_13_ = bf16[4,80,640]{2,1,0:T(8,128)(2,1)S(1)} fusion(bf16[1,80,640]{2,1,0:T(8,128)(2,1)S(1)} %bitcast.23, bf16[1,80,640]{2,1,0:T(8,128)(2,1)S(1)} %bitcast.24, bf16[1,80,640]{2,1,0:T(8,128)(2,1)S(1)} %bitcast.22, bf16[1,80,640]{2,1,0:T(8,128)(2,1)} %bitcast.21), kind=kLoop, calls=%fused_computation.1 | loop fusion | flops 614400 | bytes 819200 | tf_op jit(solution)/shard_map/stack | solution.py:125
  16.7 1.6 %collective-permute-start.16 = (bf16[4,80,640]{2,1,0:T(8,128)(2,1)S(1)}, bf16[4,80,640]{2,1,0:T(8,128)(2,1)S(1)}, u32[]{:S(2)}, u32[]{:S(2)}) collective-permute-start(bf16[4,80,640]{2,1,0:T(8,128)(2,1)S(1)} %pad_maximum_fusion.1.refs_13_), channel_id=1, source_target_pairs={{0,4},{2,6},{4,0},{6,2},{8,12},{10,14},{12,8},{14,10},{16,20},{18,... | collective-permute-start | bytes 1228808 | tf_op jit(solution)/shard_map/ppermute | solution.py:120
  18.3 0.5 collective-permute-start.1
  18.8 2.7 %collective-permute-start = (bf16[3,32,640]{2,1,0:T(8,128)(2,1)}, bf16[3,32,640]{2,1,0:T(8,128)(2,1)S(1)}, u32[]{:S(2)}, u32[]{:S(2)}) collective-permute-start(bf16[3,32,640]{2,1,0:T(8,128)(2,1)} %bitcast.15), channel_id=1, source_target_pairs={{0,8},{2,10},{4,12},{6,14},{8,0},{10,2},{12,4},{14,6},{16,24},{18,... | collective-permute-start | bytes 368648 | tf_op jit(solution)/shard_map/ppermute | solution.py:120
  21.5 1.2 %collective-permute-start.2 = (bf16[3,32,640]{2,1,0:T(8,128)(2,1)}, bf16[3,32,640]{2,1,0:T(8,128)(2,1)S(1)}, u32[]{:S(2)}, u32[]{:S(2)}) collective-permute-start(bf16[3,32,640]{2,1,0:T(8,128)(2,1)} %bitcast.16), channel_id=1, source_target_pairs={{0,24},{2,26},{4,28},{6,30},{8,16},{10,18},{12,20},{14,22},{16,8},... | collective-permute-start | bytes 368648 | tf_op jit(solution)/shard_map/ppermute | solution.py:120
  22.7 1.5 %collective-permute-start.15 = (bf16[4,80,640]{2,1,0:T(8,128)(2,1)S(1)}, bf16[4,80,640]{2,1,0:T(8,128)(2,1)S(1)}, u32[]{:S(2)}, u32[]{:S(2)}) collective-permute-start(bf16[4,80,640]{2,1,0:T(8,128)(2,1)S(1)} %pad_maximum_fusion.1.refs_13_), channel_id=1, source_target_pairs={{0,2},{2,0},{4,6},{6,4},{8,10},{10,8},{12,14},{14,12},{16,18},{18,... | collective-permute-start | bytes 1228808 | tf_op jit(solution)/shard_map/ppermute | solution.py:120
  24.2 5.3 %collective-permute-done.1 = bf16[3,32,640]{2,1,0:T(8,128)(2,1)S(1)} collective-permute-done((bf16[3,32,640]{2,1,0:T(8,128)(2,1)}, bf16[3,32,640]{2,1,0:T(8,128)(2,1)S(1)}, u32[]{:S(2)}, u32[]{:S(2)}) %collective-permute-start.1) | collective-permute-done | bytes 122912 | tf_op jit(solution)/shard_map/ppermute | solution.py:120
  29.5 1.0 %pad_maximum_fusion.refs_3_ = bf16[4,3,32,640]{3,2,1,0:T(8,128)(2,1)S(1)} fusion(bf16[1,3,32,640]{3,2,1,0:T(8,128)(2,1)S(1)} %bitcast.20, bf16[1,3,32,640]{3,2,1,0:T(8,128)(2,1)S(1)} %bitcast.18, bf16[1,3,32,640]{3,2,1,0:T(8,128)(2,1)S(1)} %bitcast.19, bf16[1,3,32,640]{3,2,1,0:T(8,128)(2,1)} %bitcast.17), kind=kLoop, calls=%fused_computation | loop fusion | flops 737280 | bytes 983040 | tf_op jit(solution)/shard_map/stack | solution.py:125
  30.5 0.0 copy-start.16
  30.5 0.0 copy-start.17
  30.5 0.6 collective-permute-start.4
  31.1 1.5 %collective-permute-start.3 = (bf16[4,3,32,640]{3,2,1,0:T(8,128)(2,1)S(1)}, bf16[4,3,32,640]{3,2,1,0:T(8,128)(2,1)}, u32[]{:S(2)}, u32[]{:S(2)}) collective-permute-start(bf16[4,3,32,640]{3,2,1,0:T(8,128)(2,1)S(1)} %pad_maximum_fusion.refs_3_), channel_id=1, source_target_pairs={{0,2},{2,0},{4,6},{6,4},{8,10},{10,8},{12,14},{14,12},{16,18},{18,... | collective-permute-start | bytes 1474568 | tf_op jit(solution)/shard_map/ppermute | solution.py:120
  32.6 0.2 collective-permute-start.19
  32.8 1.0 %slice.19 = f32[2,512,256]{2,1,0:T(8,128)} slice(f32[3,512,256]{2,1,0:T(8,128)S(1)} %copy-done), slice={[0:2], [0:512], [0:256]} | slice | bytes 2097152 | tf_op jit(solution)/shard_map/slice | solution.py:256
  33.8 0.3 collective-permute-start.24
  34.2 7.4 %collective-permute-done.4.refs_5_ = bf16[4,3,32,640]{3,2,1,0:T(8,128)(2,1)} collective-permute-done((bf16[4,3,32,640]{3,2,1,0:T(8,128)(2,1)S(1)}, bf16[4,3,32,640]{3,2,1,0:T(8,128)(2,1)}, u32[]{:S(2)}, u32[]{:S(2)}) %collective-permute-start.4) | collective-permute-done | bytes 491552 | tf_op jit(solution)/shard_map/ppermute | solution.py:120
  41.5 1.5 %collective-permute-start.17 = (bf16[2,80,640]{2,1,0:T(8,128)(2,1)S(1)}, bf16[2,80,640]{2,1,0:T(8,128)(2,1)S(1)}, u32[]{:S(2)}, u32[]{:S(2)}) collective-permute-start(bf16[2,80,640]{2,1,0:T(8,128)(2,1)S(1)} %slice.22), channel_id=1, source_target_pairs={{0,2},{2,0},{4,6},{6,4},{8,10},{10,8},{12,14},{14,12},{16,18},{18,... | collective-permute-start | bytes 614408 | tf_op jit(solution)/shard_map/ppermute | solution.py:120
  43.0 1.0 %slice.20 = bf16[2,3,32,640]{3,2,1,0:T(8,128)(2,1)S(1)} slice(bf16[4,3,32,640]{3,2,1,0:T(8,128)(2,1)} %collective-permute-done.4.refs_5_), slice={[0:2], [0:3], [0:32], [0:640]} | slice | bytes 491520 | tf_op jit(solution)/shard_map/slice | solution.py:129
  44.0 0.6 collective-permute-start.18
  44.6 0.5 collective-permute-start.5
  45.2 0.0 collective-permute-done.3.refs_4_
  45.2 1.0 %slice.21 = bf16[2,3,32,640]{3,2,1,0:T(8,128)(2,1)S(1)} slice(bf16[4,3,32,640]{3,2,1,0:T(8,128)(2,1)} %collective-permute-done.3.refs_4_), slice={[2:4], [0:3], [0:32], [0:640]} | slice | bytes 491520 | tf_op jit(solution)/shard_map/slice | solution.py:130
  46.2 3.4 %collective-permute-done.17.refs_16_ = bf16[2,80,640]{2,1,0:T(8,128)(2,1)S(1)} collective-permute-done((bf16[2,80,640]{2,1,0:T(8,128)(2,1)S(1)}, bf16[2,80,640]{2,1,0:T(8,128)(2,1)S(1)}, u32[]{:S(2)}, u32[]{:S(2)}) %collective-permute-start.17) | collective-permute-done | bytes 204832 | tf_op jit(solution)/shard_map/ppermute | solution.py:120
  49.6 1.5 %collective-permute-start.6 = (bf16[2,3,32,640]{3,2,1,0:T(8,128)(2,1)S(1)}, bf16[2,3,32,640]{3,2,1,0:T(8,128)(2,1)}, u32[]{:S(2)}, u32[]{:S(2)}) collective-permute-start(bf16[2,3,32,640]{3,2,1,0:T(8,128)(2,1)S(1)} %slice.21), channel_id=1, source_target_pairs={{0,4},{2,6},{4,0},{6,2},{8,12},{10,14},{12,8},{14,10},{16,20},{18,... | collective-permute-start | bytes 737288 | tf_op jit(solution)/shard_map/ppermute | solution.py:120
  51.0 3.5 %collective-permute-done.5.refs_6_ = bf16[2,3,32,640]{3,2,1,0:T(8,128)(2,1)} collective-permute-done((bf16[2,3,32,640]{3,2,1,0:T(8,128)(2,1)S(1)}, bf16[2,3,32,640]{3,2,1,0:T(8,128)(2,1)}, u32[]{:S(2)}, u32[]{:S(2)}) %collective-permute-start.5) | collective-permute-done | bytes 245792 | tf_op jit(solution)/shard_map/ppermute | solution.py:120
  54.5 2.3 %collective-permute-done.6.refs_7_ = bf16[2,3,32,640]{3,2,1,0:T(8,128)(2,1)} collective-permute-done((bf16[2,3,32,640]{3,2,1,0:T(8,128)(2,1)S(1)}, bf16[2,3,32,640]{3,2,1,0:T(8,128)(2,1)}, u32[]{:S(2)}, u32[]{:S(2)}) %collective-permute-start.6) | collective-permute-done | bytes 245792 | tf_op jit(solution)/shard_map/ppermute | solution.py:120
  56.7 0.5 collective-permute-start.8
  57.2 0.1 collective-permute-start.23
  57.3 1.8 %collective-permute-done.23.refs_22_ = bf16[2,80,640]{2,1,0:T(8,128)(2,1)S(1)} collective-permute-done((bf16[2,80,640]{2,1,0:T(8,128)(2,1)S(1)}, bf16[2,80,640]{2,1,0:T(8,128)(2,1)S(1)}, u32[]{:S(2)}, u32[]{:S(2)}) %collective-permute-start.23) | collective-permute-done | bytes 204832 | tf_op jit(solution)/shard_map/ppermute | solution.py:255
  59.2 0.1 collective-permute-start.10
  59.3 0.4 collective-permute-start.11
  59.8 0.1 copy-done.15
  59.8 0.2 copy-done.12
  60.1 0.6 reshape.10.refs_1_
  60.7 0.6 reshape.11.refs_2_
  61.3 1.4 %copy.8 = bf16[2,512,512]{1,2,0:T(8,128)(2,1)} copy(bf16[2,512,512]{2,1,0:T(8,128)(2,1)S(1)} %copy-done.1) | data formatting | bytes 2097152 | tf_op args[4]
  62.6 0.7 pad_add_fusion.refs_0_
  63.4 0.9 copy-done.4
  64.3 0.1 copy-done.8
  64.4 0.2 copy-done.9
  64.6 26.5 %selected_inverse.1 = (f32[3,40,512]{2,1,0:T(8,128)}, f32[3,512,256]{2,1,0:T(8,128)}) custom-call(s32[2]{0:T(128)} %pad_add_fusion.refs_0_, s32[30]{0:T(128)} %reshape.10.refs_1_, s32[30]{0:T(128)} %reshape.11.refs_2_, bf16[4,3,32,640]{3,2,1,0:T(8,128)(2,1)} %copy-done.2, bf16[4,3,32,640]{3,2,1,0:T(8,128)(2,1)} %collective-permute-done.3.refs_4_, ...), custom_call_target="tpu_custom_call" | custom-call | tf_op jit(solution)/shard_map/selected_inverse/pallas_call | solution.py:267
  (50 shorter events, 0.1 us)
Async XLA Ops:
  0.6 32.2 %copy-start = (f32[3,512,256]{2,1,0:T(8,128)S(1)}, f32[3,512,256]{2,1,0:T(8,128)}, u32[]{:S(2)}) copy-start(f32[3,512,256]{2,1,0:T(8,128)} %refs_25_.1) | copy-start | bytes 4718596
  0.6 6.2 %collective-permute-start.12 = (bf16[80,640]{1,0:T(8,128)(2,1)}, bf16[80,640]{1,0:T(8,128)(2,1)S(1)}, u32[]{:S(2)}, u32[]{:S(2)}) collective-permute-start(bf16[80,640]{1,0:T(8,128)(2,1)} %param.6), channel_id=1, source_target_pairs={{0,8},{2,10},{4,12},{6,14},{8,0},{10,2},{12,4},{14,6},{16,24},{18,... | collective-permute-start | bytes 307208 | tf_op jit(solution)/shard_map/ppermute | solution.py:120
  3.7 8.6 %collective-permute-start.14 = (bf16[80,640]{1,0:T(8,128)(2,1)}, bf16[80,640]{1,0:T(8,128)(2,1)S(1)}, u32[]{:S(2)}, u32[]{:S(2)}) collective-permute-start(bf16[80,640]{1,0:T(8,128)(2,1)} %param.6), channel_id=1, source_target_pairs={{0,24},{2,26},{4,28},{6,30},{8,16},{10,18},{12,20},{14,22},{16,8},... | collective-permute-start | bytes 307208 | tf_op jit(solution)/shard_map/ppermute | solution.py:120
  6.2 9.5 %collective-permute-start.13 = (bf16[80,640]{1,0:T(8,128)(2,1)}, bf16[80,640]{1,0:T(8,128)(2,1)S(1)}, u32[]{:S(2)}, u32[]{:S(2)}) collective-permute-start(bf16[80,640]{1,0:T(8,128)(2,1)} %param.6), channel_id=1, source_target_pairs={{0,16},{2,18},{4,20},{6,22},{8,24},{10,26},{12,28},{14,30},{16,0},... | collective-permute-start | bytes 307208 | tf_op jit(solution)/shard_map/ppermute | solution.py:120
  16.7 17.4 %copy-start.3 = (bf16[4,80,640]{2,1,0:T(8,128)(2,1)}, bf16[4,80,640]{2,1,0:T(8,128)(2,1)S(1)}, u32[]{:S(2)}) copy-start(bf16[4,80,640]{2,1,0:T(8,128)(2,1)S(1)} %pad_maximum_fusion.1.refs_13_) | copy-start | bytes 1228804
  16.7 15.9 %collective-permute-start.16 = (bf16[4,80,640]{2,1,0:T(8,128)(2,1)S(1)}, bf16[4,80,640]{2,1,0:T(8,128)(2,1)S(1)}, u32[]{:S(2)}, u32[]{:S(2)}) collective-permute-start(bf16[4,80,640]{2,1,0:T(8,128)(2,1)S(1)} %pad_maximum_fusion.1.refs_13_), channel_id=1, source_target_pairs={{0,4},{2,6},{4,0},{6,2},{8,12},{10,14},{12,8},{14,10},{16,20},{18,... | collective-permute-start | bytes 1228808 | tf_op jit(solution)/shard_map/ppermute | solution.py:120
  18.3 11.2 %collective-permute-start.1 = (bf16[3,32,640]{2,1,0:T(8,128)(2,1)}, bf16[3,32,640]{2,1,0:T(8,128)(2,1)S(1)}, u32[]{:S(2)}, u32[]{:S(2)}) collective-permute-start(bf16[3,32,640]{2,1,0:T(8,128)(2,1)} %bitcast.14), channel_id=1, source_target_pairs={{0,16},{2,18},{4,20},{6,22},{8,24},{10,26},{12,28},{14,30},{16,0},... | collective-permute-start | bytes 368648 | tf_op jit(solution)/shard_map/ppermute | solution.py:120
  18.8 10.7 %collective-permute-start = (bf16[3,32,640]{2,1,0:T(8,128)(2,1)}, bf16[3,32,640]{2,1,0:T(8,128)(2,1)S(1)}, u32[]{:S(2)}, u32[]{:S(2)}) collective-permute-start(bf16[3,32,640]{2,1,0:T(8,128)(2,1)} %bitcast.15), channel_id=1, source_target_pairs={{0,8},{2,10},{4,12},{6,14},{8,0},{10,2},{12,4},{14,6},{16,24},{18,... | collective-permute-start | bytes 368648 | tf_op jit(solution)/shard_map/ppermute | solution.py:120
  21.5 8.0 %collective-permute-start.2 = (bf16[3,32,640]{2,1,0:T(8,128)(2,1)}, bf16[3,32,640]{2,1,0:T(8,128)(2,1)S(1)}, u32[]{:S(2)}, u32[]{:S(2)}) collective-permute-start(bf16[3,32,640]{2,1,0:T(8,128)(2,1)} %bitcast.16), channel_id=1, source_target_pairs={{0,24},{2,26},{4,28},{6,30},{8,16},{10,18},{12,20},{14,22},{16,8},... | collective-permute-start | bytes 368648 | tf_op jit(solution)/shard_map/ppermute | solution.py:120
  22.7 11.2 %collective-permute-start.15 = (bf16[4,80,640]{2,1,0:T(8,128)(2,1)S(1)}, bf16[4,80,640]{2,1,0:T(8,128)(2,1)S(1)}, u32[]{:S(2)}, u32[]{:S(2)}) collective-permute-start(bf16[4,80,640]{2,1,0:T(8,128)(2,1)S(1)} %pad_maximum_fusion.1.refs_13_), channel_id=1, source_target_pairs={{0,2},{2,0},{4,6},{6,4},{8,10},{10,8},{12,14},{14,12},{16,18},{18,... | collective-permute-start | bytes 1228808 | tf_op jit(solution)/shard_map/ppermute | solution.py:120
  30.5 13.6 %copy-start.2 = (bf16[4,3,32,640]{3,2,1,0:T(8,128)(2,1)}, bf16[4,3,32,640]{3,2,1,0:T(8,128)(2,1)S(1)}, u32[]{:S(2)}) copy-start(bf16[4,3,32,640]{3,2,1,0:T(8,128)(2,1)S(1)} %pad_maximum_fusion.refs_3_) | copy-start | bytes 1474564
  30.5 29.6 %copy-start.16 = (s32[3,10]{1,0:T(4,128)S(1)}, s32[3,10]{1,0:T(4,128)}, u32[]{:S(2)}) copy-start(s32[3,10]{1,0:T(4,128)} %param.8) | copy-start | bytes 364
  30.5 30.2 %copy-start.17 = (s32[3,10]{1,0:T(4,128)S(1)}, s32[3,10]{1,0:T(4,128)}, u32[]{:S(2)}) copy-start(s32[3,10]{1,0:T(4,128)} %param.9) | copy-start | bytes 364
  30.5 30.8 %copy-start.1 = (bf16[2,512,512]{2,1,0:T(8,128)(2,1)S(1)}, bf16[2,512,512]{2,1,0:T(8,128)(2,1)}, u32[]{:S(2)}) copy-start(bf16[2,512,512]{2,1,0:T(8,128)(2,1)} %refs_23_.1) | copy-start | bytes 3145732
  30.5 11.0 %collective-permute-start.4 = (bf16[4,3,32,640]{3,2,1,0:T(8,128)(2,1)S(1)}, bf16[4,3,32,640]{3,2,1,0:T(8,128)(2,1)}, u32[]{:S(2)}, u32[]{:S(2)}) collective-permute-start(bf16[4,3,32,640]{3,2,1,0:T(8,128)(2,1)S(1)} %pad_maximum_fusion.refs_3_), channel_id=1, source_target_pairs={{0,4},{2,6},{4,0},{6,2},{8,12},{10,14},{12,8},{14,10},{16,20},{18,... | collective-permute-start | bytes 1474568 | tf_op jit(solution)/shard_map/ppermute | solution.py:120
  31.1 13.5 %collective-permute-start.7 = (bf16[4,3,32,640]{3,2,1,0:T(8,128)(2,1)S(1)}, bf16[4,3,32,640]{3,2,1,0:T(8,128)(2,1)S(1)}, u32[]{:S(2)}, u32[]{:S(2)}) collective-permute-start(bf16[4,3,32,640]{3,2,1,0:T(8,128)(2,1)S(1)} %pad_maximum_fusion.refs_3_), channel_id=1, source_target_pairs={{0,1},{1,0},{2,3},{3,2},{4,5},{5,4},{6,7},{7,6},{8,9},{9,8},{10,11... | collective-permute-start | bytes 1474568 | tf_op jit(solution)/shard_map/ppermute | solution.py:255
  31.1 14.1 %collective-permute-start.3 = (bf16[4,3,32,640]{3,2,1,0:T(8,128)(2,1)S(1)}, bf16[4,3,32,640]{3,2,1,0:T(8,128)(2,1)}, u32[]{:S(2)}, u32[]{:S(2)}) collective-permute-start(bf16[4,3,32,640]{3,2,1,0:T(8,128)(2,1)S(1)} %pad_maximum_fusion.refs_3_), channel_id=1, source_target_pairs={{0,2},{2,0},{4,6},{6,4},{8,10},{10,8},{12,14},{14,12},{16,18},{18,... | collective-permute-start | bytes 1474568 | tf_op jit(solution)/shard_map/ppermute | solution.py:120
  32.6 12.6 %copy-start.5 = (bf16[4,80,640]{2,1,0:T(8,128)(2,1)}, bf16[4,80,640]{2,1,0:T(8,128)(2,1)S(1)}, u32[]{:S(2)}) copy-start(bf16[4,80,640]{2,1,0:T(8,128)(2,1)S(1)} %collective-permute-done.16.refs_15_) | copy-start | bytes 1228804
  32.6 11.5 %collective-permute-start.19 = (bf16[4,80,640]{2,1,0:T(8,128)(2,1)S(1)}, bf16[4,80,640]{2,1,0:T(8,128)(2,1)S(1)}, u32[]{:S(2)}, u32[]{:S(2)}) collective-permute-start(bf16[4,80,640]{2,1,0:T(8,128)(2,1)S(1)} %pad_maximum_fusion.1.refs_13_), channel_id=1, source_target_pairs={{0,1},{1,0},{2,3},{3,2},{4,5},{5,4},{6,7},{7,6},{8,9},{9,8},{10,11... | collective-permute-start | bytes 1228808 | tf_op jit(solution)/shard_map/ppermute | solution.py:255
  33.8 23.4 %copy-start.6 = (bf16[4,80,640]{2,1,0:T(8,128)(2,1)}, bf16[4,80,640]{2,1,0:T(8,128)(2,1)S(1)}, u32[]{:S(2)}) copy-start(bf16[4,80,640]{2,1,0:T(8,128)(2,1)S(1)} %collective-permute-done.15.refs_14_) | copy-start | bytes 1228804
  33.8 29.5 %collective-permute-start.24 = (f32[2,512,256]{2,1,0:T(8,128)}, f32[2,512,256]{2,1,0:T(8,128)S(1)}, u32[]{:S(2)}, u32[]{:S(2)}) collective-permute-start(f32[2,512,256]{2,1,0:T(8,128)} %slice.19), channel_id=1, source_target_pairs={{0,1},{1,0},{2,3},{3,2},{4,5},{5,4},{6,7},{7,6},{8,9},{9,8},{10,11... | collective-permute-start | bytes 3145736 | tf_op jit(solution)/shard_map/ppermute | solution.py:255
  41.5 8.0 %collective-permute-start.17 = (bf16[2,80,640]{2,1,0:T(8,128)(2,1)S(1)}, bf16[2,80,640]{2,1,0:T(8,128)(2,1)S(1)}, u32[]{:S(2)}, u32[]{:S(2)}) collective-permute-start(bf16[2,80,640]{2,1,0:T(8,128)(2,1)S(1)} %slice.22), channel_id=1, source_target_pairs={{0,2},{2,0},{4,6},{6,4},{8,10},{10,8},{12,14},{14,12},{16,18},{18,... | collective-permute-start | bytes 614408 | tf_op jit(solution)/shard_map/ppermute | solution.py:120
  44.0 15.7 %copy-start.10 = (bf16[4,80,640]{2,1,0:T(8,128)(2,1)}, bf16[4,80,640]{2,1,0:T(8,128)(2,1)S(1)}, u32[]{:S(2)}) copy-start(bf16[4,80,640]{2,1,0:T(8,128)(2,1)S(1)} %collective-permute-done.19.refs_18_) | copy-start | bytes 1228804
  44.0 7.0 %collective-permute-start.18 = (bf16[2,80,640]{2,1,0:T(8,128)(2,1)S(1)}, bf16[2,80,640]{2,1,0:T(8,128)(2,1)S(1)}, u32[]{:S(2)}, u32[]{:S(2)}) collective-permute-start(bf16[2,80,640]{2,1,0:T(8,128)(2,1)S(1)} %slice.23), channel_id=1, source_target_pairs={{0,4},{2,6},{4,0},{6,2},{8,12},{10,14},{12,8},{14,10},{16,20},{18,... | collective-permute-start | bytes 614408 | tf_op jit(solution)/shard_map/ppermute | solution.py:120
  44.6 14.7 %copy-start.7 = (bf16[4,3,32,640]{3,2,1,0:T(8,128)(2,1)}, bf16[4,3,32,640]{3,2,1,0:T(8,128)(2,1)S(1)}, u32[]{:S(2)}) copy-start(bf16[4,3,32,640]{3,2,1,0:T(8,128)(2,1)S(1)} %collective-permute-done.7.refs_8_) | copy-start | bytes 1474564
  44.6 9.8 %collective-permute-start.5 = (bf16[2,3,32,640]{3,2,1,0:T(8,128)(2,1)S(1)}, bf16[2,3,32,640]{3,2,1,0:T(8,128)(2,1)}, u32[]{:S(2)}, u32[]{:S(2)}) collective-permute-start(bf16[2,3,32,640]{3,2,1,0:T(8,128)(2,1)S(1)} %slice.20), channel_id=1, source_target_pairs={{0,2},{2,0},{4,6},{6,4},{8,10},{10,8},{12,14},{14,12},{16,18},{18,... | collective-permute-start | bytes 737288 | tf_op jit(solution)/shard_map/ppermute | solution.py:120
  45.2 12.0 %collective-permute-start.21 = (bf16[4,80,640]{2,1,0:T(8,128)(2,1)S(1)}, bf16[4,80,640]{2,1,0:T(8,128)(2,1)S(1)}, u32[]{:S(2)}, u32[]{:S(2)}) collective-permute-start(bf16[4,80,640]{2,1,0:T(8,128)(2,1)S(1)} %collective-permute-done.16.refs_15_), channel_id=1, source_target_pairs={{0,1},{1,0},{2,3},{3,2},{4,5},{5,4},{6,7},{7,6},{8,9},{9,8},{10,11... | collective-permute-start | bytes 1228808 | tf_op jit(solution)/shard_map/ppermute | solution.py:255
  49.5 10.2 %copy-start.13 = (bf16[2,80,640]{2,1,0:T(8,128)(2,1)}, bf16[2,80,640]{2,1,0:T(8,128)(2,1)S(1)}, u32[]{:S(2)}) copy-start(bf16[2,80,640]{2,1,0:T(8,128)(2,1)S(1)} %collective-permute-done.17.refs_16_) | copy-start | bytes 614404
  49.6 7.2 %collective-permute-start.6 = (bf16[2,3,32,640]{3,2,1,0:T(8,128)(2,1)S(1)}, bf16[2,3,32,640]{3,2,1,0:T(8,128)(2,1)}, u32[]{:S(2)}, u32[]{:S(2)}) collective-permute-start(bf16[2,3,32,640]{3,2,1,0:T(8,128)(2,1)S(1)} %slice.21), channel_id=1, source_target_pairs={{0,4},{2,6},{4,0},{6,2},{8,12},{10,14},{12,8},{14,10},{16,20},{18,... | collective-permute-start | bytes 737288 | tf_op jit(solution)/shard_map/ppermute | solution.py:120
  51.0 8.8 %copy-start.14 = (bf16[2,80,640]{2,1,0:T(8,128)(2,1)}, bf16[2,80,640]{2,1,0:T(8,128)(2,1)S(1)}, u32[]{:S(2)}) copy-start(bf16[2,80,640]{2,1,0:T(8,128)(2,1)S(1)} %collective-permute-done.18.refs_17_) | copy-start | bytes 614404
  51.0 5.7 %collective-permute-start.22 = (bf16[2,80,640]{2,1,0:T(8,128)(2,1)S(1)}, bf16[2,80,640]{2,1,0:T(8,128)(2,1)}, u32[]{:S(2)}, u32[]{:S(2)}) collective-permute-start(bf16[2,80,640]{2,1,0:T(8,128)(2,1)S(1)} %collective-permute-done.17.refs_16_), channel_id=1, source_target_pairs={{0,1},{1,0},{2,3},{3,2},{4,5},{5,4},{6,7},{7,6},{8,9},{9,8},{10,11... | collective-permute-start | bytes 614408 | tf_op jit(solution)/shard_map/ppermute | solution.py:255
  54.5 4.8 %collective-permute-start.20 = (bf16[4,80,640]{2,1,0:T(8,128)(2,1)S(1)}, bf16[4,80,640]{2,1,0:T(8,128)(2,1)S(1)}, u32[]{:S(2)}, u32[]{:S(2)}) collective-permute-start(bf16[4,80,640]{2,1,0:T(8,128)(2,1)S(1)} %collective-permute-done.15.refs_14_), channel_id=1, source_target_pairs={{0,1},{1,0},{2,3},{3,2},{4,5},{5,4},{6,7},{7,6},{8,9},{9,8},{10,11... | collective-permute-start | bytes 1228808 | tf_op jit(solution)/shard_map/ppermute | solution.py:255
  56.7 6.6 %collective-permute-start.9 = (bf16[4,3,32,640]{3,2,1,0:T(8,128)(2,1)}, bf16[4,3,32,640]{3,2,1,0:T(8,128)(2,1)S(1)}, u32[]{:S(2)}, u32[]{:S(2)}) collective-permute-start(bf16[4,3,32,640]{3,2,1,0:T(8,128)(2,1)} %collective-permute-done.4.refs_5_), channel_id=1, source_target_pairs={{0,1},{1,0},{2,3},{3,2},{4,5},{5,4},{6,7},{7,6},{8,9},{9,8},{10,11... | collective-permute-start | bytes 1474568 | tf_op jit(solution)/shard_map/ppermute | solution.py:255
  56.7 6.6 %collective-permute-start.8 = (bf16[4,3,32,640]{3,2,1,0:T(8,128)(2,1)}, bf16[4,3,32,640]{3,2,1,0:T(8,128)(2,1)S(1)}, u32[]{:S(2)}, u32[]{:S(2)}) collective-permute-start(bf16[4,3,32,640]{3,2,1,0:T(8,128)(2,1)} %collective-permute-done.3.refs_4_), channel_id=1, source_target_pairs={{0,1},{1,0},{2,3},{3,2},{4,5},{5,4},{6,7},{7,6},{8,9},{9,8},{10,11... | collective-permute-start | bytes 1474568 | tf_op jit(solution)/shard_map/ppermute | solution.py:255
  57.2 6.1 %copy-start.11 = (bf16[4,80,640]{2,1,0:T(8,128)(2,1)}, bf16[4,80,640]{2,1,0:T(8,128)(2,1)S(1)}, u32[]{:S(2)}) copy-start(bf16[4,80,640]{2,1,0:T(8,128)(2,1)S(1)} %collective-permute-done.21.refs_20_) | copy-start | bytes 1228804
  57.2 1.9 %collective-permute-start.23 = (bf16[2,80,640]{2,1,0:T(8,128)(2,1)S(1)}, bf16[2,80,640]{2,1,0:T(8,128)(2,1)S(1)}, u32[]{:S(2)}, u32[]{:S(2)}) collective-permute-start(bf16[2,80,640]{2,1,0:T(8,128)(2,1)S(1)} %collective-permute-done.18.refs_17_), channel_id=1, source_target_pairs={{0,1},{1,0},{2,3},{3,2},{4,5},{5,4},{6,7},{7,6},{8,9},{9,8},{10,11... | collective-permute-start | bytes 614408 | tf_op jit(solution)/shard_map/ppermute | solution.py:255
  59.2 0.7 copy-start.15
  59.2 4.2 %collective-permute-start.10 = (bf16[2,3,32,640]{3,2,1,0:T(8,128)(2,1)}, bf16[2,3,32,640]{3,2,1,0:T(8,128)(2,1)}, u32[]{:S(2)}, u32[]{:S(2)}) collective-permute-start(bf16[2,3,32,640]{3,2,1,0:T(8,128)(2,1)} %collective-permute-done.5.refs_6_), channel_id=1, source_target_pairs={{0,1},{1,0},{2,3},{3,2},{4,5},{5,4},{6,7},{7,6},{8,9},{9,8},{10,11... | collective-permute-start | bytes 737288 | tf_op jit(solution)/shard_map/ppermute | solution.py:255
  59.3 0.7 copy-start.12
  59.3 4.0 %collective-permute-start.11 = (bf16[2,3,32,640]{3,2,1,0:T(8,128)(2,1)}, bf16[2,3,32,640]{3,2,1,0:T(8,128)(2,1)}, u32[]{:S(2)}, u32[]{:S(2)}) collective-permute-start(bf16[2,3,32,640]{3,2,1,0:T(8,128)(2,1)} %collective-permute-done.6.refs_7_), channel_id=1, source_target_pairs={{0,1},{1,0},{2,3},{3,2},{4,5},{5,4},{6,7},{7,6},{8,9},{9,8},{10,11... | collective-permute-start | bytes 737288 | tf_op jit(solution)/shard_map/ppermute | solution.py:255
  63.3 1.0 %copy-start.4 = (f32[2,512,256]{2,1,0:T(8,128)}, f32[2,512,256]{2,1,0:T(8,128)S(1)}, u32[]{:S(2)}) copy-start(f32[2,512,256]{2,1,0:T(8,128)S(1)} %collective-permute-done.24.refs_26_) | copy-start | bytes 3145732
  63.3 1.1 %copy-start.8 = (bf16[4,3,32,640]{3,2,1,0:T(8,128)(2,1)}, bf16[4,3,32,640]{3,2,1,0:T(8,128)(2,1)S(1)}, u32[]{:S(2)}) copy-start(bf16[4,3,32,640]{3,2,1,0:T(8,128)(2,1)S(1)} %collective-permute-done.9.refs_10_) | copy-start | bytes 1474564
  63.3 1.3 %copy-start.9 = (bf16[4,3,32,640]{3,2,1,0:T(8,128)(2,1)}, bf16[4,3,32,640]{3,2,1,0:T(8,128)(2,1)S(1)}, u32[]{:S(2)}) copy-start(bf16[4,3,32,640]{3,2,1,0:T(8,128)(2,1)S(1)} %collective-permute-done.8.refs_9_) | copy-start | bytes 1474564

commit v2 on v0

--- a/solution.py
+++ b/solution.py
@@ -1,9 +1,18 @@
+import functools
+
 import jax
 import jax.numpy as jnp
 from jax import lax
+from jax.experimental import pallas as pl
+from jax.experimental.pallas import tpu as pltpu
 from jax.sharding import PartitionSpec as P
 
 highest = lax.Precision.HIGHEST
+f32 = jnp.float32
+bf16 = jnp.bfloat16
+
+REPLICATE_BYTES = 12 * 2**20
+VMEM_LIMIT = 40 * 2**20
 
 
 def routed(gathered, occupancy, row_block, nblocks):
@@ -56,7 +65,7 @@
     )
 
 
-def per_device(inverse_block, factor_cols, occupancy, row_block, coupling, diag_inverse):
+def grid_plan(inverse_block, factor_cols, occupancy, row_block, coupling, diag_inverse):
     column = lax.axis_index("col")
     row_first = (lax.axis_index("row") == 0).astype(jnp.float32)
     row_parts = lax.axis_size("row")
@@ -108,9 +117,269 @@
     return (jnp.stack(column_list), diagonals)
 
 
+def swap(value, axis, bit, parts):
+    return lax.ppermute(value, axis, [(i, i ^ bit) for i in range(parts)])
+
+
+def across(value):
+    return lax.ppermute(value, "col", [(0, 1), (1, 0)])
+
+
+def along_line(own, row_parts):
+    return [own] + [swap(own, "row", 4 * k, row_parts) for k in range(1, row_parts // 4)]
+
+
+def over_plane(own, row_parts):
+    return swap(own, "row", 1, row_parts), swap(own, "row", 2, row_parts)
+
+
+def after(values, *events):
+    return lax.optimization_barrier((values, events))[0]
+
+
+def split2(value):
+    high = value.astype(bf16)
+    return high, (value - high.astype(f32)).astype(bf16)
+
+
+def nn(a, b):
+    return lax.dot_general(a, b, (((1,), (0,)), ((), ())), preferred_element_type=f32)
+
+
+def nt(a, b):
+    return lax.dot_general(a, b, (((1,), (1,)), ((), ())), preferred_element_type=f32)
+
+
+def nn2(pair, b):
+    return nn(pair[0], b) + nn(pair[1], b)
+
+
+def nn2r(a, pair):
+    return nn(a, pair[0]) + nn(a, pair[1])
+
+
+def owner_of(row, wave, count, j, i):
+    return 4 * ((row // 4) ^ (wave * count + i)) + ((row % 4) ^ j)
+
+
+def place_kernel(dims, *refs):
+    supers, width, rows, span, part = dims
+    occ_ref, block_ref = refs[:2]
+    f_refs, z_ref, z_other_ref, link_ref = refs[2:6], refs[6], refs[7], refs[8]
+    pt, col_out, f_all, sem = refs[9:]
+    row, col = lax.axis_index("row"), lax.axis_index("col")
+    copies = []
+    for side in range(2):
+        for wave in range(2):
+            source = f_refs[2 * side + wave]
+            for j in range(4):
+                for i in range(source.shape[1]):
+                    owner = owner_of(row, wave, source.shape[1], j, i)
+                    target = col if side == 0 else 1 - col
+                    copies.append(pltpu.make_async_copy(source.at[j, i], f_all.at[target, owner], sem))
+    for copy in copies:
+        copy.start()
+    for copy in copies:
+        copy.wait()
+    per_side = span // 128
+    for s in range(supers):
+        for b in range(2 * per_side):
+            lane = (b % per_side) * 128
+            blk = f_all[b // per_side, :, s * part : (s + 1) * part, lane : lane + 128].reshape(width, 128)
+            keep = jnp.where(occ_ref[s, b] > 0, blk, jnp.zeros_like(blk))
+            pt[s, :, pl.ds(pl.multiple_of(block_ref[s, b] * 128, 128), 128)] = keep
+    local_rows = z_ref.shape[0]
+    tile = local_rows // 2
+    mine, theirs = z_ref[...], z_other_ref[...]
+    z_own = jnp.concatenate([jnp.where(col == 0, mine, theirs), jnp.where(col == 0, theirs, mine)], axis=1)
+    previous = None
+    for s in range(supers):
+        current = -nt(z_own, pt[s])
+        if s > 0:
+            current = current - nn2(split2(previous), link_ref[s - 1])
+        col_out[s] = jnp.where(col == 0, current[:tile], current[tile:])
+        previous = current
+
+
+def add_rows(wave, dims, col, row, pt, z_refs, link_ref, sums, scratch):
+    width, span = dims
+    z_all, c0h, c0l, c1h, c1l, p1h, p1l, c2h, c2l, tmp, sem = scratch
+    half_rows = z_all.shape[0]
+    half_w = width // 2
+    copies = []
+    for side in range(2):
+        target = col if side == 0 else 1 - col
+        source = z_refs[side]
+        local_rows = source.shape[2]
+        for j in range(4):
+            for i in range(source.shape[1]):
+                place = owner_of(row, wave, source.shape[1], j, i) % (half_rows // local_rows)
+                copies.append(
+                    pltpu.make_async_copy(
+                        source.at[j, i],
+                        z_all.at[
+                            pl.ds(pl.multiple_of(place * local_rows, local_rows), local_rows),
+                            pl.ds(pl.multiple_of(target * span, span), span),
+                        ],
+                        sem,
+                    )
+                )
+    for copy in copies:
+        copy.start()
+    for copy in copies:
+        copy.wait()
+    c_rows = pl.ds(pl.multiple_of(col * half_w, half_w), half_w)
+    half = owner_of(row, wave, z_refs[0].shape[1], 0, 0) // (half_rows // local_rows)
+    lanes = pl.ds(pl.multiple_of(half * half_rows, half_rows), half_rows)
+    zm = z_all[...]
+    cols0 = split2(-nt(zm, pt[0]))
+    c0h[...], c0l[...] = cols0
+    tmp[...] = nn2(cols0, link_ref[0])
+    p1h[...], p1l[...] = split2(tmp[...])
+    tmp[...] += nt(zm, pt[1])
+    cols1 = split2(-tmp[...])
+    c1h[...], c1l[...] = cols1
+    cols2 = -(nt(zm, pt[2, c_rows, :]) + nn2(cols1, link_ref[1, :, c_rows]))
+    c2h[...], c2l[...] = split2(cols2)
+    left = pt[1, :, lanes]
+    terms = [
+        nn2r(pt[0, :, lanes], (c0h[...], c0l[...])),
+        nn2r(left, (p1h[...], p1l[...])),
+        nn2r(left, (c1h[...], c1l[...])),
+        nn2r(pt[2, c_rows, lanes], (c1h[...], c1l[...])),
+        nn2r(pt[2, :, lanes], (c2h[...], c2l[...])),
+    ]
+    for total, term in zip(sums, terms):
+        total[...] = term if wave == 0 else total[...] + term
+
+
+def first_kernel(dims, *refs):
+    pt, z_refs, link_ref = refs[0], refs[1:3], refs[3]
+    add_rows(0, dims, lax.axis_index("col"), lax.axis_index("row"), pt, z_refs, link_ref, refs[4:9], refs[9:])
+
+
+def last_kernel(dims, rows, *refs):
+    pt, z_refs, link_ref, diag_ref, diag_other_ref = refs[0], refs[1:3], refs[3], refs[4], refs[5]
+    before, diag_out, sums, scratch = refs[6:11], refs[11], refs[12:17], refs[17:]
+    col = lax.axis_index("col")
+    width, _ = dims
+    half_w = width // 2
+    for total, value in zip(sums, before):
+        total[...] = value[...]
+    add_rows(1, dims, col, lax.axis_index("row"), pt, z_refs, link_ref, sums, scratch)
+    s0, u1, s1, n2, s2 = sums
+    scale = 1.0 / rows
+    c_rows = pl.ds(pl.multiple_of(col * half_w, half_w), half_w)
+
+    def whole(s):
+        mine, theirs = diag_ref[s], diag_other_ref[s]
+        return jnp.concatenate([jnp.where(col == 0, mine, theirs), jnp.where(col == 0, theirs, mine)], axis=1)
+
+    d0 = whole(0) - s0[...] * scale
+    i1 = s1[...] - u1[...].T
+    d1 = whole(1) - i1 * scale + nn2r(link_ref[0].T, split2(nn2(split2(d0), link_ref[0])))
+    i2 = s2[...] - nn2(split2(n2[...]), link_ref[1]).T
+    d2 = diag_ref[2] - i2 * scale + nn2r(link_ref[1].T, split2(nn2(split2(d1), link_ref[1, :, c_rows])))
+    diag_out[0] = jnp.where(col == 0, d0[:, :half_w], d0[:, half_w:])
+    diag_out[1] = jnp.where(col == 0, d1[:, :half_w], d1[:, half_w:])
+    diag_out[2] = d2
+
+
+def replicated_plan(inverse_block, factor_cols, occupancy, row_block, coupling, diag_inverse):
+    row_parts = lax.axis_size("row")
+    supers, span, part = factor_cols.shape
+    width = part * row_parts
+    local_rows = inverse_block.shape[0]
+    rows = local_rows * row_parts
+    count = row_parts // 8
+    any_spec = pl.BlockSpec(memory_space=pl.ANY)
+    smem = pl.BlockSpec(memory_space=pltpu.SMEM)
+    vmem = pl.BlockSpec(memory_space=pltpu.VMEM)
+    shape = jax.ShapeDtypeStruct
+
+    def call(body, name, flops, **kwargs):
+        return pl.pallas_call(
+            body,
+            compiler_params=pltpu.CompilerParams(vmem_limit_bytes=VMEM_LIMIT),
+            cost_estimate=pl.CostEstimate(flops=flops, bytes_accessed=8 * 2**20, transcendentals=0),
+            name=name,
+            **kwargs,
+        )
+
+    f_own = jnp.transpose(factor_cols, (0, 2, 1)).reshape(supers * part, span)
+    f_parts = along_line(f_own, row_parts)
+    f_a, f_b = jnp.stack(f_parts[:count]), jnp.stack(f_parts[count:])
+    f_ax, f_ay = over_plane(f_a, row_parts)
+    f_bx, f_by = over_plane(f_b, row_parts)
+    z_cross = across(inverse_block)
+    z_parts = along_line(after(inverse_block, f_b), row_parts)
+    z_a, z_b = jnp.stack(z_parts[:count]), jnp.stack(z_parts[count:])
+    f_ay, f_bx = after((f_ay, f_bx), z_b)
+    f_far_a, f_far_b = swap(f_ay, "row", 1, row_parts), swap(f_bx, "row", 2, row_parts)
+    z_a = after(z_a, f_ay, f_bx)
+    z_ax, z_ay = over_plane(z_a, row_parts)
+    f_mine = [jnp.stack([f_a, f_ax, f_ay, f_far_a]), jnp.stack([f_b, f_bx, f_by, f_far_b])]
+    f_all = f_mine + [across(v) for v in f_mine]
+    z_b = after(z_b, z_ax, z_ay)
+    z_bx, z_by = over_plane(z_b, row_parts)
+    z_far_a = swap(z_ay, "row", 1, row_parts)
+    z_first = jnp.stack([z_a, z_ax, z_ay, z_far_a])
+    z_first_other = across(z_first)
+    diag_other = across(diag_inverse)
+
+    pt, columns = call(
+        functools.partial(place_kernel, (supers, width, rows, span, part)),
+        "place", 4 * 10**9,
+        out_shape=(shape((supers, width, rows), bf16), shape((supers, local_rows // 2, width), f32)),
+        in_specs=[smem] * 2 + [any_spec] * 4 + [vmem] * 3,
+        out_specs=(vmem, vmem),
+        scratch_shapes=[pltpu.VMEM((2, row_parts, supers * part, span), bf16), pltpu.SemaphoreType.DMA],
+    )(occupancy, row_block, *f_all, inverse_block, z_cross, coupling)
+
+    z_bx, pt = after((z_bx, pt), pt)
+    z_far_b = swap(z_bx, "row", 2, row_parts)
+    dims = (width, span)
+    half_rows, half_w = rows // 2, width // 2
+    sum_shapes = [(width, width), (width, width), (width, width), (half_w, width), (width, half_w)]
+    scratch = (
+        [pltpu.VMEM((half_rows, 2 * span), bf16)]
+        + [pltpu.VMEM((half_rows, width), bf16)] * 6
+        + [pltpu.VMEM((half_rows, half_w), bf16)] * 2
+        + [pltpu.VMEM((half_rows, width), f32), pltpu.SemaphoreType.DMA]
+    )
+    sums = call(
+        functools.partial(first_kernel, dims),
+        "own_half", 12 * 10**9,
+        out_shape=tuple(shape(v, f32) for v in sum_shapes),
+        in_specs=[vmem] + [any_spec] * 2 + [vmem],
+        out_specs=(vmem,) * 5,
+        scratch_shapes=scratch,
+    )(pt, z_first, z_first_other, coupling)
+    z_far_b, *sums = after((z_far_b, *sums), sums[0])
+    z_last = jnp.stack([z_b, z_bx, z_by, z_far_b])
+    z_last_other = across(z_last)
+    diagonals = call(
+        functools.partial(last_kernel, dims, rows),
+        "other_half", 15 * 10**9,
+        out_shape=shape((supers, width, half_w), f32),
+        in_specs=[vmem] + [any_spec] * 2 + [vmem] * 8,
+        out_specs=vmem,
+        scratch_shapes=[pltpu.VMEM(v, f32) for v in sum_shapes] + scratch,
+    )(pt, z_last, z_last_other, coupling, diag_inverse, diag_other, *sums)
+    return columns, diagonals
+
+
 def solution(mesh):
+    row_parts, col_parts = mesh.shape["row"], mesh.shape["col"]
     in_specs = (P("row", "col"), P(None, "col", "row"), P(), P(), P(), P(None, None, "col"))
     out_specs = (P(None, ("row", "col"), None), P(None, None, "col"))
+
+    def per_device(inverse_block, factor_cols, *rest):
+        held = (inverse_block.size + factor_cols.size) * 2 * row_parts * col_parts
+        fits = held <= REPLICATE_BYTES and col_parts == 2 and row_parts in (8, 16)
+        plan = replicated_plan if fits else grid_plan
+        return plan(inverse_block, factor_cols, *rest)
+
     return jax.shard_map(
         per_device, mesh=mesh, in_specs=in_specs, out_specs=out_specs, check_vma=False
     )

time: 250 us -> 92.3 us (0.37)
  waiting for transfers between devices: 188 us -> 39.9 us
  Pallas kernels: 0 us -> 28 us
  local copies, waits for them, and re-layouts: 16.7 us -> 0.02 us
  matrix products: 15.4 us -> 0 us
  between operations: 14.1 us -> 0.96 us
  starting transfers between devices: 8.53 us -> 21.6 us
  other arithmetic: 4.87 us -> 1.58 us
    psum x1 -> x0, waiting for transfers between devices: 137 us -> none  [per_device(): totals = lax.psum(jnp.stack(partial_list), ('row', 'col'))]
    all_gather x1 -> x0, waiting for transfers between devices: 48.8 us -> none  [per_device(): column_full = lax.all_gather(column_part, 'row', axis=1, tiled=True)]
    ppermute x0 -> x24, waiting for transfers between devices: none -> 39.9 us  [the longest x18 35.7 us: swap(): return lax.ppermute(value, axis, [(i, i ^ bit) for i in range(parts)])]
    pallas_call x0 -> x3, Pallas kernels: none -> 28 us  [the longest x1 11.4 us: replicated_plan(): call(functools.partial(last_kernel, dims, rows), 'other_half', 15 * 10 **...]
    ppermute x0 -> x24, starting transfers between devices: none -> 21.6 us  [the longest x18 20.8 us: swap(): return lax.ppermute(value, axis, [(i, i ^ bit) for i in range(parts)])]
    dot_general x14 -> x0, matrix products: 15.4 us -> none  [the longest x3 3.44 us: local_step(): jnp.dot(coupled.T, own.T, precision=highest)]
    all_to_all x1 -> x0, starting transfers between devices: 8.23 us -> none  [per_device(): lax.all_to_all(outgoing, 'row', split_axis=1, concat_axis=1, tiled=True)]
    unnamed x25 -> x10, local copies, waits for them, and re-layouts: 5.5 us -> 0.02 us
  transfers between devices with their start and end apart: 4 -> 24, of which waited for: 3 -> 12; matrix products, arithmetic and copies ran while one was open for 5% -> 2% of each run, Pallas kernels for 0% -> 18%
where the time goes in v2:
time: 92.3 us; the launch traced here: 92.1 us
  waiting for transfers between devices  39.9 us (43%)
  Pallas kernels  28 us (30%)
  starting transfers between devices  21.6 us (23%)
  other arithmetic  1.58 us (2%)
  between operations  0.96 us (1%)
    ppermute x18, waiting for transfers between devices, swap(): return lax.ppermute(value, axis, [(i, i ^ bit) for i in range(parts)])  35.7 us
    ppermute x18, starting transfers between devices, swap(): return lax.ppermute(value, axis, [(i, i ^ bit) for i in range(parts)])  20.8 us
    pallas_call x1, Pallas kernels, replicated_plan(): call(functools.partial(last_kernel, dims, rows), 'other_half', 15 * 10 **...  11.4 us
    pallas_call x1, Pallas kernels, replicated_plan(): call(functools.partial(place_kernel, (supers, width, rows, span, part)),...  9.25 us
    pallas_call x1, Pallas kernels, replicated_plan(): call(functools.partial(first_kernel, dims), 'own_half', 12 * 10 ** 9, out...  7.32 us
    ppermute x6, waiting for transfers between devices, across(): return lax.ppermute(value, 'col', [(0, 1), (1, 0)])  4.21 us
  transfers between devices with their start and end apart: 24, of which 12 were waited for; matrix products, arithmetic and copies ran while one was open for 2% of the time, Pallas kernels for 18%

profile of v2, /device:TPU:0, one launch (start us, length us, event | category | flops | bytes accessed | tf_op | source)
XLA Modules:
  0.0 92.1 jit_solution(11374706211840146271)
XLA Ops:
  0.6 0.0 copy-start
  0.6 5.1 %collective-permute-start.4 = (bf16[96,640]{1,0:T(8,128)(2,1)}, bf16[96,640]{1,0:T(8,128)(2,1)S(1)}, u32[]{:S(2)}, u32[]{:S(2)}) collective-permute-start(bf16[96,640]{1,0:T(8,128)(2,1)} %bitcast.45), channel_id=1, source_target_pairs={{0,24},{2,26},{4,28},{6,30},{8,16},{10,18},{12,20},{14,22},{16,8},... | collective-permute-start | bytes 368648 | tf_op jit(solution)/shard_map/ppermute | solution.py:121
  5.8 0.6 collective-permute-start
  6.4 3.8 %collective-permute-done.4 = bf16[96,640]{1,0:T(8,128)(2,1)S(1)} collective-permute-done((bf16[96,640]{1,0:T(8,128)(2,1)}, bf16[96,640]{1,0:T(8,128)(2,1)S(1)}, u32[]{:S(2)}, u32[]{:S(2)}) %collective-permute-start.4) | collective-permute-done | bytes 122912 | tf_op jit(solution)/shard_map/ppermute | solution.py:121
  10.2 6.1 %collective-permute-done.3 = bf16[96,640]{1,0:T(8,128)(2,1)S(1)} collective-permute-done((bf16[96,640]{1,0:T(8,128)(2,1)}, bf16[96,640]{1,0:T(8,128)(2,1)S(1)}, u32[]{:S(2)}, u32[]{:S(2)}) %collective-permute-start.3) | collective-permute-done | bytes 122912 | tf_op jit(solution)/shard_map/ppermute | solution.py:121
  16.4 1.6 %collective-permute-start.5 = (bf16[2,96,640]{2,1,0:T(8,128)(2,1)S(1)}, bf16[2,96,640]{2,1,0:T(8,128)(2,1)S(1)}, u32[]{:S(2)}, u32[]{:S(2)}) collective-permute-start(bf16[2,96,640]{2,1,0:T(8,128)(2,1)S(1)} %get-tuple-element.43), channel_id=1, source_target_pairs={{0,2},{2,0},{4,6},{6,4},{8,10},{10,8},{12,14},{14,12},{16,18},{18,... | collective-permute-start | bytes 737288 | tf_op jit(solution)/shard_map/ppermute | solution.py:121
  17.9 0.9 %fusion.1 = (bf16[1,2,96,640]{3,2,1,0:T(8,128)(2,1)S(1)}, bf16[2,96,640]{2,1,0:T(8,128)(2,1)S(1)}) fusion(bf16[1,96,640]{2,1,0:T(8,128)(2,1)S(1)} %bitcast.49, bf16[1,96,640]{2,1,0:T(8,128)(2,1)} %bitcast.48), kind=kLoop, calls=%fused_computation.9 | loop fusion | flops 122880 | bytes 737280 | tf_op jit(solution)/shard_map/stack | solution.py:321
  18.9 1.6 %collective-permute-start.2 = (bf16[2,96,640]{2,1,0:T(8,128)(2,1)S(1)}, bf16[2,96,640]{2,1,0:T(8,128)(2,1)S(1)}, u32[]{:S(2)}, u32[]{:S(2)}) collective-permute-start(bf16[2,96,640]{2,1,0:T(8,128)(2,1)S(1)} %get-tuple-element.45), channel_id=1, source_target_pairs={{0,4},{2,6},{4,0},{6,2},{8,12},{10,14},{12,8},{14,10},{16,20},{18,... | collective-permute-start | bytes 737288 | tf_op jit(solution)/shard_map/ppermute | solution.py:121
  20.5 2.5 %collective-permute-start.7 = (bf16[80,640]{1,0:T(8,128)(2,1)}, bf16[80,640]{1,0:T(8,128)(2,1)S(1)}, u32[]{:S(2)}, u32[]{:S(2)}) collective-permute-start(bf16[80,640]{1,0:T(8,128)(2,1)} %refs_6_.1), channel_id=1, source_target_pairs={{0,24},{2,26},{4,28},{6,30},{8,16},{10,18},{12,20},{14,22},{16,8},... | collective-permute-start | bytes 307208 | tf_op jit(solution)/shard_map/ppermute | solution.py:121
  22.9 0.0 collective-permute-start.6
  23.0 0.5 collective-permute-start.9
  23.5 3.7 %collective-permute-done.7 = bf16[80,640]{1,0:T(8,128)(2,1)S(1)} collective-permute-done((bf16[80,640]{1,0:T(8,128)(2,1)}, bf16[80,640]{1,0:T(8,128)(2,1)S(1)}, u32[]{:S(2)}, u32[]{:S(2)}) %collective-permute-start.7) | collective-permute-done | bytes 102432 | tf_op jit(solution)/shard_map/ppermute | solution.py:121
  27.1 4.0 %collective-permute-done.6 = bf16[80,640]{1,0:T(8,128)(2,1)S(1)} collective-permute-done((bf16[80,640]{1,0:T(8,128)(2,1)}, bf16[80,640]{1,0:T(8,128)(2,1)S(1)}, u32[]{:S(2)}, u32[]{:S(2)}) %collective-permute-start.6) | collective-permute-done | bytes 102432 | tf_op jit(solution)/shard_map/ppermute | solution.py:121
  31.2 0.6 collective-permute-start.10
  31.8 0.0 collective-permute-start.14
  31.8 0.5 collective-permute-start.1
  32.3 1.5 %collective-permute-start.8 = (bf16[2,96,640]{2,1,0:T(8,128)(2,1)S(1)}, bf16[2,96,640]{2,1,0:T(8,128)(2,1)S(1)}, u32[]{:S(2)}, u32[]{:S(2)}) collective-permute-start(bf16[2,96,640]{2,1,0:T(8,128)(2,1)S(1)} %collective-permute-done.2), channel_id=1, source_target_pairs={{0,2},{2,0},{4,6},{6,4},{8,10},{10,8},{12,14},{14,12},{16,18},{18,... | collective-permute-start | bytes 737288 | tf_op jit(solution)/shard_map/ppermute | solution.py:121
  33.8 2.6 %collective-permute-done.14 = bf16[80,640]{1,0:T(8,128)(2,1)S(1)} collective-permute-done((bf16[80,640]{1,0:T(8,128)(2,1)S(1)}, bf16[80,640]{1,0:T(8,128)(2,1)S(1)}, u32[]{:S(2)}, u32[]{:S(2)}) %collective-permute-start.14) | collective-permute-done | bytes 102432 | tf_op jit(solution)/shard_map/ppermute | solution.py:121
  36.4 1.6 %collective-permute-start.16 = (bf16[2,80,640]{2,1,0:T(8,128)(2,1)S(1)}, bf16[2,80,640]{2,1,0:T(8,128)(2,1)S(1)}, u32[]{:S(2)}, u32[]{:S(2)}) collective-permute-start(bf16[2,80,640]{2,1,0:T(8,128)(2,1)S(1)} %pad_maximum_fusion.7), channel_id=1, source_target_pairs={{0,4},{2,6},{4,0},{6,2},{8,12},{10,14},{12,8},{14,10},{16,20},{18,... | collective-permute-start | bytes 614408 | tf_op jit(solution)/shard_map/ppermute | solution.py:121
  38.0 1.7 %collective-permute-done.10 = bf16[2,96,640]{2,1,0:T(8,128)(2,1)S(1)} collective-permute-done((bf16[2,96,640]{2,1,0:T(8,128)(2,1)S(1)}, bf16[2,96,640]{2,1,0:T(8,128)(2,1)S(1)}, u32[]{:S(2)}, u32[]{:S(2)}) %collective-permute-start.10) | collective-permute-done | bytes 245792 | tf_op jit(solution)/shard_map/ppermute | solution.py:121
  39.7 0.1 pad_maximum_fusion.1.refs_3_
  39.9 0.1 collective-permute-start.12
  39.9 0.7 collective-permute-done.1
  40.6 3.3 %collective-permute-done.8 = bf16[2,96,640]{2,1,0:T(8,128)(2,1)S(1)} collective-permute-done((bf16[2,96,640]{2,1,0:T(8,128)(2,1)S(1)}, bf16[2,96,640]{2,1,0:T(8,128)(2,1)S(1)}, u32[]{:S(2)}, u32[]{:S(2)}) %collective-permute-start.8) | collective-permute-done | bytes 245792 | tf_op jit(solution)/shard_map/ppermute | solution.py:121
  43.9 0.1 pad_maximum_fusion.refs_2_
  44.1 0.1 collective-permute-start.11
  44.2 0.6 collective-permute-start.15
  44.8 1.5 %collective-permute-start.20 = (bf16[2,80,640]{2,1,0:T(8,128)(2,1)S(1)}, bf16[2,80,640]{2,1,0:T(8,128)(2,1)S(1)}, u32[]{:S(2)}, u32[]{:S(2)}) collective-permute-start(bf16[2,80,640]{2,1,0:T(8,128)(2,1)S(1)} %collective-permute-done.16), channel_id=1, source_target_pairs={{0,2},{2,0},{4,6},{6,4},{8,10},{10,8},{12,14},{14,12},{16,18},{18,... | collective-permute-start | bytes 614408 | tf_op jit(solution)/shard_map/ppermute | solution.py:121
  46.3 5.8 %collective-permute-done.15 = bf16[2,80,640]{2,1,0:T(8,128)(2,1)S(1)} collective-permute-done((bf16[2,80,640]{2,1,0:T(8,128)(2,1)S(1)}, bf16[2,80,640]{2,1,0:T(8,128)(2,1)S(1)}, u32[]{:S(2)}, u32[]{:S(2)}) %collective-permute-start.15) | collective-permute-done | bytes 204832 | tf_op jit(solution)/shard_map/ppermute | solution.py:121
  52.1 3.9 %collective-permute-done.20 = bf16[2,80,640]{2,1,0:T(8,128)(2,1)S(1)} collective-permute-done((bf16[2,80,640]{2,1,0:T(8,128)(2,1)S(1)}, bf16[2,80,640]{2,1,0:T(8,128)(2,1)S(1)}, u32[]{:S(2)}, u32[]{:S(2)}) %collective-permute-start.20) | collective-permute-done | bytes 204832 | tf_op jit(solution)/shard_map/ppermute | solution.py:121
  56.1 0.1 pad_maximum_fusion.2.refs_1_
  56.2 0.1 collective-permute-start.21
  56.3 0.5 collective-permute-start.13
  56.8 0.1 collective-permute-start.23
  56.8 1.9 %collective-permute-done.13.refs_7_ = bf16[80,640]{1,0:T(8,128)(2,1)S(1)} collective-permute-done((bf16[80,640]{1,0:T(8,128)(2,1)S(1)}, bf16[80,640]{1,0:T(8,128)(2,1)S(1)}, u32[]{:S(2)}, u32[]{:S(2)}) %collective-permute-start.13) | collective-permute-done | bytes 102432 | tf_op jit(solution)/shard_map/ppermute | solution.py:125
  58.7 1.5 %collective-permute-start.18 = (bf16[2,80,640]{2,1,0:T(8,128)(2,1)S(1)}, bf16[2,80,640]{2,1,0:T(8,128)(2,1)S(1)}, u32[]{:S(2)}, u32[]{:S(2)}) collective-permute-start(bf16[2,80,640]{2,1,0:T(8,128)(2,1)S(1)} %pad_maximum_fusion.6), channel_id=1, source_target_pairs={{0,4},{2,6},{4,0},{6,2},{8,12},{10,14},{12,8},{14,10},{16,20},{18,... | collective-permute-start | bytes 614408 | tf_op jit(solution)/shard_map/ppermute | solution.py:121
  60.3 0.0 collective-permute-done.12.refs_5_
  60.3 0.5 collective-permute-start.17
  60.8 0.0 collective-permute-done.11.refs_4_
  60.8 9.2 %place.1 = (bf16[3,512,1280]{2,1,0:T(8,128)(2,1)S(1)}, f32[3,40,512]{2,1,0:T(8,128)}) custom-call(s32[3,10]{1,0:T(4,128)S(1)} %copy-done.3, s32[3,10]{1,0:T(4,128)S(1)} %copy-done.4, bf16[4,2,96,640]{3,2,1,0:T(8,128)(2,1)S(1)} %pad_maximum_fusion.refs_2_, bf16[4,2,96,640]{3,2,1,0:T(8,128)(2,1)S(1)} %pad_maximum_fusion.1.refs_3_, ...), custom_call_target="tpu_custom_call" | custom-call | flops 4000000000 | bytes 8388608 | tf_op jit(solution)/shard_map/place/pallas_call | solution.py:330
  70.1 0.0 collective-permute-done.17
  70.1 0.6 collective-permute-start.19
  70.6 0.0 collective-permute-done.21.refs_2_
  70.6 7.3 %own_half.1 = (f32[512,512]{1,0:T(8,128)S(1)}, f32[512,512]{1,0:T(8,128)S(1)}, f32[512,512]{1,0:T(8,128)S(1)}, f32[256,512]{1,0:T(8,128)S(1)}, f32[512,256]{1,0:T(8,128)S(1)}) custom-call(bf16[3,512,1280]{2,1,0:T(8,128)(2,1)S(1)} %get-tuple-element.29.refs_0_, bf16[4,2,80,640]{3,2,1,0:T(8,128)(2,1)S(1)} %pad_maximum_fusion.2.refs_1_, ...), custom_call_target="tpu_custom_call" | custom-call | flops 12000000000 | bytes 8388608 | tf_op jit(solution)/shard_map/own_half/pallas_call | solution.py:350
  78.0 0.1 pad_maximum_fusion.3.refs_1_
  78.1 0.1 collective-permute-start.22
  78.2 2.3 %collective-permute-done.22.refs_2_ = bf16[4,2,80,640]{3,2,1,0:T(8,128)(2,1)S(1)} collective-permute-done((bf16[4,2,80,640]{3,2,1,0:T(8,128)(2,1)S(1)}, bf16[4,2,80,640]{3,2,1,0:T(8,128)(2,1)S(1)}, u32[]{:S(2)}, u32[]{:S(2)}) %collective-permute-start.22) | collective-permute-done | bytes 819232 | tf_op jit(solution)/shard_map/ppermute | solution.py:125
  80.5 11.4 %other_half.1 = f32[3,512,256]{2,1,0:T(8,128)} custom-call(bf16[3,512,1280]{2,1,0:T(8,128)(2,1)S(1)} %get-tuple-element.29.refs_0_, bf16[4,2,80,640]{3,2,1,0:T(8,128)(2,1)S(1)} %pad_maximum_fusion.3.refs_1_, bf16[4,2,80,640]{3,2,1,0:T(8,128)(2,1)S(1)} %collective-permute-done.22.refs_2_, bf16[2,512,512]{2,1,0:T(8,128)(2,1)S(1)} %copy-done.2, ...), custom_call_target="tpu_custom_call" | custom-call | flops 15000000512 | bytes 8388608 | tf_op jit(solution)/shard_map/other_half/pallas_call | solution.py:361
  (21 shorter events, 0.1 us)
Async XLA Ops:
  0.6 31.1 %copy-start = (bf16[80,640]{1,0:T(8,128)(2,1)S(1)}, bf16[80,640]{1,0:T(8,128)(2,1)}, u32[]{:S(2)}) copy-start(bf16[80,640]{1,0:T(8,128)(2,1)} %refs_6_.1) | copy-start | bytes 307204
  0.6 9.6 %collective-permute-start.4 = (bf16[96,640]{1,0:T(8,128)(2,1)}, bf16[96,640]{1,0:T(8,128)(2,1)S(1)}, u32[]{:S(2)}, u32[]{:S(2)}) collective-permute-start(bf16[96,640]{1,0:T(8,128)(2,1)} %bitcast.45), channel_id=1, source_target_pairs={{0,24},{2,26},{4,28},{6,30},{8,16},{10,18},{12,20},{14,22},{16,8},... | collective-permute-start | bytes 368648 | tf_op jit(solution)/shard_map/ppermute | solution.py:121
  5.8 10.6 %collective-permute-start.3 = (bf16[96,640]{1,0:T(8,128)(2,1)}, bf16[96,640]{1,0:T(8,128)(2,1)S(1)}, u32[]{:S(2)}, u32[]{:S(2)}) collective-permute-start(bf16[96,640]{1,0:T(8,128)(2,1)} %bitcast.46), channel_id=1, source_target_pairs={{0,16},{2,18},{4,20},{6,22},{8,24},{10,26},{12,28},{14,30},{16,0},... | collective-permute-start | bytes 368648 | tf_op jit(solution)/shard_map/ppermute | solution.py:121
  5.8 12.2 %collective-permute-start = (bf16[96,640]{1,0:T(8,128)(2,1)}, bf16[96,640]{1,0:T(8,128)(2,1)S(1)}, u32[]{:S(2)}, u32[]{:S(2)}) collective-permute-start(bf16[96,640]{1,0:T(8,128)(2,1)} %bitcast.47), channel_id=1, source_target_pairs={{0,8},{2,10},{4,12},{6,14},{8,0},{10,2},{12,4},{14,6},{16,24},{18,... | collective-permute-start | bytes 368648 | tf_op jit(solution)/shard_map/ppermute | solution.py:121
  16.4 14.8 %collective-permute-start.5 = (bf16[2,96,640]{2,1,0:T(8,128)(2,1)S(1)}, bf16[2,96,640]{2,1,0:T(8,128)(2,1)S(1)}, u32[]{:S(2)}, u32[]{:S(2)}) collective-permute-start(bf16[2,96,640]{2,1,0:T(8,128)(2,1)S(1)} %get-tuple-element.43), channel_id=1, source_target_pairs={{0,2},{2,0},{4,6},{6,4},{8,10},{10,8},{12,14},{14,12},{16,18},{18,... | collective-permute-start | bytes 737288 | tf_op jit(solution)/shard_map/ppermute | solution.py:121
  18.9 12.3 %collective-permute-start.2 = (bf16[2,96,640]{2,1,0:T(8,128)(2,1)S(1)}, bf16[2,96,640]{2,1,0:T(8,128)(2,1)S(1)}, u32[]{:S(2)}, u32[]{:S(2)}) collective-permute-start(bf16[2,96,640]{2,1,0:T(8,128)(2,1)S(1)} %get-tuple-element.45), channel_id=1, source_target_pairs={{0,4},{2,6},{4,0},{6,2},{8,12},{10,14},{12,8},{14,10},{16,20},{18,... | collective-permute-start | bytes 737288 | tf_op jit(solution)/shard_map/ppermute | solution.py:121
  20.5 6.7 %collective-permute-start.7 = (bf16[80,640]{1,0:T(8,128)(2,1)}, bf16[80,640]{1,0:T(8,128)(2,1)S(1)}, u32[]{:S(2)}, u32[]{:S(2)}) collective-permute-start(bf16[80,640]{1,0:T(8,128)(2,1)} %refs_6_.1), channel_id=1, source_target_pairs={{0,24},{2,26},{4,28},{6,30},{8,16},{10,18},{12,20},{14,22},{16,8},... | collective-permute-start | bytes 307208 | tf_op jit(solution)/shard_map/ppermute | solution.py:121
  22.9 8.2 %collective-permute-start.6 = (bf16[80,640]{1,0:T(8,128)(2,1)}, bf16[80,640]{1,0:T(8,128)(2,1)S(1)}, u32[]{:S(2)}, u32[]{:S(2)}) collective-permute-start(bf16[80,640]{1,0:T(8,128)(2,1)} %refs_6_.1), channel_id=1, source_target_pairs={{0,16},{2,18},{4,20},{6,22},{8,24},{10,26},{12,28},{14,30},{16,0},... | collective-permute-start | bytes 307208 | tf_op jit(solution)/shard_map/ppermute | solution.py:121
  23.0 15.1 %collective-permute-start.9 = (bf16[2,96,640]{2,1,0:T(8,128)(2,1)S(1)}, bf16[2,96,640]{2,1,0:T(8,128)(2,1)S(1)}, u32[]{:S(2)}, u32[]{:S(2)}) collective-permute-start(bf16[2,96,640]{2,1,0:T(8,128)(2,1)S(1)} %get-tuple-element.43), channel_id=1, source_target_pairs={{0,4},{2,6},{4,0},{6,2},{8,12},{10,14},{12,8},{14,10},{16,20},{18,... | collective-permute-start | bytes 737288 | tf_op jit(solution)/shard_map/ppermute | solution.py:121
  31.2 8.5 %collective-permute-start.10 = (bf16[2,96,640]{2,1,0:T(8,128)(2,1)S(1)}, bf16[2,96,640]{2,1,0:T(8,128)(2,1)S(1)}, u32[]{:S(2)}, u32[]{:S(2)}) collective-permute-start(bf16[2,96,640]{2,1,0:T(8,128)(2,1)S(1)} %collective-permute-done.5), channel_id=1, source_target_pairs={{0,4},{2,6},{4,0},{6,2},{8,12},{10,14},{12,8},{14,10},{16,20},{18,... | collective-permute-start | bytes 737288 | tf_op jit(solution)/shard_map/ppermute | solution.py:121
  31.8 4.7 %collective-permute-start.14 = (bf16[80,640]{1,0:T(8,128)(2,1)S(1)}, bf16[80,640]{1,0:T(8,128)(2,1)S(1)}, u32[]{:S(2)}, u32[]{:S(2)}) collective-permute-start(bf16[80,640]{1,0:T(8,128)(2,1)S(1)} %copy-done), channel_id=1, source_target_pairs={{0,8},{2,10},{4,12},{6,14},{8,0},{10,2},{12,4},{14,6},{16,24},{18,... | collective-permute-start | bytes 307208 | tf_op jit(solution)/shard_map/ppermute | solution.py:121
  31.8 8.9 %collective-permute-start.1 = (bf16[2,96,640]{2,1,0:T(8,128)(2,1)S(1)}, bf16[2,96,640]{2,1,0:T(8,128)(2,1)S(1)}, u32[]{:S(2)}, u32[]{:S(2)}) collective-permute-start(bf16[2,96,640]{2,1,0:T(8,128)(2,1)S(1)} %get-tuple-element.45), channel_id=1, source_target_pairs={{0,2},{2,0},{4,6},{6,4},{8,10},{10,8},{12,14},{14,12},{16,18},{18,... | collective-permute-start | bytes 737288 | tf_op jit(solution)/shard_map/ppermute | solution.py:121
  32.3 11.6 %collective-permute-start.8 = (bf16[2,96,640]{2,1,0:T(8,128)(2,1)S(1)}, bf16[2,96,640]{2,1,0:T(8,128)(2,1)S(1)}, u32[]{:S(2)}, u32[]{:S(2)}) collective-permute-start(bf16[2,96,640]{2,1,0:T(8,128)(2,1)S(1)} %collective-permute-done.2), channel_id=1, source_target_pairs={{0,2},{2,0},{4,6},{6,4},{8,10},{10,8},{12,14},{14,12},{16,18},{18,... | collective-permute-start | bytes 737288 | tf_op jit(solution)/shard_map/ppermute | solution.py:121
  36.4 8.3 %collective-permute-start.16 = (bf16[2,80,640]{2,1,0:T(8,128)(2,1)S(1)}, bf16[2,80,640]{2,1,0:T(8,128)(2,1)S(1)}, u32[]{:S(2)}, u32[]{:S(2)}) collective-permute-start(bf16[2,80,640]{2,1,0:T(8,128)(2,1)S(1)} %pad_maximum_fusion.7), channel_id=1, source_target_pairs={{0,4},{2,6},{4,0},{6,2},{8,12},{10,14},{12,8},{14,10},{16,20},{18,... | collective-permute-start | bytes 614408 | tf_op jit(solution)/shard_map/ppermute | solution.py:121
  39.9 20.4 %collective-permute-start.12 = (bf16[4,2,96,640]{3,2,1,0:T(8,128)(2,1)S(1)}, bf16[4,2,96,640]{3,2,1,0:T(8,128)(2,1)S(1)}, u32[]{:S(2)}, u32[]{:S(2)}) collective-permute-start(bf16[4,2,96,640]{3,2,1,0:T(8,128)(2,1)S(1)} %pad_maximum_fusion.1.refs_3_), channel_id=1, source_target_pairs={{0,1},{1,0},{2,3},{3,2},{4,5},{5,4},{6,7},{7,6},{8,9},{9,8},{10,11... | collective-permute-start | bytes 2949128 | tf_op jit(solution)/shard_map/ppermute | solution.py:125
  43.9 12.8 %copy-start.1 = (f32[3,512,256]{2,1,0:T(8,128)S(1)}, f32[3,512,256]{2,1,0:T(8,128)}, u32[]{:S(2)}) copy-start(f32[3,512,256]{2,1,0:T(8,128)} %refs_4_.1) | copy-start | bytes 4718596
  43.9 16.9 %copy-start.2 = (bf16[2,512,512]{2,1,0:T(8,128)(2,1)S(1)}, bf16[2,512,512]{2,1,0:T(8,128)(2,1)}, u32[]{:S(2)}) copy-start(bf16[2,512,512]{2,1,0:T(8,128)(2,1)} %refs_3_.3) | copy-start | bytes 3145732
  43.9 16.9 %copy-start.3 = (s32[3,10]{1,0:T(4,128)S(1)}, s32[3,10]{1,0:T(4,128)}, u32[]{:S(2)}) copy-start(s32[3,10]{1,0:T(4,128)} %refs_0_.1) | copy-start | bytes 364
  43.9 16.9 %copy-start.4 = (s32[3,10]{1,0:T(4,128)S(1)}, s32[3,10]{1,0:T(4,128)}, u32[]{:S(2)}) copy-start(s32[3,10]{1,0:T(4,128)} %refs_1_.1) | copy-start | bytes 364
  44.1 16.7 %collective-permute-start.11 = (bf16[4,2,96,640]{3,2,1,0:T(8,128)(2,1)S(1)}, bf16[4,2,96,640]{3,2,1,0:T(8,128)(2,1)S(1)}, u32[]{:S(2)}, u32[]{:S(2)}) collective-permute-start(bf16[4,2,96,640]{3,2,1,0:T(8,128)(2,1)S(1)} %pad_maximum_fusion.refs_2_), channel_id=1, source_target_pairs={{0,1},{1,0},{2,3},{3,2},{4,5},{5,4},{6,7},{7,6},{8,9},{9,8},{10,11... | collective-permute-start | bytes 2949128 | tf_op jit(solution)/shard_map/ppermute | solution.py:125
  44.2 7.9 %collective-permute-start.15 = (bf16[2,80,640]{2,1,0:T(8,128)(2,1)S(1)}, bf16[2,80,640]{2,1,0:T(8,128)(2,1)S(1)}, u32[]{:S(2)}, u32[]{:S(2)}) collective-permute-start(bf16[2,80,640]{2,1,0:T(8,128)(2,1)S(1)} %pad_maximum_fusion.7), channel_id=1, source_target_pairs={{0,2},{2,0},{4,6},{6,4},{8,10},{10,8},{12,14},{14,12},{16,18},{18,... | collective-permute-start | bytes 614408 | tf_op jit(solution)/shard_map/ppermute | solution.py:121
  44.8 11.3 %collective-permute-start.20 = (bf16[2,80,640]{2,1,0:T(8,128)(2,1)S(1)}, bf16[2,80,640]{2,1,0:T(8,128)(2,1)S(1)}, u32[]{:S(2)}, u32[]{:S(2)}) collective-permute-start(bf16[2,80,640]{2,1,0:T(8,128)(2,1)S(1)} %collective-permute-done.16), channel_id=1, source_target_pairs={{0,2},{2,0},{4,6},{6,4},{8,10},{10,8},{12,14},{14,12},{16,18},{18,... | collective-permute-start | bytes 614408 | tf_op jit(solution)/shard_map/ppermute | solution.py:121
  56.2 14.5 %collective-permute-start.21 = (bf16[4,2,80,640]{3,2,1,0:T(8,128)(2,1)S(1)}, bf16[4,2,80,640]{3,2,1,0:T(8,128)(2,1)S(1)}, u32[]{:S(2)}, u32[]{:S(2)}) collective-permute-start(bf16[4,2,80,640]{3,2,1,0:T(8,128)(2,1)S(1)} %pad_maximum_fusion.2.refs_1_), channel_id=1, source_target_pairs={{0,1},{1,0},{2,3},{3,2},{4,5},{5,4},{6,7},{7,6},{8,9},{9,8},{10,11... | collective-permute-start | bytes 2457608 | tf_op jit(solution)/shard_map/ppermute | solution.py:125
  56.3 2.5 %collective-permute-start.13 = (bf16[80,640]{1,0:T(8,128)(2,1)S(1)}, bf16[80,640]{1,0:T(8,128)(2,1)S(1)}, u32[]{:S(2)}, u32[]{:S(2)}) collective-permute-start(bf16[80,640]{1,0:T(8,128)(2,1)S(1)} %copy-done), channel_id=1, source_target_pairs={{0,1},{1,0},{2,3},{3,2},{4,5},{5,4},{6,7},{7,6},{8,9},{9,8},{10,11... | collective-permute-start | bytes 307208 | tf_op jit(solution)/shard_map/ppermute | solution.py:125
  56.8 21.4 %collective-permute-start.23 = (f32[3,512,256]{2,1,0:T(8,128)S(1)}, f32[3,512,256]{2,1,0:T(8,128)S(1)}, u32[]{:S(2)}, u32[]{:S(2)}) collective-permute-start(f32[3,512,256]{2,1,0:T(8,128)S(1)} %copy-done.1), channel_id=1, source_target_pairs={{0,1},{1,0},{2,3},{3,2},{4,5},{5,4},{6,7},{7,6},{8,9},{9,8},{10,11... | collective-permute-start | bytes 4718600 | tf_op jit(solution)/shard_map/ppermute | solution.py:125
  58.7 19.3 %collective-permute-start.18 = (bf16[2,80,640]{2,1,0:T(8,128)(2,1)S(1)}, bf16[2,80,640]{2,1,0:T(8,128)(2,1)S(1)}, u32[]{:S(2)}, u32[]{:S(2)}) collective-permute-start(bf16[2,80,640]{2,1,0:T(8,128)(2,1)S(1)} %pad_maximum_fusion.6), channel_id=1, source_target_pairs={{0,4},{2,6},{4,0},{6,2},{8,12},{10,14},{12,8},{14,10},{16,20},{18,... | collective-permute-start | bytes 614408 | tf_op jit(solution)/shard_map/ppermute | solution.py:121
  60.3 9.8 %collective-permute-start.17 = (bf16[2,80,640]{2,1,0:T(8,128)(2,1)S(1)}, bf16[2,80,640]{2,1,0:T(8,128)(2,1)S(1)}, u32[]{:S(2)}, u32[]{:S(2)}) collective-permute-start(bf16[2,80,640]{2,1,0:T(8,128)(2,1)S(1)} %pad_maximum_fusion.6), channel_id=1, source_target_pairs={{0,2},{2,0},{4,6},{6,4},{8,10},{10,8},{12,14},{14,12},{16,18},{18,... | collective-permute-start | bytes 614408 | tf_op jit(solution)/shard_map/ppermute | solution.py:121
  70.1 7.9 %collective-permute-start.19 = (bf16[2,80,640]{2,1,0:T(8,128)(2,1)S(1)}, bf16[2,80,640]{2,1,0:T(8,128)(2,1)S(1)}, u32[]{:S(2)}, u32[]{:S(2)}) collective-permute-start(bf16[2,80,640]{2,1,0:T(8,128)(2,1)S(1)} %collective-permute-done.17), channel_id=1, source_target_pairs={{0,4},{2,6},{4,0},{6,2},{8,12},{10,14},{12,8},{14,10},{16,20},{18,... | collective-permute-start | bytes 614408 | tf_op jit(solution)/shard_map/ppermute | solution.py:121
  78.1 2.4 %collective-permute-start.22 = (bf16[4,2,80,640]{3,2,1,0:T(8,128)(2,1)S(1)}, bf16[4,2,80,640]{3,2,1,0:T(8,128)(2,1)S(1)}, u32[]{:S(2)}, u32[]{:S(2)}) collective-permute-start(bf16[4,2,80,640]{3,2,1,0:T(8,128)(2,1)S(1)} %pad_maximum_fusion.3.refs_1_), channel_id=1, source_target_pairs={{0,1},{1,0},{2,3},{3,2},{4,5},{5,4},{6,7},{7,6},{8,9},{9,8},{10,11... | collective-permute-start | bytes 2457608 | tf_op jit(solution)/shard_map/ppermute | solution.py:125

commit v3 on v2

--- a/solution.py
+++ b/solution.py
@@ -125,14 +125,6 @@
     return lax.ppermute(value, "col", [(0, 1), (1, 0)])
 
 
-def along_line(own, row_parts):
-    return [own] + [swap(own, "row", 4 * k, row_parts) for k in range(1, row_parts // 4)]
-
-
-def over_plane(own, row_parts):
-    return swap(own, "row", 1, row_parts), swap(own, "row", 2, row_parts)
-
-
 def after(values, *events):
     return lax.optimization_barrier((values, events))[0]
 
@@ -165,43 +157,32 @@
 def place_kernel(dims, *refs):
     supers, width, rows, span, part = dims
     occ_ref, block_ref = refs[:2]
-    f_refs, z_ref, z_other_ref, link_ref = refs[2:6], refs[6], refs[7], refs[8]
-    pt, col_out, f_all, sem = refs[9:]
+    f_refs, pt = refs[2:6], refs[6]
     row, col = lax.axis_index("row"), lax.axis_index("col")
-    copies = []
+    per_side = span // 128
     for side in range(2):
-        for wave in range(2):
-            source = f_refs[2 * side + wave]
-            for j in range(4):
-                for i in range(source.shape[1]):
-                    owner = owner_of(row, wave, source.shape[1], j, i)
-                    target = col if side == 0 else 1 - col
-                    copies.append(pltpu.make_async_copy(source.at[j, i], f_all.at[target, owner], sem))
-    for copy in copies:
-        copy.start()
-    for copy in copies:
-        copy.wait()
-    per_side = span // 128
+        target = col if side == 0 else 1 - col
+        for s in range(supers):
+            for b in range(per_side):
+                lanes = pl.ds(pl.multiple_of(block_ref[s, target * per_side + b] * 128, 128), 128)
+                for wave in range(2):
+                    source = f_refs[2 * side + wave]
+                    for j in range(4):
+                        for i in range(source.shape[1]):
+                            first = owner_of(row, wave, source.shape[1], j, i) * part
+                            pt[s, pl.ds(pl.multiple_of(first, part), part), lanes] = source[
+                                j, i, s * part : (s + 1) * part, b * 128 : (b + 1) * 128
+                            ]
     for s in range(supers):
         for b in range(2 * per_side):
-            lane = (b % per_side) * 128
-            blk = f_all[b // per_side, :, s * part : (s + 1) * part, lane : lane + 128].reshape(width, 128)
-            keep = jnp.where(occ_ref[s, b] > 0, blk, jnp.zeros_like(blk))
-            pt[s, :, pl.ds(pl.multiple_of(block_ref[s, b] * 128, 128), 128)] = keep
-    local_rows = z_ref.shape[0]
-    tile = local_rows // 2
-    mine, theirs = z_ref[...], z_other_ref[...]
-    z_own = jnp.concatenate([jnp.where(col == 0, mine, theirs), jnp.where(col == 0, theirs, mine)], axis=1)
-    previous = None
-    for s in range(supers):
-        current = -nt(z_own, pt[s])
-        if s > 0:
-            current = current - nn2(split2(previous), link_ref[s - 1])
-        col_out[s] = jnp.where(col == 0, current[:tile], current[tile:])
-        previous = current
-
-
-def add_rows(wave, dims, col, row, pt, z_refs, link_ref, sums, scratch):
+
+            @pl.when(occ_ref[s, b] == 0)
+            def _():
+                lanes = pl.ds(pl.multiple_of(block_ref[s, b] * 128, 128), 128)
+                pt[s, :, lanes] = jnp.zeros((width, 128), bf16)
+
+
+def add_rows(wave, skip, dims, col, row, pt, z_refs, link_ref, sums, scratch):
     width, span = dims
     z_all, c0h, c0l, c1h, c1l, p1h, p1l, c2h, c2l, tmp, sem = scratch
     half_rows = z_all.shape[0]
@@ -210,13 +191,13 @@
     for side in range(2):
         target = col if side == 0 else 1 - col
         source = z_refs[side]
-        local_rows = source.shape[2]
+        local_rows = source.shape[2] - skip
         for j in range(4):
             for i in range(source.shape[1]):
                 place = owner_of(row, wave, source.shape[1], j, i) % (half_rows // local_rows)
                 copies.append(
                     pltpu.make_async_copy(
-                        source.at[j, i],
+                        source.at[j, i, pl.ds(skip, local_rows)],
                         z_all.at[
                             pl.ds(pl.multiple_of(place * local_rows, local_rows), local_rows),
                             pl.ds(pl.multiple_of(target * span, span), span),
@@ -253,9 +234,23 @@
         total[...] = term if wave == 0 else total[...] + term
 
 
-def first_kernel(dims, *refs):
+def first_kernel(dims, skip, *refs):
     pt, z_refs, link_ref = refs[0], refs[1:3], refs[3]
-    add_rows(0, dims, lax.axis_index("col"), lax.axis_index("row"), pt, z_refs, link_ref, refs[4:9], refs[9:])
+    sums, col_out, scratch = refs[4:9], refs[9], refs[10:]
+    col, row = lax.axis_index("col"), lax.axis_index("row")
+    add_rows(0, skip, dims, col, row, pt, z_refs, link_ref, sums, scratch)
+    z_all, c0h, c0l, c1h, c1l = scratch[:5]
+    tile = col_out.shape[1]
+    place = row % (z_all.shape[0] // (2 * tile))
+    own = pl.ds(pl.multiple_of(place * 2 * tile, 2 * tile), 2 * tile)
+    cols1 = (c1h[own, :], c1l[own, :])
+    mine = [
+        c0h[own, :].astype(f32) + c0l[own, :].astype(f32),
+        cols1[0].astype(f32) + cols1[1].astype(f32),
+        -(nt(z_all[own, :], pt[2]) + nn2(cols1, link_ref[1])),
+    ]
+    for s, value in enumerate(mine):
+        col_out[s] = jnp.where(col == 0, value[:tile], value[tile:])
 
 
 def last_kernel(dims, rows, *refs):
@@ -266,7 +261,7 @@
     half_w = width // 2
     for total, value in zip(sums, before):
         total[...] = value[...]
-    add_rows(1, dims, col, lax.axis_index("row"), pt, z_refs, link_ref, sums, scratch)
+    add_rows(1, 0, dims, col, lax.axis_index("row"), pt, z_refs, link_ref, sums, scratch)
     s0, u1, s1, n2, s2 = sums
     scale = 1.0 / rows
     c_rows = pl.ds(pl.multiple_of(col * half_w, half_w), half_w)
@@ -306,38 +301,49 @@
             **kwargs,
         )
 
+    outer = row_parts // 4
+    x = lambda value: swap(value, "row", 1, row_parts)
+    y = lambda value: swap(value, "row", 2, row_parts)
+    line = lambda value, k: swap(value, "row", 4 * k, row_parts)
+
+    def far(over_x, over_y, i):
+        return x(over_y) if i % 2 == 0 else y(over_x)
+
+    def late_wave(parts, *events):
+        own = after(jnp.stack(parts), *events)
+        return own, x(own), y(own)
+
     f_own = jnp.transpose(factor_cols, (0, 2, 1)).reshape(supers * part, span)
-    f_parts = along_line(f_own, row_parts)
-    f_a, f_b = jnp.stack(f_parts[:count]), jnp.stack(f_parts[count:])
-    f_ax, f_ay = over_plane(f_a, row_parts)
-    f_bx, f_by = over_plane(f_b, row_parts)
-    z_cross = across(inverse_block)
-    z_parts = along_line(after(inverse_block, f_b), row_parts)
-    z_a, z_b = jnp.stack(z_parts[:count]), jnp.stack(z_parts[count:])
-    f_ay, f_bx = after((f_ay, f_bx), z_b)
-    f_far_a, f_far_b = swap(f_ay, "row", 1, row_parts), swap(f_bx, "row", 2, row_parts)
-    z_a = after(z_a, f_ay, f_bx)
-    z_ax, z_ay = over_plane(z_a, row_parts)
-    f_mine = [jnp.stack([f_a, f_ax, f_ay, f_far_a]), jnp.stack([f_b, f_bx, f_by, f_far_b])]
-    f_all = f_mine + [across(v) for v in f_mine]
-    z_b = after(z_b, z_ax, z_ay)
-    z_bx, z_by = over_plane(z_b, row_parts)
-    z_far_a = swap(z_ay, "row", 1, row_parts)
-    z_first = jnp.stack([z_a, z_ax, z_ay, z_far_a])
-    z_first_other = across(z_first)
+    f_late = [line(f_own, k) for k in range(count, outer)]
+    own = jnp.concatenate([f_own, inverse_block], axis=0)
+    early = []
+    for k in range(count):
+        value = own if k == 0 else line(own, k)
+        value = after(value, *early[-1][1:3]) if k else value
+        over_x, over_y = x(value), y(value)
+        early.append([value, over_x, over_y, far(over_x, over_y, k)])
+    first = jnp.stack([jnp.stack([p[j] for p in early]) for j in range(4)])
+    first_other = across(first)
+    block = after(inverse_block, *f_late, *early[-1][1:3])
+    z_late = [line(block, k) for k in range(count, outer)]
+    f_b, f_bx, f_by = late_wave(f_late, *early[-1][1:3], early[0][3])
+    f_bx, f_by = after((f_bx, f_by), *z_late)
+    f_far = jnp.stack([far(f_bx[i], f_by[i], i) for i in range(count)])
+    f_last = jnp.stack([f_b, f_bx, f_by, f_far])
+    f_last_other = across(f_last)
+    z_b, z_bx, z_by = late_wave(z_late, f_bx, f_by)
     diag_other = across(diag_inverse)
 
-    pt, columns = call(
+    pt = call(
         functools.partial(place_kernel, (supers, width, rows, span, part)),
-        "place", 4 * 10**9,
-        out_shape=(shape((supers, width, rows), bf16), shape((supers, local_rows // 2, width), f32)),
-        in_specs=[smem] * 2 + [any_spec] * 4 + [vmem] * 3,
-        out_specs=(vmem, vmem),
-        scratch_shapes=[pltpu.VMEM((2, row_parts, supers * part, span), bf16), pltpu.SemaphoreType.DMA],
-    )(occupancy, row_block, *f_all, inverse_block, z_cross, coupling)
-
-    z_bx, pt = after((z_bx, pt), pt)
-    z_far_b = swap(z_bx, "row", 2, row_parts)
+        "place", 2 * 10**9,
+        out_shape=shape((supers, width, rows), bf16),
+        in_specs=[smem] * 2 + [vmem] * 4,
+        out_specs=vmem,
+    )(occupancy, row_block, first, f_last, first_other, f_last_other)
+
+    z_bx, z_by, pt = after((z_bx, z_by, pt), pt)
+    z_far = jnp.stack([far(z_bx[i], z_by[i], i) for i in range(count)])
     dims = (width, span)
     half_rows, half_w = rows // 2, width // 2
     sum_shapes = [(width, width), (width, width), (width, width), (half_w, width), (width, half_w)]
@@ -347,20 +353,20 @@
         + [pltpu.VMEM((half_rows, half_w), bf16)] * 2
         + [pltpu.VMEM((half_rows, width), f32), pltpu.SemaphoreType.DMA]
     )
-    sums = call(
-        functools.partial(first_kernel, dims),
-        "own_half", 12 * 10**9,
-        out_shape=tuple(shape(v, f32) for v in sum_shapes),
+    *sums, columns = call(
+        functools.partial(first_kernel, dims, supers * part),
+        "own_half", 8 * 10**9,
+        out_shape=tuple(shape(v, f32) for v in sum_shapes) + (shape((supers, local_rows // 2, width), f32),),
         in_specs=[vmem] + [any_spec] * 2 + [vmem],
-        out_specs=(vmem,) * 5,
+        out_specs=(vmem,) * 6,
         scratch_shapes=scratch,
-    )(pt, z_first, z_first_other, coupling)
-    z_far_b, *sums = after((z_far_b, *sums), sums[0])
-    z_last = jnp.stack([z_b, z_bx, z_by, z_far_b])
+    )(pt, first, first_other, coupling)
+    z_far, *sums = after((z_far, *sums), sums[0])
+    z_last = jnp.stack([z_b, z_bx, z_by, z_far])
     z_last_other = across(z_last)
     diagonals = call(
         functools.partial(last_kernel, dims, rows),
-        "other_half", 15 * 10**9,
+        "other_half", 12 * 10**9,
         out_shape=shape((supers, width, half_w), f32),
         in_specs=[vmem] + [any_spec] * 2 + [vmem] * 8,
         out_specs=vmem,

time: 92.3 us -> 74.9 us (0.81)
  waiting for transfers between devices: 39.9 us -> 24.3 us
  Pallas kernels: 28 us -> 21.7 us
  starting transfers between devices: 21.6 us -> 25.7 us
    ppermute x18 -> x19, waiting for transfers between devices: 35.7 us -> 21.5 us  [swap(): return lax.ppermute(value, axis, [(i, i ^ bit) for i in range(parts)])]
    pallas_call x1, Pallas kernels: 9.25 us -> 2.08 us  [replicated_plan(): call(functools.partial(place_kernel, (supers, width, rows, span, part)),...]
    ppermute x18 -> x19, starting transfers between devices: 20.8 us -> 25.4 us  [swap(): return lax.ppermute(value, axis, [(i, i ^ bit) for i in range(parts)])]
    ppermute x6 -> x4, waiting for transfers between devices: 4.21 us -> 2.86 us  [across(): return lax.ppermute(value, 'col', [(0, 1), (1, 0)])]
    another operation x8 -> x12, other arithmetic: 1.58 us -> 1.88 us  [the longest x6 1.5 us: replicated_plan(): first = jnp.stack([jnp.stack([p[j] for p in early]) for j in range(4)])]
  transfers between devices with their start and end apart: 24 -> 23, of which waited for: 12 -> 11; matrix products, arithmetic and copies ran while one was open for 2% -> 1% of each run, Pallas kernels for 18% -> 14%
where the time goes in v3:
time: 74.9 us; the launch traced here: 74.7 us
  starting transfers between devices  25.7 us (34%)
  waiting for transfers between devices  24.3 us (32%)
  Pallas kernels  21.7 us (29%)
  other arithmetic  1.88 us (3%)
  between operations  1.03 us (1%)
    ppermute x19, starting transfers between devices, swap(): return lax.ppermute(value, axis, [(i, i ^ bit) for i in range(parts)])  25.4 us
    ppermute x19, waiting for transfers between devices, swap(): return lax.ppermute(value, axis, [(i, i ^ bit) for i in range(parts)])  21.5 us
    pallas_call x1, Pallas kernels, replicated_plan(): call(functools.partial(last_kernel, dims, rows), 'other_half', 12 * 10 **...  11.5 us
    pallas_call x1, Pallas kernels, replicated_plan(): call(functools.partial(first_kernel, dims, supers * part), 'own_half', 8...  8.13 us
    ppermute x4, waiting for transfers between devices, across(): return lax.ppermute(value, 'col', [(0, 1), (1, 0)])  2.86 us
    pallas_call x1, Pallas kernels, replicated_plan(): call(functools.partial(place_kernel, (supers, width, rows, span, part)),...  2.08 us
  transfers between devices with their start and end apart: 23, of which 11 were waited for; matrix products, arithmetic and copies ran while one was open for 1% of the time, Pallas kernels for 14%

profile of v3, /device:TPU:0, one launch (start us, length us, event | category | flops | bytes accessed | tf_op | source)
XLA Modules:
  0.0 74.7 jit_solution(8053814147780332396)
XLA Ops:
  0.6 1.0 %fusion = (bf16[1,176,640]{2,1,0:T(8,128)(2,1)S(1)}, bf16[176,640]{1,0:T(8,128)(2,1)S(1)}) fusion(bf16[80,640]{1,0:T(8,128)(2,1)} %param.6, bf16[96,640]{1,0:T(8,128)(2,1)} %bitcast.59), kind=kLoop, calls=%fused_computation.16 | loop fusion | flops 450560 | bytes 675840 | tf_op jit(solution)/shard_map/stack | solution.py:325
  1.7 3.1 %collective-permute-start.2 = (bf16[176,640]{1,0:T(8,128)(2,1)S(1)}, bf16[176,640]{1,0:T(8,128)(2,1)S(1)}, u32[]{:S(2)}, u32[]{:S(2)}) collective-permute-start(bf16[176,640]{1,0:T(8,128)(2,1)S(1)} %get-tuple-element.45), channel_id=1, source_target_pairs={{0,8},{2,10},{4,12},{6,14},{8,0},{10,2},{12,4},{14,6},{16,24},{18,... | collective-permute-start | bytes 675848 | tf_op jit(solution)/shard_map/ppermute | solution.py:121
  4.8 1.5 %collective-permute-start.3 = (bf16[176,640]{1,0:T(8,128)(2,1)S(1)}, bf16[176,640]{1,0:T(8,128)(2,1)S(1)}, u32[]{:S(2)}, u32[]{:S(2)}) collective-permute-start(bf16[176,640]{1,0:T(8,128)(2,1)S(1)} %get-tuple-element.45), channel_id=1, source_target_pairs={{0,2},{2,0},{4,6},{6,4},{8,10},{10,8},{12,14},{14,12},{16,18},{18,... | collective-permute-start | bytes 675848 | tf_op jit(solution)/shard_map/ppermute | solution.py:121
  6.2 1.5 %collective-permute-start.4 = (bf16[176,640]{1,0:T(8,128)(2,1)S(1)}, bf16[176,640]{1,0:T(8,128)(2,1)S(1)}, u32[]{:S(2)}, u32[]{:S(2)}) collective-permute-start(bf16[176,640]{1,0:T(8,128)(2,1)S(1)} %get-tuple-element.45), channel_id=1, source_target_pairs={{0,4},{2,6},{4,0},{6,2},{8,12},{10,14},{12,8},{14,10},{16,20},{18,... | collective-permute-start | bytes 675848 | tf_op jit(solution)/shard_map/ppermute | solution.py:121
  7.8 2.6 %collective-permute-start = (bf16[96,640]{1,0:T(8,128)(2,1)}, bf16[96,640]{1,0:T(8,128)(2,1)S(1)}, u32[]{:S(2)}, u32[]{:S(2)}) collective-permute-start(bf16[96,640]{1,0:T(8,128)(2,1)} %bitcast.60), channel_id=1, source_target_pairs={{0,16},{2,18},{4,20},{6,22},{8,24},{10,26},{12,28},{14,30},{16,0},... | collective-permute-start | bytes 368648 | tf_op jit(solution)/shard_map/ppermute | solution.py:121
  10.4 0.2 collective-permute-start.1
  10.6 1.1 %collective-permute-done.3 = bf16[176,640]{1,0:T(8,128)(2,1)S(1)} collective-permute-done((bf16[176,640]{1,0:T(8,128)(2,1)S(1)}, bf16[176,640]{1,0:T(8,128)(2,1)S(1)}, u32[]{:S(2)}, u32[]{:S(2)}) %collective-permute-start.3) | collective-permute-done | bytes 225312 | tf_op jit(solution)/shard_map/ppermute | solution.py:121
  11.7 1.2 %collective-permute-done.4 = bf16[176,640]{1,0:T(8,128)(2,1)S(1)} collective-permute-done((bf16[176,640]{1,0:T(8,128)(2,1)S(1)}, bf16[176,640]{1,0:T(8,128)(2,1)S(1)}, u32[]{:S(2)}, u32[]{:S(2)}) %collective-permute-start.4) | collective-permute-done | bytes 225312 | tf_op jit(solution)/shard_map/ppermute | solution.py:121
  12.9 0.5 collective-permute-start.5
  13.5 2.0 %collective-permute-start.6 = (bf16[176,640]{1,0:T(8,128)(2,1)S(1)}, bf16[176,640]{1,0:T(8,128)(2,1)S(1)}, u32[]{:S(2)}, u32[]{:S(2)}) collective-permute-start(bf16[176,640]{1,0:T(8,128)(2,1)S(1)} %collective-permute-done.2), channel_id=1, source_target_pairs={{0,4},{2,6},{4,0},{6,2},{8,12},{10,14},{12,8},{14,10},{16,20},{18,... | collective-permute-start | bytes 675848 | tf_op jit(solution)/shard_map/ppermute | solution.py:121
  15.5 1.0 %collective-permute-start.9 = (bf16[176,640]{1,0:T(8,128)(2,1)S(1)}, bf16[176,640]{1,0:T(8,128)(2,1)S(1)}, u32[]{:S(2)}, u32[]{:S(2)}) collective-permute-start(bf16[176,640]{1,0:T(8,128)(2,1)S(1)} %collective-permute-done.4), channel_id=1, source_target_pairs={{0,2},{2,0},{4,6},{6,4},{8,10},{10,8},{12,14},{14,12},{16,18},{18,... | collective-permute-start | bytes 675848 | tf_op jit(solution)/shard_map/ppermute | solution.py:121
  16.5 3.2 %collective-permute-done = bf16[96,640]{1,0:T(8,128)(2,1)S(1)} collective-permute-done((bf16[96,640]{1,0:T(8,128)(2,1)}, bf16[96,640]{1,0:T(8,128)(2,1)S(1)}, u32[]{:S(2)}, u32[]{:S(2)}) %collective-permute-start) | collective-permute-done | bytes 122912 | tf_op jit(solution)/shard_map/ppermute | solution.py:121
  19.7 0.1 maximum_bitcast_fusion
  19.8 1.3 %collective-permute-done.5 = bf16[176,640]{1,0:T(8,128)(2,1)S(1)} collective-permute-done((bf16[176,640]{1,0:T(8,128)(2,1)S(1)}, bf16[176,640]{1,0:T(8,128)(2,1)S(1)}, u32[]{:S(2)}, u32[]{:S(2)}) %collective-permute-start.5) | collective-permute-done | bytes 225312 | tf_op jit(solution)/shard_map/ppermute | solution.py:121
  21.1 2.2 %collective-permute-start.8 = (bf16[80,640]{1,0:T(8,128)(2,1)S(1)}, bf16[80,640]{1,0:T(8,128)(2,1)S(1)}, u32[]{:S(2)}, u32[]{:S(2)}) collective-permute-start(bf16[80,640]{1,0:T(8,128)(2,1)S(1)} %copy-done.4), channel_id=1, source_target_pairs={{0,24},{2,26},{4,28},{6,30},{8,16},{10,18},{12,20},{14,22},{16,8},... | collective-permute-start | bytes 307208 | tf_op jit(solution)/shard_map/ppermute | solution.py:121
  23.4 0.4 collective-permute-start.7
  23.8 1.9 %collective-permute-start.10 = (bf16[2,96,640]{2,1,0:T(8,128)(2,1)S(1)}, bf16[2,96,640]{2,1,0:T(8,128)(2,1)S(1)}, u32[]{:S(2)}, u32[]{:S(2)}) collective-permute-start(bf16[2,96,640]{2,1,0:T(8,128)(2,1)S(1)} %pad_maximum_fusion.3), channel_id=1, source_target_pairs={{0,2},{2,0},{4,6},{6,4},{8,10},{10,8},{12,14},{14,12},{16,18},{18,... | collective-permute-start | bytes 737288 | tf_op jit(solution)/shard_map/ppermute | solution.py:121
  25.7 1.9 %collective-permute-start.11 = (bf16[2,96,640]{2,1,0:T(8,128)(2,1)S(1)}, bf16[2,96,640]{2,1,0:T(8,128)(2,1)S(1)}, u32[]{:S(2)}, u32[]{:S(2)}) collective-permute-start(bf16[2,96,640]{2,1,0:T(8,128)(2,1)S(1)} %pad_maximum_fusion.3), channel_id=1, source_target_pairs={{0,4},{2,6},{4,0},{6,2},{8,12},{10,14},{12,8},{14,10},{16,20},{18,... | collective-permute-start | bytes 737288 | tf_op jit(solution)/shard_map/ppermute | solution.py:121
  27.6 0.2 collective-permute-start.14
  27.7 0.1 maximum_bitcast_fusion.2
  27.8 0.1 maximum_bitcast_fusion.1
  27.8 6.5 %collective-permute-done.14 = bf16[176,640]{1,0:T(8,128)(2,1)S(1)} collective-permute-done((bf16[176,640]{1,0:T(8,128)(2,1)S(1)}, bf16[176,640]{1,0:T(8,128)(2,1)S(1)}, u32[]{:S(2)}, u32[]{:S(2)}) %collective-permute-start.14) | collective-permute-done | bytes 225312 | tf_op jit(solution)/shard_map/ppermute | solution.py:121
  34.3 0.1 maximum_bitcast_fusion.3
  34.4 0.3 pad_maximum_fusion.refs_2_.refs_1_
  34.6 0.0 copy-start.2
  34.6 0.0 copy-start
  34.7 0.0 copy-start.1
  34.7 0.1 collective-permute-start.17
  34.8 1.9 %collective-permute-start.16 = (bf16[96,640]{1,0:T(8,128)(2,1)S(1)}, bf16[96,640]{1,0:T(8,128)(2,1)S(1)}, u32[]{:S(2)}, u32[]{:S(2)}) collective-permute-start(bf16[96,640]{1,0:T(8,128)(2,1)S(1)} %slice_bitcast_fusion), channel_id=1, source_target_pairs={{0,4},{2,6},{4,0},{6,2},{8,12},{10,14},{12,8},{14,10},{16,20},{18,... | collective-permute-start | bytes 368648 | tf_op jit(solution)/shard_map/ppermute | solution.py:121
  36.8 0.8 %collective-permute-start.15 = (bf16[96,640]{1,0:T(8,128)(2,1)S(1)}, bf16[96,640]{1,0:T(8,128)(2,1)S(1)}, u32[]{:S(2)}, u32[]{:S(2)}) collective-permute-start(bf16[96,640]{1,0:T(8,128)(2,1)S(1)} %slice_bitcast_fusion.1), channel_id=1, source_target_pairs={{0,2},{2,0},{4,6},{6,4},{8,10},{10,8},{12,14},{14,12},{16,18},{18,... | collective-permute-start | bytes 368648 | tf_op jit(solution)/shard_map/ppermute | solution.py:121
  37.6 3.1 %collective-permute-done.16 = bf16[96,640]{1,0:T(8,128)(2,1)S(1)} collective-permute-done((bf16[96,640]{1,0:T(8,128)(2,1)S(1)}, bf16[96,640]{1,0:T(8,128)(2,1)S(1)}, u32[]{:S(2)}, u32[]{:S(2)}) %collective-permute-start.16) | collective-permute-done | bytes 122912 | tf_op jit(solution)/shard_map/ppermute | solution.py:121
  40.7 1.5 %collective-permute-done.15 = bf16[96,640]{1,0:T(8,128)(2,1)S(1)} collective-permute-done((bf16[96,640]{1,0:T(8,128)(2,1)S(1)}, bf16[96,640]{1,0:T(8,128)(2,1)S(1)}, u32[]{:S(2)}, u32[]{:S(2)}) %collective-permute-start.15) | collective-permute-done | bytes 122912 | tf_op jit(solution)/shard_map/ppermute | solution.py:121
  42.3 0.1 pad_maximum_fusion.1.refs_3_
  42.4 0.1 collective-permute-start.18
  42.6 0.0 copy-start.3
  42.6 0.8 %collective-permute-start.12 = (bf16[2,80,640]{2,1,0:T(8,128)(2,1)S(1)}, bf16[2,80,640]{2,1,0:T(8,128)(2,1)S(1)}, u32[]{:S(2)}, u32[]{:S(2)}) collective-permute-start(bf16[2,80,640]{2,1,0:T(8,128)(2,1)S(1)} %pad_maximum_fusion.5), channel_id=1, source_target_pairs={{0,2},{2,0},{4,6},{6,4},{8,10},{10,8},{12,14},{14,12},{16,18},{18,... | collective-permute-start | bytes 614408 | tf_op jit(solution)/shard_map/ppermute | solution.py:121
  43.4 1.1 %collective-permute-start.13 = (bf16[2,80,640]{2,1,0:T(8,128)(2,1)S(1)}, bf16[2,80,640]{2,1,0:T(8,128)(2,1)S(1)}, u32[]{:S(2)}, u32[]{:S(2)}) collective-permute-start(bf16[2,80,640]{2,1,0:T(8,128)(2,1)S(1)} %pad_maximum_fusion.5), channel_id=1, source_target_pairs={{0,4},{2,6},{4,0},{6,2},{8,12},{10,14},{12,8},{14,10},{16,20},{18,... | collective-permute-start | bytes 614408 | tf_op jit(solution)/shard_map/ppermute | solution.py:121
  44.5 0.5 collective-permute-done.18.refs_5_
  45.1 2.1 %place.1.refs_0_ = bf16[3,512,1280]{2,1,0:T(8,128)(2,1)S(1)} custom-call(s32[3,10]{1,0:T(4,128)S(1)} %copy-done, s32[3,10]{1,0:T(4,128)S(1)} %copy-done.1, bf16[4,2,176,640]{3,2,1,0:T(8,128)(2,1)S(1)} %pad_maximum_fusion.refs_2_.refs_1_, bf16[4,2,96,640]{3,2,1,0:T(8,128)(2,1)S(1)} %pad_maximum_fusion.1.refs_3_, ...), custom_call_target="tpu_custom_call" | custom-call | flops 2000000000 | bytes 8388608 | tf_op jit(solution)/shard_map/place/pallas_call | solution.py:337
  47.2 2.9 %collective-permute-done.12 = bf16[2,80,640]{2,1,0:T(8,128)(2,1)S(1)} collective-permute-done((bf16[2,80,640]{2,1,0:T(8,128)(2,1)S(1)}, bf16[2,80,640]{2,1,0:T(8,128)(2,1)S(1)}, u32[]{:S(2)}, u32[]{:S(2)}) %collective-permute-start.12) | collective-permute-done | bytes 204832 | tf_op jit(solution)/shard_map/ppermute | solution.py:121
  50.1 0.5 collective-permute-done.13
  50.6 1.2 %collective-permute-start.20 = (bf16[80,640]{1,0:T(8,128)(2,1)S(1)}, bf16[80,640]{1,0:T(8,128)(2,1)S(1)}, u32[]{:S(2)}, u32[]{:S(2)}) collective-permute-start(bf16[80,640]{1,0:T(8,128)(2,1)S(1)} %slice_bitcast_fusion.2), channel_id=1, source_target_pairs={{0,4},{2,6},{4,0},{6,2},{8,12},{10,14},{12,8},{14,10},{16,20},{18,... | collective-permute-start | bytes 307208 | tf_op jit(solution)/shard_map/ppermute | solution.py:121
  51.8 0.5 collective-permute-start.19
  52.3 8.1 %own_half.1 = (f32[512,512]{1,0:T(8,128)S(1)}, f32[512,512]{1,0:T(8,128)S(1)}, f32[512,512]{1,0:T(8,128)S(1)}, f32[256,512]{1,0:T(8,128)S(1)}, f32[512,256]{1,0:T(8,128)S(1)}, /*index=5*/f32[3,40,512]{2,1,0:T(8,128)}) custom-call(bf16[3,512,1280]{2,1,0:T(8,128)(2,1)S(1)} %place.1.refs_0_, bf16[4,2,176,640]{3,2,1,0:T(8,128)(2,1)S(1)} %pad_maximum_fusion.refs_2_.refs_1_, ...), custom_call_target="tpu_custom_call" | custom-call | flops 8000000000 | bytes 8388608 | tf_op jit(solution)/shard_map/own_half/pallas_call | solution.py:356
  60.5 0.1 pad_maximum_fusion.2.refs_1_
  60.6 0.1 collective-permute-start.21
  60.7 2.3 %collective-permute-done.21.refs_2_ = bf16[4,2,80,640]{3,2,1,0:T(8,128)(2,1)S(1)} collective-permute-done((bf16[4,2,80,640]{3,2,1,0:T(8,128)(2,1)S(1)}, bf16[4,2,80,640]{3,2,1,0:T(8,128)(2,1)S(1)}, u32[]{:S(2)}, u32[]{:S(2)}) %collective-permute-start.21) | collective-permute-done | bytes 819232 | tf_op jit(solution)/shard_map/ppermute | solution.py:125
  63.0 11.5 %other_half.1 = f32[3,512,256]{2,1,0:T(8,128)} custom-call(bf16[3,512,1280]{2,1,0:T(8,128)(2,1)S(1)} %place.1.refs_0_, bf16[4,2,80,640]{3,2,1,0:T(8,128)(2,1)S(1)} %pad_maximum_fusion.2.refs_1_, bf16[4,2,80,640]{3,2,1,0:T(8,128)(2,1)S(1)} %collective-permute-done.21.refs_2_, bf16[2,512,512]{2,1,0:T(8,128)(2,1)S(1)} %copy-done.3, ...), custom_call_target="tpu_custom_call" | custom-call | flops 12000000000 | bytes 8388608 | tf_op jit(solution)/shard_map/other_half/pallas_call | solution.py:367
  (27 shorter events, 0.2 us)
Async XLA Ops:
  0.6 20.5 %copy-start.4 = (bf16[80,640]{1,0:T(8,128)(2,1)S(1)}, bf16[80,640]{1,0:T(8,128)(2,1)}, u32[]{:S(2)}) copy-start(bf16[80,640]{1,0:T(8,128)(2,1)} %param.6) | copy-start | bytes 307204
  1.7 8.9 %collective-permute-start.2 = (bf16[176,640]{1,0:T(8,128)(2,1)S(1)}, bf16[176,640]{1,0:T(8,128)(2,1)S(1)}, u32[]{:S(2)}, u32[]{:S(2)}) collective-permute-start(bf16[176,640]{1,0:T(8,128)(2,1)S(1)} %get-tuple-element.45), channel_id=1, source_target_pairs={{0,8},{2,10},{4,12},{6,14},{8,0},{10,2},{12,4},{14,6},{16,24},{18,... | collective-permute-start | bytes 675848 | tf_op jit(solution)/shard_map/ppermute | solution.py:121
  4.8 7.0 %collective-permute-start.3 = (bf16[176,640]{1,0:T(8,128)(2,1)S(1)}, bf16[176,640]{1,0:T(8,128)(2,1)S(1)}, u32[]{:S(2)}, u32[]{:S(2)}) collective-permute-start(bf16[176,640]{1,0:T(8,128)(2,1)S(1)} %get-tuple-element.45), channel_id=1, source_target_pairs={{0,2},{2,0},{4,6},{6,4},{8,10},{10,8},{12,14},{14,12},{16,18},{18,... | collective-permute-start | bytes 675848 | tf_op jit(solution)/shard_map/ppermute | solution.py:121
  6.2 6.7 %collective-permute-start.4 = (bf16[176,640]{1,0:T(8,128)(2,1)S(1)}, bf16[176,640]{1,0:T(8,128)(2,1)S(1)}, u32[]{:S(2)}, u32[]{:S(2)}) collective-permute-start(bf16[176,640]{1,0:T(8,128)(2,1)S(1)} %get-tuple-element.45), channel_id=1, source_target_pairs={{0,4},{2,6},{4,0},{6,2},{8,12},{10,14},{12,8},{14,10},{16,20},{18,... | collective-permute-start | bytes 675848 | tf_op jit(solution)/shard_map/ppermute | solution.py:121
  7.8 11.9 %collective-permute-start = (bf16[96,640]{1,0:T(8,128)(2,1)}, bf16[96,640]{1,0:T(8,128)(2,1)S(1)}, u32[]{:S(2)}, u32[]{:S(2)}) collective-permute-start(bf16[96,640]{1,0:T(8,128)(2,1)} %bitcast.60), channel_id=1, source_target_pairs={{0,16},{2,18},{4,20},{6,22},{8,24},{10,26},{12,28},{14,30},{16,0},... | collective-permute-start | bytes 368648 | tf_op jit(solution)/shard_map/ppermute | solution.py:121
  10.4 9.3 %collective-permute-start.1 = (bf16[96,640]{1,0:T(8,128)(2,1)}, bf16[96,640]{1,0:T(8,128)(2,1)S(1)}, u32[]{:S(2)}, u32[]{:S(2)}) collective-permute-start(bf16[96,640]{1,0:T(8,128)(2,1)} %bitcast.61), channel_id=1, source_target_pairs={{0,24},{2,26},{4,28},{6,30},{8,16},{10,18},{12,20},{14,22},{16,8},... | collective-permute-start | bytes 368648 | tf_op jit(solution)/shard_map/ppermute | solution.py:121
  12.9 8.2 %collective-permute-start.5 = (bf16[176,640]{1,0:T(8,128)(2,1)S(1)}, bf16[176,640]{1,0:T(8,128)(2,1)S(1)}, u32[]{:S(2)}, u32[]{:S(2)}) collective-permute-start(bf16[176,640]{1,0:T(8,128)(2,1)S(1)} %collective-permute-done.2), channel_id=1, source_target_pairs={{0,2},{2,0},{4,6},{6,4},{8,10},{10,8},{12,14},{14,12},{16,18},{18,... | collective-permute-start | bytes 675848 | tf_op jit(solution)/shard_map/ppermute | solution.py:121
  13.5 7.7 %collective-permute-start.6 = (bf16[176,640]{1,0:T(8,128)(2,1)S(1)}, bf16[176,640]{1,0:T(8,128)(2,1)S(1)}, u32[]{:S(2)}, u32[]{:S(2)}) collective-permute-start(bf16[176,640]{1,0:T(8,128)(2,1)S(1)} %collective-permute-done.2), channel_id=1, source_target_pairs={{0,4},{2,6},{4,0},{6,2},{8,12},{10,14},{12,8},{14,10},{16,20},{18,... | collective-permute-start | bytes 675848 | tf_op jit(solution)/shard_map/ppermute | solution.py:121
  15.5 8.3 %collective-permute-start.9 = (bf16[176,640]{1,0:T(8,128)(2,1)S(1)}, bf16[176,640]{1,0:T(8,128)(2,1)S(1)}, u32[]{:S(2)}, u32[]{:S(2)}) collective-permute-start(bf16[176,640]{1,0:T(8,128)(2,1)S(1)} %collective-permute-done.4), channel_id=1, source_target_pairs={{0,2},{2,0},{4,6},{6,4},{8,10},{10,8},{12,14},{14,12},{16,18},{18,... | collective-permute-start | bytes 675848 | tf_op jit(solution)/shard_map/ppermute | solution.py:121
  21.1 13.6 %collective-permute-start.8 = (bf16[80,640]{1,0:T(8,128)(2,1)S(1)}, bf16[80,640]{1,0:T(8,128)(2,1)S(1)}, u32[]{:S(2)}, u32[]{:S(2)}) collective-permute-start(bf16[80,640]{1,0:T(8,128)(2,1)S(1)} %copy-done.4), channel_id=1, source_target_pairs={{0,24},{2,26},{4,28},{6,30},{8,16},{10,18},{12,20},{14,22},{16,8},... | collective-permute-start | bytes 307208 | tf_op jit(solution)/shard_map/ppermute | solution.py:121
  23.4 11.4 %collective-permute-start.7 = (bf16[80,640]{1,0:T(8,128)(2,1)S(1)}, bf16[80,640]{1,0:T(8,128)(2,1)S(1)}, u32[]{:S(2)}, u32[]{:S(2)}) collective-permute-start(bf16[80,640]{1,0:T(8,128)(2,1)S(1)} %copy-done.4), channel_id=1, source_target_pairs={{0,16},{2,18},{4,20},{6,22},{8,24},{10,26},{12,28},{14,30},{16,0},... | collective-permute-start | bytes 307208 | tf_op jit(solution)/shard_map/ppermute | solution.py:121
  23.8 11.0 %collective-permute-start.10 = (bf16[2,96,640]{2,1,0:T(8,128)(2,1)S(1)}, bf16[2,96,640]{2,1,0:T(8,128)(2,1)S(1)}, u32[]{:S(2)}, u32[]{:S(2)}) collective-permute-start(bf16[2,96,640]{2,1,0:T(8,128)(2,1)S(1)} %pad_maximum_fusion.3), channel_id=1, source_target_pairs={{0,2},{2,0},{4,6},{6,4},{8,10},{10,8},{12,14},{14,12},{16,18},{18,... | collective-permute-start | bytes 737288 | tf_op jit(solution)/shard_map/ppermute | solution.py:121
  25.7 9.1 %collective-permute-start.11 = (bf16[2,96,640]{2,1,0:T(8,128)(2,1)S(1)}, bf16[2,96,640]{2,1,0:T(8,128)(2,1)S(1)}, u32[]{:S(2)}, u32[]{:S(2)}) collective-permute-start(bf16[2,96,640]{2,1,0:T(8,128)(2,1)S(1)} %pad_maximum_fusion.3), channel_id=1, source_target_pairs={{0,4},{2,6},{4,0},{6,2},{8,12},{10,14},{12,8},{14,10},{16,20},{18,... | collective-permute-start | bytes 737288 | tf_op jit(solution)/shard_map/ppermute | solution.py:121
  27.6 6.7 %collective-permute-start.14 = (bf16[176,640]{1,0:T(8,128)(2,1)S(1)}, bf16[176,640]{1,0:T(8,128)(2,1)S(1)}, u32[]{:S(2)}, u32[]{:S(2)}) collective-permute-start(bf16[176,640]{1,0:T(8,128)(2,1)S(1)} %collective-permute-done.5), channel_id=1, source_target_pairs={{0,4},{2,6},{4,0},{6,2},{8,12},{10,14},{12,8},{14,10},{16,20},{18,... | collective-permute-start | bytes 675848 | tf_op jit(solution)/shard_map/ppermute | solution.py:121
  34.6 9.9 %copy-start.2 = (f32[3,512,256]{2,1,0:T(8,128)S(1)}, f32[3,512,256]{2,1,0:T(8,128)}, u32[]{:S(2)}) copy-start(f32[3,512,256]{2,1,0:T(8,128)} %refs_4_.1) | copy-start | bytes 4718596
  34.6 10.4 %copy-start = (s32[3,10]{1,0:T(4,128)S(1)}, s32[3,10]{1,0:T(4,128)}, u32[]{:S(2)}) copy-start(s32[3,10]{1,0:T(4,128)} %refs_0_.1) | copy-start | bytes 364
  34.7 10.4 %copy-start.1 = (s32[3,10]{1,0:T(4,128)S(1)}, s32[3,10]{1,0:T(4,128)}, u32[]{:S(2)}) copy-start(s32[3,10]{1,0:T(4,128)} %refs_1_.1) | copy-start | bytes 364
  34.7 10.4 %collective-permute-start.17 = (bf16[4,2,176,640]{3,2,1,0:T(8,128)(2,1)S(1)}, bf16[4,2,176,640]{3,2,1,0:T(8,128)(2,1)S(1)}, u32[]{:S(2)}, u32[]{:S(2)}) collective-permute-start(bf16[4,2,176,640]{3,2,1,0:T(8,128)(2,1)S(1)} %pad_maximum_fusion.refs_2_.refs_1_), channel_id=1, source_target_pairs={{0,1},{1,0},{2,3},{3,2},{4,5},{5,4},{6,7},{7,6},{8,9},{9,8},{10,11... | collective-permute-start | bytes 5406728 | tf_op jit(solution)/shard_map/ppermute | solution.py:125
  34.8 5.9 %collective-permute-start.16 = (bf16[96,640]{1,0:T(8,128)(2,1)S(1)}, bf16[96,640]{1,0:T(8,128)(2,1)S(1)}, u32[]{:S(2)}, u32[]{:S(2)}) collective-permute-start(bf16[96,640]{1,0:T(8,128)(2,1)S(1)} %slice_bitcast_fusion), channel_id=1, source_target_pairs={{0,4},{2,6},{4,0},{6,2},{8,12},{10,14},{12,8},{14,10},{16,20},{18,... | collective-permute-start | bytes 368648 | tf_op jit(solution)/shard_map/ppermute | solution.py:121
  36.8 5.5 %collective-permute-start.15 = (bf16[96,640]{1,0:T(8,128)(2,1)S(1)}, bf16[96,640]{1,0:T(8,128)(2,1)S(1)}, u32[]{:S(2)}, u32[]{:S(2)}) collective-permute-start(bf16[96,640]{1,0:T(8,128)(2,1)S(1)} %slice_bitcast_fusion.1), channel_id=1, source_target_pairs={{0,2},{2,0},{4,6},{6,4},{8,10},{10,8},{12,14},{14,12},{16,18},{18,... | collective-permute-start | bytes 368648 | tf_op jit(solution)/shard_map/ppermute | solution.py:121
  42.4 2.6 %collective-permute-start.18 = (bf16[4,2,96,640]{3,2,1,0:T(8,128)(2,1)S(1)}, bf16[4,2,96,640]{3,2,1,0:T(8,128)(2,1)S(1)}, u32[]{:S(2)}, u32[]{:S(2)}) collective-permute-start(bf16[4,2,96,640]{3,2,1,0:T(8,128)(2,1)S(1)} %pad_maximum_fusion.1.refs_3_), channel_id=1, source_target_pairs={{0,1},{1,0},{2,3},{3,2},{4,5},{5,4},{6,7},{7,6},{8,9},{9,8},{10,11... | collective-permute-start | bytes 2949128 | tf_op jit(solution)/shard_map/ppermute | solution.py:125
  42.6 9.8 %copy-start.3 = (bf16[2,512,512]{2,1,0:T(8,128)(2,1)S(1)}, bf16[2,512,512]{2,1,0:T(8,128)(2,1)}, u32[]{:S(2)}) copy-start(bf16[2,512,512]{2,1,0:T(8,128)(2,1)} %refs_3_.3) | copy-start | bytes 3145732
  42.6 7.5 %collective-permute-start.12 = (bf16[2,80,640]{2,1,0:T(8,128)(2,1)S(1)}, bf16[2,80,640]{2,1,0:T(8,128)(2,1)S(1)}, u32[]{:S(2)}, u32[]{:S(2)}) collective-permute-start(bf16[2,80,640]{2,1,0:T(8,128)(2,1)S(1)} %pad_maximum_fusion.5), channel_id=1, source_target_pairs={{0,2},{2,0},{4,6},{6,4},{8,10},{10,8},{12,14},{14,12},{16,18},{18,... | collective-permute-start | bytes 614408 | tf_op jit(solution)/shard_map/ppermute | solution.py:121
  43.4 7.2 %collective-permute-start.13 = (bf16[2,80,640]{2,1,0:T(8,128)(2,1)S(1)}, bf16[2,80,640]{2,1,0:T(8,128)(2,1)S(1)}, u32[]{:S(2)}, u32[]{:S(2)}) collective-permute-start(bf16[2,80,640]{2,1,0:T(8,128)(2,1)S(1)} %pad_maximum_fusion.5), channel_id=1, source_target_pairs={{0,4},{2,6},{4,0},{6,2},{8,12},{10,14},{12,8},{14,10},{16,20},{18,... | collective-permute-start | bytes 614408 | tf_op jit(solution)/shard_map/ppermute | solution.py:121
  44.5 16.2 %collective-permute-start.22 = (f32[3,512,256]{2,1,0:T(8,128)S(1)}, f32[3,512,256]{2,1,0:T(8,128)S(1)}, u32[]{:S(2)}, u32[]{:S(2)}) collective-permute-start(f32[3,512,256]{2,1,0:T(8,128)S(1)} %copy-done.2), channel_id=1, source_target_pairs={{0,1},{1,0},{2,3},{3,2},{4,5},{5,4},{6,7},{7,6},{8,9},{9,8},{10,11... | collective-permute-start | bytes 4718600 | tf_op jit(solution)/shard_map/ppermute | solution.py:125
  50.6 9.9 %collective-permute-start.20 = (bf16[80,640]{1,0:T(8,128)(2,1)S(1)}, bf16[80,640]{1,0:T(8,128)(2,1)S(1)}, u32[]{:S(2)}, u32[]{:S(2)}) collective-permute-start(bf16[80,640]{1,0:T(8,128)(2,1)S(1)} %slice_bitcast_fusion.2), channel_id=1, source_target_pairs={{0,4},{2,6},{4,0},{6,2},{8,12},{10,14},{12,8},{14,10},{16,20},{18,... | collective-permute-start | bytes 307208 | tf_op jit(solution)/shard_map/ppermute | solution.py:121
  51.8 8.7 %collective-permute-start.19 = (bf16[80,640]{1,0:T(8,128)(2,1)S(1)}, bf16[80,640]{1,0:T(8,128)(2,1)S(1)}, u32[]{:S(2)}, u32[]{:S(2)}) collective-permute-start(bf16[80,640]{1,0:T(8,128)(2,1)S(1)} %slice_bitcast_fusion.3), channel_id=1, source_target_pairs={{0,2},{2,0},{4,6},{6,4},{8,10},{10,8},{12,14},{14,12},{16,18},{18,... | collective-permute-start | bytes 307208 | tf_op jit(solution)/shard_map/ppermute | solution.py:121
  60.6 2.4 %collective-permute-start.21 = (bf16[4,2,80,640]{3,2,1,0:T(8,128)(2,1)S(1)}, bf16[4,2,80,640]{3,2,1,0:T(8,128)(2,1)S(1)}, u32[]{:S(2)}, u32[]{:S(2)}) collective-permute-start(bf16[4,2,80,640]{3,2,1,0:T(8,128)(2,1)S(1)} %pad_maximum_fusion.2.refs_1_), channel_id=1, source_target_pairs={{0,1},{1,0},{2,3},{3,2},{4,5},{5,4},{6,7},{7,6},{8,9},{9,8},{10,11... | collective-permute-start | bytes 2457608 | tf_op jit(solution)/shard_map/ppermute | solution.py:125

commit v4 on v3

--- a/solution.py
+++ b/solution.py
@@ -322,16 +322,23 @@
         value = after(value, *early[-1][1:3]) if k else value
         over_x, over_y = x(value), y(value)
         early.append([value, over_x, over_y, far(over_x, over_y, k)])
-    first = jnp.stack([jnp.stack([p[j] for p in early]) for j in range(4)])
-    first_other = across(first)
     block = after(inverse_block, *f_late, *early[-1][1:3])
     z_late = [line(block, k) for k in range(count, outer)]
     f_b, f_bx, f_by = late_wave(f_late, *early[-1][1:3], early[0][3])
-    f_bx, f_by = after((f_bx, f_by), *z_late)
-    f_far = jnp.stack([far(f_bx[i], f_by[i], i) for i in range(count)])
-    f_last = jnp.stack([f_b, f_bx, f_by, f_far])
+    first = jnp.stack([jnp.stack([p[j] for p in early]) for j in range(4)])
+    first_other = across(first)
+    z_b = jnp.stack(z_late)
+    f_rows = supers * part
+    z_flat = z_b.reshape(count * local_rows, span)
+    by_x = [f_by[i] for i in range(0, count, 2)] + [z_flat]
+    by_y = [f_bx[i] for i in range(1, count, 2)] + [z_flat]
+    by_x, by_y = x(jnp.concatenate(by_x, axis=0)), y(jnp.concatenate(by_y, axis=0))
+    f_far = [(by_x, by_y)[i % 2][i // 2 * f_rows : (i // 2 + 1) * f_rows] for i in range(count)]
+    z_bx = by_x[-count * local_rows :].reshape(z_b.shape)
+    z_by = by_y[-count * local_rows :].reshape(z_b.shape)
+    f_last = jnp.stack([f_b, f_bx, f_by, jnp.stack(f_far)])
     f_last_other = across(f_last)
-    z_b, z_bx, z_by = late_wave(z_late, f_bx, f_by)
+    z_far = jnp.stack([far(z_bx[i], z_by[i], i) for i in range(count)])
     diag_other = across(diag_inverse)
 
     pt = call(
@@ -342,8 +349,9 @@
         out_specs=vmem,
     )(occupancy, row_block, first, f_last, first_other, f_last_other)
 
-    z_bx, z_by, pt = after((z_bx, z_by, pt), pt)
-    z_far = jnp.stack([far(z_bx[i], z_by[i], i) for i in range(count)])
+    z_far, pt = after((z_far, pt), pt)
+    z_last = jnp.stack([z_b, z_bx, z_by, z_far])
+    z_last_other = across(z_last)
     dims = (width, span)
     half_rows, half_w = rows // 2, width // 2
     sum_shapes = [(width, width), (width, width), (width, width), (half_w, width), (width, half_w)]
@@ -361,9 +369,6 @@
         out_specs=(vmem,) * 6,
         scratch_shapes=scratch,
     )(pt, first, first_other, coupling)
-    z_far, *sums = after((z_far, *sums), sums[0])
-    z_last = jnp.stack([z_b, z_bx, z_by, z_far])
-    z_last_other = across(z_last)
     diagonals = call(
         functools.partial(last_kernel, dims, rows),
         "other_half", 12 * 10**9,

time: 74.9 us -> 78.4 us (1.047)
  waiting for transfers between devices: 24.3 us -> 27 us
    ppermute x19 -> x17, waiting for transfers between devices: 21.5 us -> 27 us  [swap(): return lax.ppermute(value, axis, [(i, i ^ bit) for i in range(parts)])]
    ppermute x4, waiting for transfers between devices: 2.86 us -> 0.01 us  [across(): return lax.ppermute(value, 'col', [(0, 1), (1, 0)])]
    ppermute x19 -> x17, starting transfers between devices: 25.4 us -> 25.5 us  [swap(): return lax.ppermute(value, axis, [(i, i ^ bit) for i in range(parts)])]
  transfers between devices with their start and end apart: 23 -> 21, of which waited for: 11 -> 11; matrix products, arithmetic and copies ran while one was open for 1% -> 1% of each run, Pallas kernels for 14% -> 13%
where the time goes in v4:
time: 78.4 us; the launch traced here: 78.2 us
  waiting for transfers between devices  27 us (34%)
  starting transfers between devices  26.2 us (33%)
  Pallas kernels  21.8 us (28%)
  other arithmetic  1.96 us (2%)
  between operations  1.09 us (1%)
    ppermute x17, waiting for transfers between devices, swap(): return lax.ppermute(value, axis, [(i, i ^ bit) for i in range(parts)])  27 us
    ppermute x17, starting transfers between devices, swap(): return lax.ppermute(value, axis, [(i, i ^ bit) for i in range(parts)])  25.5 us
    pallas_call x1, Pallas kernels, replicated_plan(): call(functools.partial(last_kernel, dims, rows), 'other_half', 12 * 10 **...  11.5 us
    pallas_call x1, Pallas kernels, replicated_plan(): call(functools.partial(first_kernel, dims, supers * part), 'own_half', 8...  8.18 us
    pallas_call x1, Pallas kernels, replicated_plan(): call(functools.partial(place_kernel, (supers, width, rows, span, part)),...  2.06 us
  transfers between devices with their start and end apart: 21, of which 11 were waited for; matrix products, arithmetic and copies ran while one was open for 1% of the time, Pallas kernels for 13%

profile of v4, /device:TPU:0, one launch (start us, length us, event | category | flops | bytes accessed | tf_op | source)
XLA Modules:
  0.0 78.2 jit_solution(6994012753556167752)
XLA Ops:
  0.6 1.0 %fusion.1 = (bf16[1,176,640]{2,1,0:T(8,128)(2,1)S(1)}, bf16[176,640]{1,0:T(8,128)(2,1)S(1)}) fusion(bf16[80,640]{1,0:T(8,128)(2,1)} %param.6, bf16[96,640]{1,0:T(8,128)(2,1)} %bitcast.59), kind=kLoop, calls=%fused_computation.19 | loop fusion | flops 450560 | bytes 675840 | tf_op jit(solution)/shard_map/stack | solution.py:328
  1.7 3.1 %collective-permute-start.2 = (bf16[176,640]{1,0:T(8,128)(2,1)S(1)}, bf16[176,640]{1,0:T(8,128)(2,1)S(1)}, u32[]{:S(2)}, u32[]{:S(2)}) collective-permute-start(bf16[176,640]{1,0:T(8,128)(2,1)S(1)} %get-tuple-element.25), channel_id=1, source_target_pairs={{0,8},{2,10},{4,12},{6,14},{8,0},{10,2},{12,4},{14,6},{16,24},{18,... | collective-permute-start | bytes 675848 | tf_op jit(solution)/shard_map/ppermute | solution.py:121
  4.8 1.5 %collective-permute-start.3 = (bf16[176,640]{1,0:T(8,128)(2,1)S(1)}, bf16[176,640]{1,0:T(8,128)(2,1)S(1)}, u32[]{:S(2)}, u32[]{:S(2)}) collective-permute-start(bf16[176,640]{1,0:T(8,128)(2,1)S(1)} %get-tuple-element.25), channel_id=1, source_target_pairs={{0,2},{2,0},{4,6},{6,4},{8,10},{10,8},{12,14},{14,12},{16,18},{18,... | collective-permute-start | bytes 675848 | tf_op jit(solution)/shard_map/ppermute | solution.py:121
  6.2 1.5 %collective-permute-start.4 = (bf16[176,640]{1,0:T(8,128)(2,1)S(1)}, bf16[176,640]{1,0:T(8,128)(2,1)S(1)}, u32[]{:S(2)}, u32[]{:S(2)}) collective-permute-start(bf16[176,640]{1,0:T(8,128)(2,1)S(1)} %get-tuple-element.25), channel_id=1, source_target_pairs={{0,4},{2,6},{4,0},{6,2},{8,12},{10,14},{12,8},{14,10},{16,20},{18,... | collective-permute-start | bytes 675848 | tf_op jit(solution)/shard_map/ppermute | solution.py:121
  7.8 2.6 %collective-permute-start = (bf16[96,640]{1,0:T(8,128)(2,1)}, bf16[96,640]{1,0:T(8,128)(2,1)S(1)}, u32[]{:S(2)}, u32[]{:S(2)}) collective-permute-start(bf16[96,640]{1,0:T(8,128)(2,1)} %bitcast.60), channel_id=1, source_target_pairs={{0,16},{2,18},{4,20},{6,22},{8,24},{10,26},{12,28},{14,30},{16,0},... | collective-permute-start | bytes 368648 | tf_op jit(solution)/shard_map/ppermute | solution.py:121
  10.4 0.2 collective-permute-start.1
  10.6 1.1 %collective-permute-done.3 = bf16[176,640]{1,0:T(8,128)(2,1)S(1)} collective-permute-done((bf16[176,640]{1,0:T(8,128)(2,1)S(1)}, bf16[176,640]{1,0:T(8,128)(2,1)S(1)}, u32[]{:S(2)}, u32[]{:S(2)}) %collective-permute-start.3) | collective-permute-done | bytes 225312 | tf_op jit(solution)/shard_map/ppermute | solution.py:121
  11.7 1.2 %collective-permute-done.4 = bf16[176,640]{1,0:T(8,128)(2,1)S(1)} collective-permute-done((bf16[176,640]{1,0:T(8,128)(2,1)S(1)}, bf16[176,640]{1,0:T(8,128)(2,1)S(1)}, u32[]{:S(2)}, u32[]{:S(2)}) %collective-permute-start.4) | collective-permute-done | bytes 225312 | tf_op jit(solution)/shard_map/ppermute | solution.py:121
  12.9 0.5 collective-permute-start.5
  13.5 2.0 %collective-permute-start.6 = (bf16[176,640]{1,0:T(8,128)(2,1)S(1)}, bf16[176,640]{1,0:T(8,128)(2,1)S(1)}, u32[]{:S(2)}, u32[]{:S(2)}) collective-permute-start(bf16[176,640]{1,0:T(8,128)(2,1)S(1)} %collective-permute-done.2), channel_id=1, source_target_pairs={{0,4},{2,6},{4,0},{6,2},{8,12},{10,14},{12,8},{14,10},{16,20},{18,... | collective-permute-start | bytes 675848 | tf_op jit(solution)/shard_map/ppermute | solution.py:121
  15.5 1.0 %collective-permute-start.7 = (bf16[176,640]{1,0:T(8,128)(2,1)S(1)}, bf16[176,640]{1,0:T(8,128)(2,1)S(1)}, u32[]{:S(2)}, u32[]{:S(2)}) collective-permute-start(bf16[176,640]{1,0:T(8,128)(2,1)S(1)} %collective-permute-done.4), channel_id=1, source_target_pairs={{0,2},{2,0},{4,6},{6,4},{8,10},{10,8},{12,14},{14,12},{16,18},{18,... | collective-permute-start | bytes 675848 | tf_op jit(solution)/shard_map/ppermute | solution.py:121
  16.5 3.2 %collective-permute-done = bf16[96,640]{1,0:T(8,128)(2,1)S(1)} collective-permute-done((bf16[96,640]{1,0:T(8,128)(2,1)}, bf16[96,640]{1,0:T(8,128)(2,1)S(1)}, u32[]{:S(2)}, u32[]{:S(2)}) %collective-permute-start) | collective-permute-done | bytes 122912 | tf_op jit(solution)/shard_map/ppermute | solution.py:121
  19.7 0.1 maximum_bitcast_fusion
  19.8 1.3 %collective-permute-done.5 = bf16[176,640]{1,0:T(8,128)(2,1)S(1)} collective-permute-done((bf16[176,640]{1,0:T(8,128)(2,1)S(1)}, bf16[176,640]{1,0:T(8,128)(2,1)S(1)}, u32[]{:S(2)}, u32[]{:S(2)}) %collective-permute-start.5) | collective-permute-done | bytes 225312 | tf_op jit(solution)/shard_map/ppermute | solution.py:121
  21.1 2.2 %collective-permute-start.10 = (bf16[80,640]{1,0:T(8,128)(2,1)S(1)}, bf16[80,640]{1,0:T(8,128)(2,1)S(1)}, u32[]{:S(2)}, u32[]{:S(2)}) collective-permute-start(bf16[80,640]{1,0:T(8,128)(2,1)S(1)} %copy-done.6), channel_id=1, source_target_pairs={{0,24},{2,26},{4,28},{6,30},{8,16},{10,18},{12,20},{14,22},{16,8},... | collective-permute-start | bytes 307208 | tf_op jit(solution)/shard_map/ppermute | solution.py:121
  23.4 0.4 collective-permute-start.9
  23.8 1.9 %collective-permute-start.8 = (bf16[2,96,640]{2,1,0:T(8,128)(2,1)S(1)}, bf16[2,96,640]{2,1,0:T(8,128)(2,1)S(1)}, u32[]{:S(2)}, u32[]{:S(2)}) collective-permute-start(bf16[2,96,640]{2,1,0:T(8,128)(2,1)S(1)} %pad_maximum_fusion.5), channel_id=1, source_target_pairs={{0,2},{2,0},{4,6},{6,4},{8,10},{10,8},{12,14},{14,12},{16,18},{18,... | collective-permute-start | bytes 737288 | tf_op jit(solution)/shard_map/ppermute | solution.py:121
  25.7 1.9 %collective-permute-start.13 = (bf16[2,96,640]{2,1,0:T(8,128)(2,1)S(1)}, bf16[2,96,640]{2,1,0:T(8,128)(2,1)S(1)}, u32[]{:S(2)}, u32[]{:S(2)}) collective-permute-start(bf16[2,96,640]{2,1,0:T(8,128)(2,1)S(1)} %pad_maximum_fusion.5), channel_id=1, source_target_pairs={{0,4},{2,6},{4,0},{6,2},{8,12},{10,14},{12,8},{14,10},{16,20},{18,... | collective-permute-start | bytes 737288 | tf_op jit(solution)/shard_map/ppermute | solution.py:121
  27.6 0.1 maximum_bitcast_fusion.2
  27.6 0.2 collective-permute-start.16
  27.8 0.1 maximum_bitcast_fusion.1
  27.9 2.7 %collective-permute-done.9 = bf16[80,640]{1,0:T(8,128)(2,1)S(1)} collective-permute-done((bf16[80,640]{1,0:T(8,128)(2,1)S(1)}, bf16[80,640]{1,0:T(8,128)(2,1)S(1)}, u32[]{:S(2)}, u32[]{:S(2)}) %collective-permute-start.9) | collective-permute-done | bytes 102432 | tf_op jit(solution)/shard_map/ppermute | solution.py:121
  30.7 3.5 %collective-permute-done.13 = bf16[2,96,640]{2,1,0:T(8,128)(2,1)S(1)} collective-permute-done((bf16[2,96,640]{2,1,0:T(8,128)(2,1)S(1)}, bf16[2,96,640]{2,1,0:T(8,128)(2,1)S(1)}, u32[]{:S(2)}, u32[]{:S(2)}) %collective-permute-start.13) | collective-permute-done | bytes 245792 | tf_op jit(solution)/shard_map/ppermute | solution.py:121
  34.2 0.1 pad_maximum_fusion.4
  34.2 2.2 %collective-permute-start.11 = (bf16[256,640]{1,0:T(8,128)(2,1)S(1)}, bf16[256,640]{1,0:T(8,128)(2,1)S(1)}, u32[]{:S(2)}, u32[]{:S(2)}) collective-permute-start(bf16[256,640]{1,0:T(8,128)(2,1)S(1)} %get-tuple-element.28), channel_id=1, source_target_pairs={{0,4},{2,6},{4,0},{6,2},{8,12},{10,14},{12,8},{14,10},{16,20},{18,... | collective-permute-start | bytes 983048 | tf_op jit(solution)/shard_map/ppermute | solution.py:121
  36.4 1.4 %collective-permute-done.16 = bf16[176,640]{1,0:T(8,128)(2,1)S(1)} collective-permute-done((bf16[176,640]{1,0:T(8,128)(2,1)S(1)}, bf16[176,640]{1,0:T(8,128)(2,1)S(1)}, u32[]{:S(2)}, u32[]{:S(2)}) %collective-permute-start.16) | collective-permute-done | bytes 225312 | tf_op jit(solution)/shard_map/ppermute | solution.py:121
  37.8 0.1 maximum_bitcast_fusion.3
  37.9 0.3 pad_maximum_fusion.refs_2_.refs_1_
  38.1 0.0 copy-start.2
  38.2 0.1 collective-permute-start.17
  38.2 1.5 %collective-permute-start.14 = (bf16[256,640]{1,0:T(8,128)(2,1)S(1)}, bf16[256,640]{1,0:T(8,128)(2,1)S(1)}, u32[]{:S(2)}, u32[]{:S(2)}) collective-permute-start(bf16[256,640]{1,0:T(8,128)(2,1)S(1)} %get-tuple-element.29), channel_id=1, source_target_pairs={{0,2},{2,0},{4,6},{6,4},{8,10},{10,8},{12,14},{14,12},{16,18},{18,... | collective-permute-start | bytes 983048 | tf_op jit(solution)/shard_map/ppermute | solution.py:121
  39.7 1.7 %collective-permute-done.11 = bf16[256,640]{1,0:T(8,128)(2,1)S(1)} collective-permute-done((bf16[256,640]{1,0:T(8,128)(2,1)S(1)}, bf16[256,640]{1,0:T(8,128)(2,1)S(1)}, u32[]{:S(2)}, u32[]{:S(2)}) %collective-permute-start.11) | collective-permute-done | bytes 327712 | tf_op jit(solution)/shard_map/ppermute | solution.py:121
  41.5 6.9 %collective-permute-done.14 = bf16[256,640]{1,0:T(8,128)(2,1)S(1)} collective-permute-done((bf16[256,640]{1,0:T(8,128)(2,1)S(1)}, bf16[256,640]{1,0:T(8,128)(2,1)S(1)}, u32[]{:S(2)}, u32[]{:S(2)}) %collective-permute-start.14) | collective-permute-done | bytes 327712 | tf_op jit(solution)/shard_map/ppermute | solution.py:121
  48.4 0.0 copy-start.1
  48.4 0.1 pad_maximum_fusion.1.refs_3_
  48.6 0.1 collective-permute-start.18
  48.7 0.5 collective-permute-start.20
  49.2 1.9 %collective-permute-start.15 = (bf16[80,640]{1,0:T(8,128)(2,1)S(1)}, bf16[80,640]{1,0:T(8,128)(2,1)S(1)}, u32[]{:S(2)}, u32[]{:S(2)}) collective-permute-start(bf16[80,640]{1,0:T(8,128)(2,1)S(1)} %slice.39), channel_id=1, source_target_pairs={{0,4},{2,6},{4,0},{6,2},{8,12},{10,14},{12,8},{14,10},{16,20},{18,... | collective-permute-start | bytes 307208 | tf_op jit(solution)/shard_map/ppermute | solution.py:121
  51.1 0.8 %collective-permute-start.12 = (bf16[80,640]{1,0:T(8,128)(2,1)S(1)}, bf16[80,640]{1,0:T(8,128)(2,1)S(1)}, u32[]{:S(2)}, u32[]{:S(2)}) collective-permute-start(bf16[80,640]{1,0:T(8,128)(2,1)S(1)} %slice.37), channel_id=1, source_target_pairs={{0,2},{2,0},{4,6},{6,4},{8,10},{10,8},{12,14},{14,12},{16,18},{18,... | collective-permute-start | bytes 307208 | tf_op jit(solution)/shard_map/ppermute | solution.py:121
  52.0 2.3 %collective-permute-done.15 = bf16[80,640]{1,0:T(8,128)(2,1)S(1)} collective-permute-done((bf16[80,640]{1,0:T(8,128)(2,1)S(1)}, bf16[80,640]{1,0:T(8,128)(2,1)S(1)}, u32[]{:S(2)}, u32[]{:S(2)}) %collective-permute-start.15) | collective-permute-done | bytes 102432 | tf_op jit(solution)/shard_map/ppermute | solution.py:121
  54.3 1.6 %collective-permute-done.12 = bf16[80,640]{1,0:T(8,128)(2,1)S(1)} collective-permute-done((bf16[80,640]{1,0:T(8,128)(2,1)S(1)}, bf16[80,640]{1,0:T(8,128)(2,1)S(1)}, u32[]{:S(2)}, u32[]{:S(2)}) %collective-permute-start.12) | collective-permute-done | bytes 102432 | tf_op jit(solution)/shard_map/ppermute | solution.py:121
  55.9 0.0 slice-start
  55.9 0.0 copy-start.3
  56.0 2.1 %place.1.refs_0_ = bf16[3,512,1280]{2,1,0:T(8,128)(2,1)S(1)} custom-call(s32[3,10]{1,0:T(4,128)S(1)} %copy-done, s32[3,10]{1,0:T(4,128)S(1)} %copy-done.1, bf16[4,2,176,640]{3,2,1,0:T(8,128)(2,1)S(1)} %pad_maximum_fusion.refs_2_.refs_1_, bf16[4,2,96,640]{3,2,1,0:T(8,128)(2,1)S(1)} %pad_maximum_fusion.1.refs_3_, ...), custom_call_target="tpu_custom_call" | custom-call | flops 2000000000 | bytes 8388608 | tf_op jit(solution)/shard_map/place/pallas_call | solution.py:344
  58.1 0.1 pad_maximum_fusion.2.refs_1_
  58.2 0.1 collective-permute-start.19
  58.3 8.2 %own_half.1 = (f32[512,512]{1,0:T(8,128)S(1)}, f32[512,512]{1,0:T(8,128)S(1)}, f32[512,512]{1,0:T(8,128)S(1)}, f32[256,512]{1,0:T(8,128)S(1)}, f32[512,256]{1,0:T(8,128)S(1)}, /*index=5*/f32[3,40,512]{2,1,0:T(8,128)}) custom-call(bf16[3,512,1280]{2,1,0:T(8,128)(2,1)S(1)} %place.1.refs_0_, bf16[4,2,176,640]{3,2,1,0:T(8,128)(2,1)S(1)} %pad_maximum_fusion.refs_2_.refs_1_, ...), custom_call_target="tpu_custom_call" | custom-call | flops 8000000000 | bytes 8388608 | tf_op jit(solution)/shard_map/own_half/pallas_call | solution.py:364
  66.5 11.5 %other_half.1 = f32[3,512,256]{2,1,0:T(8,128)} custom-call(bf16[3,512,1280]{2,1,0:T(8,128)(2,1)S(1)} %place.1.refs_0_, bf16[4,2,80,640]{3,2,1,0:T(8,128)(2,1)S(1)} %pad_maximum_fusion.2.refs_1_, bf16[4,2,80,640]{3,2,1,0:T(8,128)(2,1)S(1)} %collective-permute-done.19.refs_2_, bf16[2,512,512]{2,1,0:T(8,128)(2,1)S(1)} %copy-done.3, ...), custom_call_target="tpu_custom_call" | custom-call | flops 12000000000 | bytes 8388608 | tf_op jit(solution)/shard_map/other_half/pallas_call | solution.py:372
  (34 shorter events, 0.2 us)
Async XLA Ops:
  0.6 20.5 %copy-start.6 = (bf16[80,640]{1,0:T(8,128)(2,1)S(1)}, bf16[80,640]{1,0:T(8,128)(2,1)}, u32[]{:S(2)}) copy-start(bf16[80,640]{1,0:T(8,128)(2,1)} %param.6) | copy-start | bytes 307204
  1.7 8.9 %collective-permute-start.2 = (bf16[176,640]{1,0:T(8,128)(2,1)S(1)}, bf16[176,640]{1,0:T(8,128)(2,1)S(1)}, u32[]{:S(2)}, u32[]{:S(2)}) collective-permute-start(bf16[176,640]{1,0:T(8,128)(2,1)S(1)} %get-tuple-element.25), channel_id=1, source_target_pairs={{0,8},{2,10},{4,12},{6,14},{8,0},{10,2},{12,4},{14,6},{16,24},{18,... | collective-permute-start | bytes 675848 | tf_op jit(solution)/shard_map/ppermute | solution.py:121
  4.8 7.0 %collective-permute-start.3 = (bf16[176,640]{1,0:T(8,128)(2,1)S(1)}, bf16[176,640]{1,0:T(8,128)(2,1)S(1)}, u32[]{:S(2)}, u32[]{:S(2)}) collective-permute-start(bf16[176,640]{1,0:T(8,128)(2,1)S(1)} %get-tuple-element.25), channel_id=1, source_target_pairs={{0,2},{2,0},{4,6},{6,4},{8,10},{10,8},{12,14},{14,12},{16,18},{18,... | collective-permute-start | bytes 675848 | tf_op jit(solution)/shard_map/ppermute | solution.py:121
  6.2 6.7 %collective-permute-start.4 = (bf16[176,640]{1,0:T(8,128)(2,1)S(1)}, bf16[176,640]{1,0:T(8,128)(2,1)S(1)}, u32[]{:S(2)}, u32[]{:S(2)}) collective-permute-start(bf16[176,640]{1,0:T(8,128)(2,1)S(1)} %get-tuple-element.25), channel_id=1, source_target_pairs={{0,4},{2,6},{4,0},{6,2},{8,12},{10,14},{12,8},{14,10},{16,20},{18,... | collective-permute-start | bytes 675848 | tf_op jit(solution)/shard_map/ppermute | solution.py:121
  7.8 11.9 %collective-permute-start = (bf16[96,640]{1,0:T(8,128)(2,1)}, bf16[96,640]{1,0:T(8,128)(2,1)S(1)}, u32[]{:S(2)}, u32[]{:S(2)}) collective-permute-start(bf16[96,640]{1,0:T(8,128)(2,1)} %bitcast.60), channel_id=1, source_target_pairs={{0,16},{2,18},{4,20},{6,22},{8,24},{10,26},{12,28},{14,30},{16,0},... | collective-permute-start | bytes 368648 | tf_op jit(solution)/shard_map/ppermute | solution.py:121
  10.4 9.3 %collective-permute-start.1 = (bf16[96,640]{1,0:T(8,128)(2,1)}, bf16[96,640]{1,0:T(8,128)(2,1)S(1)}, u32[]{:S(2)}, u32[]{:S(2)}) collective-permute-start(bf16[96,640]{1,0:T(8,128)(2,1)} %bitcast.61), channel_id=1, source_target_pairs={{0,24},{2,26},{4,28},{6,30},{8,16},{10,18},{12,20},{14,22},{16,8},... | collective-permute-start | bytes 368648 | tf_op jit(solution)/shard_map/ppermute | solution.py:121
  12.9 8.2 %collective-permute-start.5 = (bf16[176,640]{1,0:T(8,128)(2,1)S(1)}, bf16[176,640]{1,0:T(8,128)(2,1)S(1)}, u32[]{:S(2)}, u32[]{:S(2)}) collective-permute-start(bf16[176,640]{1,0:T(8,128)(2,1)S(1)} %collective-permute-done.2), channel_id=1, source_target_pairs={{0,2},{2,0},{4,6},{6,4},{8,10},{10,8},{12,14},{14,12},{16,18},{18,... | collective-permute-start | bytes 675848 | tf_op jit(solution)/shard_map/ppermute | solution.py:121
  13.5 7.7 %collective-permute-start.6 = (bf16[176,640]{1,0:T(8,128)(2,1)S(1)}, bf16[176,640]{1,0:T(8,128)(2,1)S(1)}, u32[]{:S(2)}, u32[]{:S(2)}) collective-permute-start(bf16[176,640]{1,0:T(8,128)(2,1)S(1)} %collective-permute-done.2), channel_id=1, source_target_pairs={{0,4},{2,6},{4,0},{6,2},{8,12},{10,14},{12,8},{14,10},{16,20},{18,... | collective-permute-start | bytes 675848 | tf_op jit(solution)/shard_map/ppermute | solution.py:121
  15.5 8.3 %collective-permute-start.7 = (bf16[176,640]{1,0:T(8,128)(2,1)S(1)}, bf16[176,640]{1,0:T(8,128)(2,1)S(1)}, u32[]{:S(2)}, u32[]{:S(2)}) collective-permute-start(bf16[176,640]{1,0:T(8,128)(2,1)S(1)} %collective-permute-done.4), channel_id=1, source_target_pairs={{0,2},{2,0},{4,6},{6,4},{8,10},{10,8},{12,14},{14,12},{16,18},{18,... | collective-permute-start | bytes 675848 | tf_op jit(solution)/shard_map/ppermute | solution.py:121
  21.1 6.8 %collective-permute-start.10 = (bf16[80,640]{1,0:T(8,128)(2,1)S(1)}, bf16[80,640]{1,0:T(8,128)(2,1)S(1)}, u32[]{:S(2)}, u32[]{:S(2)}) collective-permute-start(bf16[80,640]{1,0:T(8,128)(2,1)S(1)} %copy-done.6), channel_id=1, source_target_pairs={{0,24},{2,26},{4,28},{6,30},{8,16},{10,18},{12,20},{14,22},{16,8},... | collective-permute-start | bytes 307208 | tf_op jit(solution)/shard_map/ppermute | solution.py:121
  23.4 7.2 %collective-permute-start.9 = (bf16[80,640]{1,0:T(8,128)(2,1)S(1)}, bf16[80,640]{1,0:T(8,128)(2,1)S(1)}, u32[]{:S(2)}, u32[]{:S(2)}) collective-permute-start(bf16[80,640]{1,0:T(8,128)(2,1)S(1)} %copy-done.6), channel_id=1, source_target_pairs={{0,16},{2,18},{4,20},{6,22},{8,24},{10,26},{12,28},{14,30},{16,0},... | collective-permute-start | bytes 307208 | tf_op jit(solution)/shard_map/ppermute | solution.py:121
  23.8 6.8 %collective-permute-start.8 = (bf16[2,96,640]{2,1,0:T(8,128)(2,1)S(1)}, bf16[2,96,640]{2,1,0:T(8,128)(2,1)S(1)}, u32[]{:S(2)}, u32[]{:S(2)}) collective-permute-start(bf16[2,96,640]{2,1,0:T(8,128)(2,1)S(1)} %pad_maximum_fusion.5), channel_id=1, source_target_pairs={{0,2},{2,0},{4,6},{6,4},{8,10},{10,8},{12,14},{14,12},{16,18},{18,... | collective-permute-start | bytes 737288 | tf_op jit(solution)/shard_map/ppermute | solution.py:121
  25.7 8.4 %collective-permute-start.13 = (bf16[2,96,640]{2,1,0:T(8,128)(2,1)S(1)}, bf16[2,96,640]{2,1,0:T(8,128)(2,1)S(1)}, u32[]{:S(2)}, u32[]{:S(2)}) collective-permute-start(bf16[2,96,640]{2,1,0:T(8,128)(2,1)S(1)} %pad_maximum_fusion.5), channel_id=1, source_target_pairs={{0,4},{2,6},{4,0},{6,2},{8,12},{10,14},{12,8},{14,10},{16,20},{18,... | collective-permute-start | bytes 737288 | tf_op jit(solution)/shard_map/ppermute | solution.py:121
  27.6 10.2 %collective-permute-start.16 = (bf16[176,640]{1,0:T(8,128)(2,1)S(1)}, bf16[176,640]{1,0:T(8,128)(2,1)S(1)}, u32[]{:S(2)}, u32[]{:S(2)}) collective-permute-start(bf16[176,640]{1,0:T(8,128)(2,1)S(1)} %collective-permute-done.5), channel_id=1, source_target_pairs={{0,4},{2,6},{4,0},{6,2},{8,12},{10,14},{12,8},{14,10},{16,20},{18,... | collective-permute-start | bytes 675848 | tf_op jit(solution)/shard_map/ppermute | solution.py:121
  34.2 7.3 %collective-permute-start.11 = (bf16[256,640]{1,0:T(8,128)(2,1)S(1)}, bf16[256,640]{1,0:T(8,128)(2,1)S(1)}, u32[]{:S(2)}, u32[]{:S(2)}) collective-permute-start(bf16[256,640]{1,0:T(8,128)(2,1)S(1)} %get-tuple-element.28), channel_id=1, source_target_pairs={{0,4},{2,6},{4,0},{6,2},{8,12},{10,14},{12,8},{14,10},{16,20},{18,... | collective-permute-start | bytes 983048 | tf_op jit(solution)/shard_map/ppermute | solution.py:121
  38.1 10.5 %copy-start.2 = (f32[3,512,256]{2,1,0:T(8,128)S(1)}, f32[3,512,256]{2,1,0:T(8,128)}, u32[]{:S(2)}) copy-start(f32[3,512,256]{2,1,0:T(8,128)} %refs_4_.1) | copy-start | bytes 4718596
  38.2 17.8 %collective-permute-start.17 = (bf16[4,2,176,640]{3,2,1,0:T(8,128)(2,1)S(1)}, bf16[4,2,176,640]{3,2,1,0:T(8,128)(2,1)S(1)}, u32[]{:S(2)}, u32[]{:S(2)}) collective-permute-start(bf16[4,2,176,640]{3,2,1,0:T(8,128)(2,1)S(1)} %pad_maximum_fusion.refs_2_.refs_1_), channel_id=1, source_target_pairs={{0,1},{1,0},{2,3},{3,2},{4,5},{5,4},{6,7},{7,6},{8,9},{9,8},{10,11... | collective-permute-start | bytes 5406728 | tf_op jit(solution)/shard_map/ppermute | solution.py:125
  38.2 10.1 %collective-permute-start.14 = (bf16[256,640]{1,0:T(8,128)(2,1)S(1)}, bf16[256,640]{1,0:T(8,128)(2,1)S(1)}, u32[]{:S(2)}, u32[]{:S(2)}) collective-permute-start(bf16[256,640]{1,0:T(8,128)(2,1)S(1)} %get-tuple-element.29), channel_id=1, source_target_pairs={{0,2},{2,0},{4,6},{6,4},{8,10},{10,8},{12,14},{14,12},{16,18},{18,... | collective-permute-start | bytes 983048 | tf_op jit(solution)/shard_map/ppermute | solution.py:121
  41.5 10.5 %copy-start.4 = (bf16[256,640]{1,0:T(8,128)(2,1)}, bf16[256,640]{1,0:T(8,128)(2,1)S(1)}, u32[]{:S(2)}) copy-start(bf16[256,640]{1,0:T(8,128)(2,1)S(1)} %collective-permute-done.11) | copy-start | bytes 983044
  48.4 3.6 %copy-start.5 = (bf16[256,640]{1,0:T(8,128)(2,1)}, bf16[256,640]{1,0:T(8,128)(2,1)S(1)}, u32[]{:S(2)}) copy-start(bf16[256,640]{1,0:T(8,128)(2,1)S(1)} %collective-permute-done.14) | copy-start | bytes 983044
  48.4 7.5 %copy-start = (s32[3,10]{1,0:T(4,128)S(1)}, s32[3,10]{1,0:T(4,128)}, u32[]{:S(2)}) copy-start(s32[3,10]{1,0:T(4,128)} %refs_0_.1) | copy-start | bytes 364
  48.4 7.5 %copy-start.1 = (s32[3,10]{1,0:T(4,128)S(1)}, s32[3,10]{1,0:T(4,128)}, u32[]{:S(2)}) copy-start(s32[3,10]{1,0:T(4,128)} %refs_1_.1) | copy-start | bytes 364
  48.6 7.3 %collective-permute-start.18 = (bf16[4,2,96,640]{3,2,1,0:T(8,128)(2,1)S(1)}, bf16[4,2,96,640]{3,2,1,0:T(8,128)(2,1)S(1)}, u32[]{:S(2)}, u32[]{:S(2)}) collective-permute-start(bf16[4,2,96,640]{3,2,1,0:T(8,128)(2,1)S(1)} %pad_maximum_fusion.1.refs_3_), channel_id=1, source_target_pairs={{0,1},{1,0},{2,3},{3,2},{4,5},{5,4},{6,7},{7,6},{8,9},{9,8},{10,11... | collective-permute-start | bytes 2949128 | tf_op jit(solution)/shard_map/ppermute | solution.py:125
  48.7 17.8 %collective-permute-start.20 = (f32[3,512,256]{2,1,0:T(8,128)S(1)}, f32[3,512,256]{2,1,0:T(8,128)S(1)}, u32[]{:S(2)}, u32[]{:S(2)}) collective-permute-start(f32[3,512,256]{2,1,0:T(8,128)S(1)} %copy-done.2), channel_id=1, source_target_pairs={{0,1},{1,0},{2,3},{3,2},{4,5},{5,4},{6,7},{7,6},{8,9},{9,8},{10,11... | collective-permute-start | bytes 4718600 | tf_op jit(solution)/shard_map/ppermute | solution.py:125
  49.2 5.1 %collective-permute-start.15 = (bf16[80,640]{1,0:T(8,128)(2,1)S(1)}, bf16[80,640]{1,0:T(8,128)(2,1)S(1)}, u32[]{:S(2)}, u32[]{:S(2)}) collective-permute-start(bf16[80,640]{1,0:T(8,128)(2,1)S(1)} %slice.39), channel_id=1, source_target_pairs={{0,4},{2,6},{4,0},{6,2},{8,12},{10,14},{12,8},{14,10},{16,20},{18,... | collective-permute-start | bytes 307208 | tf_op jit(solution)/shard_map/ppermute | solution.py:121
  51.1 4.7 %collective-permute-start.12 = (bf16[80,640]{1,0:T(8,128)(2,1)S(1)}, bf16[80,640]{1,0:T(8,128)(2,1)S(1)}, u32[]{:S(2)}, u32[]{:S(2)}) collective-permute-start(bf16[80,640]{1,0:T(8,128)(2,1)S(1)} %slice.37), channel_id=1, source_target_pairs={{0,2},{2,0},{4,6},{6,4},{8,10},{10,8},{12,14},{14,12},{16,18},{18,... | collective-permute-start | bytes 307208 | tf_op jit(solution)/shard_map/ppermute | solution.py:121
  55.9 2.1 %slice-start = ((bf16[256,640]{1,0:T(8,128)(2,1)}), bf16[160,640]{1,0:T(8,128)(2,1)S(1)}, s32[]{:S(2)}) async-start(bf16[256,640]{1,0:T(8,128)(2,1)} %copy-done.4), calls=%async_computation | async-start | bytes 409600 | tf_op jit(solution)/shard_map/slice | solution.py:338
  55.9 2.1 %slice-start.1 = ((bf16[256,640]{1,0:T(8,128)(2,1)}), bf16[160,640]{1,0:T(8,128)(2,1)S(1)}, s32[]{:S(2)}) async-start(bf16[256,640]{1,0:T(8,128)(2,1)} %copy-done.5), calls=%async_computation.1 | async-start | bytes 409600 | tf_op jit(solution)/shard_map/slice | solution.py:337
  55.9 2.4 %copy-start.3 = (bf16[2,512,512]{2,1,0:T(8,128)(2,1)S(1)}, bf16[2,512,512]{2,1,0:T(8,128)(2,1)}, u32[]{:S(2)}) copy-start(bf16[2,512,512]{2,1,0:T(8,128)(2,1)} %refs_3_.3) | copy-start | bytes 3145732
  58.2 8.3 %collective-permute-start.19 = (bf16[4,2,80,640]{3,2,1,0:T(8,128)(2,1)S(1)}, bf16[4,2,80,640]{3,2,1,0:T(8,128)(2,1)S(1)}, u32[]{:S(2)}, u32[]{:S(2)}) collective-permute-start(bf16[4,2,80,640]{3,2,1,0:T(8,128)(2,1)S(1)} %pad_maximum_fusion.2.refs_1_), channel_id=1, source_target_pairs={{0,1},{1,0},{2,3},{3,2},{4,5},{5,4},{6,7},{7,6},{8,9},{9,8},{10,11... | collective-permute-start | bytes 2457608 | tf_op jit(solution)/shard_map/ppermute | solution.py:125

commit v5 on v3

--- a/solution.py
+++ b/solution.py
@@ -182,7 +182,7 @@
                 pt[s, :, lanes] = jnp.zeros((width, 128), bf16)
 
 
-def add_rows(wave, skip, dims, col, row, pt, z_refs, link_ref, sums, scratch):
+def add_rows(wave, skip, dims, col, row, pt, z_refs, link_ref, before, sums, scratch):
     width, span = dims
     z_all, c0h, c0l, c1h, c1l, p1h, p1l, c2h, c2l, tmp, sem = scratch
     half_rows = z_all.shape[0]
@@ -230,15 +230,15 @@
         nn2r(pt[2, c_rows, lanes], (c1h[...], c1l[...])),
         nn2r(pt[2, :, lanes], (c2h[...], c2l[...])),
     ]
-    for total, term in zip(sums, terms):
-        total[...] = term if wave == 0 else total[...] + term
+    for i, term in enumerate(terms):
+        sums[i][...] = before[i][...] + term if before else term
 
 
 def first_kernel(dims, skip, *refs):
     pt, z_refs, link_ref = refs[0], refs[1:3], refs[3]
     sums, col_out, scratch = refs[4:9], refs[9], refs[10:]
     col, row = lax.axis_index("col"), lax.axis_index("row")
-    add_rows(0, skip, dims, col, row, pt, z_refs, link_ref, sums, scratch)
+    add_rows(0, skip, dims, col, row, pt, z_refs, link_ref, (), sums, scratch)
     z_all, c0h, c0l, c1h, c1l = scratch[:5]
     tile = col_out.shape[1]
     place = row % (z_all.shape[0] // (2 * tile))
@@ -259,9 +259,7 @@
     col = lax.axis_index("col")
     width, _ = dims
     half_w = width // 2
-    for total, value in zip(sums, before):
-        total[...] = value[...]
-    add_rows(1, 0, dims, col, lax.axis_index("row"), pt, z_refs, link_ref, sums, scratch)
+    add_rows(1, 0, dims, col, lax.axis_index("row"), pt, z_refs, link_ref, before, sums, scratch)
     s0, u1, s1, n2, s2 = sums
     scale = 1.0 / rows
     c_rows = pl.ds(pl.multiple_of(col * half_w, half_w), half_w)
@@ -330,8 +328,8 @@
     f_bx, f_by = after((f_bx, f_by), *z_late)
     f_far = jnp.stack([far(f_bx[i], f_by[i], i) for i in range(count)])
     f_last = jnp.stack([f_b, f_bx, f_by, f_far])
-    f_last_other = across(f_last)
     z_b, z_bx, z_by = late_wave(z_late, f_bx, f_by)
+    f_last_other = across(after(f_last, z_bx, z_by))
     diag_other = across(diag_inverse)
 
     pt = call(
@@ -342,8 +340,10 @@
         out_specs=vmem,
     )(occupancy, row_block, first, f_last, first_other, f_last_other)
 
-    z_bx, z_by, pt = after((z_bx, z_by, pt), pt)
     z_far = jnp.stack([far(z_bx[i], z_by[i], i) for i in range(count)])
+    z_far, pt = after((z_far, pt), pt)
+    z_last = jnp.stack([z_b, z_bx, z_by, z_far])
+    z_last_other = across(z_last)
     dims = (width, span)
     half_rows, half_w = rows // 2, width // 2
     sum_shapes = [(width, width), (width, width), (width, width), (half_w, width), (width, half_w)]
@@ -361,9 +361,6 @@
         out_specs=(vmem,) * 6,
         scratch_shapes=scratch,
     )(pt, first, first_other, coupling)
-    z_far, *sums = after((z_far, *sums), sums[0])
-    z_last = jnp.stack([z_b, z_bx, z_by, z_far])
-    z_last_other = across(z_last)
     diagonals = call(
         functools.partial(last_kernel, dims, rows),
         "other_half", 12 * 10**9,

time: 74.9 us -> 74.5 us (level)
    ppermute x4, waiting for transfers between devices: 2.86 us -> 0.01 us  [across(): return lax.ppermute(value, 'col', [(0, 1), (1, 0)])]
    ppermute x19, waiting for transfers between devices: 21.5 us -> 23.8 us  [swap(): return lax.ppermute(value, axis, [(i, i ^ bit) for i in range(parts)])]
  transfers between devices with their start and end apart: 23 -> 23, of which waited for: 11 -> 10; matrix products, arithmetic and copies ran while one was open for 1% -> 1% of each run, Pallas kernels for 14% -> 14%
where the time goes in v5:
time: 74.5 us; the launch traced here: 74.3 us
  starting transfers between devices  26 us (35%)
  waiting for transfers between devices  23.8 us (32%)
  Pallas kernels  21.6 us (29%)
  other arithmetic  1.88 us (3%)
  between operations  1.03 us (1%)
    ppermute x19, starting transfers between devices, swap(): return lax.ppermute(value, axis, [(i, i ^ bit) for i in range(parts)])  25.3 us
    ppermute x19, waiting for transfers between devices, swap(): return lax.ppermute(value, axis, [(i, i ^ bit) for i in range(parts)])  23.8 us
    pallas_call x1, Pallas kernels, replicated_plan(): call(functools.partial(last_kernel, dims, rows), 'other_half', 12 * 10 **...  11.3 us
    pallas_call x1, Pallas kernels, replicated_plan(): call(functools.partial(first_kernel, dims, supers * part), 'own_half', 8...  8.18 us
    pallas_call x1, Pallas kernels, replicated_plan(): call(functools.partial(place_kernel, (supers, width, rows, span, part)),...  2.08 us
    another operation x6, other arithmetic, replicated_plan(): first = jnp.stack([jnp.stack([p[j] for p in early]) for j in range(4)])  1.5 us
  transfers between devices with their start and end apart: 23, of which 10 were waited for; matrix products, arithmetic and copies ran while one was open for 1% of the time, Pallas kernels for 14%

profile of v5, /device:TPU:0, one launch (start us, length us, event | category | flops | bytes accessed | tf_op | source)
XLA Modules:
  0.0 74.3 jit_solution(3957129606608127532)
XLA Ops:
  0.6 1.0 %fusion = (bf16[1,176,640]{2,1,0:T(8,128)(2,1)S(1)}, bf16[176,640]{1,0:T(8,128)(2,1)S(1)}) fusion(bf16[80,640]{1,0:T(8,128)(2,1)} %param.6, bf16[96,640]{1,0:T(8,128)(2,1)} %bitcast.59), kind=kLoop, calls=%fused_computation.16 | loop fusion | flops 450560 | bytes 675840 | tf_op jit(solution)/shard_map/stack | solution.py:323
  1.7 3.1 %collective-permute-start.2 = (bf16[176,640]{1,0:T(8,128)(2,1)S(1)}, bf16[176,640]{1,0:T(8,128)(2,1)S(1)}, u32[]{:S(2)}, u32[]{:S(2)}) collective-permute-start(bf16[176,640]{1,0:T(8,128)(2,1)S(1)} %get-tuple-element.33), channel_id=1, source_target_pairs={{0,8},{2,10},{4,12},{6,14},{8,0},{10,2},{12,4},{14,6},{16,24},{18,... | collective-permute-start | bytes 675848 | tf_op jit(solution)/shard_map/ppermute | solution.py:121
  4.8 1.5 %collective-permute-start.3 = (bf16[176,640]{1,0:T(8,128)(2,1)S(1)}, bf16[176,640]{1,0:T(8,128)(2,1)S(1)}, u32[]{:S(2)}, u32[]{:S(2)}) collective-permute-start(bf16[176,640]{1,0:T(8,128)(2,1)S(1)} %get-tuple-element.33), channel_id=1, source_target_pairs={{0,2},{2,0},{4,6},{6,4},{8,10},{10,8},{12,14},{14,12},{16,18},{18,... | collective-permute-start | bytes 675848 | tf_op jit(solution)/shard_map/ppermute | solution.py:121
  6.2 1.5 %collective-permute-start.4 = (bf16[176,640]{1,0:T(8,128)(2,1)S(1)}, bf16[176,640]{1,0:T(8,128)(2,1)S(1)}, u32[]{:S(2)}, u32[]{:S(2)}) collective-permute-start(bf16[176,640]{1,0:T(8,128)(2,1)S(1)} %get-tuple-element.33), channel_id=1, source_target_pairs={{0,4},{2,6},{4,0},{6,2},{8,12},{10,14},{12,8},{14,10},{16,20},{18,... | collective-permute-start | bytes 675848 | tf_op jit(solution)/shard_map/ppermute | solution.py:121
  7.8 2.6 %collective-permute-start = (bf16[96,640]{1,0:T(8,128)(2,1)}, bf16[96,640]{1,0:T(8,128)(2,1)S(1)}, u32[]{:S(2)}, u32[]{:S(2)}) collective-permute-start(bf16[96,640]{1,0:T(8,128)(2,1)} %bitcast.60), channel_id=1, source_target_pairs={{0,16},{2,18},{4,20},{6,22},{8,24},{10,26},{12,28},{14,30},{16,0},... | collective-permute-start | bytes 368648 | tf_op jit(solution)/shard_map/ppermute | solution.py:121
  10.4 0.2 collective-permute-start.1
  10.6 1.1 %collective-permute-done.3 = bf16[176,640]{1,0:T(8,128)(2,1)S(1)} collective-permute-done((bf16[176,640]{1,0:T(8,128)(2,1)S(1)}, bf16[176,640]{1,0:T(8,128)(2,1)S(1)}, u32[]{:S(2)}, u32[]{:S(2)}) %collective-permute-start.3) | collective-permute-done | bytes 225312 | tf_op jit(solution)/shard_map/ppermute | solution.py:121
  11.7 1.2 %collective-permute-done.4 = bf16[176,640]{1,0:T(8,128)(2,1)S(1)} collective-permute-done((bf16[176,640]{1,0:T(8,128)(2,1)S(1)}, bf16[176,640]{1,0:T(8,128)(2,1)S(1)}, u32[]{:S(2)}, u32[]{:S(2)}) %collective-permute-start.4) | collective-permute-done | bytes 225312 | tf_op jit(solution)/shard_map/ppermute | solution.py:121
  12.9 0.5 collective-permute-start.5
  13.5 2.0 %collective-permute-start.6 = (bf16[176,640]{1,0:T(8,128)(2,1)S(1)}, bf16[176,640]{1,0:T(8,128)(2,1)S(1)}, u32[]{:S(2)}, u32[]{:S(2)}) collective-permute-start(bf16[176,640]{1,0:T(8,128)(2,1)S(1)} %collective-permute-done.2), channel_id=1, source_target_pairs={{0,4},{2,6},{4,0},{6,2},{8,12},{10,14},{12,8},{14,10},{16,20},{18,... | collective-permute-start | bytes 675848 | tf_op jit(solution)/shard_map/ppermute | solution.py:121
  15.5 1.0 %collective-permute-start.9 = (bf16[176,640]{1,0:T(8,128)(2,1)S(1)}, bf16[176,640]{1,0:T(8,128)(2,1)S(1)}, u32[]{:S(2)}, u32[]{:S(2)}) collective-permute-start(bf16[176,640]{1,0:T(8,128)(2,1)S(1)} %collective-permute-done.4), channel_id=1, source_target_pairs={{0,2},{2,0},{4,6},{6,4},{8,10},{10,8},{12,14},{14,12},{16,18},{18,... | collective-permute-start | bytes 675848 | tf_op jit(solution)/shard_map/ppermute | solution.py:121
  16.5 3.2 %collective-permute-done = bf16[96,640]{1,0:T(8,128)(2,1)S(1)} collective-permute-done((bf16[96,640]{1,0:T(8,128)(2,1)}, bf16[96,640]{1,0:T(8,128)(2,1)S(1)}, u32[]{:S(2)}, u32[]{:S(2)}) %collective-permute-start) | collective-permute-done | bytes 122912 | tf_op jit(solution)/shard_map/ppermute | solution.py:121
  19.7 0.1 maximum_bitcast_fusion
  19.8 1.3 %collective-permute-done.5 = bf16[176,640]{1,0:T(8,128)(2,1)S(1)} collective-permute-done((bf16[176,640]{1,0:T(8,128)(2,1)S(1)}, bf16[176,640]{1,0:T(8,128)(2,1)S(1)}, u32[]{:S(2)}, u32[]{:S(2)}) %collective-permute-start.5) | collective-permute-done | bytes 225312 | tf_op jit(solution)/shard_map/ppermute | solution.py:121
  21.1 0.0 collective-permute-done.6
  21.1 2.2 %collective-permute-start.8 = (bf16[80,640]{1,0:T(8,128)(2,1)S(1)}, bf16[80,640]{1,0:T(8,128)(2,1)S(1)}, u32[]{:S(2)}, u32[]{:S(2)}) collective-permute-start(bf16[80,640]{1,0:T(8,128)(2,1)S(1)} %copy-done.4), channel_id=1, source_target_pairs={{0,24},{2,26},{4,28},{6,30},{8,16},{10,18},{12,20},{14,22},{16,8},... | collective-permute-start | bytes 307208 | tf_op jit(solution)/shard_map/ppermute | solution.py:121
  23.4 0.4 collective-permute-start.7
  23.8 0.0 collective-permute-done.9
  23.8 1.9 %collective-permute-start.10 = (bf16[2,96,640]{2,1,0:T(8,128)(2,1)S(1)}, bf16[2,96,640]{2,1,0:T(8,128)(2,1)S(1)}, u32[]{:S(2)}, u32[]{:S(2)}) collective-permute-start(bf16[2,96,640]{2,1,0:T(8,128)(2,1)S(1)} %pad_maximum_fusion.3), channel_id=1, source_target_pairs={{0,2},{2,0},{4,6},{6,4},{8,10},{10,8},{12,14},{14,12},{16,18},{18,... | collective-permute-start | bytes 737288 | tf_op jit(solution)/shard_map/ppermute | solution.py:121
  25.7 1.9 %collective-permute-start.11 = (bf16[2,96,640]{2,1,0:T(8,128)(2,1)S(1)}, bf16[2,96,640]{2,1,0:T(8,128)(2,1)S(1)}, u32[]{:S(2)}, u32[]{:S(2)}) collective-permute-start(bf16[2,96,640]{2,1,0:T(8,128)(2,1)S(1)} %pad_maximum_fusion.3), channel_id=1, source_target_pairs={{0,4},{2,6},{4,0},{6,2},{8,12},{10,14},{12,8},{14,10},{16,20},{18,... | collective-permute-start | bytes 737288 | tf_op jit(solution)/shard_map/ppermute | solution.py:121
  27.6 0.2 collective-permute-start.16
  27.7 0.1 maximum_bitcast_fusion.2
  27.8 0.1 maximum_bitcast_fusion.1
  27.8 6.5 %collective-permute-done.16 = bf16[176,640]{1,0:T(8,128)(2,1)S(1)} collective-permute-done((bf16[176,640]{1,0:T(8,128)(2,1)S(1)}, bf16[176,640]{1,0:T(8,128)(2,1)S(1)}, u32[]{:S(2)}, u32[]{:S(2)}) %collective-permute-start.16) | collective-permute-done | bytes 225312 | tf_op jit(solution)/shard_map/ppermute | solution.py:121
  34.3 0.1 maximum_bitcast_fusion.3
  34.4 0.3 pad_maximum_fusion.refs_2_.refs_1_
  34.6 0.0 copy-start.2
  34.6 0.1 collective-permute-start.19
  34.7 0.0 collective-permute-done.8
  34.8 1.9 %collective-permute-start.18 = (bf16[96,640]{1,0:T(8,128)(2,1)S(1)}, bf16[96,640]{1,0:T(8,128)(2,1)S(1)}, u32[]{:S(2)}, u32[]{:S(2)}) collective-permute-start(bf16[96,640]{1,0:T(8,128)(2,1)S(1)} %slice_bitcast_fusion), channel_id=1, source_target_pairs={{0,4},{2,6},{4,0},{6,2},{8,12},{10,14},{12,8},{14,10},{16,20},{18,... | collective-permute-start | bytes 368648 | tf_op jit(solution)/shard_map/ppermute | solution.py:121
  36.7 0.8 %collective-permute-start.17 = (bf16[96,640]{1,0:T(8,128)(2,1)S(1)}, bf16[96,640]{1,0:T(8,128)(2,1)S(1)}, u32[]{:S(2)}, u32[]{:S(2)}) collective-permute-start(bf16[96,640]{1,0:T(8,128)(2,1)S(1)} %slice_bitcast_fusion.1), channel_id=1, source_target_pairs={{0,2},{2,0},{4,6},{6,4},{8,10},{10,8},{12,14},{14,12},{16,18},{18,... | collective-permute-start | bytes 368648 | tf_op jit(solution)/shard_map/ppermute | solution.py:121
  37.6 1.3 %collective-permute-start.14 = (bf16[2,80,640]{2,1,0:T(8,128)(2,1)S(1)}, bf16[2,80,640]{2,1,0:T(8,128)(2,1)S(1)}, u32[]{:S(2)}, u32[]{:S(2)}) collective-permute-start(bf16[2,80,640]{2,1,0:T(8,128)(2,1)S(1)} %pad_maximum_fusion.5), channel_id=1, source_target_pairs={{0,2},{2,0},{4,6},{6,4},{8,10},{10,8},{12,14},{14,12},{16,18},{18,... | collective-permute-start | bytes 614408 | tf_op jit(solution)/shard_map/ppermute | solution.py:121
  38.9 0.2 collective-permute-start.12
  39.1 1.6 %collective-permute-done.18 = bf16[96,640]{1,0:T(8,128)(2,1)S(1)} collective-permute-done((bf16[96,640]{1,0:T(8,128)(2,1)S(1)}, bf16[96,640]{1,0:T(8,128)(2,1)S(1)}, u32[]{:S(2)}, u32[]{:S(2)}) %collective-permute-start.18) | collective-permute-done | bytes 122912 | tf_op jit(solution)/shard_map/ppermute | solution.py:121
  40.7 2.3 %collective-permute-done.17 = bf16[96,640]{1,0:T(8,128)(2,1)S(1)} collective-permute-done((bf16[96,640]{1,0:T(8,128)(2,1)S(1)}, bf16[96,640]{1,0:T(8,128)(2,1)S(1)}, u32[]{:S(2)}, u32[]{:S(2)}) %collective-permute-start.17) | collective-permute-done | bytes 122912 | tf_op jit(solution)/shard_map/ppermute | solution.py:121
  43.0 0.1 pad_maximum_fusion.1.refs_3_
  43.1 3.5 %collective-permute-done.14 = bf16[2,80,640]{2,1,0:T(8,128)(2,1)S(1)} collective-permute-done((bf16[2,80,640]{2,1,0:T(8,128)(2,1)S(1)}, bf16[2,80,640]{2,1,0:T(8,128)(2,1)S(1)}, u32[]{:S(2)}, u32[]{:S(2)}) %collective-permute-start.14) | collective-permute-done | bytes 204832 | tf_op jit(solution)/shard_map/ppermute | solution.py:121
  46.6 0.5 collective-permute-start.22
  47.1 0.4 collective-permute-start.15
  47.5 1.7 %collective-permute-start.13 = (bf16[80,640]{1,0:T(8,128)(2,1)S(1)}, bf16[80,640]{1,0:T(8,128)(2,1)S(1)}, u32[]{:S(2)}, u32[]{:S(2)}) collective-permute-start(bf16[80,640]{1,0:T(8,128)(2,1)S(1)} %slice_bitcast_fusion.3), channel_id=1, source_target_pairs={{0,2},{2,0},{4,6},{6,4},{8,10},{10,8},{12,14},{14,12},{16,18},{18,... | collective-permute-start | bytes 307208 | tf_op jit(solution)/shard_map/ppermute | solution.py:121
  49.2 2.9 %collective-permute-done.15 = bf16[80,640]{1,0:T(8,128)(2,1)S(1)} collective-permute-done((bf16[80,640]{1,0:T(8,128)(2,1)S(1)}, bf16[80,640]{1,0:T(8,128)(2,1)S(1)}, u32[]{:S(2)}, u32[]{:S(2)}) %collective-permute-start.15) | collective-permute-done | bytes 102432 | tf_op jit(solution)/shard_map/ppermute | solution.py:121
  52.1 0.2 collective-permute-done.13
  52.3 0.0 copy-start.3
  52.3 2.1 %place.1.refs_0_ = bf16[3,512,1280]{2,1,0:T(8,128)(2,1)S(1)} custom-call(s32[3,10]{1,0:T(4,128)S(1)} %copy-done, s32[3,10]{1,0:T(4,128)S(1)} %copy-done.1, bf16[4,2,176,640]{3,2,1,0:T(8,128)(2,1)S(1)} %pad_maximum_fusion.refs_2_.refs_1_, bf16[4,2,96,640]{3,2,1,0:T(8,128)(2,1)S(1)} %pad_maximum_fusion.1.refs_3_, ...), custom_call_target="tpu_custom_call" | custom-call | flops 2000000000 | bytes 8388608 | tf_op jit(solution)/shard_map/place/pallas_call | solution.py:335
  54.4 0.1 pad_maximum_fusion.2.refs_1_
  54.5 0.1 collective-permute-start.21
  54.6 8.2 %own_half.1 = (f32[512,512]{1,0:T(8,128)S(1)}, f32[512,512]{1,0:T(8,128)S(1)}, f32[512,512]{1,0:T(8,128)S(1)}, f32[256,512]{1,0:T(8,128)S(1)}, f32[512,256]{1,0:T(8,128)S(1)}, /*index=5*/f32[3,40,512]{2,1,0:T(8,128)}) custom-call(bf16[3,512,1280]{2,1,0:T(8,128)(2,1)S(1)} %place.1.refs_0_, bf16[4,2,176,640]{3,2,1,0:T(8,128)(2,1)S(1)} %pad_maximum_fusion.refs_2_.refs_1_, ...), custom_call_target="tpu_custom_call" | custom-call | flops 8000000000 | bytes 8388608 | tf_op jit(solution)/shard_map/own_half/pallas_call | solution.py:356
  62.8 11.3 %other_half.1 = f32[3,512,256]{2,1,0:T(8,128)} custom-call(bf16[3,512,1280]{2,1,0:T(8,128)(2,1)S(1)} %place.1.refs_0_, bf16[4,2,80,640]{3,2,1,0:T(8,128)(2,1)S(1)} %pad_maximum_fusion.2.refs_1_, bf16[4,2,80,640]{3,2,1,0:T(8,128)(2,1)S(1)} %collective-permute-done.21.refs_2_, bf16[2,512,512]{2,1,0:T(8,128)(2,1)S(1)} %copy-done.3, ...), custom_call_target="tpu_custom_call" | custom-call | flops 12000000000 | bytes 8388608 | tf_op jit(solution)/shard_map/other_half/pallas_call | solution.py:364
  (27 shorter events, 0.2 us)
Async XLA Ops:
  0.6 20.5 %copy-start.4 = (bf16[80,640]{1,0:T(8,128)(2,1)S(1)}, bf16[80,640]{1,0:T(8,128)(2,1)}, u32[]{:S(2)}) copy-start(bf16[80,640]{1,0:T(8,128)(2,1)} %param.6) | copy-start | bytes 307204
  1.7 8.9 %collective-permute-start.2 = (bf16[176,640]{1,0:T(8,128)(2,1)S(1)}, bf16[176,640]{1,0:T(8,128)(2,1)S(1)}, u32[]{:S(2)}, u32[]{:S(2)}) collective-permute-start(bf16[176,640]{1,0:T(8,128)(2,1)S(1)} %get-tuple-element.33), channel_id=1, source_target_pairs={{0,8},{2,10},{4,12},{6,14},{8,0},{10,2},{12,4},{14,6},{16,24},{18,... | collective-permute-start | bytes 675848 | tf_op jit(solution)/shard_map/ppermute | solution.py:121
  4.8 7.0 %collective-permute-start.3 = (bf16[176,640]{1,0:T(8,128)(2,1)S(1)}, bf16[176,640]{1,0:T(8,128)(2,1)S(1)}, u32[]{:S(2)}, u32[]{:S(2)}) collective-permute-start(bf16[176,640]{1,0:T(8,128)(2,1)S(1)} %get-tuple-element.33), channel_id=1, source_target_pairs={{0,2},{2,0},{4,6},{6,4},{8,10},{10,8},{12,14},{14,12},{16,18},{18,... | collective-permute-start | bytes 675848 | tf_op jit(solution)/shard_map/ppermute | solution.py:121
  6.2 6.7 %collective-permute-start.4 = (bf16[176,640]{1,0:T(8,128)(2,1)S(1)}, bf16[176,640]{1,0:T(8,128)(2,1)S(1)}, u32[]{:S(2)}, u32[]{:S(2)}) collective-permute-start(bf16[176,640]{1,0:T(8,128)(2,1)S(1)} %get-tuple-element.33), channel_id=1, source_target_pairs={{0,4},{2,6},{4,0},{6,2},{8,12},{10,14},{12,8},{14,10},{16,20},{18,... | collective-permute-start | bytes 675848 | tf_op jit(solution)/shard_map/ppermute | solution.py:121
  7.8 11.9 %collective-permute-start = (bf16[96,640]{1,0:T(8,128)(2,1)}, bf16[96,640]{1,0:T(8,128)(2,1)S(1)}, u32[]{:S(2)}, u32[]{:S(2)}) collective-permute-start(bf16[96,640]{1,0:T(8,128)(2,1)} %bitcast.60), channel_id=1, source_target_pairs={{0,16},{2,18},{4,20},{6,22},{8,24},{10,26},{12,28},{14,30},{16,0},... | collective-permute-start | bytes 368648 | tf_op jit(solution)/shard_map/ppermute | solution.py:121
  10.4 9.3 %collective-permute-start.1 = (bf16[96,640]{1,0:T(8,128)(2,1)}, bf16[96,640]{1,0:T(8,128)(2,1)S(1)}, u32[]{:S(2)}, u32[]{:S(2)}) collective-permute-start(bf16[96,640]{1,0:T(8,128)(2,1)} %bitcast.61), channel_id=1, source_target_pairs={{0,24},{2,26},{4,28},{6,30},{8,16},{10,18},{12,20},{14,22},{16,8},... | collective-permute-start | bytes 368648 | tf_op jit(solution)/shard_map/ppermute | solution.py:121
  12.9 8.2 %collective-permute-start.5 = (bf16[176,640]{1,0:T(8,128)(2,1)S(1)}, bf16[176,640]{1,0:T(8,128)(2,1)S(1)}, u32[]{:S(2)}, u32[]{:S(2)}) collective-permute-start(bf16[176,640]{1,0:T(8,128)(2,1)S(1)} %collective-permute-done.2), channel_id=1, source_target_pairs={{0,2},{2,0},{4,6},{6,4},{8,10},{10,8},{12,14},{14,12},{16,18},{18,... | collective-permute-start | bytes 675848 | tf_op jit(solution)/shard_map/ppermute | solution.py:121
  13.5 7.7 %collective-permute-start.6 = (bf16[176,640]{1,0:T(8,128)(2,1)S(1)}, bf16[176,640]{1,0:T(8,128)(2,1)S(1)}, u32[]{:S(2)}, u32[]{:S(2)}) collective-permute-start(bf16[176,640]{1,0:T(8,128)(2,1)S(1)} %collective-permute-done.2), channel_id=1, source_target_pairs={{0,4},{2,6},{4,0},{6,2},{8,12},{10,14},{12,8},{14,10},{16,20},{18,... | collective-permute-start | bytes 675848 | tf_op jit(solution)/shard_map/ppermute | solution.py:121
  15.5 8.3 %collective-permute-start.9 = (bf16[176,640]{1,0:T(8,128)(2,1)S(1)}, bf16[176,640]{1,0:T(8,128)(2,1)S(1)}, u32[]{:S(2)}, u32[]{:S(2)}) collective-permute-start(bf16[176,640]{1,0:T(8,128)(2,1)S(1)} %collective-permute-done.4), channel_id=1, source_target_pairs={{0,2},{2,0},{4,6},{6,4},{8,10},{10,8},{12,14},{14,12},{16,18},{18,... | collective-permute-start | bytes 675848 | tf_op jit(solution)/shard_map/ppermute | solution.py:121
  21.1 13.6 %collective-permute-start.8 = (bf16[80,640]{1,0:T(8,128)(2,1)S(1)}, bf16[80,640]{1,0:T(8,128)(2,1)S(1)}, u32[]{:S(2)}, u32[]{:S(2)}) collective-permute-start(bf16[80,640]{1,0:T(8,128)(2,1)S(1)} %copy-done.4), channel_id=1, source_target_pairs={{0,24},{2,26},{4,28},{6,30},{8,16},{10,18},{12,20},{14,22},{16,8},... | collective-permute-start | bytes 307208 | tf_op jit(solution)/shard_map/ppermute | solution.py:121
  23.4 11.4 %collective-permute-start.7 = (bf16[80,640]{1,0:T(8,128)(2,1)S(1)}, bf16[80,640]{1,0:T(8,128)(2,1)S(1)}, u32[]{:S(2)}, u32[]{:S(2)}) collective-permute-start(bf16[80,640]{1,0:T(8,128)(2,1)S(1)} %copy-done.4), channel_id=1, source_target_pairs={{0,16},{2,18},{4,20},{6,22},{8,24},{10,26},{12,28},{14,30},{16,0},... | collective-permute-start | bytes 307208 | tf_op jit(solution)/shard_map/ppermute | solution.py:121
  23.8 11.0 %collective-permute-start.10 = (bf16[2,96,640]{2,1,0:T(8,128)(2,1)S(1)}, bf16[2,96,640]{2,1,0:T(8,128)(2,1)S(1)}, u32[]{:S(2)}, u32[]{:S(2)}) collective-permute-start(bf16[2,96,640]{2,1,0:T(8,128)(2,1)S(1)} %pad_maximum_fusion.3), channel_id=1, source_target_pairs={{0,2},{2,0},{4,6},{6,4},{8,10},{10,8},{12,14},{14,12},{16,18},{18,... | collective-permute-start | bytes 737288 | tf_op jit(solution)/shard_map/ppermute | solution.py:121
  25.7 9.1 %collective-permute-start.11 = (bf16[2,96,640]{2,1,0:T(8,128)(2,1)S(1)}, bf16[2,96,640]{2,1,0:T(8,128)(2,1)S(1)}, u32[]{:S(2)}, u32[]{:S(2)}) collective-permute-start(bf16[2,96,640]{2,1,0:T(8,128)(2,1)S(1)} %pad_maximum_fusion.3), channel_id=1, source_target_pairs={{0,4},{2,6},{4,0},{6,2},{8,12},{10,14},{12,8},{14,10},{16,20},{18,... | collective-permute-start | bytes 737288 | tf_op jit(solution)/shard_map/ppermute | solution.py:121
  27.6 6.7 %collective-permute-start.16 = (bf16[176,640]{1,0:T(8,128)(2,1)S(1)}, bf16[176,640]{1,0:T(8,128)(2,1)S(1)}, u32[]{:S(2)}, u32[]{:S(2)}) collective-permute-start(bf16[176,640]{1,0:T(8,128)(2,1)S(1)} %collective-permute-done.5), channel_id=1, source_target_pairs={{0,4},{2,6},{4,0},{6,2},{8,12},{10,14},{12,8},{14,10},{16,20},{18,... | collective-permute-start | bytes 675848 | tf_op jit(solution)/shard_map/ppermute | solution.py:121
  34.6 12.0 %copy-start.2 = (f32[3,512,256]{2,1,0:T(8,128)S(1)}, f32[3,512,256]{2,1,0:T(8,128)}, u32[]{:S(2)}) copy-start(f32[3,512,256]{2,1,0:T(8,128)} %refs_4_.1) | copy-start | bytes 4718596
  34.6 17.7 %collective-permute-start.19 = (bf16[4,2,176,640]{3,2,1,0:T(8,128)(2,1)S(1)}, bf16[4,2,176,640]{3,2,1,0:T(8,128)(2,1)S(1)}, u32[]{:S(2)}, u32[]{:S(2)}) collective-permute-start(bf16[4,2,176,640]{3,2,1,0:T(8,128)(2,1)S(1)} %pad_maximum_fusion.refs_2_.refs_1_), channel_id=1, source_target_pairs={{0,1},{1,0},{2,3},{3,2},{4,5},{5,4},{6,7},{7,6},{8,9},{9,8},{10,11... | collective-permute-start | bytes 5406728 | tf_op jit(solution)/shard_map/ppermute | solution.py:125
  34.8 5.9 %collective-permute-start.18 = (bf16[96,640]{1,0:T(8,128)(2,1)S(1)}, bf16[96,640]{1,0:T(8,128)(2,1)S(1)}, u32[]{:S(2)}, u32[]{:S(2)}) collective-permute-start(bf16[96,640]{1,0:T(8,128)(2,1)S(1)} %slice_bitcast_fusion), channel_id=1, source_target_pairs={{0,4},{2,6},{4,0},{6,2},{8,12},{10,14},{12,8},{14,10},{16,20},{18,... | collective-permute-start | bytes 368648 | tf_op jit(solution)/shard_map/ppermute | solution.py:121
  36.7 6.2 %collective-permute-start.17 = (bf16[96,640]{1,0:T(8,128)(2,1)S(1)}, bf16[96,640]{1,0:T(8,128)(2,1)S(1)}, u32[]{:S(2)}, u32[]{:S(2)}) collective-permute-start(bf16[96,640]{1,0:T(8,128)(2,1)S(1)} %slice_bitcast_fusion.1), channel_id=1, source_target_pairs={{0,2},{2,0},{4,6},{6,4},{8,10},{10,8},{12,14},{14,12},{16,18},{18,... | collective-permute-start | bytes 368648 | tf_op jit(solution)/shard_map/ppermute | solution.py:121
  37.6 14.8 %copy-start = (s32[3,10]{1,0:T(4,128)S(1)}, s32[3,10]{1,0:T(4,128)}, u32[]{:S(2)}) copy-start(s32[3,10]{1,0:T(4,128)} %refs_0_.1) | copy-start | bytes 364
  37.6 14.8 %copy-start.1 = (s32[3,10]{1,0:T(4,128)S(1)}, s32[3,10]{1,0:T(4,128)}, u32[]{:S(2)}) copy-start(s32[3,10]{1,0:T(4,128)} %refs_1_.1) | copy-start | bytes 364
  37.6 9.0 %collective-permute-start.14 = (bf16[2,80,640]{2,1,0:T(8,128)(2,1)S(1)}, bf16[2,80,640]{2,1,0:T(8,128)(2,1)S(1)}, u32[]{:S(2)}, u32[]{:S(2)}) collective-permute-start(bf16[2,80,640]{2,1,0:T(8,128)(2,1)S(1)} %pad_maximum_fusion.5), channel_id=1, source_target_pairs={{0,2},{2,0},{4,6},{6,4},{8,10},{10,8},{12,14},{14,12},{16,18},{18,... | collective-permute-start | bytes 614408 | tf_op jit(solution)/shard_map/ppermute | solution.py:121
  38.9 7.7 %collective-permute-start.12 = (bf16[2,80,640]{2,1,0:T(8,128)(2,1)S(1)}, bf16[2,80,640]{2,1,0:T(8,128)(2,1)S(1)}, u32[]{:S(2)}, u32[]{:S(2)}) collective-permute-start(bf16[2,80,640]{2,1,0:T(8,128)(2,1)S(1)} %pad_maximum_fusion.5), channel_id=1, source_target_pairs={{0,4},{2,6},{4,0},{6,2},{8,12},{10,14},{12,8},{14,10},{16,20},{18,... | collective-permute-start | bytes 614408 | tf_op jit(solution)/shard_map/ppermute | solution.py:121
  46.6 5.7 %collective-permute-start.20 = (bf16[4,2,96,640]{3,2,1,0:T(8,128)(2,1)S(1)}, bf16[4,2,96,640]{3,2,1,0:T(8,128)(2,1)S(1)}, u32[]{:S(2)}, u32[]{:S(2)}) collective-permute-start(bf16[4,2,96,640]{3,2,1,0:T(8,128)(2,1)S(1)} %pad_maximum_fusion.1.refs_3_), channel_id=1, source_target_pairs={{0,1},{1,0},{2,3},{3,2},{4,5},{5,4},{6,7},{7,6},{8,9},{9,8},{10,11... | collective-permute-start | bytes 2949128 | tf_op jit(solution)/shard_map/ppermute | solution.py:125
  46.6 16.2 %collective-permute-start.22 = (f32[3,512,256]{2,1,0:T(8,128)S(1)}, f32[3,512,256]{2,1,0:T(8,128)S(1)}, u32[]{:S(2)}, u32[]{:S(2)}) collective-permute-start(f32[3,512,256]{2,1,0:T(8,128)S(1)} %copy-done.2), channel_id=1, source_target_pairs={{0,1},{1,0},{2,3},{3,2},{4,5},{5,4},{6,7},{7,6},{8,9},{9,8},{10,11... | collective-permute-start | bytes 4718600 | tf_op jit(solution)/shard_map/ppermute | solution.py:125
  47.1 4.9 %collective-permute-start.15 = (bf16[80,640]{1,0:T(8,128)(2,1)S(1)}, bf16[80,640]{1,0:T(8,128)(2,1)S(1)}, u32[]{:S(2)}, u32[]{:S(2)}) collective-permute-start(bf16[80,640]{1,0:T(8,128)(2,1)S(1)} %slice_bitcast_fusion.2), channel_id=1, source_target_pairs={{0,4},{2,6},{4,0},{6,2},{8,12},{10,14},{12,8},{14,10},{16,20},{18,... | collective-permute-start | bytes 307208 | tf_op jit(solution)/shard_map/ppermute | solution.py:121
  47.5 4.7 %collective-permute-start.13 = (bf16[80,640]{1,0:T(8,128)(2,1)S(1)}, bf16[80,640]{1,0:T(8,128)(2,1)S(1)}, u32[]{:S(2)}, u32[]{:S(2)}) collective-permute-start(bf16[80,640]{1,0:T(8,128)(2,1)S(1)} %slice_bitcast_fusion.3), channel_id=1, source_target_pairs={{0,2},{2,0},{4,6},{6,4},{8,10},{10,8},{12,14},{14,12},{16,18},{18,... | collective-permute-start | bytes 307208 | tf_op jit(solution)/shard_map/ppermute | solution.py:121
  52.3 2.4 %copy-start.3 = (bf16[2,512,512]{2,1,0:T(8,128)(2,1)S(1)}, bf16[2,512,512]{2,1,0:T(8,128)(2,1)}, u32[]{:S(2)}) copy-start(bf16[2,512,512]{2,1,0:T(8,128)(2,1)} %refs_3_.3) | copy-start | bytes 3145732
  54.5 8.3 %collective-permute-start.21 = (bf16[4,2,80,640]{3,2,1,0:T(8,128)(2,1)S(1)}, bf16[4,2,80,640]{3,2,1,0:T(8,128)(2,1)S(1)}, u32[]{:S(2)}, u32[]{:S(2)}) collective-permute-start(bf16[4,2,80,640]{3,2,1,0:T(8,128)(2,1)S(1)} %pad_maximum_fusion.2.refs_1_), channel_id=1, source_target_pairs={{0,1},{1,0},{2,3},{3,2},{4,5},{5,4},{6,7},{7,6},{8,9},{9,8},{10,11... | collective-permute-start | bytes 2457608 | tf_op jit(solution)/shard_map/ppermute | solution.py:125

commit v6 on v3

--- a/solution.py
+++ b/solution.py
@@ -12,7 +12,7 @@
 bf16 = jnp.bfloat16
 
 REPLICATE_BYTES = 12 * 2**20
-VMEM_LIMIT = 40 * 2**20
+VMEM_LIMIT = 36 * 2**20
 
 
 def routed(gathered, occupancy, row_block, nblocks):
@@ -182,11 +182,8 @@
                 pt[s, :, lanes] = jnp.zeros((width, 128), bf16)
 
 
-def add_rows(wave, skip, dims, col, row, pt, z_refs, link_ref, sums, scratch):
-    width, span = dims
-    z_all, c0h, c0l, c1h, c1l, p1h, p1l, c2h, c2l, tmp, sem = scratch
+def load_rows(wave, skip, span, col, row, z_refs, z_all, sem):
     half_rows = z_all.shape[0]
-    half_w = width // 2
     copies = []
     for side in range(2):
         target = col if side == 0 else 1 - col
@@ -209,10 +206,19 @@
         copy.start()
     for copy in copies:
         copy.wait()
-    c_rows = pl.ds(pl.multiple_of(col * half_w, half_w), half_w)
-    half = owner_of(row, wave, z_refs[0].shape[1], 0, 0) // (half_rows // local_rows)
-    lanes = pl.ds(pl.multiple_of(half * half_rows, half_rows), half_rows)
-    zm = z_all[...]
+
+
+def halves(col, half_w):
+    return pl.ds(pl.multiple_of(col * half_w, half_w), half_w)
+
+
+def lanes_of(row, wave, local_rows, half_rows, count):
+    half = owner_of(row, wave, count, 0, 0) // (half_rows // local_rows)
+    return pl.ds(pl.multiple_of(half * half_rows, half_rows), half_rows)
+
+
+def row_products(pt, link_ref, zm, c_rows, held, tmp):
+    c0h, c0l, p1h, p1l, c1h, c1l, c2h, c2l = held
     cols0 = split2(-nt(zm, pt[0]))
     c0h[...], c0l[...] = cols0
     tmp[...] = nn2(cols0, link_ref[0])
@@ -222,58 +228,80 @@
     c1h[...], c1l[...] = cols1
     cols2 = -(nt(zm, pt[2, c_rows, :]) + nn2(cols1, link_ref[1, :, c_rows]))
     c2h[...], c2l[...] = split2(cols2)
-    left = pt[1, :, lanes]
-    terms = [
-        nn2r(pt[0, :, lanes], (c0h[...], c0l[...])),
-        nn2r(left, (p1h[...], p1l[...])),
-        nn2r(left, (c1h[...], c1l[...])),
-        nn2r(pt[2, c_rows, lanes], (c1h[...], c1l[...])),
-        nn2r(pt[2, :, lanes], (c2h[...], c2l[...])),
-    ]
-    for total, term in zip(sums, terms):
-        total[...] = term if wave == 0 else total[...] + term
-
-
-def first_kernel(dims, skip, *refs):
+
+
+def rows_kernel(dims, skip, *refs):
+    width, span = dims
     pt, z_refs, link_ref = refs[0], refs[1:3], refs[3]
-    sums, col_out, scratch = refs[4:9], refs[9], refs[10:]
+    held, z_own, z_all, tmp, sem = refs[4:12], refs[12], refs[13], refs[14], refs[15]
     col, row = lax.axis_index("col"), lax.axis_index("row")
-    add_rows(0, skip, dims, col, row, pt, z_refs, link_ref, sums, scratch)
-    z_all, c0h, c0l, c1h, c1l = scratch[:5]
+    load_rows(0, skip, span, col, row, z_refs, z_all, sem)
+    row_products(pt, link_ref, z_all[...], halves(col, width // 2), held, tmp)
+    local_rows = z_own.shape[0]
+    place = row % (z_all.shape[0] // local_rows)
+    z_own[...] = z_all[pl.ds(pl.multiple_of(place * local_rows, local_rows), local_rows), :]
+
+
+def early_sums_kernel(count, *refs):
+    pt, c0h, c0l, p1h, p1l, c1h, c1l, z_own, link_ref = refs[:9]
+    s0, u1, col_out = refs[9:]
+    col, row = lax.axis_index("col"), lax.axis_index("row")
+    local_rows, half_rows = z_own.shape[0], c0h.shape[0]
+    lanes = lanes_of(row, 0, local_rows, half_rows, count)
+    s0[...] = nn2r(pt[0, :, lanes], (c0h[...], c0l[...]))
+    u1[...] = nn2r(pt[1, :, lanes], (p1h[...], p1l[...]))
     tile = col_out.shape[1]
-    place = row % (z_all.shape[0] // (2 * tile))
-    own = pl.ds(pl.multiple_of(place * 2 * tile, 2 * tile), 2 * tile)
+    place = row % (half_rows // local_rows)
+    own = pl.ds(pl.multiple_of(place * local_rows, local_rows), local_rows)
     cols1 = (c1h[own, :], c1l[own, :])
     mine = [
         c0h[own, :].astype(f32) + c0l[own, :].astype(f32),
         cols1[0].astype(f32) + cols1[1].astype(f32),
-        -(nt(z_all[own, :], pt[2]) + nn2(cols1, link_ref[1])),
+        -(nt(z_own[...], pt[2]) + nn2(cols1, link_ref[1])),
     ]
     for s, value in enumerate(mine):
         col_out[s] = jnp.where(col == 0, value[:tile], value[tile:])
 
 
+def late_sums_kernel(count, local_rows, *refs):
+    pt, c1h, c1l, c2h, c2l = refs[:5]
+    s1, n2, s2 = refs[5:]
+    col, row = lax.axis_index("col"), lax.axis_index("row")
+    half_rows, half_w = c2h.shape
+    lanes = lanes_of(row, 0, local_rows, half_rows, count)
+    s1[...] = nn2r(pt[1, :, lanes], (c1h[...], c1l[...]))
+    n2[...] = nn2r(pt[2, halves(col, half_w), lanes], (c1h[...], c1l[...]))
+    s2[...] = nn2r(pt[2, :, lanes], (c2h[...], c2l[...]))
+
+
 def last_kernel(dims, rows, *refs):
+    width, span = dims
     pt, z_refs, link_ref, diag_ref, diag_other_ref = refs[0], refs[1:3], refs[3], refs[4], refs[5]
-    before, diag_out, sums, scratch = refs[6:11], refs[11], refs[12:17], refs[17:]
-    col = lax.axis_index("col")
-    width, _ = dims
+    before, diag_out, held, z_all, tmp, sem = refs[6:11], refs[11], refs[12:20], refs[20], refs[21], refs[22]
+    col, row = lax.axis_index("col"), lax.axis_index("row")
     half_w = width // 2
-    for total, value in zip(sums, before):
-        total[...] = value[...]
-    add_rows(1, 0, dims, col, lax.axis_index("row"), pt, z_refs, link_ref, sums, scratch)
-    s0, u1, s1, n2, s2 = sums
+    half_rows = z_all.shape[0]
+    c_rows = halves(col, half_w)
+    load_rows(1, 0, span, col, row, z_refs, z_all, sem)
+    row_products(pt, link_ref, z_all[...], c_rows, held, tmp)
+    c0h, c0l, p1h, p1l, c1h, c1l, c2h, c2l = held
+    lanes = lanes_of(row, 1, z_refs[0].shape[2], half_rows, z_refs[0].shape[1])
+    left = pt[1, :, lanes]
+    s0 = before[0][...] + nn2r(pt[0, :, lanes], (c0h[...], c0l[...]))
+    u1 = before[1][...] + nn2r(left, (p1h[...], p1l[...]))
+    s1 = before[2][...] + nn2r(left, (c1h[...], c1l[...]))
+    n2 = before[3][...] + nn2r(pt[2, c_rows, lanes], (c1h[...], c1l[...]))
+    s2 = before[4][...] + nn2r(pt[2, :, lanes], (c2h[...], c2l[...]))
     scale = 1.0 / rows
-    c_rows = pl.ds(pl.multiple_of(col * half_w, half_w), half_w)
 
     def whole(s):
         mine, theirs = diag_ref[s], diag_other_ref[s]
         return jnp.concatenate([jnp.where(col == 0, mine, theirs), jnp.where(col == 0, theirs, mine)], axis=1)
 
-    d0 = whole(0) - s0[...] * scale
-    i1 = s1[...] - u1[...].T
+    d0 = whole(0) - s0 * scale
+    i1 = s1 - u1.T
     d1 = whole(1) - i1 * scale + nn2r(link_ref[0].T, split2(nn2(split2(d0), link_ref[0])))
-    i2 = s2[...] - nn2(split2(n2[...]), link_ref[1]).T
+    i2 = s2 - nn2(split2(n2), link_ref[1]).T
     d2 = diag_ref[2] - i2 * scale + nn2r(link_ref[1].T, split2(nn2(split2(d1), link_ref[1, :, c_rows])))
     diag_out[0] = jnp.where(col == 0, d0[:, :half_w], d0[:, half_w:])
     diag_out[1] = jnp.where(col == 0, d1[:, :half_w], d1[:, half_w:])
@@ -342,35 +370,46 @@
         out_specs=vmem,
     )(occupancy, row_block, first, f_last, first_other, f_last_other)
 
-    z_bx, z_by, pt = after((z_bx, z_by, pt), pt)
-    z_far = jnp.stack([far(z_bx[i], z_by[i], i) for i in range(count)])
     dims = (width, span)
     half_rows, half_w = rows // 2, width // 2
-    sum_shapes = [(width, width), (width, width), (width, width), (half_w, width), (width, half_w)]
-    scratch = (
-        [pltpu.VMEM((half_rows, 2 * span), bf16)]
-        + [pltpu.VMEM((half_rows, width), bf16)] * 6
-        + [pltpu.VMEM((half_rows, half_w), bf16)] * 2
-        + [pltpu.VMEM((half_rows, width), f32), pltpu.SemaphoreType.DMA]
-    )
-    *sums, columns = call(
-        functools.partial(first_kernel, dims, supers * part),
-        "own_half", 8 * 10**9,
-        out_shape=tuple(shape(v, f32) for v in sum_shapes) + (shape((supers, local_rows // 2, width), f32),),
+    held_shapes = [(half_rows, width)] * 6 + [(half_rows, half_w)] * 2
+    work = [pltpu.VMEM((half_rows, 2 * span), bf16), pltpu.VMEM((half_rows, width), f32), pltpu.SemaphoreType.DMA]
+    *held, z_own = call(
+        functools.partial(rows_kernel, dims, supers * part),
+        "own_half_rows", 4 * 10**9,
+        out_shape=tuple(shape(v, bf16) for v in held_shapes) + (shape((local_rows, 2 * span), bf16),),
         in_specs=[vmem] + [any_spec] * 2 + [vmem],
-        out_specs=(vmem,) * 6,
-        scratch_shapes=scratch,
+        out_specs=(vmem,) * 9,
+        scratch_shapes=work,
     )(pt, first, first_other, coupling)
-    z_far, *sums = after((z_far, *sums), sums[0])
+    z_bx, z_by, *held = after((z_bx, z_by, *held), held[0])
+    z_far = jnp.stack([far(z_bx[i], z_by[i], i) for i in range(count)])
+    c0h, c0l, p1h, p1l, c1h, c1l, c2h, c2l = held
+    s0, u1, columns = call(
+        functools.partial(early_sums_kernel, count),
+        "early_sums", 3 * 10**9,
+        out_shape=(shape((width, width), f32),) * 2 + (shape((supers, local_rows // 2, width), f32),),
+        in_specs=[vmem] * 9,
+        out_specs=(vmem,) * 3,
+    )(pt, c0h, c0l, p1h, p1l, c1h, c1l, z_own, coupling)
+    z_far, c1h = after((z_far, c1h), s0)
     z_last = jnp.stack([z_b, z_bx, z_by, z_far])
     z_last_other = across(z_last)
+    s1, n2, s2 = call(
+        functools.partial(late_sums_kernel, count, local_rows),
+        "late_sums", 2 * 10**9,
+        out_shape=(shape((width, width), f32), shape((half_w, width), f32), shape((width, half_w), f32)),
+        in_specs=[vmem] * 5,
+        out_specs=(vmem,) * 3,
+    )(pt, c1h, c1l, c2h, c2l)
+    sums = [s0, u1, s1, n2, s2]
     diagonals = call(
         functools.partial(last_kernel, dims, rows),
         "other_half", 12 * 10**9,
         out_shape=shape((supers, width, half_w), f32),
         in_specs=[vmem] + [any_spec] * 2 + [vmem] * 8,
         out_specs=vmem,
-        scratch_shapes=[pltpu.VMEM(v, f32) for v in sum_shapes] + scratch,
+        scratch_shapes=[pltpu.VMEM(v, bf16) for v in held_shapes] + work,
     )(pt, z_last, z_last_other, coupling, diag_inverse, diag_other, *sums)
     return columns, diagonals
 

time: 74.9 us -> 75.3 us (level)
  waiting for transfers between devices: 24.3 us -> 21.7 us
  starting transfers between devices: 25.7 us -> 27.3 us
  Pallas kernels: 21.7 us -> 23.1 us
    ppermute x4, waiting for transfers between devices: 2.86 us -> 0.51 us  [across(): return lax.ppermute(value, 'col', [(0, 1), (1, 0)])]
    pallas_call x1 -> x3, Pallas kernels: 8.13 us -> 9.78 us  [the longest x1 4.96 us: replicated_plan(): call(functools.partial(rows_kernel, dims, supers * part), 'own_half_rows'...]
    ppermute x19, starting transfers between devices: 25.4 us -> 26.6 us  [swap(): return lax.ppermute(value, axis, [(i, i ^ bit) for i in range(parts)])]
  transfers between devices with their start and end apart: 23 -> 23, of which waited for: 11 -> 10; matrix products, arithmetic and copies ran while one was open for 1% -> 1% of each run, Pallas kernels for 14% -> 16%
where the time goes in v6:
time: 75.3 us; the launch traced here: 75.1 us
  starting transfers between devices  27.3 us (36%)
  Pallas kernels  23.1 us (31%)
  waiting for transfers between devices  21.7 us (29%)
  other arithmetic  1.88 us (2%)
  between operations  1.05 us (1%)
    ppermute x19, starting transfers between devices, swap(): return lax.ppermute(value, axis, [(i, i ^ bit) for i in range(parts)])  26.6 us
    ppermute x19, waiting for transfers between devices, swap(): return lax.ppermute(value, axis, [(i, i ^ bit) for i in range(parts)])  21.1 us
    pallas_call x1, Pallas kernels, replicated_plan(): call(functools.partial(last_kernel, dims, rows), 'other_half', 12 * 10 **...  11.3 us
    pallas_call x1, Pallas kernels, replicated_plan(): call(functools.partial(rows_kernel, dims, supers * part), 'own_half_rows'...  4.96 us
    pallas_call x1, Pallas kernels, replicated_plan(): call(functools.partial(early_sums_kernel, count), 'early_sums', 3 * 10 **...  3.02 us
    pallas_call x1, Pallas kernels, replicated_plan(): call(functools.partial(place_kernel, (supers, width, rows, span, part)),...  2.06 us
    pallas_call x1, Pallas kernels, replicated_plan(): call(functools.partial(late_sums_kernel, count, local_rows), 'late_sums',...  1.8 us
  transfers between devices with their start and end apart: 23, of which 10 were waited for; matrix products, arithmetic and copies ran while one was open for 1% of the time, Pallas kernels for 16%

profile of v6, /device:TPU:0, one launch (start us, length us, event | category | flops | bytes accessed | tf_op | source)
XLA Modules:
  0.0 75.1 jit_solution(11740181477319045462)
XLA Ops:
  0.6 1.0 %fusion = (bf16[1,176,640]{2,1,0:T(8,128)(2,1)S(1)}, bf16[176,640]{1,0:T(8,128)(2,1)S(1)}) fusion(bf16[80,640]{1,0:T(8,128)(2,1)} %param.6, bf16[96,640]{1,0:T(8,128)(2,1)} %bitcast.59), kind=kLoop, calls=%fused_computation.16 | loop fusion | flops 450560 | bytes 675840 | tf_op jit(solution)/shard_map/stack | solution.py:353
  1.7 3.0 %collective-permute-start.2 = (bf16[176,640]{1,0:T(8,128)(2,1)S(1)}, bf16[176,640]{1,0:T(8,128)(2,1)S(1)}, u32[]{:S(2)}, u32[]{:S(2)}) collective-permute-start(bf16[176,640]{1,0:T(8,128)(2,1)S(1)} %get-tuple-element.69), channel_id=1, source_target_pairs={{0,4},{2,6},{4,0},{6,2},{8,12},{10,14},{12,8},{14,10},{16,20},{18,... | collective-permute-start | bytes 675848 | tf_op jit(solution)/shard_map/ppermute | solution.py:121
  4.7 1.5 %collective-permute-start.1 = (bf16[176,640]{1,0:T(8,128)(2,1)S(1)}, bf16[176,640]{1,0:T(8,128)(2,1)S(1)}, u32[]{:S(2)}, u32[]{:S(2)}) collective-permute-start(bf16[176,640]{1,0:T(8,128)(2,1)S(1)} %get-tuple-element.69), channel_id=1, source_target_pairs={{0,2},{2,0},{4,6},{6,4},{8,10},{10,8},{12,14},{14,12},{16,18},{18,... | collective-permute-start | bytes 675848 | tf_op jit(solution)/shard_map/ppermute | solution.py:121
  6.2 1.6 %collective-permute-start = (bf16[176,640]{1,0:T(8,128)(2,1)S(1)}, bf16[176,640]{1,0:T(8,128)(2,1)S(1)}, u32[]{:S(2)}, u32[]{:S(2)}) collective-permute-start(bf16[176,640]{1,0:T(8,128)(2,1)S(1)} %get-tuple-element.69), channel_id=1, source_target_pairs={{0,8},{2,10},{4,12},{6,14},{8,0},{10,2},{12,4},{14,6},{16,24},{18,... | collective-permute-start | bytes 675848 | tf_op jit(solution)/shard_map/ppermute | solution.py:121
  7.8 2.6 %collective-permute-start.7 = (bf16[96,640]{1,0:T(8,128)(2,1)}, bf16[96,640]{1,0:T(8,128)(2,1)S(1)}, u32[]{:S(2)}, u32[]{:S(2)}) collective-permute-start(bf16[96,640]{1,0:T(8,128)(2,1)} %bitcast.60), channel_id=1, source_target_pairs={{0,16},{2,18},{4,20},{6,22},{8,24},{10,26},{12,28},{14,30},{16,0},... | collective-permute-start | bytes 368648 | tf_op jit(solution)/shard_map/ppermute | solution.py:121
  10.4 0.2 collective-permute-start.8
  10.6 1.1 %collective-permute-done.1 = bf16[176,640]{1,0:T(8,128)(2,1)S(1)} collective-permute-done((bf16[176,640]{1,0:T(8,128)(2,1)S(1)}, bf16[176,640]{1,0:T(8,128)(2,1)S(1)}, u32[]{:S(2)}, u32[]{:S(2)}) %collective-permute-start.1) | collective-permute-done | bytes 225312 | tf_op jit(solution)/shard_map/ppermute | solution.py:121
  11.7 3.6 %collective-permute-done = bf16[176,640]{1,0:T(8,128)(2,1)S(1)} collective-permute-done((bf16[176,640]{1,0:T(8,128)(2,1)S(1)}, bf16[176,640]{1,0:T(8,128)(2,1)S(1)}, u32[]{:S(2)}, u32[]{:S(2)}) %collective-permute-start) | collective-permute-done | bytes 225312 | tf_op jit(solution)/shard_map/ppermute | solution.py:121
  15.3 0.5 collective-permute-start.3
  15.8 0.2 collective-permute-start.4
  16.0 1.8 %collective-permute-start.5 = (bf16[176,640]{1,0:T(8,128)(2,1)S(1)}, bf16[176,640]{1,0:T(8,128)(2,1)S(1)}, u32[]{:S(2)}, u32[]{:S(2)}) collective-permute-start(bf16[176,640]{1,0:T(8,128)(2,1)S(1)} %collective-permute-done.2), channel_id=1, source_target_pairs={{0,2},{2,0},{4,6},{6,4},{8,10},{10,8},{12,14},{14,12},{16,18},{18,... | collective-permute-start | bytes 675848 | tf_op jit(solution)/shard_map/ppermute | solution.py:121
  17.8 2.5 %collective-permute-done.8 = bf16[96,640]{1,0:T(8,128)(2,1)S(1)} collective-permute-done((bf16[96,640]{1,0:T(8,128)(2,1)}, bf16[96,640]{1,0:T(8,128)(2,1)S(1)}, u32[]{:S(2)}, u32[]{:S(2)}) %collective-permute-start.8) | collective-permute-done | bytes 122912 | tf_op jit(solution)/shard_map/ppermute | solution.py:121
  20.3 0.1 maximum_bitcast_fusion
  20.4 2.0 %collective-permute-done.3 = bf16[176,640]{1,0:T(8,128)(2,1)S(1)} collective-permute-done((bf16[176,640]{1,0:T(8,128)(2,1)S(1)}, bf16[176,640]{1,0:T(8,128)(2,1)S(1)}, u32[]{:S(2)}, u32[]{:S(2)}) %collective-permute-start.3) | collective-permute-done | bytes 225312 | tf_op jit(solution)/shard_map/ppermute | solution.py:121
  22.4 3.2 %collective-permute-done.5 = bf16[176,640]{1,0:T(8,128)(2,1)S(1)} collective-permute-done((bf16[176,640]{1,0:T(8,128)(2,1)S(1)}, bf16[176,640]{1,0:T(8,128)(2,1)S(1)}, u32[]{:S(2)}, u32[]{:S(2)}) %collective-permute-start.5) | collective-permute-done | bytes 225312 | tf_op jit(solution)/shard_map/ppermute | solution.py:121
  25.5 0.5 collective-permute-start.9
  26.1 2.6 %collective-permute-start.11 = (bf16[80,640]{1,0:T(8,128)(2,1)S(1)}, bf16[80,640]{1,0:T(8,128)(2,1)S(1)}, u32[]{:S(2)}, u32[]{:S(2)}) collective-permute-start(bf16[80,640]{1,0:T(8,128)(2,1)S(1)} %copy-done.4), channel_id=1, source_target_pairs={{0,16},{2,18},{4,20},{6,22},{8,24},{10,26},{12,28},{14,30},{16,0},... | collective-permute-start | bytes 307208 | tf_op jit(solution)/shard_map/ppermute | solution.py:121
  28.6 2.0 %collective-permute-start.12 = (bf16[80,640]{1,0:T(8,128)(2,1)S(1)}, bf16[80,640]{1,0:T(8,128)(2,1)S(1)}, u32[]{:S(2)}, u32[]{:S(2)}) collective-permute-start(bf16[80,640]{1,0:T(8,128)(2,1)S(1)} %copy-done.4), channel_id=1, source_target_pairs={{0,24},{2,26},{4,28},{6,30},{8,16},{10,18},{12,20},{14,22},{16,8},... | collective-permute-start | bytes 307208 | tf_op jit(solution)/shard_map/ppermute | solution.py:121
  30.7 2.0 %collective-permute-start.6 = (bf16[176,640]{1,0:T(8,128)(2,1)S(1)}, bf16[176,640]{1,0:T(8,128)(2,1)S(1)}, u32[]{:S(2)}, u32[]{:S(2)}) collective-permute-start(bf16[176,640]{1,0:T(8,128)(2,1)S(1)} %collective-permute-done.3), channel_id=1, source_target_pairs={{0,4},{2,6},{4,0},{6,2},{8,12},{10,14},{12,8},{14,10},{16,20},{18,... | collective-permute-start | bytes 675848 | tf_op jit(solution)/shard_map/ppermute | solution.py:121
  32.7 0.1 maximum_bitcast_fusion.1
  32.7 0.1 maximum_bitcast_fusion.2
  32.8 3.8 %collective-permute-done.6 = bf16[176,640]{1,0:T(8,128)(2,1)S(1)} collective-permute-done((bf16[176,640]{1,0:T(8,128)(2,1)S(1)}, bf16[176,640]{1,0:T(8,128)(2,1)S(1)}, u32[]{:S(2)}, u32[]{:S(2)}) %collective-permute-start.6) | collective-permute-done | bytes 225312 | tf_op jit(solution)/shard_map/ppermute | solution.py:121
  36.6 0.1 maximum_bitcast_fusion.3
  36.7 0.3 pad_maximum_fusion.refs_2_.refs_1_
  37.0 0.0 copy-start.2
  37.0 0.0 copy-start
  37.0 0.1 collective-permute-start.15
  37.1 1.6 %collective-permute-start.13 = (bf16[96,640]{1,0:T(8,128)(2,1)S(1)}, bf16[96,640]{1,0:T(8,128)(2,1)S(1)}, u32[]{:S(2)}, u32[]{:S(2)}) collective-permute-start(bf16[96,640]{1,0:T(8,128)(2,1)S(1)} %slice_bitcast_fusion.1), channel_id=1, source_target_pairs={{0,2},{2,0},{4,6},{6,4},{8,10},{10,8},{12,14},{14,12},{16,18},{18,... | collective-permute-start | bytes 368648 | tf_op jit(solution)/shard_map/ppermute | solution.py:121
  38.8 2.1 %collective-permute-start.14 = (bf16[96,640]{1,0:T(8,128)(2,1)S(1)}, bf16[96,640]{1,0:T(8,128)(2,1)S(1)}, u32[]{:S(2)}, u32[]{:S(2)}) collective-permute-start(bf16[96,640]{1,0:T(8,128)(2,1)S(1)} %slice_bitcast_fusion), channel_id=1, source_target_pairs={{0,4},{2,6},{4,0},{6,2},{8,12},{10,14},{12,8},{14,10},{16,20},{18,... | collective-permute-start | bytes 368648 | tf_op jit(solution)/shard_map/ppermute | solution.py:121
  40.9 2.0 %collective-permute-done.13 = bf16[96,640]{1,0:T(8,128)(2,1)S(1)} collective-permute-done((bf16[96,640]{1,0:T(8,128)(2,1)S(1)}, bf16[96,640]{1,0:T(8,128)(2,1)S(1)}, u32[]{:S(2)}, u32[]{:S(2)}) %collective-permute-start.13) | collective-permute-done | bytes 122912 | tf_op jit(solution)/shard_map/ppermute | solution.py:121
  42.9 1.7 %collective-permute-done.14 = bf16[96,640]{1,0:T(8,128)(2,1)S(1)} collective-permute-done((bf16[96,640]{1,0:T(8,128)(2,1)S(1)}, bf16[96,640]{1,0:T(8,128)(2,1)S(1)}, u32[]{:S(2)}, u32[]{:S(2)}) %collective-permute-start.14) | collective-permute-done | bytes 122912 | tf_op jit(solution)/shard_map/ppermute | solution.py:121
  44.6 0.1 pad_maximum_fusion.1.refs_3_
  44.8 0.1 collective-permute-start.16
  44.9 0.5 collective-permute-start.22
  45.4 0.0 copy-start.3
  45.4 0.5 collective-permute-start.17
  45.9 1.7 %collective-permute-start.18 = (bf16[2,80,640]{2,1,0:T(8,128)(2,1)S(1)}, bf16[2,80,640]{2,1,0:T(8,128)(2,1)S(1)}, u32[]{:S(2)}, u32[]{:S(2)}) collective-permute-start(bf16[2,80,640]{2,1,0:T(8,128)(2,1)S(1)} %pad_maximum_fusion.5), channel_id=1, source_target_pairs={{0,4},{2,6},{4,0},{6,2},{8,12},{10,14},{12,8},{14,10},{16,20},{18,... | collective-permute-start | bytes 614408 | tf_op jit(solution)/shard_map/ppermute | solution.py:121
  47.7 2.1 %place.1.refs_0_ = bf16[3,512,1280]{2,1,0:T(8,128)(2,1)S(1)} custom-call(s32[3,10]{1,0:T(4,128)S(1)} %copy-done, s32[3,10]{1,0:T(4,128)S(1)} %copy-done.1, bf16[4,2,176,640]{3,2,1,0:T(8,128)(2,1)S(1)} %pad_maximum_fusion.refs_2_.refs_1_, bf16[4,2,96,640]{3,2,1,0:T(8,128)(2,1)S(1)} %pad_maximum_fusion.1.refs_3_, ...), custom_call_target="tpu_custom_call" | custom-call | flops 2000000000 | bytes 8388608 | tf_op jit(solution)/shard_map/place/pallas_call | solution.py:365
  49.7 5.0 %own_half_rows.1 = (bf16[640,512]{1,0:T(8,128)(2,1)S(1)}, bf16[640,512]{1,0:T(8,128)(2,1)S(1)}, bf16[640,512]{1,0:T(8,128)(2,1)S(1)}, bf16[640,512]{1,0:T(8,128)...) custom-call(bf16[3,512,1280]{2,1,0:T(8,128)(2,1)S(1)} %place.1.refs_, ...), custom_call_target="tpu_custom_call" | custom-call | flops 4000000000 | bytes 8388608 | tf_op jit(solution)/shard_map/own_half_rows/pallas_call | solution.py:377
  54.7 1.6 %collective-permute-start.19 = (bf16[80,640]{1,0:T(8,128)(2,1)S(1)}, bf16[80,640]{1,0:T(8,128)(2,1)S(1)}, u32[]{:S(2)}, u32[]{:S(2)}) collective-permute-start(bf16[80,640]{1,0:T(8,128)(2,1)S(1)} %slice_bitcast_fusion.3), channel_id=1, source_target_pairs={{0,2},{2,0},{4,6},{6,4},{8,10},{10,8},{12,14},{14,12},{16,18},{18,... | collective-permute-start | bytes 307208 | tf_op jit(solution)/shard_map/ppermute | solution.py:121
  56.4 0.4 collective-permute-start.20
  56.8 3.0 %early_sums.1 = (f32[512,512]{1,0:T(8,128)S(1)}, f32[512,512]{1,0:T(8,128)S(1)}, f32[3,40,512]{2,1,0:T(8,128)}) custom-call(bf16[3,512,1280]{2,1,0:T(8,128)(2,1)S(1)} %place.1.refs_0_, bf16[640,512]{1,0:T(8,128)(2,1)S(1)} %get-tuple-element.49.refs_1_, bf16[640,512]{1,0:T(8,128)(2,1)S(1)} %get-tuple-element.50.refs_2_, ...), custom_call_target="tpu_custom_call" | custom-call | flops 3000000000 | bytes 8388608 | tf_op jit(solution)/shard_map/early_sums/pallas_call | solution.py:388
  59.9 1.3 %collective-permute-done.20 = bf16[80,640]{1,0:T(8,128)(2,1)S(1)} collective-permute-done((bf16[80,640]{1,0:T(8,128)(2,1)S(1)}, bf16[80,640]{1,0:T(8,128)(2,1)S(1)}, u32[]{:S(2)}, u32[]{:S(2)}) %collective-permute-start.20) | collective-permute-done | bytes 102432 | tf_op jit(solution)/shard_map/ppermute | solution.py:121
  61.1 0.1 pad_maximum_fusion.2.refs_1_
  61.3 0.1 collective-permute-start.21
  61.4 1.8 %late_sums.1 = (f32[512,512]{1,0:T(8,128)S(1)}, f32[256,512]{1,0:T(8,128)S(1)}, f32[512,256]{1,0:T(8,128)S(1)}) custom-call(bf16[3,512,1280]{2,1,0:T(8,128)(2,1)S(1)} %place.1.refs_0_, bf16[640,512]{1,0:T(8,128)(2,1)S(1)} %get-tuple-element.62.refs_5_.refs_1_, bf16[640,512]{1,0:T(8,128)(2,1)S(1)} %get-tuple-element.54.refs_6_.refs_2_, ...), custom_call_target="tpu_custom_call" | custom-call | flops 2000000000 | bytes 8388608 | tf_op jit(solution)/shard_map/late_sums/pallas_call | solution.py:398
  63.2 0.5 collective-permute-done.21.refs_2_
  63.7 11.3 %other_half.1 = f32[3,512,256]{2,1,0:T(8,128)} custom-call(bf16[3,512,1280]{2,1,0:T(8,128)(2,1)S(1)} %place.1.refs_0_, bf16[4,2,80,640]{3,2,1,0:T(8,128)(2,1)S(1)} %pad_maximum_fusion.2.refs_1_, bf16[4,2,80,640]{3,2,1,0:T(8,128)(2,1)S(1)} %collective-permute-done.21.refs_2_, bf16[2,512,512]{2,1,0:T(8,128)(2,1)S(1)} %copy-done.3, ...), custom_call_target="tpu_custom_call" | custom-call | flops 12000000000 | bytes 8388608 | tf_op jit(solution)/shard_map/other_half/pallas_call | solution.py:406
  (29 shorter events, 0.2 us)
Async XLA Ops:
  0.6 25.4 %copy-start.4 = (bf16[80,640]{1,0:T(8,128)(2,1)S(1)}, bf16[80,640]{1,0:T(8,128)(2,1)}, u32[]{:S(2)}) copy-start(bf16[80,640]{1,0:T(8,128)(2,1)} %param.6) | copy-start | bytes 307204
  1.7 8.9 %collective-permute-start.2 = (bf16[176,640]{1,0:T(8,128)(2,1)S(1)}, bf16[176,640]{1,0:T(8,128)(2,1)S(1)}, u32[]{:S(2)}, u32[]{:S(2)}) collective-permute-start(bf16[176,640]{1,0:T(8,128)(2,1)S(1)} %get-tuple-element.69), channel_id=1, source_target_pairs={{0,4},{2,6},{4,0},{6,2},{8,12},{10,14},{12,8},{14,10},{16,20},{18,... | collective-permute-start | bytes 675848 | tf_op jit(solution)/shard_map/ppermute | solution.py:121
  4.7 7.0 %collective-permute-start.1 = (bf16[176,640]{1,0:T(8,128)(2,1)S(1)}, bf16[176,640]{1,0:T(8,128)(2,1)S(1)}, u32[]{:S(2)}, u32[]{:S(2)}) collective-permute-start(bf16[176,640]{1,0:T(8,128)(2,1)S(1)} %get-tuple-element.69), channel_id=1, source_target_pairs={{0,2},{2,0},{4,6},{6,4},{8,10},{10,8},{12,14},{14,12},{16,18},{18,... | collective-permute-start | bytes 675848 | tf_op jit(solution)/shard_map/ppermute | solution.py:121
  6.2 9.1 %collective-permute-start = (bf16[176,640]{1,0:T(8,128)(2,1)S(1)}, bf16[176,640]{1,0:T(8,128)(2,1)S(1)}, u32[]{:S(2)}, u32[]{:S(2)}) collective-permute-start(bf16[176,640]{1,0:T(8,128)(2,1)S(1)} %get-tuple-element.69), channel_id=1, source_target_pairs={{0,8},{2,10},{4,12},{6,14},{8,0},{10,2},{12,4},{14,6},{16,24},{18,... | collective-permute-start | bytes 675848 | tf_op jit(solution)/shard_map/ppermute | solution.py:121
  7.8 10.0 %collective-permute-start.7 = (bf16[96,640]{1,0:T(8,128)(2,1)}, bf16[96,640]{1,0:T(8,128)(2,1)S(1)}, u32[]{:S(2)}, u32[]{:S(2)}) collective-permute-start(bf16[96,640]{1,0:T(8,128)(2,1)} %bitcast.60), channel_id=1, source_target_pairs={{0,16},{2,18},{4,20},{6,22},{8,24},{10,26},{12,28},{14,30},{16,0},... | collective-permute-start | bytes 368648 | tf_op jit(solution)/shard_map/ppermute | solution.py:121
  10.4 9.9 %collective-permute-start.8 = (bf16[96,640]{1,0:T(8,128)(2,1)}, bf16[96,640]{1,0:T(8,128)(2,1)S(1)}, u32[]{:S(2)}, u32[]{:S(2)}) collective-permute-start(bf16[96,640]{1,0:T(8,128)(2,1)} %bitcast.61), channel_id=1, source_target_pairs={{0,24},{2,26},{4,28},{6,30},{8,16},{10,18},{12,20},{14,22},{16,8},... | collective-permute-start | bytes 368648 | tf_op jit(solution)/shard_map/ppermute | solution.py:121
  15.3 7.1 %collective-permute-start.3 = (bf16[176,640]{1,0:T(8,128)(2,1)S(1)}, bf16[176,640]{1,0:T(8,128)(2,1)S(1)}, u32[]{:S(2)}, u32[]{:S(2)}) collective-permute-start(bf16[176,640]{1,0:T(8,128)(2,1)S(1)} %collective-permute-done), channel_id=1, source_target_pairs={{0,2},{2,0},{4,6},{6,4},{8,10},{10,8},{12,14},{14,12},{16,18},{18,... | collective-permute-start | bytes 675848 | tf_op jit(solution)/shard_map/ppermute | solution.py:121
  15.8 6.6 %collective-permute-start.4 = (bf16[176,640]{1,0:T(8,128)(2,1)S(1)}, bf16[176,640]{1,0:T(8,128)(2,1)S(1)}, u32[]{:S(2)}, u32[]{:S(2)}) collective-permute-start(bf16[176,640]{1,0:T(8,128)(2,1)S(1)} %collective-permute-done), channel_id=1, source_target_pairs={{0,4},{2,6},{4,0},{6,2},{8,12},{10,14},{12,8},{14,10},{16,20},{18,... | collective-permute-start | bytes 675848 | tf_op jit(solution)/shard_map/ppermute | solution.py:121
  16.0 9.5 %collective-permute-start.5 = (bf16[176,640]{1,0:T(8,128)(2,1)S(1)}, bf16[176,640]{1,0:T(8,128)(2,1)S(1)}, u32[]{:S(2)}, u32[]{:S(2)}) collective-permute-start(bf16[176,640]{1,0:T(8,128)(2,1)S(1)} %collective-permute-done.2), channel_id=1, source_target_pairs={{0,2},{2,0},{4,6},{6,4},{8,10},{10,8},{12,14},{14,12},{16,18},{18,... | collective-permute-start | bytes 675848 | tf_op jit(solution)/shard_map/ppermute | solution.py:121
  25.5 11.6 %collective-permute-start.10 = (bf16[2,96,640]{2,1,0:T(8,128)(2,1)S(1)}, bf16[2,96,640]{2,1,0:T(8,128)(2,1)S(1)}, u32[]{:S(2)}, u32[]{:S(2)}) collective-permute-start(bf16[2,96,640]{2,1,0:T(8,128)(2,1)S(1)} %pad_maximum_fusion.3), channel_id=1, source_target_pairs={{0,4},{2,6},{4,0},{6,2},{8,12},{10,14},{12,8},{14,10},{16,20},{18,... | collective-permute-start | bytes 737288 | tf_op jit(solution)/shard_map/ppermute | solution.py:121
  25.5 11.6 %collective-permute-start.9 = (bf16[2,96,640]{2,1,0:T(8,128)(2,1)S(1)}, bf16[2,96,640]{2,1,0:T(8,128)(2,1)S(1)}, u32[]{:S(2)}, u32[]{:S(2)}) collective-permute-start(bf16[2,96,640]{2,1,0:T(8,128)(2,1)S(1)} %pad_maximum_fusion.3), channel_id=1, source_target_pairs={{0,2},{2,0},{4,6},{6,4},{8,10},{10,8},{12,14},{14,12},{16,18},{18,... | collective-permute-start | bytes 737288 | tf_op jit(solution)/shard_map/ppermute | solution.py:121
  26.1 11.0 %collective-permute-start.11 = (bf16[80,640]{1,0:T(8,128)(2,1)S(1)}, bf16[80,640]{1,0:T(8,128)(2,1)S(1)}, u32[]{:S(2)}, u32[]{:S(2)}) collective-permute-start(bf16[80,640]{1,0:T(8,128)(2,1)S(1)} %copy-done.4), channel_id=1, source_target_pairs={{0,16},{2,18},{4,20},{6,22},{8,24},{10,26},{12,28},{14,30},{16,0},... | collective-permute-start | bytes 307208 | tf_op jit(solution)/shard_map/ppermute | solution.py:121
  28.6 8.4 %collective-permute-start.12 = (bf16[80,640]{1,0:T(8,128)(2,1)S(1)}, bf16[80,640]{1,0:T(8,128)(2,1)S(1)}, u32[]{:S(2)}, u32[]{:S(2)}) collective-permute-start(bf16[80,640]{1,0:T(8,128)(2,1)S(1)} %copy-done.4), channel_id=1, source_target_pairs={{0,24},{2,26},{4,28},{6,30},{8,16},{10,18},{12,20},{14,22},{16,8},... | collective-permute-start | bytes 307208 | tf_op jit(solution)/shard_map/ppermute | solution.py:121
  30.7 6.0 %collective-permute-start.6 = (bf16[176,640]{1,0:T(8,128)(2,1)S(1)}, bf16[176,640]{1,0:T(8,128)(2,1)S(1)}, u32[]{:S(2)}, u32[]{:S(2)}) collective-permute-start(bf16[176,640]{1,0:T(8,128)(2,1)S(1)} %collective-permute-done.3), channel_id=1, source_target_pairs={{0,4},{2,6},{4,0},{6,2},{8,12},{10,14},{12,8},{14,10},{16,20},{18,... | collective-permute-start | bytes 675848 | tf_op jit(solution)/shard_map/ppermute | solution.py:121
  37.0 7.9 %copy-start.2 = (f32[3,512,256]{2,1,0:T(8,128)S(1)}, f32[3,512,256]{2,1,0:T(8,128)}, u32[]{:S(2)}) copy-start(f32[3,512,256]{2,1,0:T(8,128)} %refs_4_.1) | copy-start | bytes 4718596
  37.0 10.7 %copy-start = (s32[3,10]{1,0:T(4,128)S(1)}, s32[3,10]{1,0:T(4,128)}, u32[]{:S(2)}) copy-start(s32[3,10]{1,0:T(4,128)} %refs_0_.1) | copy-start | bytes 364
  37.0 10.7 %copy-start.1 = (s32[3,10]{1,0:T(4,128)S(1)}, s32[3,10]{1,0:T(4,128)}, u32[]{:S(2)}) copy-start(s32[3,10]{1,0:T(4,128)} %refs_1_.1) | copy-start | bytes 364
  37.0 10.6 %collective-permute-start.15 = (bf16[4,2,176,640]{3,2,1,0:T(8,128)(2,1)S(1)}, bf16[4,2,176,640]{3,2,1,0:T(8,128)(2,1)S(1)}, u32[]{:S(2)}, u32[]{:S(2)}) collective-permute-start(bf16[4,2,176,640]{3,2,1,0:T(8,128)(2,1)S(1)} %pad_maximum_fusion.refs_2_.refs_1_), channel_id=1, source_target_pairs={{0,1},{1,0},{2,3},{3,2},{4,5},{5,4},{6,7},{7,6},{8,9},{9,8},{10,11... | collective-permute-start | bytes 5406728 | tf_op jit(solution)/shard_map/ppermute | solution.py:125
  37.1 5.8 %collective-permute-start.13 = (bf16[96,640]{1,0:T(8,128)(2,1)S(1)}, bf16[96,640]{1,0:T(8,128)(2,1)S(1)}, u32[]{:S(2)}, u32[]{:S(2)}) collective-permute-start(bf16[96,640]{1,0:T(8,128)(2,1)S(1)} %slice_bitcast_fusion.1), channel_id=1, source_target_pairs={{0,2},{2,0},{4,6},{6,4},{8,10},{10,8},{12,14},{14,12},{16,18},{18,... | collective-permute-start | bytes 368648 | tf_op jit(solution)/shard_map/ppermute | solution.py:121
  38.8 5.8 %collective-permute-start.14 = (bf16[96,640]{1,0:T(8,128)(2,1)S(1)}, bf16[96,640]{1,0:T(8,128)(2,1)S(1)}, u32[]{:S(2)}, u32[]{:S(2)}) collective-permute-start(bf16[96,640]{1,0:T(8,128)(2,1)S(1)} %slice_bitcast_fusion), channel_id=1, source_target_pairs={{0,4},{2,6},{4,0},{6,2},{8,12},{10,14},{12,8},{14,10},{16,20},{18,... | collective-permute-start | bytes 368648 | tf_op jit(solution)/shard_map/ppermute | solution.py:121
  44.8 2.9 %collective-permute-start.16 = (bf16[4,2,96,640]{3,2,1,0:T(8,128)(2,1)S(1)}, bf16[4,2,96,640]{3,2,1,0:T(8,128)(2,1)S(1)}, u32[]{:S(2)}, u32[]{:S(2)}) collective-permute-start(bf16[4,2,96,640]{3,2,1,0:T(8,128)(2,1)S(1)} %pad_maximum_fusion.1.refs_3_), channel_id=1, source_target_pairs={{0,1},{1,0},{2,3},{3,2},{4,5},{5,4},{6,7},{7,6},{8,9},{9,8},{10,11... | collective-permute-start | bytes 2949128 | tf_op jit(solution)/shard_map/ppermute | solution.py:125
  44.9 18.3 %collective-permute-start.22 = (f32[3,512,256]{2,1,0:T(8,128)S(1)}, f32[3,512,256]{2,1,0:T(8,128)S(1)}, u32[]{:S(2)}, u32[]{:S(2)}) collective-permute-start(f32[3,512,256]{2,1,0:T(8,128)S(1)} %copy-done.2), channel_id=1, source_target_pairs={{0,1},{1,0},{2,3},{3,2},{4,5},{5,4},{6,7},{7,6},{8,9},{9,8},{10,11... | collective-permute-start | bytes 4718600 | tf_op jit(solution)/shard_map/ppermute | solution.py:125
  45.4 4.4 %copy-start.3 = (bf16[2,512,512]{2,1,0:T(8,128)(2,1)S(1)}, bf16[2,512,512]{2,1,0:T(8,128)(2,1)}, u32[]{:S(2)}) copy-start(bf16[2,512,512]{2,1,0:T(8,128)(2,1)} %refs_3_.3) | copy-start | bytes 3145732
  45.4 9.3 %collective-permute-start.17 = (bf16[2,80,640]{2,1,0:T(8,128)(2,1)S(1)}, bf16[2,80,640]{2,1,0:T(8,128)(2,1)S(1)}, u32[]{:S(2)}, u32[]{:S(2)}) collective-permute-start(bf16[2,80,640]{2,1,0:T(8,128)(2,1)S(1)} %pad_maximum_fusion.5), channel_id=1, source_target_pairs={{0,2},{2,0},{4,6},{6,4},{8,10},{10,8},{12,14},{14,12},{16,18},{18,... | collective-permute-start | bytes 614408 | tf_op jit(solution)/shard_map/ppermute | solution.py:121
  45.9 8.8 %collective-permute-start.18 = (bf16[2,80,640]{2,1,0:T(8,128)(2,1)S(1)}, bf16[2,80,640]{2,1,0:T(8,128)(2,1)S(1)}, u32[]{:S(2)}, u32[]{:S(2)}) collective-permute-start(bf16[2,80,640]{2,1,0:T(8,128)(2,1)S(1)} %pad_maximum_fusion.5), channel_id=1, source_target_pairs={{0,4},{2,6},{4,0},{6,2},{8,12},{10,14},{12,8},{14,10},{16,20},{18,... | collective-permute-start | bytes 614408 | tf_op jit(solution)/shard_map/ppermute | solution.py:121
  54.7 5.1 %collective-permute-start.19 = (bf16[80,640]{1,0:T(8,128)(2,1)S(1)}, bf16[80,640]{1,0:T(8,128)(2,1)S(1)}, u32[]{:S(2)}, u32[]{:S(2)}) collective-permute-start(bf16[80,640]{1,0:T(8,128)(2,1)S(1)} %slice_bitcast_fusion.3), channel_id=1, source_target_pairs={{0,2},{2,0},{4,6},{6,4},{8,10},{10,8},{12,14},{14,12},{16,18},{18,... | collective-permute-start | bytes 307208 | tf_op jit(solution)/shard_map/ppermute | solution.py:121
  56.4 4.7 %collective-permute-start.20 = (bf16[80,640]{1,0:T(8,128)(2,1)S(1)}, bf16[80,640]{1,0:T(8,128)(2,1)S(1)}, u32[]{:S(2)}, u32[]{:S(2)}) collective-permute-start(bf16[80,640]{1,0:T(8,128)(2,1)S(1)} %slice_bitcast_fusion.2), channel_id=1, source_target_pairs={{0,4},{2,6},{4,0},{6,2},{8,12},{10,14},{12,8},{14,10},{16,20},{18,... | collective-permute-start | bytes 307208 | tf_op jit(solution)/shard_map/ppermute | solution.py:121
  61.3 2.4 %collective-permute-start.21 = (bf16[4,2,80,640]{3,2,1,0:T(8,128)(2,1)S(1)}, bf16[4,2,80,640]{3,2,1,0:T(8,128)(2,1)S(1)}, u32[]{:S(2)}, u32[]{:S(2)}) collective-permute-start(bf16[4,2,80,640]{3,2,1,0:T(8,128)(2,1)S(1)} %pad_maximum_fusion.2.refs_1_), channel_id=1, source_target_pairs={{0,1},{1,0},{2,3},{3,2},{4,5},{5,4},{6,7},{7,6},{8,9},{9,8},{10,11... | collective-permute-start | bytes 2457608 | tf_op jit(solution)/shard_map/ppermute | solution.py:125

commit v7 on v6

--- a/solution.py
+++ b/solution.py
@@ -329,7 +329,6 @@
             **kwargs,
         )
 
-    outer = row_parts // 4
     x = lambda value: swap(value, "row", 1, row_parts)
     y = lambda value: swap(value, "row", 2, row_parts)
     line = lambda value, k: swap(value, "row", 4 * k, row_parts)
@@ -337,13 +336,10 @@
     def far(over_x, over_y, i):
         return x(over_y) if i % 2 == 0 else y(over_x)
 
-    def late_wave(parts, *events):
-        own = after(jnp.stack(parts), *events)
-        return own, x(own), y(own)
-
-    f_own = jnp.transpose(factor_cols, (0, 2, 1)).reshape(supers * part, span)
-    f_late = [line(f_own, k) for k in range(count, outer)]
-    own = jnp.concatenate([f_own, inverse_block], axis=0)
+    f_rows = supers * part
+    own = jnp.concatenate(
+        [jnp.transpose(factor_cols, (0, 2, 1)).reshape(f_rows, span), inverse_block], axis=0
+    )
     early = []
     for k in range(count):
         value = own if k == 0 else line(own, k)
@@ -352,14 +348,17 @@
         early.append([value, over_x, over_y, far(over_x, over_y, k)])
     first = jnp.stack([jnp.stack([p[j] for p in early]) for j in range(4)])
     first_other = across(first)
-    block = after(inverse_block, *f_late, *early[-1][1:3])
-    z_late = [line(block, k) for k in range(count, outer)]
-    f_b, f_bx, f_by = late_wave(f_late, *early[-1][1:3], early[0][3])
-    f_bx, f_by = after((f_bx, f_by), *z_late)
+    f_late = line(jnp.stack([p[0][:f_rows] for p in early]), count)
+    z_near = after(jnp.stack([p[0][f_rows:] for p in early]), f_late, *early[-1][1:3])
+    z_late = line(z_near, count)
+    f_b = after(f_late, *early[-1][1:3], early[0][3])
+    f_bx, f_by = x(f_b), y(f_b)
+    f_bx, f_by = after((f_bx, f_by), z_late)
     f_far = jnp.stack([far(f_bx[i], f_by[i], i) for i in range(count)])
     f_last = jnp.stack([f_b, f_bx, f_by, f_far])
     f_last_other = across(f_last)
-    z_b, z_bx, z_by = late_wave(z_late, f_bx, f_by)
+    z_b = after(z_late, f_bx, f_by)
+    z_bx, z_by = x(z_b), y(z_b)
     diag_other = across(diag_inverse)
 
     pt = call(

time: 75.3 us -> 76.4 us (1.015)
  waiting for transfers between devices: 21.7 us -> 28.1 us
  starting transfers between devices: 27.3 us -> 21.1 us
  other arithmetic: 1.88 us -> 2.79 us
    ppermute x19 -> x17, waiting for transfers between devices: 21.1 us -> 27.5 us  [swap(): return lax.ppermute(value, axis, [(i, i ^ bit) for i in range(parts)])]
    ppermute x19 -> x17, starting transfers between devices: 26.6 us -> 20.4 us  [swap(): return lax.ppermute(value, axis, [(i, i ^ bit) for i in range(parts)])]
    another operation x2, other arithmetic: 0.06 us -> 0.96 us  [the longest x1 0.93 us: replicated_plan(): f_late = line(jnp.stack([p[0][:f_rows] for p in early]), count)]
  transfers between devices with their start and end apart: 23 -> 21, of which waited for: 10 -> 12; matrix products, arithmetic and copies ran while one was open for 1% -> 2% of each run, Pallas kernels for 16% -> 16%
where the time goes in v7:
time: 76.4 us; the launch traced here: 76.2 us
  waiting for transfers between devices  28.1 us (37%)
  Pallas kernels  23.1 us (30%)
  starting transfers between devices  21.1 us (28%)
  other arithmetic  2.79 us (4%)
  between operations  1.04 us (1%)
    ppermute x17, waiting for transfers between devices, swap(): return lax.ppermute(value, axis, [(i, i ^ bit) for i in range(parts)])  27.5 us
    ppermute x17, starting transfers between devices, swap(): return lax.ppermute(value, axis, [(i, i ^ bit) for i in range(parts)])  20.4 us
    pallas_call x1, Pallas kernels, replicated_plan(): call(functools.partial(last_kernel, dims, rows), 'other_half', 12 * 10 **...  11.3 us
    pallas_call x1, Pallas kernels, replicated_plan(): call(functools.partial(rows_kernel, dims, supers * part), 'own_half_rows'...  4.96 us
    pallas_call x1, Pallas kernels, replicated_plan(): call(functools.partial(early_sums_kernel, count), 'early_sums', 3 * 10 **...  3.02 us
    pallas_call x1, Pallas kernels, replicated_plan(): call(functools.partial(place_kernel, (supers, width, rows, span, part)),...  2.06 us
    pallas_call x1, Pallas kernels, replicated_plan(): call(functools.partial(late_sums_kernel, count, local_rows), 'late_sums',...  1.8 us
  transfers between devices with their start and end apart: 21, of which 12 were waited for; matrix products, arithmetic and copies ran while one was open for 2% of the time, Pallas kernels for 16%

profile of v7, /device:TPU:0, one launch (start us, length us, event | category | flops | bytes accessed | tf_op | source)
XLA Modules:
  0.0 76.2 jit_solution(16337173473694117933)
XLA Ops:
  0.6 1.0 %fusion = (bf16[1,176,640]{2,1,0:T(8,128)(2,1)S(1)}, bf16[176,640]{1,0:T(8,128)(2,1)S(1)}) fusion(bf16[80,640]{1,0:T(8,128)(2,1)} %param.6, bf16[96,640]{1,0:T(8,128)(2,1)} %bitcast.52), kind=kLoop, calls=%fused_computation.18 | loop fusion | flops 450560 | bytes 675840 | tf_op jit(solution)/shard_map/stack | solution.py:349
  1.7 3.0 %collective-permute-start.2 = (bf16[176,640]{1,0:T(8,128)(2,1)S(1)}, bf16[176,640]{1,0:T(8,128)(2,1)S(1)}, u32[]{:S(2)}, u32[]{:S(2)}) collective-permute-start(bf16[176,640]{1,0:T(8,128)(2,1)S(1)} %get-tuple-element.69), channel_id=1, source_target_pairs={{0,4},{2,6},{4,0},{6,2},{8,12},{10,14},{12,8},{14,10},{16,20},{18,... | collective-permute-start | bytes 675848 | tf_op jit(solution)/shard_map/ppermute | solution.py:121
  4.7 1.5 %collective-permute-start.1 = (bf16[176,640]{1,0:T(8,128)(2,1)S(1)}, bf16[176,640]{1,0:T(8,128)(2,1)S(1)}, u32[]{:S(2)}, u32[]{:S(2)}) collective-permute-start(bf16[176,640]{1,0:T(8,128)(2,1)S(1)} %get-tuple-element.69), channel_id=1, source_target_pairs={{0,2},{2,0},{4,6},{6,4},{8,10},{10,8},{12,14},{14,12},{16,18},{18,... | collective-permute-start | bytes 675848 | tf_op jit(solution)/shard_map/ppermute | solution.py:121
  6.2 1.6 %collective-permute-start = (bf16[176,640]{1,0:T(8,128)(2,1)S(1)}, bf16[176,640]{1,0:T(8,128)(2,1)S(1)}, u32[]{:S(2)}, u32[]{:S(2)}) collective-permute-start(bf16[176,640]{1,0:T(8,128)(2,1)S(1)} %get-tuple-element.69), channel_id=1, source_target_pairs={{0,8},{2,10},{4,12},{6,14},{8,0},{10,2},{12,4},{14,6},{16,24},{18,... | collective-permute-start | bytes 675848 | tf_op jit(solution)/shard_map/ppermute | solution.py:121
  7.8 2.4 %collective-permute-done.2 = bf16[176,640]{1,0:T(8,128)(2,1)S(1)} collective-permute-done((bf16[176,640]{1,0:T(8,128)(2,1)S(1)}, bf16[176,640]{1,0:T(8,128)(2,1)S(1)}, u32[]{:S(2)}, u32[]{:S(2)}) %collective-permute-start.2) | collective-permute-done | bytes 225312 | tf_op jit(solution)/shard_map/ppermute | solution.py:121
  10.2 1.5 %collective-permute-done.1 = bf16[176,640]{1,0:T(8,128)(2,1)S(1)} collective-permute-done((bf16[176,640]{1,0:T(8,128)(2,1)S(1)}, bf16[176,640]{1,0:T(8,128)(2,1)S(1)}, u32[]{:S(2)}, u32[]{:S(2)}) %collective-permute-start.1) | collective-permute-done | bytes 225312 | tf_op jit(solution)/shard_map/ppermute | solution.py:121
  11.7 1.2 %collective-permute-done = bf16[176,640]{1,0:T(8,128)(2,1)S(1)} collective-permute-done((bf16[176,640]{1,0:T(8,128)(2,1)S(1)}, bf16[176,640]{1,0:T(8,128)(2,1)S(1)}, u32[]{:S(2)}, u32[]{:S(2)}) %collective-permute-start) | collective-permute-done | bytes 225312 | tf_op jit(solution)/shard_map/ppermute | solution.py:121
  12.9 0.5 collective-permute-start.3
  13.4 0.4 collective-permute-start.4
  13.8 0.9 %pad_maximum_fusion.3 = bf16[2,96,640]{2,1,0:T(8,128)(2,1)S(1)} fusion(bf16[1,96,640]{2,1,0:T(8,128)(2,1)S(1)} %slice_bitcast_fusion.2, bf16[1,96,640]{2,1,0:T(8,128)(2,1)} %bitcast.53), kind=kLoop, calls=%fused_computation.7 | loop fusion | flops 122880 | bytes 491520 | tf_op jit(solution)/shard_map/stack | solution.py:351
  14.7 2.8 %collective-permute-start.7 = (bf16[2,96,640]{2,1,0:T(8,128)(2,1)S(1)}, bf16[2,96,640]{2,1,0:T(8,128)(2,1)S(1)}, u32[]{:S(2)}, u32[]{:S(2)}) collective-permute-start(bf16[2,96,640]{2,1,0:T(8,128)(2,1)S(1)} %pad_maximum_fusion.3), channel_id=1, source_target_pairs={{0,16},{2,18},{4,20},{6,22},{8,24},{10,26},{12,28},{14,30},{16,0},... | collective-permute-start | bytes 737288 | tf_op jit(solution)/shard_map/ppermute | solution.py:121
  17.6 1.5 %collective-permute-start.5 = (bf16[176,640]{1,0:T(8,128)(2,1)S(1)}, bf16[176,640]{1,0:T(8,128)(2,1)S(1)}, u32[]{:S(2)}, u32[]{:S(2)}) collective-permute-start(bf16[176,640]{1,0:T(8,128)(2,1)S(1)} %collective-permute-done.2), channel_id=1, source_target_pairs={{0,2},{2,0},{4,6},{6,4},{8,10},{10,8},{12,14},{14,12},{16,18},{18,... | collective-permute-start | bytes 675848 | tf_op jit(solution)/shard_map/ppermute | solution.py:121
  19.0 0.1 maximum_bitcast_fusion
  19.1 0.7 collective-permute-done.3
  19.9 0.9 %collective-permute-start.6 = (bf16[176,640]{1,0:T(8,128)(2,1)S(1)}, bf16[176,640]{1,0:T(8,128)(2,1)S(1)}, u32[]{:S(2)}, u32[]{:S(2)}) collective-permute-start(bf16[176,640]{1,0:T(8,128)(2,1)S(1)} %collective-permute-done.3), channel_id=1, source_target_pairs={{0,4},{2,6},{4,0},{6,2},{8,12},{10,14},{12,8},{14,10},{16,20},{18,... | collective-permute-start | bytes 675848 | tf_op jit(solution)/shard_map/ppermute | solution.py:121
  20.7 0.1 maximum_bitcast_fusion.1
  20.8 0.1 maximum_bitcast_fusion.2
  20.9 2.8 %collective-permute-done.5 = bf16[176,640]{1,0:T(8,128)(2,1)S(1)} collective-permute-done((bf16[176,640]{1,0:T(8,128)(2,1)S(1)}, bf16[176,640]{1,0:T(8,128)(2,1)S(1)}, u32[]{:S(2)}, u32[]{:S(2)}) %collective-permute-start.5) | collective-permute-done | bytes 225312 | tf_op jit(solution)/shard_map/ppermute | solution.py:121
  23.7 3.2 %collective-permute-done.7 = bf16[2,96,640]{2,1,0:T(8,128)(2,1)S(1)} collective-permute-done((bf16[2,96,640]{2,1,0:T(8,128)(2,1)S(1)}, bf16[2,96,640]{2,1,0:T(8,128)(2,1)S(1)}, u32[]{:S(2)}, u32[]{:S(2)}) %collective-permute-start.7) | collective-permute-done | bytes 245792 | tf_op jit(solution)/shard_map/ppermute | solution.py:121
  26.9 1.3 %collective-permute-start.8 = (bf16[2,96,640]{2,1,0:T(8,128)(2,1)S(1)}, bf16[2,96,640]{2,1,0:T(8,128)(2,1)S(1)}, u32[]{:S(2)}, u32[]{:S(2)}) collective-permute-start(bf16[2,96,640]{2,1,0:T(8,128)(2,1)S(1)} %collective-permute-done.7), channel_id=1, source_target_pairs={{0,2},{2,0},{4,6},{6,4},{8,10},{10,8},{12,14},{14,12},{16,18},{18,... | collective-permute-start | bytes 737288 | tf_op jit(solution)/shard_map/ppermute | solution.py:121
  28.3 1.5 %collective-permute-start.9 = (bf16[2,96,640]{2,1,0:T(8,128)(2,1)S(1)}, bf16[2,96,640]{2,1,0:T(8,128)(2,1)S(1)}, u32[]{:S(2)}, u32[]{:S(2)}) collective-permute-start(bf16[2,96,640]{2,1,0:T(8,128)(2,1)S(1)} %collective-permute-done.7), channel_id=1, source_target_pairs={{0,4},{2,6},{4,0},{6,2},{8,12},{10,14},{12,8},{14,10},{16,20},{18,... | collective-permute-start | bytes 737288 | tf_op jit(solution)/shard_map/ppermute | solution.py:121
  29.8 0.1 maximum_bitcast_fusion.3
  29.8 0.3 pad_maximum_fusion.refs_2_.refs_1_
  30.1 0.0 copy-start.2
  30.1 0.0 copy-start
  30.2 0.1 collective-permute-start.13
  30.2 10.2 %collective-permute-done.10 = bf16[2,80,640]{2,1,0:T(8,128)(2,1)S(1)} collective-permute-done((bf16[2,80,640]{2,1,0:T(8,128)(2,1)S(1)}, bf16[2,80,640]{2,1,0:T(8,128)(2,1)S(1)}, u32[]{:S(2)}, u32[]{:S(2)}) %collective-permute-start.10) | collective-permute-done | bytes 204832 | tf_op jit(solution)/shard_map/ppermute | solution.py:121
  40.5 0.6 collective-permute-start.11
  41.1 0.7 collective-permute-start.12
  41.8 3.6 %collective-permute-done.11 = bf16[96,640]{1,0:T(8,128)(2,1)S(1)} collective-permute-done((bf16[96,640]{1,0:T(8,128)(2,1)S(1)}, bf16[96,640]{1,0:T(8,128)(2,1)S(1)}, u32[]{:S(2)}, u32[]{:S(2)}) %collective-permute-start.11) | collective-permute-done | bytes 122912 | tf_op jit(solution)/shard_map/ppermute | solution.py:121
  45.4 0.7 collective-permute-done.12
  46.1 0.1 pad_maximum_fusion.1.refs_3_
  46.3 0.1 collective-permute-start.14
  46.4 0.5 collective-permute-start.20
  46.8 1.4 %collective-permute-start.15 = (bf16[2,80,640]{2,1,0:T(8,128)(2,1)S(1)}, bf16[2,80,640]{2,1,0:T(8,128)(2,1)S(1)}, u32[]{:S(2)}, u32[]{:S(2)}) collective-permute-start(bf16[2,80,640]{2,1,0:T(8,128)(2,1)S(1)} %collective-permute-done.10), channel_id=1, source_target_pairs={{0,2},{2,0},{4,6},{6,4},{8,10},{10,8},{12,14},{14,12},{16,18},{18,... | collective-permute-start | bytes 614408 | tf_op jit(solution)/shard_map/ppermute | solution.py:121
  48.3 0.5 collective-permute-start.16
  48.8 0.1 collective-permute-done.14.refs_5_
  48.9 2.1 %place.1.refs_0_ = bf16[3,512,1280]{2,1,0:T(8,128)(2,1)S(1)} custom-call(s32[3,10]{1,0:T(4,128)S(1)} %copy-done, s32[3,10]{1,0:T(4,128)S(1)} %copy-done.1, bf16[4,2,176,640]{3,2,1,0:T(8,128)(2,1)S(1)} %pad_maximum_fusion.refs_2_.refs_1_, bf16[4,2,96,640]{3,2,1,0:T(8,128)(2,1)S(1)} %pad_maximum_fusion.1.refs_3_, ...), custom_call_target="tpu_custom_call" | custom-call | flops 2000000000 | bytes 8388608 | tf_op jit(solution)/shard_map/place/pallas_call | solution.py:364
  51.0 5.0 %own_half_rows.1 = (bf16[640,512]{1,0:T(8,128)(2,1)S(1)}, bf16[640,512]{1,0:T(8,128)(2,1)S(1)}, bf16[640,512]{1,0:T(8,128)(2,1)S(1)}, bf16[640,512]{1,0:T(8,128)...) custom-call(bf16[3,512,1280]{2,1,0:T(8,128)(2,1)S(1)} %place.1.refs_, ...), custom_call_target="tpu_custom_call" | custom-call | flops 4000000000 | bytes 8388608 | tf_op jit(solution)/shard_map/own_half_rows/pallas_call | solution.py:376
  56.0 1.5 %collective-permute-start.17 = (bf16[80,640]{1,0:T(8,128)(2,1)S(1)}, bf16[80,640]{1,0:T(8,128)(2,1)S(1)}, u32[]{:S(2)}, u32[]{:S(2)}) collective-permute-start(bf16[80,640]{1,0:T(8,128)(2,1)S(1)} %slice_bitcast_fusion.4), channel_id=1, source_target_pairs={{0,2},{2,0},{4,6},{6,4},{8,10},{10,8},{12,14},{14,12},{16,18},{18,... | collective-permute-start | bytes 307208 | tf_op jit(solution)/shard_map/ppermute | solution.py:121
  57.5 0.6 collective-permute-start.18
  58.1 3.0 %early_sums.1 = (f32[512,512]{1,0:T(8,128)S(1)}, f32[512,512]{1,0:T(8,128)S(1)}, f32[3,40,512]{2,1,0:T(8,128)}) custom-call(bf16[3,512,1280]{2,1,0:T(8,128)(2,1)S(1)} %place.1.refs_0_, bf16[640,512]{1,0:T(8,128)(2,1)S(1)} %get-tuple-element.49.refs_1_, bf16[640,512]{1,0:T(8,128)(2,1)S(1)} %get-tuple-element.50.refs_2_, ...), custom_call_target="tpu_custom_call" | custom-call | flops 3000000000 | bytes 8388608 | tf_op jit(solution)/shard_map/early_sums/pallas_call | solution.py:387
  61.2 1.1 %collective-permute-done.18 = bf16[80,640]{1,0:T(8,128)(2,1)S(1)} collective-permute-done((bf16[80,640]{1,0:T(8,128)(2,1)S(1)}, bf16[80,640]{1,0:T(8,128)(2,1)S(1)}, u32[]{:S(2)}, u32[]{:S(2)}) %collective-permute-start.18) | collective-permute-done | bytes 102432 | tf_op jit(solution)/shard_map/ppermute | solution.py:121
  62.3 0.1 pad_maximum_fusion.2.refs_1_
  62.4 0.1 collective-permute-start.19
  62.5 1.8 %late_sums.1 = (f32[512,512]{1,0:T(8,128)S(1)}, f32[256,512]{1,0:T(8,128)S(1)}, f32[512,256]{1,0:T(8,128)S(1)}) custom-call(bf16[3,512,1280]{2,1,0:T(8,128)(2,1)S(1)} %place.1.refs_0_, bf16[640,512]{1,0:T(8,128)(2,1)S(1)} %get-tuple-element.62.refs_5_.refs_1_, bf16[640,512]{1,0:T(8,128)(2,1)S(1)} %get-tuple-element.54.refs_6_.refs_2_, ...), custom_call_target="tpu_custom_call" | custom-call | flops 2000000000 | bytes 8388608 | tf_op jit(solution)/shard_map/late_sums/pallas_call | solution.py:397
  64.3 0.5 collective-permute-done.19.refs_2_
  64.8 11.3 %other_half.1 = f32[3,512,256]{2,1,0:T(8,128)} custom-call(bf16[3,512,1280]{2,1,0:T(8,128)(2,1)S(1)} %place.1.refs_0_, bf16[4,2,80,640]{3,2,1,0:T(8,128)(2,1)S(1)} %pad_maximum_fusion.2.refs_1_, bf16[4,2,80,640]{3,2,1,0:T(8,128)(2,1)S(1)} %collective-permute-done.19.refs_2_, bf16[2,512,512]{2,1,0:T(8,128)(2,1)S(1)} %copy-done.3, ...), custom_call_target="tpu_custom_call" | custom-call | flops 12000000000 | bytes 8388608 | tf_op jit(solution)/shard_map/other_half/pallas_call | solution.py:405
  (27 shorter events, 0.2 us)
Async XLA Ops:
  0.6 18.5 %copy-start.4 = (bf16[80,640]{1,0:T(8,128)(2,1)S(1)}, bf16[80,640]{1,0:T(8,128)(2,1)}, u32[]{:S(2)}) copy-start(bf16[80,640]{1,0:T(8,128)(2,1)} %param.6) | copy-start | bytes 307204
  1.7 8.5 %collective-permute-start.2 = (bf16[176,640]{1,0:T(8,128)(2,1)S(1)}, bf16[176,640]{1,0:T(8,128)(2,1)S(1)}, u32[]{:S(2)}, u32[]{:S(2)}) collective-permute-start(bf16[176,640]{1,0:T(8,128)(2,1)S(1)} %get-tuple-element.69), channel_id=1, source_target_pairs={{0,4},{2,6},{4,0},{6,2},{8,12},{10,14},{12,8},{14,10},{16,20},{18,... | collective-permute-start | bytes 675848 | tf_op jit(solution)/shard_map/ppermute | solution.py:121
  4.7 7.0 %collective-permute-start.1 = (bf16[176,640]{1,0:T(8,128)(2,1)S(1)}, bf16[176,640]{1,0:T(8,128)(2,1)S(1)}, u32[]{:S(2)}, u32[]{:S(2)}) collective-permute-start(bf16[176,640]{1,0:T(8,128)(2,1)S(1)} %get-tuple-element.69), channel_id=1, source_target_pairs={{0,2},{2,0},{4,6},{6,4},{8,10},{10,8},{12,14},{14,12},{16,18},{18,... | collective-permute-start | bytes 675848 | tf_op jit(solution)/shard_map/ppermute | solution.py:121
  6.2 6.7 %collective-permute-start = (bf16[176,640]{1,0:T(8,128)(2,1)S(1)}, bf16[176,640]{1,0:T(8,128)(2,1)S(1)}, u32[]{:S(2)}, u32[]{:S(2)}) collective-permute-start(bf16[176,640]{1,0:T(8,128)(2,1)S(1)} %get-tuple-element.69), channel_id=1, source_target_pairs={{0,8},{2,10},{4,12},{6,14},{8,0},{10,2},{12,4},{14,6},{16,24},{18,... | collective-permute-start | bytes 675848 | tf_op jit(solution)/shard_map/ppermute | solution.py:121
  12.9 7.0 %collective-permute-start.3 = (bf16[176,640]{1,0:T(8,128)(2,1)S(1)}, bf16[176,640]{1,0:T(8,128)(2,1)S(1)}, u32[]{:S(2)}, u32[]{:S(2)}) collective-permute-start(bf16[176,640]{1,0:T(8,128)(2,1)S(1)} %collective-permute-done), channel_id=1, source_target_pairs={{0,2},{2,0},{4,6},{6,4},{8,10},{10,8},{12,14},{14,12},{16,18},{18,... | collective-permute-start | bytes 675848 | tf_op jit(solution)/shard_map/ppermute | solution.py:121
  13.4 7.4 %collective-permute-start.4 = (bf16[176,640]{1,0:T(8,128)(2,1)S(1)}, bf16[176,640]{1,0:T(8,128)(2,1)S(1)}, u32[]{:S(2)}, u32[]{:S(2)}) collective-permute-start(bf16[176,640]{1,0:T(8,128)(2,1)S(1)} %collective-permute-done), channel_id=1, source_target_pairs={{0,4},{2,6},{4,0},{6,2},{8,12},{10,14},{12,8},{14,10},{16,20},{18,... | collective-permute-start | bytes 675848 | tf_op jit(solution)/shard_map/ppermute | solution.py:121
  14.7 12.2 %collective-permute-start.7 = (bf16[2,96,640]{2,1,0:T(8,128)(2,1)S(1)}, bf16[2,96,640]{2,1,0:T(8,128)(2,1)S(1)}, u32[]{:S(2)}, u32[]{:S(2)}) collective-permute-start(bf16[2,96,640]{2,1,0:T(8,128)(2,1)S(1)} %pad_maximum_fusion.3), channel_id=1, source_target_pairs={{0,16},{2,18},{4,20},{6,22},{8,24},{10,26},{12,28},{14,30},{16,0},... | collective-permute-start | bytes 737288 | tf_op jit(solution)/shard_map/ppermute | solution.py:121
  17.6 6.1 %collective-permute-start.5 = (bf16[176,640]{1,0:T(8,128)(2,1)S(1)}, bf16[176,640]{1,0:T(8,128)(2,1)S(1)}, u32[]{:S(2)}, u32[]{:S(2)}) collective-permute-start(bf16[176,640]{1,0:T(8,128)(2,1)S(1)} %collective-permute-done.2), channel_id=1, source_target_pairs={{0,2},{2,0},{4,6},{6,4},{8,10},{10,8},{12,14},{14,12},{16,18},{18,... | collective-permute-start | bytes 675848 | tf_op jit(solution)/shard_map/ppermute | solution.py:121
  19.9 9.9 %collective-permute-start.6 = (bf16[176,640]{1,0:T(8,128)(2,1)S(1)}, bf16[176,640]{1,0:T(8,128)(2,1)S(1)}, u32[]{:S(2)}, u32[]{:S(2)}) collective-permute-start(bf16[176,640]{1,0:T(8,128)(2,1)S(1)} %collective-permute-done.3), channel_id=1, source_target_pairs={{0,4},{2,6},{4,0},{6,2},{8,12},{10,14},{12,8},{14,10},{16,20},{18,... | collective-permute-start | bytes 675848 | tf_op jit(solution)/shard_map/ppermute | solution.py:121
  26.9 13.5 %collective-permute-start.8 = (bf16[2,96,640]{2,1,0:T(8,128)(2,1)S(1)}, bf16[2,96,640]{2,1,0:T(8,128)(2,1)S(1)}, u32[]{:S(2)}, u32[]{:S(2)}) collective-permute-start(bf16[2,96,640]{2,1,0:T(8,128)(2,1)S(1)} %collective-permute-done.7), channel_id=1, source_target_pairs={{0,2},{2,0},{4,6},{6,4},{8,10},{10,8},{12,14},{14,12},{16,18},{18,... | collective-permute-start | bytes 737288 | tf_op jit(solution)/shard_map/ppermute | solution.py:121
  28.3 12.2 %collective-permute-start.9 = (bf16[2,96,640]{2,1,0:T(8,128)(2,1)S(1)}, bf16[2,96,640]{2,1,0:T(8,128)(2,1)S(1)}, u32[]{:S(2)}, u32[]{:S(2)}) collective-permute-start(bf16[2,96,640]{2,1,0:T(8,128)(2,1)S(1)} %collective-permute-done.7), channel_id=1, source_target_pairs={{0,4},{2,6},{4,0},{6,2},{8,12},{10,14},{12,8},{14,10},{16,20},{18,... | collective-permute-start | bytes 737288 | tf_op jit(solution)/shard_map/ppermute | solution.py:121
  29.8 10.6 %collective-permute-start.10 = (bf16[2,80,640]{2,1,0:T(8,128)(2,1)S(1)}, bf16[2,80,640]{2,1,0:T(8,128)(2,1)S(1)}, u32[]{:S(2)}, u32[]{:S(2)}) collective-permute-start(bf16[2,80,640]{2,1,0:T(8,128)(2,1)S(1)} %pad_maximum_fusion.5), channel_id=1, source_target_pairs={{0,16},{2,18},{4,20},{6,22},{8,24},{10,26},{12,28},{14,30},{16,0},... | collective-permute-start | bytes 614408 | tf_op jit(solution)/shard_map/ppermute | solution.py:121
  30.1 16.2 %copy-start.2 = (f32[3,512,256]{2,1,0:T(8,128)S(1)}, f32[3,512,256]{2,1,0:T(8,128)}, u32[]{:S(2)}) copy-start(f32[3,512,256]{2,1,0:T(8,128)} %refs_4_.1) | copy-start | bytes 4718596
  30.1 18.8 %copy-start = (s32[3,10]{1,0:T(4,128)S(1)}, s32[3,10]{1,0:T(4,128)}, u32[]{:S(2)}) copy-start(s32[3,10]{1,0:T(4,128)} %refs_0_.1) | copy-start | bytes 364
  30.1 18.8 %copy-start.1 = (s32[3,10]{1,0:T(4,128)S(1)}, s32[3,10]{1,0:T(4,128)}, u32[]{:S(2)}) copy-start(s32[3,10]{1,0:T(4,128)} %refs_1_.1) | copy-start | bytes 364
  30.2 18.7 %collective-permute-start.13 = (bf16[4,2,176,640]{3,2,1,0:T(8,128)(2,1)S(1)}, bf16[4,2,176,640]{3,2,1,0:T(8,128)(2,1)S(1)}, u32[]{:S(2)}, u32[]{:S(2)}) collective-permute-start(bf16[4,2,176,640]{3,2,1,0:T(8,128)(2,1)S(1)} %pad_maximum_fusion.refs_2_.refs_1_), channel_id=1, source_target_pairs={{0,1},{1,0},{2,3},{3,2},{4,5},{5,4},{6,7},{7,6},{8,9},{9,8},{10,11... | collective-permute-start | bytes 5406728 | tf_op jit(solution)/shard_map/ppermute | solution.py:125
  40.5 4.9 %collective-permute-start.11 = (bf16[96,640]{1,0:T(8,128)(2,1)S(1)}, bf16[96,640]{1,0:T(8,128)(2,1)S(1)}, u32[]{:S(2)}, u32[]{:S(2)}) collective-permute-start(bf16[96,640]{1,0:T(8,128)(2,1)S(1)} %slice_bitcast_fusion.1), channel_id=1, source_target_pairs={{0,2},{2,0},{4,6},{6,4},{8,10},{10,8},{12,14},{14,12},{16,18},{18,... | collective-permute-start | bytes 368648 | tf_op jit(solution)/shard_map/ppermute | solution.py:121
  41.1 4.9 %collective-permute-start.12 = (bf16[96,640]{1,0:T(8,128)(2,1)S(1)}, bf16[96,640]{1,0:T(8,128)(2,1)S(1)}, u32[]{:S(2)}, u32[]{:S(2)}) collective-permute-start(bf16[96,640]{1,0:T(8,128)(2,1)S(1)} %slice_bitcast_fusion), channel_id=1, source_target_pairs={{0,4},{2,6},{4,0},{6,2},{8,12},{10,14},{12,8},{14,10},{16,20},{18,... | collective-permute-start | bytes 368648 | tf_op jit(solution)/shard_map/ppermute | solution.py:121
  46.3 4.7 %copy-start.3 = (bf16[2,512,512]{2,1,0:T(8,128)(2,1)S(1)}, bf16[2,512,512]{2,1,0:T(8,128)(2,1)}, u32[]{:S(2)}) copy-start(bf16[2,512,512]{2,1,0:T(8,128)(2,1)} %refs_3_.3) | copy-start | bytes 3145732
  46.3 2.6 %collective-permute-start.14 = (bf16[4,2,96,640]{3,2,1,0:T(8,128)(2,1)S(1)}, bf16[4,2,96,640]{3,2,1,0:T(8,128)(2,1)S(1)}, u32[]{:S(2)}, u32[]{:S(2)}) collective-permute-start(bf16[4,2,96,640]{3,2,1,0:T(8,128)(2,1)S(1)} %pad_maximum_fusion.1.refs_3_), channel_id=1, source_target_pairs={{0,1},{1,0},{2,3},{3,2},{4,5},{5,4},{6,7},{7,6},{8,9},{9,8},{10,11... | collective-permute-start | bytes 2949128 | tf_op jit(solution)/shard_map/ppermute | solution.py:125
  46.4 17.9 %collective-permute-start.20 = (f32[3,512,256]{2,1,0:T(8,128)S(1)}, f32[3,512,256]{2,1,0:T(8,128)S(1)}, u32[]{:S(2)}, u32[]{:S(2)}) collective-permute-start(f32[3,512,256]{2,1,0:T(8,128)S(1)} %copy-done.2), channel_id=1, source_target_pairs={{0,1},{1,0},{2,3},{3,2},{4,5},{5,4},{6,7},{7,6},{8,9},{9,8},{10,11... | collective-permute-start | bytes 4718600 | tf_op jit(solution)/shard_map/ppermute | solution.py:125
  46.8 9.1 %collective-permute-start.15 = (bf16[2,80,640]{2,1,0:T(8,128)(2,1)S(1)}, bf16[2,80,640]{2,1,0:T(8,128)(2,1)S(1)}, u32[]{:S(2)}, u32[]{:S(2)}) collective-permute-start(bf16[2,80,640]{2,1,0:T(8,128)(2,1)S(1)} %collective-permute-done.10), channel_id=1, source_target_pairs={{0,2},{2,0},{4,6},{6,4},{8,10},{10,8},{12,14},{14,12},{16,18},{18,... | collective-permute-start | bytes 614408 | tf_op jit(solution)/shard_map/ppermute | solution.py:121
  48.3 7.7 %collective-permute-start.16 = (bf16[2,80,640]{2,1,0:T(8,128)(2,1)S(1)}, bf16[2,80,640]{2,1,0:T(8,128)(2,1)S(1)}, u32[]{:S(2)}, u32[]{:S(2)}) collective-permute-start(bf16[2,80,640]{2,1,0:T(8,128)(2,1)S(1)} %collective-permute-done.10), channel_id=1, source_target_pairs={{0,4},{2,6},{4,0},{6,2},{8,12},{10,14},{12,8},{14,10},{16,20},{18,... | collective-permute-start | bytes 614408 | tf_op jit(solution)/shard_map/ppermute | solution.py:121
  56.0 5.2 %collective-permute-start.17 = (bf16[80,640]{1,0:T(8,128)(2,1)S(1)}, bf16[80,640]{1,0:T(8,128)(2,1)S(1)}, u32[]{:S(2)}, u32[]{:S(2)}) collective-permute-start(bf16[80,640]{1,0:T(8,128)(2,1)S(1)} %slice_bitcast_fusion.4), channel_id=1, source_target_pairs={{0,2},{2,0},{4,6},{6,4},{8,10},{10,8},{12,14},{14,12},{16,18},{18,... | collective-permute-start | bytes 307208 | tf_op jit(solution)/shard_map/ppermute | solution.py:121
  57.5 4.7 %collective-permute-start.18 = (bf16[80,640]{1,0:T(8,128)(2,1)S(1)}, bf16[80,640]{1,0:T(8,128)(2,1)S(1)}, u32[]{:S(2)}, u32[]{:S(2)}) collective-permute-start(bf16[80,640]{1,0:T(8,128)(2,1)S(1)} %slice_bitcast_fusion.3), channel_id=1, source_target_pairs={{0,4},{2,6},{4,0},{6,2},{8,12},{10,14},{12,8},{14,10},{16,20},{18,... | collective-permute-start | bytes 307208 | tf_op jit(solution)/shard_map/ppermute | solution.py:121
  62.4 2.4 %collective-permute-start.19 = (bf16[4,2,80,640]{3,2,1,0:T(8,128)(2,1)S(1)}, bf16[4,2,80,640]{3,2,1,0:T(8,128)(2,1)S(1)}, u32[]{:S(2)}, u32[]{:S(2)}) collective-permute-start(bf16[4,2,80,640]{3,2,1,0:T(8,128)(2,1)S(1)} %pad_maximum_fusion.2.refs_1_), channel_id=1, source_target_pairs={{0,1},{1,0},{2,3},{3,2},{4,5},{5,4},{6,7},{7,6},{8,9},{9,8},{10,11... | collective-permute-start | bytes 2457608 | tf_op jit(solution)/shard_map/ppermute | solution.py:125

commit v8 on v5

--- a/solution.py
+++ b/solution.py
@@ -182,7 +182,7 @@
                 pt[s, :, lanes] = jnp.zeros((width, 128), bf16)
 
 
-def add_rows(wave, skip, dims, col, row, pt, z_refs, link_ref, before, sums, scratch):
+def add_rows(wave, skip, dims, col, row, pt, z_refs, link_ref, before, sums, scratch, meanwhile=None):
     width, span = dims
     z_all, c0h, c0l, c1h, c1l, p1h, p1l, c2h, c2l, tmp, sem = scratch
     half_rows = z_all.shape[0]
@@ -207,6 +207,8 @@
                 )
     for copy in copies:
         copy.start()
+    if meanwhile is not None:
+        meanwhile()
     for copy in copies:
         copy.wait()
     c_rows = pl.ds(pl.multiple_of(col * half_w, half_w), half_w)
@@ -255,24 +257,28 @@
 
 def last_kernel(dims, rows, *refs):
     pt, z_refs, link_ref, diag_ref, diag_other_ref = refs[0], refs[1:3], refs[3], refs[4], refs[5]
-    before, diag_out, sums, scratch = refs[6:11], refs[11], refs[12:17], refs[17:]
+    before, diag_out, sums, (link_t, whole), scratch = refs[6:11], refs[11], refs[12:17], refs[17:19], refs[19:]
     col = lax.axis_index("col")
     width, _ = dims
     half_w = width // 2
-    add_rows(1, 0, dims, col, lax.axis_index("row"), pt, z_refs, link_ref, before, sums, scratch)
+
+    def meanwhile():
+        for s in range(2):
+            link_t[s] = link_ref[s].T
+            mine, theirs = diag_ref[s], diag_other_ref[s]
+            whole[s, :, :half_w] = jnp.where(col == 0, mine, theirs)
+            whole[s, :, half_w:] = jnp.where(col == 0, theirs, mine)
+
+    add_rows(1, 0, dims, col, lax.axis_index("row"), pt, z_refs, link_ref, before, sums, scratch, meanwhile)
     s0, u1, s1, n2, s2 = sums
     scale = 1.0 / rows
     c_rows = pl.ds(pl.multiple_of(col * half_w, half_w), half_w)
 
-    def whole(s):
-        mine, theirs = diag_ref[s], diag_other_ref[s]
-        return jnp.concatenate([jnp.where(col == 0, mine, theirs), jnp.where(col == 0, theirs, mine)], axis=1)
-
-    d0 = whole(0) - s0[...] * scale
+    d0 = whole[0] - s0[...] * scale
     i1 = s1[...] - u1[...].T
-    d1 = whole(1) - i1 * scale + nn2r(link_ref[0].T, split2(nn2(split2(d0), link_ref[0])))
+    d1 = whole[1] - i1 * scale + nn2r(link_t[0], split2(nn2(split2(d0), link_ref[0])))
     i2 = s2[...] - nn2(split2(n2[...]), link_ref[1]).T
-    d2 = diag_ref[2] - i2 * scale + nn2r(link_ref[1].T, split2(nn2(split2(d1), link_ref[1, :, c_rows])))
+    d2 = diag_ref[2] - i2 * scale + nn2r(link_t[1], split2(nn2(split2(d1), link_ref[1, :, c_rows])))
     diag_out[0] = jnp.where(col == 0, d0[:, :half_w], d0[:, half_w:])
     diag_out[1] = jnp.where(col == 0, d1[:, :half_w], d1[:, half_w:])
     diag_out[2] = d2
@@ -367,7 +373,9 @@
         out_shape=shape((supers, width, half_w), f32),
         in_specs=[vmem] + [any_spec] * 2 + [vmem] * 8,
         out_specs=vmem,
-        scratch_shapes=[pltpu.VMEM(v, f32) for v in sum_shapes] + scratch,
+        scratch_shapes=[pltpu.VMEM(v, f32) for v in sum_shapes]
+        + [pltpu.VMEM((2, width, width), bf16), pltpu.VMEM((2, width, width), f32)]
+        + scratch,
     )(pt, z_last, z_last_other, coupling, diag_inverse, diag_other, *sums)
     return columns, diagonals
 

time: 74.5 us -> 74.7 us (level)
  no operation moved by 1% of the time
where the time goes in v8:
time: 74.7 us; the launch traced here: 74.5 us
  starting transfers between devices  26 us (35%)
  waiting for transfers between devices  23.8 us (32%)
  Pallas kernels  21.8 us (29%)
  other arithmetic  1.88 us (3%)
  between operations  1.03 us (1%)
    ppermute x19, starting transfers between devices, swap(): return lax.ppermute(value, axis, [(i, i ^ bit) for i in range(parts)])  25.3 us
    ppermute x19, waiting for transfers between devices, swap(): return lax.ppermute(value, axis, [(i, i ^ bit) for i in range(parts)])  23.8 us
    pallas_call x1, Pallas kernels, replicated_plan(): call(functools.partial(last_kernel, dims, rows), 'other_half', 12 * 10 **...  11.6 us
    pallas_call x1, Pallas kernels, replicated_plan(): call(functools.partial(first_kernel, dims, supers * part), 'own_half', 8...  8.18 us
    pallas_call x1, Pallas kernels, replicated_plan(): call(functools.partial(place_kernel, (supers, width, rows, span, part)),...  2.06 us
    another operation x6, other arithmetic, replicated_plan(): first = jnp.stack([jnp.stack([p[j] for p in early]) for j in range(4)])  1.5 us
  transfers between devices with their start and end apart: 23, of which 10 were waited for; matrix products, arithmetic and copies ran while one was open for 1% of the time, Pallas kernels for 14%

profile of v8, /device:TPU:0, one launch (start us, length us, event | category | flops | bytes accessed | tf_op | source)
XLA Modules:
  0.0 74.5 jit_solution(13528990169921120176)
XLA Ops:
  0.6 1.0 %fusion = (bf16[1,176,640]{2,1,0:T(8,128)(2,1)S(1)}, bf16[176,640]{1,0:T(8,128)(2,1)S(1)}) fusion(bf16[80,640]{1,0:T(8,128)(2,1)} %param.6, bf16[96,640]{1,0:T(8,128)(2,1)} %bitcast.59), kind=kLoop, calls=%fused_computation.16 | loop fusion | flops 450560 | bytes 675840 | tf_op jit(solution)/shard_map/stack | solution.py:329
  1.7 3.1 %collective-permute-start.2 = (bf16[176,640]{1,0:T(8,128)(2,1)S(1)}, bf16[176,640]{1,0:T(8,128)(2,1)S(1)}, u32[]{:S(2)}, u32[]{:S(2)}) collective-permute-start(bf16[176,640]{1,0:T(8,128)(2,1)S(1)} %get-tuple-element.33), channel_id=1, source_target_pairs={{0,8},{2,10},{4,12},{6,14},{8,0},{10,2},{12,4},{14,6},{16,24},{18,... | collective-permute-start | bytes 675848 | tf_op jit(solution)/shard_map/ppermute | solution.py:121
  4.8 1.5 %collective-permute-start.3 = (bf16[176,640]{1,0:T(8,128)(2,1)S(1)}, bf16[176,640]{1,0:T(8,128)(2,1)S(1)}, u32[]{:S(2)}, u32[]{:S(2)}) collective-permute-start(bf16[176,640]{1,0:T(8,128)(2,1)S(1)} %get-tuple-element.33), channel_id=1, source_target_pairs={{0,2},{2,0},{4,6},{6,4},{8,10},{10,8},{12,14},{14,12},{16,18},{18,... | collective-permute-start | bytes 675848 | tf_op jit(solution)/shard_map/ppermute | solution.py:121
  6.2 1.5 %collective-permute-start.4 = (bf16[176,640]{1,0:T(8,128)(2,1)S(1)}, bf16[176,640]{1,0:T(8,128)(2,1)S(1)}, u32[]{:S(2)}, u32[]{:S(2)}) collective-permute-start(bf16[176,640]{1,0:T(8,128)(2,1)S(1)} %get-tuple-element.33), channel_id=1, source_target_pairs={{0,4},{2,6},{4,0},{6,2},{8,12},{10,14},{12,8},{14,10},{16,20},{18,... | collective-permute-start | bytes 675848 | tf_op jit(solution)/shard_map/ppermute | solution.py:121
  7.8 2.6 %collective-permute-start = (bf16[96,640]{1,0:T(8,128)(2,1)}, bf16[96,640]{1,0:T(8,128)(2,1)S(1)}, u32[]{:S(2)}, u32[]{:S(2)}) collective-permute-start(bf16[96,640]{1,0:T(8,128)(2,1)} %bitcast.60), channel_id=1, source_target_pairs={{0,16},{2,18},{4,20},{6,22},{8,24},{10,26},{12,28},{14,30},{16,0},... | collective-permute-start | bytes 368648 | tf_op jit(solution)/shard_map/ppermute | solution.py:121
  10.4 0.2 collective-permute-start.1
  10.6 0.0 collective-permute-done.2
  10.6 1.1 %collective-permute-done.3 = bf16[176,640]{1,0:T(8,128)(2,1)S(1)} collective-permute-done((bf16[176,640]{1,0:T(8,128)(2,1)S(1)}, bf16[176,640]{1,0:T(8,128)(2,1)S(1)}, u32[]{:S(2)}, u32[]{:S(2)}) %collective-permute-start.3) | collective-permute-done | bytes 225312 | tf_op jit(solution)/shard_map/ppermute | solution.py:121
  11.7 1.2 %collective-permute-done.4 = bf16[176,640]{1,0:T(8,128)(2,1)S(1)} collective-permute-done((bf16[176,640]{1,0:T(8,128)(2,1)S(1)}, bf16[176,640]{1,0:T(8,128)(2,1)S(1)}, u32[]{:S(2)}, u32[]{:S(2)}) %collective-permute-start.4) | collective-permute-done | bytes 225312 | tf_op jit(solution)/shard_map/ppermute | solution.py:121
  12.9 0.5 collective-permute-start.5
  13.5 2.0 %collective-permute-start.6 = (bf16[176,640]{1,0:T(8,128)(2,1)S(1)}, bf16[176,640]{1,0:T(8,128)(2,1)S(1)}, u32[]{:S(2)}, u32[]{:S(2)}) collective-permute-start(bf16[176,640]{1,0:T(8,128)(2,1)S(1)} %collective-permute-done.2), channel_id=1, source_target_pairs={{0,4},{2,6},{4,0},{6,2},{8,12},{10,14},{12,8},{14,10},{16,20},{18,... | collective-permute-start | bytes 675848 | tf_op jit(solution)/shard_map/ppermute | solution.py:121
  15.5 1.0 %collective-permute-start.9 = (bf16[176,640]{1,0:T(8,128)(2,1)S(1)}, bf16[176,640]{1,0:T(8,128)(2,1)S(1)}, u32[]{:S(2)}, u32[]{:S(2)}) collective-permute-start(bf16[176,640]{1,0:T(8,128)(2,1)S(1)} %collective-permute-done.4), channel_id=1, source_target_pairs={{0,2},{2,0},{4,6},{6,4},{8,10},{10,8},{12,14},{14,12},{16,18},{18,... | collective-permute-start | bytes 675848 | tf_op jit(solution)/shard_map/ppermute | solution.py:121
  16.5 3.2 %collective-permute-done = bf16[96,640]{1,0:T(8,128)(2,1)S(1)} collective-permute-done((bf16[96,640]{1,0:T(8,128)(2,1)}, bf16[96,640]{1,0:T(8,128)(2,1)S(1)}, u32[]{:S(2)}, u32[]{:S(2)}) %collective-permute-start) | collective-permute-done | bytes 122912 | tf_op jit(solution)/shard_map/ppermute | solution.py:121
  19.7 0.0 collective-permute-done.1
  19.7 0.1 maximum_bitcast_fusion
  19.8 1.3 %collective-permute-done.5 = bf16[176,640]{1,0:T(8,128)(2,1)S(1)} collective-permute-done((bf16[176,640]{1,0:T(8,128)(2,1)S(1)}, bf16[176,640]{1,0:T(8,128)(2,1)S(1)}, u32[]{:S(2)}, u32[]{:S(2)}) %collective-permute-start.5) | collective-permute-done | bytes 225312 | tf_op jit(solution)/shard_map/ppermute | solution.py:121
  21.1 2.2 %collective-permute-start.8 = (bf16[80,640]{1,0:T(8,128)(2,1)S(1)}, bf16[80,640]{1,0:T(8,128)(2,1)S(1)}, u32[]{:S(2)}, u32[]{:S(2)}) collective-permute-start(bf16[80,640]{1,0:T(8,128)(2,1)S(1)} %copy-done.4), channel_id=1, source_target_pairs={{0,24},{2,26},{4,28},{6,30},{8,16},{10,18},{12,20},{14,22},{16,8},... | collective-permute-start | bytes 307208 | tf_op jit(solution)/shard_map/ppermute | solution.py:121
  23.4 0.4 collective-permute-start.7
  23.8 1.9 %collective-permute-start.10 = (bf16[2,96,640]{2,1,0:T(8,128)(2,1)S(1)}, bf16[2,96,640]{2,1,0:T(8,128)(2,1)S(1)}, u32[]{:S(2)}, u32[]{:S(2)}) collective-permute-start(bf16[2,96,640]{2,1,0:T(8,128)(2,1)S(1)} %pad_maximum_fusion.3), channel_id=1, source_target_pairs={{0,2},{2,0},{4,6},{6,4},{8,10},{10,8},{12,14},{14,12},{16,18},{18,... | collective-permute-start | bytes 737288 | tf_op jit(solution)/shard_map/ppermute | solution.py:121
  25.7 1.9 %collective-permute-start.11 = (bf16[2,96,640]{2,1,0:T(8,128)(2,1)S(1)}, bf16[2,96,640]{2,1,0:T(8,128)(2,1)S(1)}, u32[]{:S(2)}, u32[]{:S(2)}) collective-permute-start(bf16[2,96,640]{2,1,0:T(8,128)(2,1)S(1)} %pad_maximum_fusion.3), channel_id=1, source_target_pairs={{0,4},{2,6},{4,0},{6,2},{8,12},{10,14},{12,8},{14,10},{16,20},{18,... | collective-permute-start | bytes 737288 | tf_op jit(solution)/shard_map/ppermute | solution.py:121
  27.6 0.2 collective-permute-start.16
  27.7 0.1 maximum_bitcast_fusion.2
  27.8 0.1 maximum_bitcast_fusion.1
  27.8 6.5 %collective-permute-done.16 = bf16[176,640]{1,0:T(8,128)(2,1)S(1)} collective-permute-done((bf16[176,640]{1,0:T(8,128)(2,1)S(1)}, bf16[176,640]{1,0:T(8,128)(2,1)S(1)}, u32[]{:S(2)}, u32[]{:S(2)}) %collective-permute-start.16) | collective-permute-done | bytes 225312 | tf_op jit(solution)/shard_map/ppermute | solution.py:121
  34.3 0.1 maximum_bitcast_fusion.3
  34.4 0.3 pad_maximum_fusion.refs_2_.refs_1_
  34.6 0.0 copy-start.2
  34.6 0.1 collective-permute-start.19
  34.7 0.0 collective-permute-done.7
  34.8 1.9 %collective-permute-start.18 = (bf16[96,640]{1,0:T(8,128)(2,1)S(1)}, bf16[96,640]{1,0:T(8,128)(2,1)S(1)}, u32[]{:S(2)}, u32[]{:S(2)}) collective-permute-start(bf16[96,640]{1,0:T(8,128)(2,1)S(1)} %slice_bitcast_fusion), channel_id=1, source_target_pairs={{0,4},{2,6},{4,0},{6,2},{8,12},{10,14},{12,8},{14,10},{16,20},{18,... | collective-permute-start | bytes 368648 | tf_op jit(solution)/shard_map/ppermute | solution.py:121
  36.7 0.8 %collective-permute-start.17 = (bf16[96,640]{1,0:T(8,128)(2,1)S(1)}, bf16[96,640]{1,0:T(8,128)(2,1)S(1)}, u32[]{:S(2)}, u32[]{:S(2)}) collective-permute-start(bf16[96,640]{1,0:T(8,128)(2,1)S(1)} %slice_bitcast_fusion.1), channel_id=1, source_target_pairs={{0,2},{2,0},{4,6},{6,4},{8,10},{10,8},{12,14},{14,12},{16,18},{18,... | collective-permute-start | bytes 368648 | tf_op jit(solution)/shard_map/ppermute | solution.py:121
  37.6 1.3 %collective-permute-start.14 = (bf16[2,80,640]{2,1,0:T(8,128)(2,1)S(1)}, bf16[2,80,640]{2,1,0:T(8,128)(2,1)S(1)}, u32[]{:S(2)}, u32[]{:S(2)}) collective-permute-start(bf16[2,80,640]{2,1,0:T(8,128)(2,1)S(1)} %pad_maximum_fusion.5), channel_id=1, source_target_pairs={{0,2},{2,0},{4,6},{6,4},{8,10},{10,8},{12,14},{14,12},{16,18},{18,... | collective-permute-start | bytes 614408 | tf_op jit(solution)/shard_map/ppermute | solution.py:121
  38.9 0.2 collective-permute-start.12
  39.1 1.6 %collective-permute-done.18 = bf16[96,640]{1,0:T(8,128)(2,1)S(1)} collective-permute-done((bf16[96,640]{1,0:T(8,128)(2,1)S(1)}, bf16[96,640]{1,0:T(8,128)(2,1)S(1)}, u32[]{:S(2)}, u32[]{:S(2)}) %collective-permute-start.18) | collective-permute-done | bytes 122912 | tf_op jit(solution)/shard_map/ppermute | solution.py:121
  40.7 2.3 %collective-permute-done.17 = bf16[96,640]{1,0:T(8,128)(2,1)S(1)} collective-permute-done((bf16[96,640]{1,0:T(8,128)(2,1)S(1)}, bf16[96,640]{1,0:T(8,128)(2,1)S(1)}, u32[]{:S(2)}, u32[]{:S(2)}) %collective-permute-start.17) | collective-permute-done | bytes 122912 | tf_op jit(solution)/shard_map/ppermute | solution.py:121
  43.0 0.1 pad_maximum_fusion.1.refs_3_
  43.1 3.5 %collective-permute-done.14 = bf16[2,80,640]{2,1,0:T(8,128)(2,1)S(1)} collective-permute-done((bf16[2,80,640]{2,1,0:T(8,128)(2,1)S(1)}, bf16[2,80,640]{2,1,0:T(8,128)(2,1)S(1)}, u32[]{:S(2)}, u32[]{:S(2)}) %collective-permute-start.14) | collective-permute-done | bytes 204832 | tf_op jit(solution)/shard_map/ppermute | solution.py:121
  46.6 0.5 collective-permute-start.22
  47.1 0.4 collective-permute-start.15
  47.5 1.7 %collective-permute-start.13 = (bf16[80,640]{1,0:T(8,128)(2,1)S(1)}, bf16[80,640]{1,0:T(8,128)(2,1)S(1)}, u32[]{:S(2)}, u32[]{:S(2)}) collective-permute-start(bf16[80,640]{1,0:T(8,128)(2,1)S(1)} %slice_bitcast_fusion.3), channel_id=1, source_target_pairs={{0,2},{2,0},{4,6},{6,4},{8,10},{10,8},{12,14},{14,12},{16,18},{18,... | collective-permute-start | bytes 307208 | tf_op jit(solution)/shard_map/ppermute | solution.py:121
  49.2 2.9 %collective-permute-done.15 = bf16[80,640]{1,0:T(8,128)(2,1)S(1)} collective-permute-done((bf16[80,640]{1,0:T(8,128)(2,1)S(1)}, bf16[80,640]{1,0:T(8,128)(2,1)S(1)}, u32[]{:S(2)}, u32[]{:S(2)}) %collective-permute-start.15) | collective-permute-done | bytes 102432 | tf_op jit(solution)/shard_map/ppermute | solution.py:121
  52.1 0.2 collective-permute-done.13
  52.3 0.0 copy-start.3
  52.3 2.1 %place.1.refs_0_ = bf16[3,512,1280]{2,1,0:T(8,128)(2,1)S(1)} custom-call(s32[3,10]{1,0:T(4,128)S(1)} %copy-done, s32[3,10]{1,0:T(4,128)S(1)} %copy-done.1, bf16[4,2,176,640]{3,2,1,0:T(8,128)(2,1)S(1)} %pad_maximum_fusion.refs_2_.refs_1_, bf16[4,2,96,640]{3,2,1,0:T(8,128)(2,1)S(1)} %pad_maximum_fusion.1.refs_3_, ...), custom_call_target="tpu_custom_call" | custom-call | flops 2000000000 | bytes 8388608 | tf_op jit(solution)/shard_map/place/pallas_call | solution.py:341
  54.4 0.1 pad_maximum_fusion.2.refs_1_
  54.5 0.1 collective-permute-start.21
  54.6 8.2 %own_half.1 = (f32[512,512]{1,0:T(8,128)S(1)}, f32[512,512]{1,0:T(8,128)S(1)}, f32[512,512]{1,0:T(8,128)S(1)}, f32[256,512]{1,0:T(8,128)S(1)}, f32[512,256]{1,0:T(8,128)S(1)}, /*index=5*/f32[3,40,512]{2,1,0:T(8,128)}) custom-call(bf16[3,512,1280]{2,1,0:T(8,128)(2,1)S(1)} %place.1.refs_0_, bf16[4,2,176,640]{3,2,1,0:T(8,128)(2,1)S(1)} %pad_maximum_fusion.refs_2_.refs_1_, ...), custom_call_target="tpu_custom_call" | custom-call | flops 8000000000 | bytes 8388608 | tf_op jit(solution)/shard_map/own_half/pallas_call | solution.py:362
  62.8 11.6 %other_half.1 = f32[3,512,256]{2,1,0:T(8,128)} custom-call(bf16[3,512,1280]{2,1,0:T(8,128)(2,1)S(1)} %place.1.refs_0_, bf16[4,2,80,640]{3,2,1,0:T(8,128)(2,1)S(1)} %pad_maximum_fusion.2.refs_1_, bf16[4,2,80,640]{3,2,1,0:T(8,128)(2,1)S(1)} %collective-permute-done.21.refs_2_, bf16[2,512,512]{2,1,0:T(8,128)(2,1)S(1)} %copy-done.3, ...), custom_call_target="tpu_custom_call" | custom-call | flops 12000000000 | bytes 8388608 | tf_op jit(solution)/shard_map/other_half/pallas_call | solution.py:370
  (27 shorter events, 0.2 us)
Async XLA Ops:
  0.6 20.5 %copy-start.4 = (bf16[80,640]{1,0:T(8,128)(2,1)S(1)}, bf16[80,640]{1,0:T(8,128)(2,1)}, u32[]{:S(2)}) copy-start(bf16[80,640]{1,0:T(8,128)(2,1)} %param.6) | copy-start | bytes 307204
  1.7 8.9 %collective-permute-start.2 = (bf16[176,640]{1,0:T(8,128)(2,1)S(1)}, bf16[176,640]{1,0:T(8,128)(2,1)S(1)}, u32[]{:S(2)}, u32[]{:S(2)}) collective-permute-start(bf16[176,640]{1,0:T(8,128)(2,1)S(1)} %get-tuple-element.33), channel_id=1, source_target_pairs={{0,8},{2,10},{4,12},{6,14},{8,0},{10,2},{12,4},{14,6},{16,24},{18,... | collective-permute-start | bytes 675848 | tf_op jit(solution)/shard_map/ppermute | solution.py:121
  4.8 7.0 %collective-permute-start.3 = (bf16[176,640]{1,0:T(8,128)(2,1)S(1)}, bf16[176,640]{1,0:T(8,128)(2,1)S(1)}, u32[]{:S(2)}, u32[]{:S(2)}) collective-permute-start(bf16[176,640]{1,0:T(8,128)(2,1)S(1)} %get-tuple-element.33), channel_id=1, source_target_pairs={{0,2},{2,0},{4,6},{6,4},{8,10},{10,8},{12,14},{14,12},{16,18},{18,... | collective-permute-start | bytes 675848 | tf_op jit(solution)/shard_map/ppermute | solution.py:121
  6.2 6.7 %collective-permute-start.4 = (bf16[176,640]{1,0:T(8,128)(2,1)S(1)}, bf16[176,640]{1,0:T(8,128)(2,1)S(1)}, u32[]{:S(2)}, u32[]{:S(2)}) collective-permute-start(bf16[176,640]{1,0:T(8,128)(2,1)S(1)} %get-tuple-element.33), channel_id=1, source_target_pairs={{0,4},{2,6},{4,0},{6,2},{8,12},{10,14},{12,8},{14,10},{16,20},{18,... | collective-permute-start | bytes 675848 | tf_op jit(solution)/shard_map/ppermute | solution.py:121
  7.8 11.9 %collective-permute-start = (bf16[96,640]{1,0:T(8,128)(2,1)}, bf16[96,640]{1,0:T(8,128)(2,1)S(1)}, u32[]{:S(2)}, u32[]{:S(2)}) collective-permute-start(bf16[96,640]{1,0:T(8,128)(2,1)} %bitcast.60), channel_id=1, source_target_pairs={{0,16},{2,18},{4,20},{6,22},{8,24},{10,26},{12,28},{14,30},{16,0},... | collective-permute-start | bytes 368648 | tf_op jit(solution)/shard_map/ppermute | solution.py:121
  10.4 9.3 %collective-permute-start.1 = (bf16[96,640]{1,0:T(8,128)(2,1)}, bf16[96,640]{1,0:T(8,128)(2,1)S(1)}, u32[]{:S(2)}, u32[]{:S(2)}) collective-permute-start(bf16[96,640]{1,0:T(8,128)(2,1)} %bitcast.61), channel_id=1, source_target_pairs={{0,24},{2,26},{4,28},{6,30},{8,16},{10,18},{12,20},{14,22},{16,8},... | collective-permute-start | bytes 368648 | tf_op jit(solution)/shard_map/ppermute | solution.py:121
  12.9 8.2 %collective-permute-start.5 = (bf16[176,640]{1,0:T(8,128)(2,1)S(1)}, bf16[176,640]{1,0:T(8,128)(2,1)S(1)}, u32[]{:S(2)}, u32[]{:S(2)}) collective-permute-start(bf16[176,640]{1,0:T(8,128)(2,1)S(1)} %collective-permute-done.2), channel_id=1, source_target_pairs={{0,2},{2,0},{4,6},{6,4},{8,10},{10,8},{12,14},{14,12},{16,18},{18,... | collective-permute-start | bytes 675848 | tf_op jit(solution)/shard_map/ppermute | solution.py:121
  13.5 7.7 %collective-permute-start.6 = (bf16[176,640]{1,0:T(8,128)(2,1)S(1)}, bf16[176,640]{1,0:T(8,128)(2,1)S(1)}, u32[]{:S(2)}, u32[]{:S(2)}) collective-permute-start(bf16[176,640]{1,0:T(8,128)(2,1)S(1)} %collective-permute-done.2), channel_id=1, source_target_pairs={{0,4},{2,6},{4,0},{6,2},{8,12},{10,14},{12,8},{14,10},{16,20},{18,... | collective-permute-start | bytes 675848 | tf_op jit(solution)/shard_map/ppermute | solution.py:121
  15.5 8.3 %collective-permute-start.9 = (bf16[176,640]{1,0:T(8,128)(2,1)S(1)}, bf16[176,640]{1,0:T(8,128)(2,1)S(1)}, u32[]{:S(2)}, u32[]{:S(2)}) collective-permute-start(bf16[176,640]{1,0:T(8,128)(2,1)S(1)} %collective-permute-done.4), channel_id=1, source_target_pairs={{0,2},{2,0},{4,6},{6,4},{8,10},{10,8},{12,14},{14,12},{16,18},{18,... | collective-permute-start | bytes 675848 | tf_op jit(solution)/shard_map/ppermute | solution.py:121
  21.1 13.6 %collective-permute-start.8 = (bf16[80,640]{1,0:T(8,128)(2,1)S(1)}, bf16[80,640]{1,0:T(8,128)(2,1)S(1)}, u32[]{:S(2)}, u32[]{:S(2)}) collective-permute-start(bf16[80,640]{1,0:T(8,128)(2,1)S(1)} %copy-done.4), channel_id=1, source_target_pairs={{0,24},{2,26},{4,28},{6,30},{8,16},{10,18},{12,20},{14,22},{16,8},... | collective-permute-start | bytes 307208 | tf_op jit(solution)/shard_map/ppermute | solution.py:121
  23.4 11.4 %collective-permute-start.7 = (bf16[80,640]{1,0:T(8,128)(2,1)S(1)}, bf16[80,640]{1,0:T(8,128)(2,1)S(1)}, u32[]{:S(2)}, u32[]{:S(2)}) collective-permute-start(bf16[80,640]{1,0:T(8,128)(2,1)S(1)} %copy-done.4), channel_id=1, source_target_pairs={{0,16},{2,18},{4,20},{6,22},{8,24},{10,26},{12,28},{14,30},{16,0},... | collective-permute-start | bytes 307208 | tf_op jit(solution)/shard_map/ppermute | solution.py:121
  23.8 11.0 %collective-permute-start.10 = (bf16[2,96,640]{2,1,0:T(8,128)(2,1)S(1)}, bf16[2,96,640]{2,1,0:T(8,128)(2,1)S(1)}, u32[]{:S(2)}, u32[]{:S(2)}) collective-permute-start(bf16[2,96,640]{2,1,0:T(8,128)(2,1)S(1)} %pad_maximum_fusion.3), channel_id=1, source_target_pairs={{0,2},{2,0},{4,6},{6,4},{8,10},{10,8},{12,14},{14,12},{16,18},{18,... | collective-permute-start | bytes 737288 | tf_op jit(solution)/shard_map/ppermute | solution.py:121
  25.7 9.1 %collective-permute-start.11 = (bf16[2,96,640]{2,1,0:T(8,128)(2,1)S(1)}, bf16[2,96,640]{2,1,0:T(8,128)(2,1)S(1)}, u32[]{:S(2)}, u32[]{:S(2)}) collective-permute-start(bf16[2,96,640]{2,1,0:T(8,128)(2,1)S(1)} %pad_maximum_fusion.3), channel_id=1, source_target_pairs={{0,4},{2,6},{4,0},{6,2},{8,12},{10,14},{12,8},{14,10},{16,20},{18,... | collective-permute-start | bytes 737288 | tf_op jit(solution)/shard_map/ppermute | solution.py:121
  27.6 6.7 %collective-permute-start.16 = (bf16[176,640]{1,0:T(8,128)(2,1)S(1)}, bf16[176,640]{1,0:T(8,128)(2,1)S(1)}, u32[]{:S(2)}, u32[]{:S(2)}) collective-permute-start(bf16[176,640]{1,0:T(8,128)(2,1)S(1)} %collective-permute-done.5), channel_id=1, source_target_pairs={{0,4},{2,6},{4,0},{6,2},{8,12},{10,14},{12,8},{14,10},{16,20},{18,... | collective-permute-start | bytes 675848 | tf_op jit(solution)/shard_map/ppermute | solution.py:121
  34.6 12.0 %copy-start.2 = (f32[3,512,256]{2,1,0:T(8,128)S(1)}, f32[3,512,256]{2,1,0:T(8,128)}, u32[]{:S(2)}) copy-start(f32[3,512,256]{2,1,0:T(8,128)} %refs_4_.1) | copy-start | bytes 4718596
  34.6 17.7 %collective-permute-start.19 = (bf16[4,2,176,640]{3,2,1,0:T(8,128)(2,1)S(1)}, bf16[4,2,176,640]{3,2,1,0:T(8,128)(2,1)S(1)}, u32[]{:S(2)}, u32[]{:S(2)}) collective-permute-start(bf16[4,2,176,640]{3,2,1,0:T(8,128)(2,1)S(1)} %pad_maximum_fusion.refs_2_.refs_1_), channel_id=1, source_target_pairs={{0,1},{1,0},{2,3},{3,2},{4,5},{5,4},{6,7},{7,6},{8,9},{9,8},{10,11... | collective-permute-start | bytes 5406728 | tf_op jit(solution)/shard_map/ppermute | solution.py:125
  34.8 5.9 %collective-permute-start.18 = (bf16[96,640]{1,0:T(8,128)(2,1)S(1)}, bf16[96,640]{1,0:T(8,128)(2,1)S(1)}, u32[]{:S(2)}, u32[]{:S(2)}) collective-permute-start(bf16[96,640]{1,0:T(8,128)(2,1)S(1)} %slice_bitcast_fusion), channel_id=1, source_target_pairs={{0,4},{2,6},{4,0},{6,2},{8,12},{10,14},{12,8},{14,10},{16,20},{18,... | collective-permute-start | bytes 368648 | tf_op jit(solution)/shard_map/ppermute | solution.py:121
  36.7 6.2 %collective-permute-start.17 = (bf16[96,640]{1,0:T(8,128)(2,1)S(1)}, bf16[96,640]{1,0:T(8,128)(2,1)S(1)}, u32[]{:S(2)}, u32[]{:S(2)}) collective-permute-start(bf16[96,640]{1,0:T(8,128)(2,1)S(1)} %slice_bitcast_fusion.1), channel_id=1, source_target_pairs={{0,2},{2,0},{4,6},{6,4},{8,10},{10,8},{12,14},{14,12},{16,18},{18,... | collective-permute-start | bytes 368648 | tf_op jit(solution)/shard_map/ppermute | solution.py:121
  37.6 14.8 %copy-start = (s32[3,10]{1,0:T(4,128)S(1)}, s32[3,10]{1,0:T(4,128)}, u32[]{:S(2)}) copy-start(s32[3,10]{1,0:T(4,128)} %refs_0_.1) | copy-start | bytes 364
  37.6 14.8 %copy-start.1 = (s32[3,10]{1,0:T(4,128)S(1)}, s32[3,10]{1,0:T(4,128)}, u32[]{:S(2)}) copy-start(s32[3,10]{1,0:T(4,128)} %refs_1_.1) | copy-start | bytes 364
  37.6 9.0 %collective-permute-start.14 = (bf16[2,80,640]{2,1,0:T(8,128)(2,1)S(1)}, bf16[2,80,640]{2,1,0:T(8,128)(2,1)S(1)}, u32[]{:S(2)}, u32[]{:S(2)}) collective-permute-start(bf16[2,80,640]{2,1,0:T(8,128)(2,1)S(1)} %pad_maximum_fusion.5), channel_id=1, source_target_pairs={{0,2},{2,0},{4,6},{6,4},{8,10},{10,8},{12,14},{14,12},{16,18},{18,... | collective-permute-start | bytes 614408 | tf_op jit(solution)/shard_map/ppermute | solution.py:121
  38.9 7.7 %collective-permute-start.12 = (bf16[2,80,640]{2,1,0:T(8,128)(2,1)S(1)}, bf16[2,80,640]{2,1,0:T(8,128)(2,1)S(1)}, u32[]{:S(2)}, u32[]{:S(2)}) collective-permute-start(bf16[2,80,640]{2,1,0:T(8,128)(2,1)S(1)} %pad_maximum_fusion.5), channel_id=1, source_target_pairs={{0,4},{2,6},{4,0},{6,2},{8,12},{10,14},{12,8},{14,10},{16,20},{18,... | collective-permute-start | bytes 614408 | tf_op jit(solution)/shard_map/ppermute | solution.py:121
  46.6 5.7 %collective-permute-start.20 = (bf16[4,2,96,640]{3,2,1,0:T(8,128)(2,1)S(1)}, bf16[4,2,96,640]{3,2,1,0:T(8,128)(2,1)S(1)}, u32[]{:S(2)}, u32[]{:S(2)}) collective-permute-start(bf16[4,2,96,640]{3,2,1,0:T(8,128)(2,1)S(1)} %pad_maximum_fusion.1.refs_3_), channel_id=1, source_target_pairs={{0,1},{1,0},{2,3},{3,2},{4,5},{5,4},{6,7},{7,6},{8,9},{9,8},{10,11... | collective-permute-start | bytes 2949128 | tf_op jit(solution)/shard_map/ppermute | solution.py:125
  46.6 16.2 %collective-permute-start.22 = (f32[3,512,256]{2,1,0:T(8,128)S(1)}, f32[3,512,256]{2,1,0:T(8,128)S(1)}, u32[]{:S(2)}, u32[]{:S(2)}) collective-permute-start(f32[3,512,256]{2,1,0:T(8,128)S(1)} %copy-done.2), channel_id=1, source_target_pairs={{0,1},{1,0},{2,3},{3,2},{4,5},{5,4},{6,7},{7,6},{8,9},{9,8},{10,11... | collective-permute-start | bytes 4718600 | tf_op jit(solution)/shard_map/ppermute | solution.py:125
  47.1 4.9 %collective-permute-start.15 = (bf16[80,640]{1,0:T(8,128)(2,1)S(1)}, bf16[80,640]{1,0:T(8,128)(2,1)S(1)}, u32[]{:S(2)}, u32[]{:S(2)}) collective-permute-start(bf16[80,640]{1,0:T(8,128)(2,1)S(1)} %slice_bitcast_fusion.2), channel_id=1, source_target_pairs={{0,4},{2,6},{4,0},{6,2},{8,12},{10,14},{12,8},{14,10},{16,20},{18,... | collective-permute-start | bytes 307208 | tf_op jit(solution)/shard_map/ppermute | solution.py:121
  47.5 4.7 %collective-permute-start.13 = (bf16[80,640]{1,0:T(8,128)(2,1)S(1)}, bf16[80,640]{1,0:T(8,128)(2,1)S(1)}, u32[]{:S(2)}, u32[]{:S(2)}) collective-permute-start(bf16[80,640]{1,0:T(8,128)(2,1)S(1)} %slice_bitcast_fusion.3), channel_id=1, source_target_pairs={{0,2},{2,0},{4,6},{6,4},{8,10},{10,8},{12,14},{14,12},{16,18},{18,... | collective-permute-start | bytes 307208 | tf_op jit(solution)/shard_map/ppermute | solution.py:121
  52.3 2.3 %copy-start.3 = (bf16[2,512,512]{2,1,0:T(8,128)(2,1)S(1)}, bf16[2,512,512]{2,1,0:T(8,128)(2,1)}, u32[]{:S(2)}) copy-start(bf16[2,512,512]{2,1,0:T(8,128)(2,1)} %refs_3_.3) | copy-start | bytes 3145732
  54.5 8.3 %collective-permute-start.21 = (bf16[4,2,80,640]{3,2,1,0:T(8,128)(2,1)S(1)}, bf16[4,2,80,640]{3,2,1,0:T(8,128)(2,1)S(1)}, u32[]{:S(2)}, u32[]{:S(2)}) collective-permute-start(bf16[4,2,80,640]{3,2,1,0:T(8,128)(2,1)S(1)} %pad_maximum_fusion.2.refs_1_), channel_id=1, source_target_pairs={{0,1},{1,0},{2,3},{3,2},{4,5},{5,4},{6,7},{7,6},{8,9},{9,8},{10,11... | collective-permute-start | bytes 2457608 | tf_op jit(solution)/shard_map/ppermute | solution.py:125

commit v9 on v6

--- a/solution.py
+++ b/solution.py
@@ -126,7 +126,7 @@
 
 
 def after(values, *events):
-    return lax.optimization_barrier((values, events))[0]
+    return lax.optimization_barrier((events, values))[1]
 
 
 def split2(value):
@@ -151,7 +151,7 @@
 
 
 def owner_of(row, wave, count, j, i):
-    return 4 * ((row // 4) ^ (wave * count + i)) + ((row % 4) ^ j)
+    return 4 * ((row // 4) ^ (wave * count + i)) + ((row % 4) ^ (3 - j))
 
 
 def place_kernel(dims, *refs):
@@ -233,34 +233,29 @@
 def rows_kernel(dims, skip, *refs):
     width, span = dims
     pt, z_refs, link_ref = refs[0], refs[1:3], refs[3]
-    held, z_own, z_all, tmp, sem = refs[4:12], refs[12], refs[13], refs[14], refs[15]
+    col_out, held, z_all, tmp, sem = refs[4], refs[5:13], refs[13], refs[14], refs[15]
     col, row = lax.axis_index("col"), lax.axis_index("row")
     load_rows(0, skip, span, col, row, z_refs, z_all, sem)
     row_products(pt, link_ref, z_all[...], halves(col, width // 2), held, tmp)
-    local_rows = z_own.shape[0]
-    place = row % (z_all.shape[0] // local_rows)
-    z_own[...] = z_all[pl.ds(pl.multiple_of(place * local_rows, local_rows), local_rows), :]
-
-
-def early_sums_kernel(count, *refs):
-    pt, c0h, c0l, p1h, p1l, c1h, c1l, z_own, link_ref = refs[:9]
-    s0, u1, col_out = refs[9:]
-    col, row = lax.axis_index("col"), lax.axis_index("row")
-    local_rows, half_rows = z_own.shape[0], c0h.shape[0]
-    lanes = lanes_of(row, 0, local_rows, half_rows, count)
-    s0[...] = nn2r(pt[0, :, lanes], (c0h[...], c0l[...]))
-    u1[...] = nn2r(pt[1, :, lanes], (p1h[...], p1l[...]))
     tile = col_out.shape[1]
-    place = row % (half_rows // local_rows)
-    own = pl.ds(pl.multiple_of(place * local_rows, local_rows), local_rows)
+    c0h, c0l, _, _, c1h, c1l, _, _ = held
+    place = row % (z_all.shape[0] // (2 * tile))
+    own = pl.ds(pl.multiple_of(place * 2 * tile, 2 * tile), 2 * tile)
     cols1 = (c1h[own, :], c1l[own, :])
     mine = [
         c0h[own, :].astype(f32) + c0l[own, :].astype(f32),
         cols1[0].astype(f32) + cols1[1].astype(f32),
-        -(nt(z_own[...], pt[2]) + nn2(cols1, link_ref[1])),
+        -(nt(z_all[own, :], pt[2]) + nn2(cols1, link_ref[1])),
     ]
     for s, value in enumerate(mine):
         col_out[s] = jnp.where(col == 0, value[:tile], value[tile:])
+
+
+def early_sums_kernel(count, local_rows, *refs):
+    pt, c0h, c0l, p1h, p1l, s0, u1 = refs
+    lanes = lanes_of(lax.axis_index("row"), 0, local_rows, c0h.shape[0], count)
+    s0[...] = nn2r(pt[0, :, lanes], (c0h[...], c0l[...]))
+    u1[...] = nn2r(pt[1, :, lanes], (p1h[...], p1l[...]))
 
 
 def late_sums_kernel(count, local_rows, *refs):
@@ -344,20 +339,21 @@
     f_own = jnp.transpose(factor_cols, (0, 2, 1)).reshape(supers * part, span)
     f_late = [line(f_own, k) for k in range(count, outer)]
     own = jnp.concatenate([f_own, inverse_block], axis=0)
+    own_again = jnp.concatenate(lax.optimization_barrier([f_own, inverse_block]), axis=0)
     early = []
     for k in range(count):
-        value = own if k == 0 else line(own, k)
+        value = own if k == 0 else line(own_again, k)
         value = after(value, *early[-1][1:3]) if k else value
         over_x, over_y = x(value), y(value)
         early.append([value, over_x, over_y, far(over_x, over_y, k)])
-    first = jnp.stack([jnp.stack([p[j] for p in early]) for j in range(4)])
+    first = jnp.stack([jnp.stack([p[j] for p in early]) for j in (3, 2, 1, 0)])
     first_other = across(first)
     block = after(inverse_block, *f_late, *early[-1][1:3])
     z_late = [line(block, k) for k in range(count, outer)]
     f_b, f_bx, f_by = late_wave(f_late, *early[-1][1:3], early[0][3])
     f_bx, f_by = after((f_bx, f_by), *z_late)
     f_far = jnp.stack([far(f_bx[i], f_by[i], i) for i in range(count)])
-    f_last = jnp.stack([f_b, f_bx, f_by, f_far])
+    f_last = jnp.stack([f_far, f_by, f_bx, f_b])
     f_last_other = across(f_last)
     z_b, z_bx, z_by = late_wave(z_late, f_bx, f_by)
     diag_other = across(diag_inverse)
@@ -374,10 +370,10 @@
     half_rows, half_w = rows // 2, width // 2
     held_shapes = [(half_rows, width)] * 6 + [(half_rows, half_w)] * 2
     work = [pltpu.VMEM((half_rows, 2 * span), bf16), pltpu.VMEM((half_rows, width), f32), pltpu.SemaphoreType.DMA]
-    *held, z_own = call(
+    columns, *held = call(
         functools.partial(rows_kernel, dims, supers * part),
         "own_half_rows", 4 * 10**9,
-        out_shape=tuple(shape(v, bf16) for v in held_shapes) + (shape((local_rows, 2 * span), bf16),),
+        out_shape=(shape((supers, local_rows // 2, width), f32),) + tuple(shape(v, bf16) for v in held_shapes),
         in_specs=[vmem] + [any_spec] * 2 + [vmem],
         out_specs=(vmem,) * 9,
         scratch_shapes=work,
@@ -385,15 +381,15 @@
     z_bx, z_by, *held = after((z_bx, z_by, *held), held[0])
     z_far = jnp.stack([far(z_bx[i], z_by[i], i) for i in range(count)])
     c0h, c0l, p1h, p1l, c1h, c1l, c2h, c2l = held
-    s0, u1, columns = call(
-        functools.partial(early_sums_kernel, count),
-        "early_sums", 3 * 10**9,
-        out_shape=(shape((width, width), f32),) * 2 + (shape((supers, local_rows // 2, width), f32),),
-        in_specs=[vmem] * 9,
-        out_specs=(vmem,) * 3,
-    )(pt, c0h, c0l, p1h, p1l, c1h, c1l, z_own, coupling)
+    s0, u1 = call(
+        functools.partial(early_sums_kernel, count, local_rows),
+        "early_sums", 2 * 10**9,
+        out_shape=(shape((width, width), f32),) * 2,
+        in_specs=[vmem] * 5,
+        out_specs=(vmem,) * 2,
+    )(pt, c0h, c0l, p1h, p1l)
     z_far, c1h = after((z_far, c1h), s0)
-    z_last = jnp.stack([z_b, z_bx, z_by, z_far])
+    z_last = jnp.stack([z_far, z_by, z_bx, z_b])
     z_last_other = across(z_last)
     s1, n2, s2 = call(
         functools.partial(late_sums_kernel, count, local_rows),

time: 75.3 us -> 73.6 us (0.977)
  starting transfers between devices: 27.3 us -> 24.6 us
  waiting for transfers between devices: 21.7 us -> 22.9 us
  Pallas kernels: 23.1 us -> 22 us
  other arithmetic: 1.88 us -> 2.85 us
    ppermute x19, starting transfers between devices: 26.6 us -> 23.9 us  [swap(): return lax.ppermute(value, axis, [(i, i ^ bit) for i in range(parts)])]
    pallas_call x1, Pallas kernels: 3.02 us -> 1.78 us  [replicated_plan(): call(functools.partial(early_sums_kernel, count, local_rows), 'early_sums...]
    ppermute x19, waiting for transfers between devices: 21.1 us -> 22.4 us  [swap(): return lax.ppermute(value, axis, [(i, i ^ bit) for i in range(parts)])]
    concatenate x0 -> x1, other arithmetic: none -> 1.01 us  [replicated_plan(): jnp.concatenate(lax.optimization_barrier([f_own, inverse_block]), axis=0)]
  transfers between devices with their start and end apart: 23 -> 23, of which waited for: 10 -> 11; matrix products, arithmetic and copies ran while one was open for 1% -> 3% of each run, Pallas kernels for 16% -> 15%
where the time goes in v9:
time: 73.6 us; the launch traced here: 73.4 us
  starting transfers between devices  24.6 us (33%)
  waiting for transfers between devices  22.9 us (31%)
  Pallas kernels  22 us (30%)
  other arithmetic  2.85 us (4%)
  between operations  1.06 us (1%)
    ppermute x19, starting transfers between devices, swap(): return lax.ppermute(value, axis, [(i, i ^ bit) for i in range(parts)])  23.9 us
    ppermute x19, waiting for transfers between devices, swap(): return lax.ppermute(value, axis, [(i, i ^ bit) for i in range(parts)])  22.4 us
    pallas_call x1, Pallas kernels, replicated_plan(): call(functools.partial(last_kernel, dims, rows), 'other_half', 12 * 10 **...  11.3 us
    pallas_call x1, Pallas kernels, replicated_plan(): call(functools.partial(rows_kernel, dims, supers * part), 'own_half_rows'...  5.03 us
    pallas_call x1, Pallas kernels, replicated_plan(): call(functools.partial(place_kernel, (supers, width, rows, span, part)),...  2.11 us
    pallas_call x1, Pallas kernels, replicated_plan(): call(functools.partial(late_sums_kernel, count, local_rows), 'late_sums',...  1.8 us
    pallas_call x1, Pallas kernels, replicated_plan(): call(functools.partial(early_sums_kernel, count, local_rows), 'early_sums...  1.78 us
  transfers between devices with their start and end apart: 23, of which 11 were waited for; matrix products, arithmetic and copies ran while one was open for 3% of the time, Pallas kernels for 15%

profile of v9, /device:TPU:0, one launch (start us, length us, event | category | flops | bytes accessed | tf_op | source)
XLA Modules:
  0.0 73.4 jit_solution(8742486171620895220)
XLA Ops:
  0.6 0.0 copy-start.4
  0.6 1.0 %pad_maximum_fusion.5 = bf16[176,640]{1,0:T(8,128)(2,1)S(1)} fusion(bf16[80,640]{1,0:T(8,128)(2,1)} %param.6, bf16[96,640]{1,0:T(8,128)(2,1)} %bitcast.50), kind=kLoop, calls=%fused_computation.10 | loop fusion | flops 450560 | bytes 450560 | tf_op jit(solution)/shard_map/concatenate | solution.py:342
  1.6 3.1 %collective-permute-start.3 = (bf16[176,640]{1,0:T(8,128)(2,1)S(1)}, bf16[176,640]{1,0:T(8,128)(2,1)S(1)}, u32[]{:S(2)}, u32[]{:S(2)}) collective-permute-start(bf16[176,640]{1,0:T(8,128)(2,1)S(1)} %pad_maximum_fusion.5), channel_id=1, source_target_pairs={{0,8},{2,10},{4,12},{6,14},{8,0},{10,2},{12,4},{14,6},{16,24},{18,... | collective-permute-start | bytes 675848 | tf_op jit(solution)/shard_map/ppermute | solution.py:121
  4.7 1.0 %fusion = (bf16[1,176,640]{2,1,0:T(8,128)(2,1)S(1)}, bf16[176,640]{1,0:T(8,128)(2,1)S(1)}) fusion(bf16[80,640]{1,0:T(8,128)(2,1)} %param.6, bf16[96,640]{1,0:T(8,128)(2,1)} %bitcast.51), kind=kLoop, calls=%fused_computation.17 | loop fusion | flops 450560 | bytes 675840 | tf_op jit(solution)/shard_map/stack | solution.py:349
  5.7 1.6 %collective-permute-start = (bf16[176,640]{1,0:T(8,128)(2,1)S(1)}, bf16[176,640]{1,0:T(8,128)(2,1)S(1)}, u32[]{:S(2)}, u32[]{:S(2)}) collective-permute-start(bf16[176,640]{1,0:T(8,128)(2,1)S(1)} %get-tuple-element.71), channel_id=1, source_target_pairs={{0,4},{2,6},{4,0},{6,2},{8,12},{10,14},{12,8},{14,10},{16,20},{18,... | collective-permute-start | bytes 675848 | tf_op jit(solution)/shard_map/ppermute | solution.py:121
  7.3 1.5 %collective-permute-start.2 = (bf16[176,640]{1,0:T(8,128)(2,1)S(1)}, bf16[176,640]{1,0:T(8,128)(2,1)S(1)}, u32[]{:S(2)}, u32[]{:S(2)}) collective-permute-start(bf16[176,640]{1,0:T(8,128)(2,1)S(1)} %get-tuple-element.71), channel_id=1, source_target_pairs={{0,2},{2,0},{4,6},{6,4},{8,10},{10,8},{12,14},{14,12},{16,18},{18,... | collective-permute-start | bytes 675848 | tf_op jit(solution)/shard_map/ppermute | solution.py:121
  8.8 2.6 %collective-permute-start.7 = (bf16[96,640]{1,0:T(8,128)(2,1)}, bf16[96,640]{1,0:T(8,128)(2,1)S(1)}, u32[]{:S(2)}, u32[]{:S(2)}) collective-permute-start(bf16[96,640]{1,0:T(8,128)(2,1)} %bitcast.52), channel_id=1, source_target_pairs={{0,16},{2,18},{4,20},{6,22},{8,24},{10,26},{12,28},{14,30},{16,0},... | collective-permute-start | bytes 368648 | tf_op jit(solution)/shard_map/ppermute | solution.py:121
  11.4 0.2 collective-permute-start.8
  11.6 1.1 %collective-permute-done = bf16[176,640]{1,0:T(8,128)(2,1)S(1)} collective-permute-done((bf16[176,640]{1,0:T(8,128)(2,1)S(1)}, bf16[176,640]{1,0:T(8,128)(2,1)S(1)}, u32[]{:S(2)}, u32[]{:S(2)}) %collective-permute-start) | collective-permute-done | bytes 225312 | tf_op jit(solution)/shard_map/ppermute | solution.py:121
  12.8 1.2 %collective-permute-done.2 = bf16[176,640]{1,0:T(8,128)(2,1)S(1)} collective-permute-done((bf16[176,640]{1,0:T(8,128)(2,1)S(1)}, bf16[176,640]{1,0:T(8,128)(2,1)S(1)}, u32[]{:S(2)}, u32[]{:S(2)}) %collective-permute-start.2) | collective-permute-done | bytes 225312 | tf_op jit(solution)/shard_map/ppermute | solution.py:121
  14.0 1.5 %collective-permute-start.4 = (bf16[176,640]{1,0:T(8,128)(2,1)S(1)}, bf16[176,640]{1,0:T(8,128)(2,1)S(1)}, u32[]{:S(2)}, u32[]{:S(2)}) collective-permute-start(bf16[176,640]{1,0:T(8,128)(2,1)S(1)} %collective-permute-done.3), channel_id=1, source_target_pairs={{0,2},{2,0},{4,6},{6,4},{8,10},{10,8},{12,14},{14,12},{16,18},{18,... | collective-permute-start | bytes 675848 | tf_op jit(solution)/shard_map/ppermute | solution.py:121
  15.5 0.5 collective-permute-start.6
  16.0 0.5 collective-permute-start.1
  16.5 3.9 %collective-permute-done.7 = bf16[96,640]{1,0:T(8,128)(2,1)S(1)} collective-permute-done((bf16[96,640]{1,0:T(8,128)(2,1)}, bf16[96,640]{1,0:T(8,128)(2,1)S(1)}, u32[]{:S(2)}, u32[]{:S(2)}) %collective-permute-start.7) | collective-permute-done | bytes 122912 | tf_op jit(solution)/shard_map/ppermute | solution.py:121
  20.5 0.1 maximum_bitcast_fusion.3
  20.5 1.7 %collective-permute-done.4 = bf16[176,640]{1,0:T(8,128)(2,1)S(1)} collective-permute-done((bf16[176,640]{1,0:T(8,128)(2,1)S(1)}, bf16[176,640]{1,0:T(8,128)(2,1)S(1)}, u32[]{:S(2)}, u32[]{:S(2)}) %collective-permute-start.4) | collective-permute-done | bytes 225312 | tf_op jit(solution)/shard_map/ppermute | solution.py:121
  22.2 2.4 %collective-permute-done.1 = bf16[176,640]{1,0:T(8,128)(2,1)S(1)} collective-permute-done((bf16[176,640]{1,0:T(8,128)(2,1)S(1)}, bf16[176,640]{1,0:T(8,128)(2,1)S(1)}, u32[]{:S(2)}, u32[]{:S(2)}) %collective-permute-start.1) | collective-permute-done | bytes 225312 | tf_op jit(solution)/shard_map/ppermute | solution.py:121
  24.6 1.5 %collective-permute-start.11 = (bf16[2,96,640]{2,1,0:T(8,128)(2,1)S(1)}, bf16[2,96,640]{2,1,0:T(8,128)(2,1)S(1)}, u32[]{:S(2)}, u32[]{:S(2)}) collective-permute-start(bf16[2,96,640]{2,1,0:T(8,128)(2,1)S(1)} %pad_maximum_fusion.3), channel_id=1, source_target_pairs={{0,2},{2,0},{4,6},{6,4},{8,10},{10,8},{12,14},{14,12},{16,18},{18,... | collective-permute-start | bytes 737288 | tf_op jit(solution)/shard_map/ppermute | solution.py:121
  26.1 0.6 collective-permute-start.12
  26.7 2.9 %collective-permute-start.10 = (bf16[80,640]{1,0:T(8,128)(2,1)S(1)}, bf16[80,640]{1,0:T(8,128)(2,1)S(1)}, u32[]{:S(2)}, u32[]{:S(2)}) collective-permute-start(bf16[80,640]{1,0:T(8,128)(2,1)S(1)} %copy-done.4), channel_id=1, source_target_pairs={{0,24},{2,26},{4,28},{6,30},{8,16},{10,18},{12,20},{14,22},{16,8},... | collective-permute-start | bytes 307208 | tf_op jit(solution)/shard_map/ppermute | solution.py:121
  29.6 1.1 %collective-permute-start.5 = (bf16[176,640]{1,0:T(8,128)(2,1)S(1)}, bf16[176,640]{1,0:T(8,128)(2,1)S(1)}, u32[]{:S(2)}, u32[]{:S(2)}) collective-permute-start(bf16[176,640]{1,0:T(8,128)(2,1)S(1)} %collective-permute-done.4), channel_id=1, source_target_pairs={{0,4},{2,6},{4,0},{6,2},{8,12},{10,14},{12,8},{14,10},{16,20},{18,... | collective-permute-start | bytes 675848 | tf_op jit(solution)/shard_map/ppermute | solution.py:121
  30.7 0.1 maximum_bitcast_fusion.1
  30.8 0.1 maximum_bitcast_fusion.2
  30.8 5.7 %collective-permute-done.5 = bf16[176,640]{1,0:T(8,128)(2,1)S(1)} collective-permute-done((bf16[176,640]{1,0:T(8,128)(2,1)S(1)}, bf16[176,640]{1,0:T(8,128)(2,1)S(1)}, u32[]{:S(2)}, u32[]{:S(2)}) %collective-permute-start.5) | collective-permute-done | bytes 225312 | tf_op jit(solution)/shard_map/ppermute | solution.py:121
  36.5 0.1 maximum_bitcast_fusion
  36.6 0.3 pad_maximum_fusion.refs_2_.refs_1_
  36.9 0.1 collective-permute-start.15
  37.0 0.3 collective-permute-start.13
  37.4 1.2 %collective-permute-start.14 = (bf16[96,640]{1,0:T(8,128)(2,1)S(1)}, bf16[96,640]{1,0:T(8,128)(2,1)S(1)}, u32[]{:S(2)}, u32[]{:S(2)}) collective-permute-start(bf16[96,640]{1,0:T(8,128)(2,1)S(1)} %slice_bitcast_fusion), channel_id=1, source_target_pairs={{0,4},{2,6},{4,0},{6,2},{8,12},{10,14},{12,8},{14,10},{16,20},{18,... | collective-permute-start | bytes 368648 | tf_op jit(solution)/shard_map/ppermute | solution.py:121
  38.6 4.2 %collective-permute-done.13 = bf16[96,640]{1,0:T(8,128)(2,1)S(1)} collective-permute-done((bf16[96,640]{1,0:T(8,128)(2,1)S(1)}, bf16[96,640]{1,0:T(8,128)(2,1)S(1)}, u32[]{:S(2)}, u32[]{:S(2)}) %collective-permute-start.13) | collective-permute-done | bytes 122912 | tf_op jit(solution)/shard_map/ppermute | solution.py:121
  42.8 0.1 collective-permute-done.14
  42.9 0.1 pad_maximum_fusion.1.refs_3_
  43.1 0.1 collective-permute-start.16
  43.2 0.5 collective-permute-start.22
  43.7 1.8 %collective-permute-start.17 = (bf16[2,80,640]{2,1,0:T(8,128)(2,1)S(1)}, bf16[2,80,640]{2,1,0:T(8,128)(2,1)S(1)}, u32[]{:S(2)}, u32[]{:S(2)}) collective-permute-start(bf16[2,80,640]{2,1,0:T(8,128)(2,1)S(1)} %pad_maximum_fusion.6), channel_id=1, source_target_pairs={{0,2},{2,0},{4,6},{6,4},{8,10},{10,8},{12,14},{14,12},{16,18},{18,... | collective-permute-start | bytes 614408 | tf_op jit(solution)/shard_map/ppermute | solution.py:121
  45.5 0.9 %collective-permute-start.18 = (bf16[2,80,640]{2,1,0:T(8,128)(2,1)S(1)}, bf16[2,80,640]{2,1,0:T(8,128)(2,1)S(1)}, u32[]{:S(2)}, u32[]{:S(2)}) collective-permute-start(bf16[2,80,640]{2,1,0:T(8,128)(2,1)S(1)} %pad_maximum_fusion.6), channel_id=1, source_target_pairs={{0,4},{2,6},{4,0},{6,2},{8,12},{10,14},{12,8},{14,10},{16,20},{18,... | collective-permute-start | bytes 614408 | tf_op jit(solution)/shard_map/ppermute | solution.py:121
  46.4 2.1 %place.1.refs_0_ = bf16[3,512,1280]{2,1,0:T(8,128)(2,1)S(1)} custom-call(s32[3,10]{1,0:T(4,128)S(1)} %copy-done, s32[3,10]{1,0:T(4,128)S(1)} %copy-done.1, bf16[4,2,176,640]{3,2,1,0:T(8,128)(2,1)S(1)} %pad_maximum_fusion.refs_2_.refs_1_, bf16[4,2,96,640]{3,2,1,0:T(8,128)(2,1)S(1)} %pad_maximum_fusion.1.refs_3_, ...), custom_call_target="tpu_custom_call" | custom-call | flops 2000000000 | bytes 8388608 | tf_op jit(solution)/shard_map/place/pallas_call | solution.py:361
  48.5 5.0 %own_half_rows.1 = (f32[3,40,512]{2,1,0:T(8,128)}, bf16[640,512]{1,0:T(8,128)(2,1)S(1)}, bf16[640,512]{1,0:T(8,128)(2,1)S(1)}, bf16[640,512]{1,0:T(8,128)(2,1)S(...) custom-call(bf16[3,512,1280]{2,1,0:T(8,128)(2,1)S(1)} %place.1.refs_, ...), custom_call_target="tpu_custom_call" | custom-call | flops 4000000000 | bytes 8388608 | tf_op jit(solution)/shard_map/own_half_rows/pallas_call | solution.py:373
  53.6 1.1 %collective-permute-start.19 = (bf16[80,640]{1,0:T(8,128)(2,1)S(1)}, bf16[80,640]{1,0:T(8,128)(2,1)S(1)}, u32[]{:S(2)}, u32[]{:S(2)}) collective-permute-start(bf16[80,640]{1,0:T(8,128)(2,1)S(1)} %slice_bitcast_fusion.3), channel_id=1, source_target_pairs={{0,2},{2,0},{4,6},{6,4},{8,10},{10,8},{12,14},{14,12},{16,18},{18,... | collective-permute-start | bytes 307208 | tf_op jit(solution)/shard_map/ppermute | solution.py:121
  54.7 0.9 %collective-permute-start.20 = (bf16[80,640]{1,0:T(8,128)(2,1)S(1)}, bf16[80,640]{1,0:T(8,128)(2,1)S(1)}, u32[]{:S(2)}, u32[]{:S(2)}) collective-permute-start(bf16[80,640]{1,0:T(8,128)(2,1)S(1)} %slice_bitcast_fusion.2), channel_id=1, source_target_pairs={{0,4},{2,6},{4,0},{6,2},{8,12},{10,14},{12,8},{14,10},{16,20},{18,... | collective-permute-start | bytes 307208 | tf_op jit(solution)/shard_map/ppermute | solution.py:121
  55.7 1.8 %early_sums.1 = (f32[512,512]{1,0:T(8,128)S(1)}, f32[512,512]{1,0:T(8,128)S(1)}) custom-call(bf16[3,512,1280]{2,1,0:T(8,128)(2,1)S(1)} %place.1.refs_0_, bf16[640,512]{1,0:T(8,128)(2,1)S(1)} %get-tuple-element.53.refs_1_, bf16[640,512]{1,0:T(8,128)(2,1)S(1)} %get-tuple-element.54.refs_2_, bf16[640,512]{1,0:T(8,128)(2,1)S(1)} %get-tuple-element.55.refs_3_, ...), custom_call_target="tpu_custom_call" | custom-call | flops 2000000000 | bytes 8388608 | tf_op jit(solution)/shard_map/early_sums/pallas_call | solution.py:384
  57.4 0.9 %collective-permute-done.19 = bf16[80,640]{1,0:T(8,128)(2,1)S(1)} collective-permute-done((bf16[80,640]{1,0:T(8,128)(2,1)S(1)}, bf16[80,640]{1,0:T(8,128)(2,1)S(1)}, u32[]{:S(2)}, u32[]{:S(2)}) %collective-permute-start.19) | collective-permute-done | bytes 102432 | tf_op jit(solution)/shard_map/ppermute | solution.py:121
  58.3 1.2 %collective-permute-done.20 = bf16[80,640]{1,0:T(8,128)(2,1)S(1)} collective-permute-done((bf16[80,640]{1,0:T(8,128)(2,1)S(1)}, bf16[80,640]{1,0:T(8,128)(2,1)S(1)}, u32[]{:S(2)}, u32[]{:S(2)}) %collective-permute-start.20) | collective-permute-done | bytes 102432 | tf_op jit(solution)/shard_map/ppermute | solution.py:121
  59.5 0.1 pad_maximum_fusion.2.refs_1_
  59.6 0.1 collective-permute-start.21
  59.7 1.8 %late_sums.1 = (f32[512,512]{1,0:T(8,128)S(1)}, f32[256,512]{1,0:T(8,128)S(1)}, f32[512,256]{1,0:T(8,128)S(1)}) custom-call(bf16[3,512,1280]{2,1,0:T(8,128)(2,1)S(1)} %place.1.refs_0_, bf16[640,512]{1,0:T(8,128)(2,1)S(1)} %get-tuple-element.63.refs_1_, bf16[640,512]{1,0:T(8,128)(2,1)S(1)} %get-tuple-element.64.refs_2_, ...), custom_call_target="tpu_custom_call" | custom-call | flops 2000000000 | bytes 8388608 | tf_op jit(solution)/shard_map/late_sums/pallas_call | solution.py:394
  61.5 0.5 collective-permute-done.21.refs_2_
  62.0 11.3 %other_half.1 = f32[3,512,256]{2,1,0:T(8,128)} custom-call(bf16[3,512,1280]{2,1,0:T(8,128)(2,1)S(1)} %place.1.refs_0_, bf16[4,2,80,640]{3,2,1,0:T(8,128)(2,1)S(1)} %pad_maximum_fusion.2.refs_1_, bf16[4,2,80,640]{3,2,1,0:T(8,128)(2,1)S(1)} %collective-permute-done.21.refs_2_, bf16[2,512,512]{2,1,0:T(8,128)(2,1)S(1)} %copy-done.3, ...), custom_call_target="tpu_custom_call" | custom-call | flops 12000000000 | bytes 8388608 | tf_op jit(solution)/shard_map/other_half/pallas_call | solution.py:402
  (30 shorter events, 0.2 us)
Async XLA Ops:
  0.6 26.1 %copy-start.4 = (bf16[80,640]{1,0:T(8,128)(2,1)S(1)}, bf16[80,640]{1,0:T(8,128)(2,1)}, u32[]{:S(2)}) copy-start(bf16[80,640]{1,0:T(8,128)(2,1)} %param.6) | copy-start | bytes 307204
  1.6 10.0 %collective-permute-start.3 = (bf16[176,640]{1,0:T(8,128)(2,1)S(1)}, bf16[176,640]{1,0:T(8,128)(2,1)S(1)}, u32[]{:S(2)}, u32[]{:S(2)}) collective-permute-start(bf16[176,640]{1,0:T(8,128)(2,1)S(1)} %pad_maximum_fusion.5), channel_id=1, source_target_pairs={{0,8},{2,10},{4,12},{6,14},{8,0},{10,2},{12,4},{14,6},{16,24},{18,... | collective-permute-start | bytes 675848 | tf_op jit(solution)/shard_map/ppermute | solution.py:121
  5.7 7.0 %collective-permute-start = (bf16[176,640]{1,0:T(8,128)(2,1)S(1)}, bf16[176,640]{1,0:T(8,128)(2,1)S(1)}, u32[]{:S(2)}, u32[]{:S(2)}) collective-permute-start(bf16[176,640]{1,0:T(8,128)(2,1)S(1)} %get-tuple-element.71), channel_id=1, source_target_pairs={{0,4},{2,6},{4,0},{6,2},{8,12},{10,14},{12,8},{14,10},{16,20},{18,... | collective-permute-start | bytes 675848 | tf_op jit(solution)/shard_map/ppermute | solution.py:121
  7.3 6.7 %collective-permute-start.2 = (bf16[176,640]{1,0:T(8,128)(2,1)S(1)}, bf16[176,640]{1,0:T(8,128)(2,1)S(1)}, u32[]{:S(2)}, u32[]{:S(2)}) collective-permute-start(bf16[176,640]{1,0:T(8,128)(2,1)S(1)} %get-tuple-element.71), channel_id=1, source_target_pairs={{0,2},{2,0},{4,6},{6,4},{8,10},{10,8},{12,14},{14,12},{16,18},{18,... | collective-permute-start | bytes 675848 | tf_op jit(solution)/shard_map/ppermute | solution.py:121
  8.8 11.6 %collective-permute-start.7 = (bf16[96,640]{1,0:T(8,128)(2,1)}, bf16[96,640]{1,0:T(8,128)(2,1)S(1)}, u32[]{:S(2)}, u32[]{:S(2)}) collective-permute-start(bf16[96,640]{1,0:T(8,128)(2,1)} %bitcast.52), channel_id=1, source_target_pairs={{0,16},{2,18},{4,20},{6,22},{8,24},{10,26},{12,28},{14,30},{16,0},... | collective-permute-start | bytes 368648 | tf_op jit(solution)/shard_map/ppermute | solution.py:121
  11.4 9.1 %collective-permute-start.8 = (bf16[96,640]{1,0:T(8,128)(2,1)}, bf16[96,640]{1,0:T(8,128)(2,1)S(1)}, u32[]{:S(2)}, u32[]{:S(2)}) collective-permute-start(bf16[96,640]{1,0:T(8,128)(2,1)} %bitcast.53), channel_id=1, source_target_pairs={{0,24},{2,26},{4,28},{6,30},{8,16},{10,18},{12,20},{14,22},{16,8},... | collective-permute-start | bytes 368648 | tf_op jit(solution)/shard_map/ppermute | solution.py:121
  14.0 8.2 %collective-permute-start.4 = (bf16[176,640]{1,0:T(8,128)(2,1)S(1)}, bf16[176,640]{1,0:T(8,128)(2,1)S(1)}, u32[]{:S(2)}, u32[]{:S(2)}) collective-permute-start(bf16[176,640]{1,0:T(8,128)(2,1)S(1)} %collective-permute-done.3), channel_id=1, source_target_pairs={{0,2},{2,0},{4,6},{6,4},{8,10},{10,8},{12,14},{14,12},{16,18},{18,... | collective-permute-start | bytes 675848 | tf_op jit(solution)/shard_map/ppermute | solution.py:121
  15.5 6.7 %collective-permute-start.6 = (bf16[176,640]{1,0:T(8,128)(2,1)S(1)}, bf16[176,640]{1,0:T(8,128)(2,1)S(1)}, u32[]{:S(2)}, u32[]{:S(2)}) collective-permute-start(bf16[176,640]{1,0:T(8,128)(2,1)S(1)} %collective-permute-done.3), channel_id=1, source_target_pairs={{0,4},{2,6},{4,0},{6,2},{8,12},{10,14},{12,8},{14,10},{16,20},{18,... | collective-permute-start | bytes 675848 | tf_op jit(solution)/shard_map/ppermute | solution.py:121
  16.0 8.6 %collective-permute-start.1 = (bf16[176,640]{1,0:T(8,128)(2,1)S(1)}, bf16[176,640]{1,0:T(8,128)(2,1)S(1)}, u32[]{:S(2)}, u32[]{:S(2)}) collective-permute-start(bf16[176,640]{1,0:T(8,128)(2,1)S(1)} %collective-permute-done), channel_id=1, source_target_pairs={{0,2},{2,0},{4,6},{6,4},{8,10},{10,8},{12,14},{14,12},{16,18},{18,... | collective-permute-start | bytes 675848 | tf_op jit(solution)/shard_map/ppermute | solution.py:121
  24.6 12.4 %collective-permute-start.11 = (bf16[2,96,640]{2,1,0:T(8,128)(2,1)S(1)}, bf16[2,96,640]{2,1,0:T(8,128)(2,1)S(1)}, u32[]{:S(2)}, u32[]{:S(2)}) collective-permute-start(bf16[2,96,640]{2,1,0:T(8,128)(2,1)S(1)} %pad_maximum_fusion.3), channel_id=1, source_target_pairs={{0,2},{2,0},{4,6},{6,4},{8,10},{10,8},{12,14},{14,12},{16,18},{18,... | collective-permute-start | bytes 737288 | tf_op jit(solution)/shard_map/ppermute | solution.py:121
  26.1 10.9 %collective-permute-start.12 = (bf16[2,96,640]{2,1,0:T(8,128)(2,1)S(1)}, bf16[2,96,640]{2,1,0:T(8,128)(2,1)S(1)}, u32[]{:S(2)}, u32[]{:S(2)}) collective-permute-start(bf16[2,96,640]{2,1,0:T(8,128)(2,1)S(1)} %pad_maximum_fusion.3), channel_id=1, source_target_pairs={{0,4},{2,6},{4,0},{6,2},{8,12},{10,14},{12,8},{14,10},{16,20},{18,... | collective-permute-start | bytes 737288 | tf_op jit(solution)/shard_map/ppermute | solution.py:121
  26.7 10.3 %collective-permute-start.10 = (bf16[80,640]{1,0:T(8,128)(2,1)S(1)}, bf16[80,640]{1,0:T(8,128)(2,1)S(1)}, u32[]{:S(2)}, u32[]{:S(2)}) collective-permute-start(bf16[80,640]{1,0:T(8,128)(2,1)S(1)} %copy-done.4), channel_id=1, source_target_pairs={{0,24},{2,26},{4,28},{6,30},{8,16},{10,18},{12,20},{14,22},{16,8},... | collective-permute-start | bytes 307208 | tf_op jit(solution)/shard_map/ppermute | solution.py:121
  29.6 7.4 %collective-permute-start.9 = (bf16[80,640]{1,0:T(8,128)(2,1)S(1)}, bf16[80,640]{1,0:T(8,128)(2,1)S(1)}, u32[]{:S(2)}, u32[]{:S(2)}) collective-permute-start(bf16[80,640]{1,0:T(8,128)(2,1)S(1)} %copy-done.4), channel_id=1, source_target_pairs={{0,16},{2,18},{4,20},{6,22},{8,24},{10,26},{12,28},{14,30},{16,0},... | collective-permute-start | bytes 307208 | tf_op jit(solution)/shard_map/ppermute | solution.py:121
  29.6 6.9 %collective-permute-start.5 = (bf16[176,640]{1,0:T(8,128)(2,1)S(1)}, bf16[176,640]{1,0:T(8,128)(2,1)S(1)}, u32[]{:S(2)}, u32[]{:S(2)}) collective-permute-start(bf16[176,640]{1,0:T(8,128)(2,1)S(1)} %collective-permute-done.4), channel_id=1, source_target_pairs={{0,4},{2,6},{4,0},{6,2},{8,12},{10,14},{12,8},{14,10},{16,20},{18,... | collective-permute-start | bytes 675848 | tf_op jit(solution)/shard_map/ppermute | solution.py:121
  36.8 6.3 %copy-start.2 = (f32[3,512,256]{2,1,0:T(8,128)S(1)}, f32[3,512,256]{2,1,0:T(8,128)}, u32[]{:S(2)}) copy-start(f32[3,512,256]{2,1,0:T(8,128)} %refs_4_.1) | copy-start | bytes 4718596
  36.8 9.5 %copy-start = (s32[3,10]{1,0:T(4,128)S(1)}, s32[3,10]{1,0:T(4,128)}, u32[]{:S(2)}) copy-start(s32[3,10]{1,0:T(4,128)} %refs_0_.1) | copy-start | bytes 364
  36.9 9.5 %copy-start.1 = (s32[3,10]{1,0:T(4,128)S(1)}, s32[3,10]{1,0:T(4,128)}, u32[]{:S(2)}) copy-start(s32[3,10]{1,0:T(4,128)} %refs_1_.1) | copy-start | bytes 364
  36.9 9.5 %collective-permute-start.15 = (bf16[4,2,176,640]{3,2,1,0:T(8,128)(2,1)S(1)}, bf16[4,2,176,640]{3,2,1,0:T(8,128)(2,1)S(1)}, u32[]{:S(2)}, u32[]{:S(2)}) collective-permute-start(bf16[4,2,176,640]{3,2,1,0:T(8,128)(2,1)S(1)} %pad_maximum_fusion.refs_2_.refs_1_), channel_id=1, source_target_pairs={{0,1},{1,0},{2,3},{3,2},{4,5},{5,4},{6,7},{7,6},{8,9},{9,8},{10,11... | collective-permute-start | bytes 5406728 | tf_op jit(solution)/shard_map/ppermute | solution.py:125
  37.0 5.8 %collective-permute-start.13 = (bf16[96,640]{1,0:T(8,128)(2,1)S(1)}, bf16[96,640]{1,0:T(8,128)(2,1)S(1)}, u32[]{:S(2)}, u32[]{:S(2)}) collective-permute-start(bf16[96,640]{1,0:T(8,128)(2,1)S(1)} %slice_bitcast_fusion.1), channel_id=1, source_target_pairs={{0,2},{2,0},{4,6},{6,4},{8,10},{10,8},{12,14},{14,12},{16,18},{18,... | collective-permute-start | bytes 368648 | tf_op jit(solution)/shard_map/ppermute | solution.py:121
  37.4 5.5 %collective-permute-start.14 = (bf16[96,640]{1,0:T(8,128)(2,1)S(1)}, bf16[96,640]{1,0:T(8,128)(2,1)S(1)}, u32[]{:S(2)}, u32[]{:S(2)}) collective-permute-start(bf16[96,640]{1,0:T(8,128)(2,1)S(1)} %slice_bitcast_fusion), channel_id=1, source_target_pairs={{0,4},{2,6},{4,0},{6,2},{8,12},{10,14},{12,8},{14,10},{16,20},{18,... | collective-permute-start | bytes 368648 | tf_op jit(solution)/shard_map/ppermute | solution.py:121
  43.1 3.3 %collective-permute-start.16 = (bf16[4,2,96,640]{3,2,1,0:T(8,128)(2,1)S(1)}, bf16[4,2,96,640]{3,2,1,0:T(8,128)(2,1)S(1)}, u32[]{:S(2)}, u32[]{:S(2)}) collective-permute-start(bf16[4,2,96,640]{3,2,1,0:T(8,128)(2,1)S(1)} %pad_maximum_fusion.1.refs_3_), channel_id=1, source_target_pairs={{0,1},{1,0},{2,3},{3,2},{4,5},{5,4},{6,7},{7,6},{8,9},{9,8},{10,11... | collective-permute-start | bytes 2949128 | tf_op jit(solution)/shard_map/ppermute | solution.py:125
  43.2 18.3 %collective-permute-start.22 = (f32[3,512,256]{2,1,0:T(8,128)S(1)}, f32[3,512,256]{2,1,0:T(8,128)S(1)}, u32[]{:S(2)}, u32[]{:S(2)}) collective-permute-start(f32[3,512,256]{2,1,0:T(8,128)S(1)} %copy-done.2), channel_id=1, source_target_pairs={{0,1},{1,0},{2,3},{3,2},{4,5},{5,4},{6,7},{7,6},{8,9},{9,8},{10,11... | collective-permute-start | bytes 4718600 | tf_op jit(solution)/shard_map/ppermute | solution.py:125
  43.7 4.8 %copy-start.3 = (bf16[2,512,512]{2,1,0:T(8,128)(2,1)S(1)}, bf16[2,512,512]{2,1,0:T(8,128)(2,1)}, u32[]{:S(2)}) copy-start(bf16[2,512,512]{2,1,0:T(8,128)(2,1)} %refs_3_.3) | copy-start | bytes 3145732
  43.7 9.8 %collective-permute-start.17 = (bf16[2,80,640]{2,1,0:T(8,128)(2,1)S(1)}, bf16[2,80,640]{2,1,0:T(8,128)(2,1)S(1)}, u32[]{:S(2)}, u32[]{:S(2)}) collective-permute-start(bf16[2,80,640]{2,1,0:T(8,128)(2,1)S(1)} %pad_maximum_fusion.6), channel_id=1, source_target_pairs={{0,2},{2,0},{4,6},{6,4},{8,10},{10,8},{12,14},{14,12},{16,18},{18,... | collective-permute-start | bytes 614408 | tf_op jit(solution)/shard_map/ppermute | solution.py:121
  45.5 8.1 %collective-permute-start.18 = (bf16[2,80,640]{2,1,0:T(8,128)(2,1)S(1)}, bf16[2,80,640]{2,1,0:T(8,128)(2,1)S(1)}, u32[]{:S(2)}, u32[]{:S(2)}) collective-permute-start(bf16[2,80,640]{2,1,0:T(8,128)(2,1)S(1)} %pad_maximum_fusion.6), channel_id=1, source_target_pairs={{0,4},{2,6},{4,0},{6,2},{8,12},{10,14},{12,8},{14,10},{16,20},{18,... | collective-permute-start | bytes 614408 | tf_op jit(solution)/shard_map/ppermute | solution.py:121
  53.6 4.7 %collective-permute-start.19 = (bf16[80,640]{1,0:T(8,128)(2,1)S(1)}, bf16[80,640]{1,0:T(8,128)(2,1)S(1)}, u32[]{:S(2)}, u32[]{:S(2)}) collective-permute-start(bf16[80,640]{1,0:T(8,128)(2,1)S(1)} %slice_bitcast_fusion.3), channel_id=1, source_target_pairs={{0,2},{2,0},{4,6},{6,4},{8,10},{10,8},{12,14},{14,12},{16,18},{18,... | collective-permute-start | bytes 307208 | tf_op jit(solution)/shard_map/ppermute | solution.py:121
  54.7 4.7 %collective-permute-start.20 = (bf16[80,640]{1,0:T(8,128)(2,1)S(1)}, bf16[80,640]{1,0:T(8,128)(2,1)S(1)}, u32[]{:S(2)}, u32[]{:S(2)}) collective-permute-start(bf16[80,640]{1,0:T(8,128)(2,1)S(1)} %slice_bitcast_fusion.2), channel_id=1, source_target_pairs={{0,4},{2,6},{4,0},{6,2},{8,12},{10,14},{12,8},{14,10},{16,20},{18,... | collective-permute-start | bytes 307208 | tf_op jit(solution)/shard_map/ppermute | solution.py:121
  59.6 2.4 %collective-permute-start.21 = (bf16[4,2,80,640]{3,2,1,0:T(8,128)(2,1)S(1)}, bf16[4,2,80,640]{3,2,1,0:T(8,128)(2,1)S(1)}, u32[]{:S(2)}, u32[]{:S(2)}) collective-permute-start(bf16[4,2,80,640]{3,2,1,0:T(8,128)(2,1)S(1)} %pad_maximum_fusion.2.refs_1_), channel_id=1, source_target_pairs={{0,1},{1,0},{2,3},{3,2},{4,5},{5,4},{6,7},{7,6},{8,9},{9,8},{10,11... | collective-permute-start | bytes 2457608 | tf_op jit(solution)/shard_map/ppermute | solution.py:125

commit v10 on v9

--- a/solution.py
+++ b/solution.py
@@ -226,6 +226,8 @@
     tmp[...] += nt(zm, pt[1])
     cols1 = split2(-tmp[...])
     c1h[...], c1l[...] = cols1
+    if c2h is None:
+        return
     cols2 = -(nt(zm, pt[2, c_rows, :]) + nn2(cols1, link_ref[1, :, c_rows]))
     c2h[...], c2l[...] = split2(cols2)
 
@@ -233,12 +235,21 @@
 def rows_kernel(dims, skip, *refs):
     width, span = dims
     pt, z_refs, link_ref = refs[0], refs[1:3], refs[3]
-    col_out, held, z_all, tmp, sem = refs[4], refs[5:13], refs[13], refs[14], refs[15]
+    z_all, held, tmp, sem = refs[4], refs[5:11], refs[11], refs[12]
     col, row = lax.axis_index("col"), lax.axis_index("row")
     load_rows(0, skip, span, col, row, z_refs, z_all, sem)
-    row_products(pt, link_ref, z_all[...], halves(col, width // 2), held, tmp)
+    row_products(pt, link_ref, z_all[...], None, (*held, None, None), tmp)
+
+
+def last_rows_kernel(*refs):
+    pt, z_all, c0h, c0l, c1h, c1l, link_ref = refs[:7]
+    col_out, c2h, c2l = refs[7:]
+    col, row = lax.axis_index("col"), lax.axis_index("row")
+    c_rows = halves(col, c2h.shape[1])
+    cols1 = (c1h[...], c1l[...])
+    cols2 = -(nt(z_all[...], pt[2, c_rows, :]) + nn2(cols1, link_ref[1, :, c_rows]))
+    c2h[...], c2l[...] = split2(cols2)
     tile = col_out.shape[1]
-    c0h, c0l, _, _, c1h, c1l, _, _ = held
     place = row % (z_all.shape[0] // (2 * tile))
     own = pl.ds(pl.multiple_of(place * 2 * tile, 2 * tile), 2 * tile)
     cols1 = (c1h[own, :], c1l[own, :])
@@ -370,17 +381,25 @@
     half_rows, half_w = rows // 2, width // 2
     held_shapes = [(half_rows, width)] * 6 + [(half_rows, half_w)] * 2
     work = [pltpu.VMEM((half_rows, 2 * span), bf16), pltpu.VMEM((half_rows, width), f32), pltpu.SemaphoreType.DMA]
-    columns, *held = call(
+    z_held, *held = call(
         functools.partial(rows_kernel, dims, supers * part),
-        "own_half_rows", 4 * 10**9,
-        out_shape=(shape((supers, local_rows // 2, width), f32),) + tuple(shape(v, bf16) for v in held_shapes),
+        "own_half_rows", 3 * 10**9,
+        out_shape=tuple(shape(v, bf16) for v in [(half_rows, 2 * span)] + held_shapes[:6]),
         in_specs=[vmem] + [any_spec] * 2 + [vmem],
-        out_specs=(vmem,) * 9,
-        scratch_shapes=work,
+        out_specs=(vmem,) * 7,
+        scratch_shapes=work[1:],
     )(pt, first, first_other, coupling)
     z_bx, z_by, *held = after((z_bx, z_by, *held), held[0])
     z_far = jnp.stack([far(z_bx[i], z_by[i], i) for i in range(count)])
-    c0h, c0l, p1h, p1l, c1h, c1l, c2h, c2l = held
+    c0h, c0l, p1h, p1l, c1h, c1l = held
+    columns, c2h, c2l = call(
+        last_rows_kernel,
+        "last_rows", 2 * 10**9,
+        out_shape=(shape((supers, local_rows // 2, width), f32),) + (shape((half_rows, half_w), bf16),) * 2,
+        in_specs=[vmem] * 7,
+        out_specs=(vmem,) * 3,
+    )(pt, z_held, c0h, c0l, c1h, c1l, coupling)
+    z_far, c0h = after((z_far, c0h), c2h)
     s0, u1 = call(
         functools.partial(early_sums_kernel, count, local_rows),
         "early_sums", 2 * 10**9,
@@ -388,7 +407,6 @@
         in_specs=[vmem] * 5,
         out_specs=(vmem,) * 2,
     )(pt, c0h, c0l, p1h, p1l)
-    z_far, c1h = after((z_far, c1h), s0)
     z_last = jnp.stack([z_far, z_by, z_bx, z_b])
     z_last_other = across(z_last)
     s1, n2, s2 = call(

time: 73.6 us -> 72.9 us (level)
    pallas_call x0 -> x1, Pallas kernels: none -> 2.13 us  [replicated_plan(): call(last_rows_kernel, 'last_rows', 2 * 10 ** 9, out_shape=(shape((supers...]
    pallas_call x1, Pallas kernels: 5.03 us -> 2.96 us  [replicated_plan(): call(functools.partial(rows_kernel, dims, supers * part), 'own_half_rows'...]
where the time goes in v10:
time: 72.9 us; the launch traced here: 72.7 us
  starting transfers between devices  24 us (33%)
  waiting for transfers between devices  22.7 us (31%)
  Pallas kernels  22 us (30%)
  other arithmetic  2.85 us (4%)
  between operations  1.06 us (1%)
    ppermute x19, starting transfers between devices, swap(): return lax.ppermute(value, axis, [(i, i ^ bit) for i in range(parts)])  23.3 us
    ppermute x19, waiting for transfers between devices, swap(): return lax.ppermute(value, axis, [(i, i ^ bit) for i in range(parts)])  22.6 us
    pallas_call x1, Pallas kernels, replicated_plan(): call(functools.partial(last_kernel, dims, rows), 'other_half', 12 * 10 **...  11.2 us
    pallas_call x1, Pallas kernels, replicated_plan(): call(functools.partial(rows_kernel, dims, supers * part), 'own_half_rows'...  2.96 us
    pallas_call x1, Pallas kernels, replicated_plan(): call(functools.partial(place_kernel, (supers, width, rows, span, part)),...  2.13 us
    pallas_call x1, Pallas kernels, replicated_plan(): call(last_rows_kernel, 'last_rows', 2 * 10 ** 9, out_shape=(shape((supers...  2.13 us
    pallas_call x1, Pallas kernels, replicated_plan(): call(functools.partial(late_sums_kernel, count, local_rows), 'late_sums',...  1.8 us
    pallas_call x1, Pallas kernels, replicated_plan(): call(functools.partial(early_sums_kernel, count, local_rows), 'early_sums...  1.79 us
  transfers between devices with their start and end apart: 23, of which 11 were waited for; matrix products, arithmetic and copies ran while one was open for 3% of the time, Pallas kernels for 15%

profile of v10, /device:TPU:0, one launch (start us, length us, event | category | flops | bytes accessed | tf_op | source)
XLA Modules:
  0.0 72.7 jit_solution(5498799925764487509)
XLA Ops:
  0.6 1.0 %pad_maximum_fusion.5 = bf16[176,640]{1,0:T(8,128)(2,1)S(1)} fusion(bf16[80,640]{1,0:T(8,128)(2,1)} %param.6, bf16[96,640]{1,0:T(8,128)(2,1)} %bitcast.50), kind=kLoop, calls=%fused_computation.10 | loop fusion | flops 450560 | bytes 450560 | tf_op jit(solution)/shard_map/concatenate | solution.py:353
  1.6 3.1 %collective-permute-start.3 = (bf16[176,640]{1,0:T(8,128)(2,1)S(1)}, bf16[176,640]{1,0:T(8,128)(2,1)S(1)}, u32[]{:S(2)}, u32[]{:S(2)}) collective-permute-start(bf16[176,640]{1,0:T(8,128)(2,1)S(1)} %pad_maximum_fusion.5), channel_id=1, source_target_pairs={{0,8},{2,10},{4,12},{6,14},{8,0},{10,2},{12,4},{14,6},{16,24},{18,... | collective-permute-start | bytes 675848 | tf_op jit(solution)/shard_map/ppermute | solution.py:121
  4.7 1.0 %fusion = (bf16[1,176,640]{2,1,0:T(8,128)(2,1)S(1)}, bf16[176,640]{1,0:T(8,128)(2,1)S(1)}) fusion(bf16[80,640]{1,0:T(8,128)(2,1)} %param.6, bf16[96,640]{1,0:T(8,128)(2,1)} %bitcast.51), kind=kLoop, calls=%fused_computation.17 | loop fusion | flops 450560 | bytes 675840 | tf_op jit(solution)/shard_map/stack | solution.py:360
  5.7 1.6 %collective-permute-start = (bf16[176,640]{1,0:T(8,128)(2,1)S(1)}, bf16[176,640]{1,0:T(8,128)(2,1)S(1)}, u32[]{:S(2)}, u32[]{:S(2)}) collective-permute-start(bf16[176,640]{1,0:T(8,128)(2,1)S(1)} %get-tuple-element.69), channel_id=1, source_target_pairs={{0,4},{2,6},{4,0},{6,2},{8,12},{10,14},{12,8},{14,10},{16,20},{18,... | collective-permute-start | bytes 675848 | tf_op jit(solution)/shard_map/ppermute | solution.py:121
  7.3 1.5 %collective-permute-start.2 = (bf16[176,640]{1,0:T(8,128)(2,1)S(1)}, bf16[176,640]{1,0:T(8,128)(2,1)S(1)}, u32[]{:S(2)}, u32[]{:S(2)}) collective-permute-start(bf16[176,640]{1,0:T(8,128)(2,1)S(1)} %get-tuple-element.69), channel_id=1, source_target_pairs={{0,2},{2,0},{4,6},{6,4},{8,10},{10,8},{12,14},{14,12},{16,18},{18,... | collective-permute-start | bytes 675848 | tf_op jit(solution)/shard_map/ppermute | solution.py:121
  8.8 2.6 %collective-permute-start.7 = (bf16[96,640]{1,0:T(8,128)(2,1)}, bf16[96,640]{1,0:T(8,128)(2,1)S(1)}, u32[]{:S(2)}, u32[]{:S(2)}) collective-permute-start(bf16[96,640]{1,0:T(8,128)(2,1)} %bitcast.52), channel_id=1, source_target_pairs={{0,16},{2,18},{4,20},{6,22},{8,24},{10,26},{12,28},{14,30},{16,0},... | collective-permute-start | bytes 368648 | tf_op jit(solution)/shard_map/ppermute | solution.py:121
  11.4 0.2 collective-permute-start.8
  11.6 1.1 %collective-permute-done = bf16[176,640]{1,0:T(8,128)(2,1)S(1)} collective-permute-done((bf16[176,640]{1,0:T(8,128)(2,1)S(1)}, bf16[176,640]{1,0:T(8,128)(2,1)S(1)}, u32[]{:S(2)}, u32[]{:S(2)}) %collective-permute-start) | collective-permute-done | bytes 225312 | tf_op jit(solution)/shard_map/ppermute | solution.py:121
  12.8 1.2 %collective-permute-done.2 = bf16[176,640]{1,0:T(8,128)(2,1)S(1)} collective-permute-done((bf16[176,640]{1,0:T(8,128)(2,1)S(1)}, bf16[176,640]{1,0:T(8,128)(2,1)S(1)}, u32[]{:S(2)}, u32[]{:S(2)}) %collective-permute-start.2) | collective-permute-done | bytes 225312 | tf_op jit(solution)/shard_map/ppermute | solution.py:121
  14.0 1.5 %collective-permute-start.4 = (bf16[176,640]{1,0:T(8,128)(2,1)S(1)}, bf16[176,640]{1,0:T(8,128)(2,1)S(1)}, u32[]{:S(2)}, u32[]{:S(2)}) collective-permute-start(bf16[176,640]{1,0:T(8,128)(2,1)S(1)} %collective-permute-done.3), channel_id=1, source_target_pairs={{0,2},{2,0},{4,6},{6,4},{8,10},{10,8},{12,14},{14,12},{16,18},{18,... | collective-permute-start | bytes 675848 | tf_op jit(solution)/shard_map/ppermute | solution.py:121
  15.5 0.5 collective-permute-start.6
  16.0 0.5 collective-permute-start.1
  16.5 3.9 %collective-permute-done.7 = bf16[96,640]{1,0:T(8,128)(2,1)S(1)} collective-permute-done((bf16[96,640]{1,0:T(8,128)(2,1)}, bf16[96,640]{1,0:T(8,128)(2,1)S(1)}, u32[]{:S(2)}, u32[]{:S(2)}) %collective-permute-start.7) | collective-permute-done | bytes 122912 | tf_op jit(solution)/shard_map/ppermute | solution.py:121
  20.5 0.1 maximum_bitcast_fusion.3
  20.5 1.7 %collective-permute-done.4 = bf16[176,640]{1,0:T(8,128)(2,1)S(1)} collective-permute-done((bf16[176,640]{1,0:T(8,128)(2,1)S(1)}, bf16[176,640]{1,0:T(8,128)(2,1)S(1)}, u32[]{:S(2)}, u32[]{:S(2)}) %collective-permute-start.4) | collective-permute-done | bytes 225312 | tf_op jit(solution)/shard_map/ppermute | solution.py:121
  22.2 2.4 %collective-permute-done.1 = bf16[176,640]{1,0:T(8,128)(2,1)S(1)} collective-permute-done((bf16[176,640]{1,0:T(8,128)(2,1)S(1)}, bf16[176,640]{1,0:T(8,128)(2,1)S(1)}, u32[]{:S(2)}, u32[]{:S(2)}) %collective-permute-start.1) | collective-permute-done | bytes 225312 | tf_op jit(solution)/shard_map/ppermute | solution.py:121
  24.6 1.5 %collective-permute-start.11 = (bf16[2,96,640]{2,1,0:T(8,128)(2,1)S(1)}, bf16[2,96,640]{2,1,0:T(8,128)(2,1)S(1)}, u32[]{:S(2)}, u32[]{:S(2)}) collective-permute-start(bf16[2,96,640]{2,1,0:T(8,128)(2,1)S(1)} %pad_maximum_fusion.3), channel_id=1, source_target_pairs={{0,2},{2,0},{4,6},{6,4},{8,10},{10,8},{12,14},{14,12},{16,18},{18,... | collective-permute-start | bytes 737288 | tf_op jit(solution)/shard_map/ppermute | solution.py:121
  26.1 0.6 collective-permute-start.12
  26.7 2.9 %collective-permute-start.10 = (bf16[80,640]{1,0:T(8,128)(2,1)S(1)}, bf16[80,640]{1,0:T(8,128)(2,1)S(1)}, u32[]{:S(2)}, u32[]{:S(2)}) collective-permute-start(bf16[80,640]{1,0:T(8,128)(2,1)S(1)} %copy-done.4), channel_id=1, source_target_pairs={{0,24},{2,26},{4,28},{6,30},{8,16},{10,18},{12,20},{14,22},{16,8},... | collective-permute-start | bytes 307208 | tf_op jit(solution)/shard_map/ppermute | solution.py:121
  29.6 1.1 %collective-permute-start.5 = (bf16[176,640]{1,0:T(8,128)(2,1)S(1)}, bf16[176,640]{1,0:T(8,128)(2,1)S(1)}, u32[]{:S(2)}, u32[]{:S(2)}) collective-permute-start(bf16[176,640]{1,0:T(8,128)(2,1)S(1)} %collective-permute-done.4), channel_id=1, source_target_pairs={{0,4},{2,6},{4,0},{6,2},{8,12},{10,14},{12,8},{14,10},{16,20},{18,... | collective-permute-start | bytes 675848 | tf_op jit(solution)/shard_map/ppermute | solution.py:121
  30.7 0.1 maximum_bitcast_fusion.1
  30.8 0.1 maximum_bitcast_fusion.2
  30.8 5.7 %collective-permute-done.5 = bf16[176,640]{1,0:T(8,128)(2,1)S(1)} collective-permute-done((bf16[176,640]{1,0:T(8,128)(2,1)S(1)}, bf16[176,640]{1,0:T(8,128)(2,1)S(1)}, u32[]{:S(2)}, u32[]{:S(2)}) %collective-permute-start.5) | collective-permute-done | bytes 225312 | tf_op jit(solution)/shard_map/ppermute | solution.py:121
  36.5 0.1 maximum_bitcast_fusion
  36.6 0.3 pad_maximum_fusion.refs_2_.refs_1_
  36.9 0.1 collective-permute-start.15
  37.0 0.3 collective-permute-start.13
  37.4 1.2 %collective-permute-start.14 = (bf16[96,640]{1,0:T(8,128)(2,1)S(1)}, bf16[96,640]{1,0:T(8,128)(2,1)S(1)}, u32[]{:S(2)}, u32[]{:S(2)}) collective-permute-start(bf16[96,640]{1,0:T(8,128)(2,1)S(1)} %slice_bitcast_fusion), channel_id=1, source_target_pairs={{0,4},{2,6},{4,0},{6,2},{8,12},{10,14},{12,8},{14,10},{16,20},{18,... | collective-permute-start | bytes 368648 | tf_op jit(solution)/shard_map/ppermute | solution.py:121
  38.6 4.2 %collective-permute-done.13 = bf16[96,640]{1,0:T(8,128)(2,1)S(1)} collective-permute-done((bf16[96,640]{1,0:T(8,128)(2,1)S(1)}, bf16[96,640]{1,0:T(8,128)(2,1)S(1)}, u32[]{:S(2)}, u32[]{:S(2)}) %collective-permute-start.13) | collective-permute-done | bytes 122912 | tf_op jit(solution)/shard_map/ppermute | solution.py:121
  42.8 0.1 collective-permute-done.14
  42.9 0.1 pad_maximum_fusion.1.refs_3_
  43.1 0.1 collective-permute-start.16
  43.2 0.5 collective-permute-start.22
  43.7 1.8 %collective-permute-start.17 = (bf16[2,80,640]{2,1,0:T(8,128)(2,1)S(1)}, bf16[2,80,640]{2,1,0:T(8,128)(2,1)S(1)}, u32[]{:S(2)}, u32[]{:S(2)}) collective-permute-start(bf16[2,80,640]{2,1,0:T(8,128)(2,1)S(1)} %pad_maximum_fusion.6), channel_id=1, source_target_pairs={{0,2},{2,0},{4,6},{6,4},{8,10},{10,8},{12,14},{14,12},{16,18},{18,... | collective-permute-start | bytes 614408 | tf_op jit(solution)/shard_map/ppermute | solution.py:121
  45.5 0.9 %collective-permute-start.18 = (bf16[2,80,640]{2,1,0:T(8,128)(2,1)S(1)}, bf16[2,80,640]{2,1,0:T(8,128)(2,1)S(1)}, u32[]{:S(2)}, u32[]{:S(2)}) collective-permute-start(bf16[2,80,640]{2,1,0:T(8,128)(2,1)S(1)} %pad_maximum_fusion.6), channel_id=1, source_target_pairs={{0,4},{2,6},{4,0},{6,2},{8,12},{10,14},{12,8},{14,10},{16,20},{18,... | collective-permute-start | bytes 614408 | tf_op jit(solution)/shard_map/ppermute | solution.py:121
  46.4 2.1 %place.1.refs_0_ = bf16[3,512,1280]{2,1,0:T(8,128)(2,1)S(1)} custom-call(s32[3,10]{1,0:T(4,128)S(1)} %copy-done.1, s32[3,10]{1,0:T(4,128)S(1)} %copy-done.2, bf16[4,2,176,640]{3,2,1,0:T(8,128)(2,1)S(1)} %pad_maximum_fusion.refs_2_.refs_1_, bf16[4,2,96,640]{3,2,1,0:T(8,128)(2,1)S(1)} %pad_maximum_fusion.1.refs_3_, ...), custom_call_target="tpu_custom_call" | custom-call | flops 2000000000 | bytes 8388608 | tf_op jit(solution)/shard_map/place/pallas_call | solution.py:372
  48.5 3.0 %own_half_rows.1 = (bf16[640,1280]{1,0:T(8,128)(2,1)S(1)}, bf16[640,512]{1,0:T(8,128)(2,1)S(1)}, bf16[640,512]{1,0:T(8,128)(2,1)S(1)}, bf16[640,512]{1,0:T(8,128...) custom-call(bf16[3,512,1280]{2,1,0:T(8,128)(2,1)S(1)} %place.1.refs_0_, ...), custom_call_target="tpu_custom_call" | custom-call | flops 3000000000 | bytes 8388608 | tf_op jit(solution)/shard_map/own_half_rows/pallas_call | solution.py:384
  51.5 0.8 %collective-permute-done.18 = bf16[2,80,640]{2,1,0:T(8,128)(2,1)S(1)} collective-permute-done((bf16[2,80,640]{2,1,0:T(8,128)(2,1)S(1)}, bf16[2,80,640]{2,1,0:T(8,128)(2,1)S(1)}, u32[]{:S(2)}, u32[]{:S(2)}) %collective-permute-start.18) | collective-permute-done | bytes 204832 | tf_op jit(solution)/shard_map/ppermute | solution.py:121
  52.3 0.4 collective-permute-start.19
  52.7 1.1 %collective-permute-start.20 = (bf16[80,640]{1,0:T(8,128)(2,1)S(1)}, bf16[80,640]{1,0:T(8,128)(2,1)S(1)}, u32[]{:S(2)}, u32[]{:S(2)}) collective-permute-start(bf16[80,640]{1,0:T(8,128)(2,1)S(1)} %slice_bitcast_fusion.2), channel_id=1, source_target_pairs={{0,4},{2,6},{4,0},{6,2},{8,12},{10,14},{12,8},{14,10},{16,20},{18,... | collective-permute-start | bytes 307208 | tf_op jit(solution)/shard_map/ppermute | solution.py:121
  53.8 2.1 %last_rows.1 = (f32[3,40,512]{2,1,0:T(8,128)}, bf16[640,256]{1,0:T(8,128)(2,1)S(1)}, bf16[640,256]{1,0:T(8,128)(2,1)S(1)}) custom-call(bf16[3,512,1280]{2,1,0:T(8,128)(2,1)S(1)} %place.1.refs_0_, bf16[640,1280]{1,0:T(8,128)(2,1)S(1)} %get-tuple-element.42.refs_1_, bf16[640,512]{1,0:T(8,128)(2,1)S(1)} %get-tuple-element.59.refs_2_.refs_1_, ...), custom_call_target="tpu_custom_call" | custom-call | flops 2000000000 | bytes 8388608 | tf_op jit(solution)/shard_map/last_rows/pallas_call | solution.py:395
  56.0 1.1 %collective-permute-done.19 = bf16[80,640]{1,0:T(8,128)(2,1)S(1)} collective-permute-done((bf16[80,640]{1,0:T(8,128)(2,1)S(1)}, bf16[80,640]{1,0:T(8,128)(2,1)S(1)}, u32[]{:S(2)}, u32[]{:S(2)}) %collective-permute-start.19) | collective-permute-done | bytes 102432 | tf_op jit(solution)/shard_map/ppermute | solution.py:121
  57.0 0.4 collective-permute-done.20
  57.5 0.1 pad_maximum_fusion.2.refs_1_
  57.6 0.1 collective-permute-start.21
  57.7 1.8 %late_sums.1 = (f32[512,512]{1,0:T(8,128)S(1)}, f32[256,512]{1,0:T(8,128)S(1)}, f32[512,256]{1,0:T(8,128)S(1)}) custom-call(bf16[3,512,1280]{2,1,0:T(8,128)(2,1)S(1)} %place.1.refs_0_, bf16[640,512]{1,0:T(8,128)(2,1)S(1)} %get-tuple-element.52.refs_4_.refs_1_, bf16[640,512]{1,0:T(8,128)(2,1)S(1)} %get-tuple-element.53.refs_5_.refs_2_, ...), custom_call_target="tpu_custom_call" | custom-call | flops 2000000000 | bytes 8388608 | tf_op jit(solution)/shard_map/late_sums/pallas_call | solution.py:412
  59.5 1.8 %early_sums.1 = (f32[512,512]{1,0:T(8,128)S(1)}, f32[512,512]{1,0:T(8,128)S(1)}) custom-call(bf16[3,512,1280]{2,1,0:T(8,128)(2,1)S(1)} %place.1.refs_0_, bf16[640,512]{1,0:T(8,128)(2,1)S(1)} %get-tuple-element.59.refs_2_.refs_1_, bf16[640,512]{1,0:T(8,128)(2,1)S(1)} %get-tuple-element.51.refs_3_.refs_2_, bf16[640,512]{1,0:T(8,128)(2,1)S(1)} %get-tuple-element.60.refs_3_, ...), custom_call_target="tpu_custom_call" | custom-call | flops 2000000000 | bytes 8388608 | tf_op jit(solution)/shard_map/early_sums/pallas_call | solution.py:403
  61.3 11.2 %other_half.1 = f32[3,512,256]{2,1,0:T(8,128)} custom-call(bf16[3,512,1280]{2,1,0:T(8,128)(2,1)S(1)} %place.1.refs_0_, bf16[4,2,80,640]{3,2,1,0:T(8,128)(2,1)S(1)} %pad_maximum_fusion.2.refs_1_, bf16[4,2,80,640]{3,2,1,0:T(8,128)(2,1)S(1)} %collective-permute-done.21.refs_2_, bf16[2,512,512]{2,1,0:T(8,128)(2,1)S(1)} %copy-done, f32[3,512,256]{2,1,0:T(8,128)S(1)} %copy-done.3, ...), custom_call_target="tpu_custom_call" | custom-call | flops 12000000000 | bytes 8388608 | tf_op jit(solution)/shard_map/other_half/pallas_call | solution.py:420
  (31 shorter events, 0.2 us)
Async XLA Ops:
  0.6 26.1 %copy-start.4 = (bf16[80,640]{1,0:T(8,128)(2,1)S(1)}, bf16[80,640]{1,0:T(8,128)(2,1)}, u32[]{:S(2)}) copy-start(bf16[80,640]{1,0:T(8,128)(2,1)} %param.6) | copy-start | bytes 307204
  1.6 10.0 %collective-permute-start.3 = (bf16[176,640]{1,0:T(8,128)(2,1)S(1)}, bf16[176,640]{1,0:T(8,128)(2,1)S(1)}, u32[]{:S(2)}, u32[]{:S(2)}) collective-permute-start(bf16[176,640]{1,0:T(8,128)(2,1)S(1)} %pad_maximum_fusion.5), channel_id=1, source_target_pairs={{0,8},{2,10},{4,12},{6,14},{8,0},{10,2},{12,4},{14,6},{16,24},{18,... | collective-permute-start | bytes 675848 | tf_op jit(solution)/shard_map/ppermute | solution.py:121
  5.7 7.0 %collective-permute-start = (bf16[176,640]{1,0:T(8,128)(2,1)S(1)}, bf16[176,640]{1,0:T(8,128)(2,1)S(1)}, u32[]{:S(2)}, u32[]{:S(2)}) collective-permute-start(bf16[176,640]{1,0:T(8,128)(2,1)S(1)} %get-tuple-element.69), channel_id=1, source_target_pairs={{0,4},{2,6},{4,0},{6,2},{8,12},{10,14},{12,8},{14,10},{16,20},{18,... | collective-permute-start | bytes 675848 | tf_op jit(solution)/shard_map/ppermute | solution.py:121
  7.3 6.7 %collective-permute-start.2 = (bf16[176,640]{1,0:T(8,128)(2,1)S(1)}, bf16[176,640]{1,0:T(8,128)(2,1)S(1)}, u32[]{:S(2)}, u32[]{:S(2)}) collective-permute-start(bf16[176,640]{1,0:T(8,128)(2,1)S(1)} %get-tuple-element.69), channel_id=1, source_target_pairs={{0,2},{2,0},{4,6},{6,4},{8,10},{10,8},{12,14},{14,12},{16,18},{18,... | collective-permute-start | bytes 675848 | tf_op jit(solution)/shard_map/ppermute | solution.py:121
  8.8 11.6 %collective-permute-start.7 = (bf16[96,640]{1,0:T(8,128)(2,1)}, bf16[96,640]{1,0:T(8,128)(2,1)S(1)}, u32[]{:S(2)}, u32[]{:S(2)}) collective-permute-start(bf16[96,640]{1,0:T(8,128)(2,1)} %bitcast.52), channel_id=1, source_target_pairs={{0,16},{2,18},{4,20},{6,22},{8,24},{10,26},{12,28},{14,30},{16,0},... | collective-permute-start | bytes 368648 | tf_op jit(solution)/shard_map/ppermute | solution.py:121
  11.4 9.1 %collective-permute-start.8 = (bf16[96,640]{1,0:T(8,128)(2,1)}, bf16[96,640]{1,0:T(8,128)(2,1)S(1)}, u32[]{:S(2)}, u32[]{:S(2)}) collective-permute-start(bf16[96,640]{1,0:T(8,128)(2,1)} %bitcast.53), channel_id=1, source_target_pairs={{0,24},{2,26},{4,28},{6,30},{8,16},{10,18},{12,20},{14,22},{16,8},... | collective-permute-start | bytes 368648 | tf_op jit(solution)/shard_map/ppermute | solution.py:121
  14.0 8.2 %collective-permute-start.4 = (bf16[176,640]{1,0:T(8,128)(2,1)S(1)}, bf16[176,640]{1,0:T(8,128)(2,1)S(1)}, u32[]{:S(2)}, u32[]{:S(2)}) collective-permute-start(bf16[176,640]{1,0:T(8,128)(2,1)S(1)} %collective-permute-done.3), channel_id=1, source_target_pairs={{0,2},{2,0},{4,6},{6,4},{8,10},{10,8},{12,14},{14,12},{16,18},{18,... | collective-permute-start | bytes 675848 | tf_op jit(solution)/shard_map/ppermute | solution.py:121
  15.5 6.7 %collective-permute-start.6 = (bf16[176,640]{1,0:T(8,128)(2,1)S(1)}, bf16[176,640]{1,0:T(8,128)(2,1)S(1)}, u32[]{:S(2)}, u32[]{:S(2)}) collective-permute-start(bf16[176,640]{1,0:T(8,128)(2,1)S(1)} %collective-permute-done.3), channel_id=1, source_target_pairs={{0,4},{2,6},{4,0},{6,2},{8,12},{10,14},{12,8},{14,10},{16,20},{18,... | collective-permute-start | bytes 675848 | tf_op jit(solution)/shard_map/ppermute | solution.py:121
  16.0 8.6 %collective-permute-start.1 = (bf16[176,640]{1,0:T(8,128)(2,1)S(1)}, bf16[176,640]{1,0:T(8,128)(2,1)S(1)}, u32[]{:S(2)}, u32[]{:S(2)}) collective-permute-start(bf16[176,640]{1,0:T(8,128)(2,1)S(1)} %collective-permute-done), channel_id=1, source_target_pairs={{0,2},{2,0},{4,6},{6,4},{8,10},{10,8},{12,14},{14,12},{16,18},{18,... | collective-permute-start | bytes 675848 | tf_op jit(solution)/shard_map/ppermute | solution.py:121
  24.6 12.4 %collective-permute-start.11 = (bf16[2,96,640]{2,1,0:T(8,128)(2,1)S(1)}, bf16[2,96,640]{2,1,0:T(8,128)(2,1)S(1)}, u32[]{:S(2)}, u32[]{:S(2)}) collective-permute-start(bf16[2,96,640]{2,1,0:T(8,128)(2,1)S(1)} %pad_maximum_fusion.3), channel_id=1, source_target_pairs={{0,2},{2,0},{4,6},{6,4},{8,10},{10,8},{12,14},{14,12},{16,18},{18,... | collective-permute-start | bytes 737288 | tf_op jit(solution)/shard_map/ppermute | solution.py:121
  26.1 10.9 %collective-permute-start.12 = (bf16[2,96,640]{2,1,0:T(8,128)(2,1)S(1)}, bf16[2,96,640]{2,1,0:T(8,128)(2,1)S(1)}, u32[]{:S(2)}, u32[]{:S(2)}) collective-permute-start(bf16[2,96,640]{2,1,0:T(8,128)(2,1)S(1)} %pad_maximum_fusion.3), channel_id=1, source_target_pairs={{0,4},{2,6},{4,0},{6,2},{8,12},{10,14},{12,8},{14,10},{16,20},{18,... | collective-permute-start | bytes 737288 | tf_op jit(solution)/shard_map/ppermute | solution.py:121
  26.7 10.3 %collective-permute-start.10 = (bf16[80,640]{1,0:T(8,128)(2,1)S(1)}, bf16[80,640]{1,0:T(8,128)(2,1)S(1)}, u32[]{:S(2)}, u32[]{:S(2)}) collective-permute-start(bf16[80,640]{1,0:T(8,128)(2,1)S(1)} %copy-done.4), channel_id=1, source_target_pairs={{0,24},{2,26},{4,28},{6,30},{8,16},{10,18},{12,20},{14,22},{16,8},... | collective-permute-start | bytes 307208 | tf_op jit(solution)/shard_map/ppermute | solution.py:121
  29.6 7.4 %collective-permute-start.9 = (bf16[80,640]{1,0:T(8,128)(2,1)S(1)}, bf16[80,640]{1,0:T(8,128)(2,1)S(1)}, u32[]{:S(2)}, u32[]{:S(2)}) collective-permute-start(bf16[80,640]{1,0:T(8,128)(2,1)S(1)} %copy-done.4), channel_id=1, source_target_pairs={{0,16},{2,18},{4,20},{6,22},{8,24},{10,26},{12,28},{14,30},{16,0},... | collective-permute-start | bytes 307208 | tf_op jit(solution)/shard_map/ppermute | solution.py:121
  29.6 6.9 %collective-permute-start.5 = (bf16[176,640]{1,0:T(8,128)(2,1)S(1)}, bf16[176,640]{1,0:T(8,128)(2,1)S(1)}, u32[]{:S(2)}, u32[]{:S(2)}) collective-permute-start(bf16[176,640]{1,0:T(8,128)(2,1)S(1)} %collective-permute-done.4), channel_id=1, source_target_pairs={{0,4},{2,6},{4,0},{6,2},{8,12},{10,14},{12,8},{14,10},{16,20},{18,... | collective-permute-start | bytes 675848 | tf_op jit(solution)/shard_map/ppermute | solution.py:121
  36.8 6.3 %copy-start.3 = (f32[3,512,256]{2,1,0:T(8,128)S(1)}, f32[3,512,256]{2,1,0:T(8,128)}, u32[]{:S(2)}) copy-start(f32[3,512,256]{2,1,0:T(8,128)} %refs_4_.1) | copy-start | bytes 4718596
  36.8 9.5 %copy-start.1 = (s32[3,10]{1,0:T(4,128)S(1)}, s32[3,10]{1,0:T(4,128)}, u32[]{:S(2)}) copy-start(s32[3,10]{1,0:T(4,128)} %refs_0_.1) | copy-start | bytes 364
  36.9 9.5 %copy-start.2 = (s32[3,10]{1,0:T(4,128)S(1)}, s32[3,10]{1,0:T(4,128)}, u32[]{:S(2)}) copy-start(s32[3,10]{1,0:T(4,128)} %refs_1_.1) | copy-start | bytes 364
  36.9 9.5 %collective-permute-start.15 = (bf16[4,2,176,640]{3,2,1,0:T(8,128)(2,1)S(1)}, bf16[4,2,176,640]{3,2,1,0:T(8,128)(2,1)S(1)}, u32[]{:S(2)}, u32[]{:S(2)}) collective-permute-start(bf16[4,2,176,640]{3,2,1,0:T(8,128)(2,1)S(1)} %pad_maximum_fusion.refs_2_.refs_1_), channel_id=1, source_target_pairs={{0,1},{1,0},{2,3},{3,2},{4,5},{5,4},{6,7},{7,6},{8,9},{9,8},{10,11... | collective-permute-start | bytes 5406728 | tf_op jit(solution)/shard_map/ppermute | solution.py:125
  37.0 5.8 %collective-permute-start.13 = (bf16[96,640]{1,0:T(8,128)(2,1)S(1)}, bf16[96,640]{1,0:T(8,128)(2,1)S(1)}, u32[]{:S(2)}, u32[]{:S(2)}) collective-permute-start(bf16[96,640]{1,0:T(8,128)(2,1)S(1)} %slice_bitcast_fusion.1), channel_id=1, source_target_pairs={{0,2},{2,0},{4,6},{6,4},{8,10},{10,8},{12,14},{14,12},{16,18},{18,... | collective-permute-start | bytes 368648 | tf_op jit(solution)/shard_map/ppermute | solution.py:121
  37.4 5.5 %collective-permute-start.14 = (bf16[96,640]{1,0:T(8,128)(2,1)S(1)}, bf16[96,640]{1,0:T(8,128)(2,1)S(1)}, u32[]{:S(2)}, u32[]{:S(2)}) collective-permute-start(bf16[96,640]{1,0:T(8,128)(2,1)S(1)} %slice_bitcast_fusion), channel_id=1, source_target_pairs={{0,4},{2,6},{4,0},{6,2},{8,12},{10,14},{12,8},{14,10},{16,20},{18,... | collective-permute-start | bytes 368648 | tf_op jit(solution)/shard_map/ppermute | solution.py:121
  43.1 3.3 %collective-permute-start.16 = (bf16[4,2,96,640]{3,2,1,0:T(8,128)(2,1)S(1)}, bf16[4,2,96,640]{3,2,1,0:T(8,128)(2,1)S(1)}, u32[]{:S(2)}, u32[]{:S(2)}) collective-permute-start(bf16[4,2,96,640]{3,2,1,0:T(8,128)(2,1)S(1)} %pad_maximum_fusion.1.refs_3_), channel_id=1, source_target_pairs={{0,1},{1,0},{2,3},{3,2},{4,5},{5,4},{6,7},{7,6},{8,9},{9,8},{10,11... | collective-permute-start | bytes 2949128 | tf_op jit(solution)/shard_map/ppermute | solution.py:125
  43.2 18.1 %collective-permute-start.22 = (f32[3,512,256]{2,1,0:T(8,128)S(1)}, f32[3,512,256]{2,1,0:T(8,128)S(1)}, u32[]{:S(2)}, u32[]{:S(2)}) collective-permute-start(f32[3,512,256]{2,1,0:T(8,128)S(1)} %copy-done.3), channel_id=1, source_target_pairs={{0,1},{1,0},{2,3},{3,2},{4,5},{5,4},{6,7},{7,6},{8,9},{9,8},{10,11... | collective-permute-start | bytes 4718600 | tf_op jit(solution)/shard_map/ppermute | solution.py:125
  43.7 4.8 %copy-start = (bf16[2,512,512]{2,1,0:T(8,128)(2,1)S(1)}, bf16[2,512,512]{2,1,0:T(8,128)(2,1)}, u32[]{:S(2)}) copy-start(bf16[2,512,512]{2,1,0:T(8,128)(2,1)} %refs_3_.3) | copy-start | bytes 3145732
  43.7 7.8 %collective-permute-start.17 = (bf16[2,80,640]{2,1,0:T(8,128)(2,1)S(1)}, bf16[2,80,640]{2,1,0:T(8,128)(2,1)S(1)}, u32[]{:S(2)}, u32[]{:S(2)}) collective-permute-start(bf16[2,80,640]{2,1,0:T(8,128)(2,1)S(1)} %pad_maximum_fusion.6), channel_id=1, source_target_pairs={{0,2},{2,0},{4,6},{6,4},{8,10},{10,8},{12,14},{14,12},{16,18},{18,... | collective-permute-start | bytes 614408 | tf_op jit(solution)/shard_map/ppermute | solution.py:121
  45.5 6.8 %collective-permute-start.18 = (bf16[2,80,640]{2,1,0:T(8,128)(2,1)S(1)}, bf16[2,80,640]{2,1,0:T(8,128)(2,1)S(1)}, u32[]{:S(2)}, u32[]{:S(2)}) collective-permute-start(bf16[2,80,640]{2,1,0:T(8,128)(2,1)S(1)} %pad_maximum_fusion.6), channel_id=1, source_target_pairs={{0,4},{2,6},{4,0},{6,2},{8,12},{10,14},{12,8},{14,10},{16,20},{18,... | collective-permute-start | bytes 614408 | tf_op jit(solution)/shard_map/ppermute | solution.py:121
  52.3 4.7 %collective-permute-start.19 = (bf16[80,640]{1,0:T(8,128)(2,1)S(1)}, bf16[80,640]{1,0:T(8,128)(2,1)S(1)}, u32[]{:S(2)}, u32[]{:S(2)}) collective-permute-start(bf16[80,640]{1,0:T(8,128)(2,1)S(1)} %slice_bitcast_fusion.3), channel_id=1, source_target_pairs={{0,2},{2,0},{4,6},{6,4},{8,10},{10,8},{12,14},{14,12},{16,18},{18,... | collective-permute-start | bytes 307208 | tf_op jit(solution)/shard_map/ppermute | solution.py:121
  52.7 4.7 %collective-permute-start.20 = (bf16[80,640]{1,0:T(8,128)(2,1)S(1)}, bf16[80,640]{1,0:T(8,128)(2,1)S(1)}, u32[]{:S(2)}, u32[]{:S(2)}) collective-permute-start(bf16[80,640]{1,0:T(8,128)(2,1)S(1)} %slice_bitcast_fusion.2), channel_id=1, source_target_pairs={{0,4},{2,6},{4,0},{6,2},{8,12},{10,14},{12,8},{14,10},{16,20},{18,... | collective-permute-start | bytes 307208 | tf_op jit(solution)/shard_map/ppermute | solution.py:121
  57.6 3.7 %collective-permute-start.21 = (bf16[4,2,80,640]{3,2,1,0:T(8,128)(2,1)S(1)}, bf16[4,2,80,640]{3,2,1,0:T(8,128)(2,1)S(1)}, u32[]{:S(2)}, u32[]{:S(2)}) collective-permute-start(bf16[4,2,80,640]{3,2,1,0:T(8,128)(2,1)S(1)} %pad_maximum_fusion.2.refs_1_), channel_id=1, source_target_pairs={{0,1},{1,0},{2,3},{3,2},{4,5},{5,4},{6,7},{7,6},{8,9},{9,8},{10,11... | collective-permute-start | bytes 2457608 | tf_op jit(solution)/shard_map/ppermute | solution.py:125

commit v11 on v10

--- a/solution.py
+++ b/solution.py
@@ -399,7 +399,16 @@
         in_specs=[vmem] * 7,
         out_specs=(vmem,) * 3,
     )(pt, z_held, c0h, c0l, c1h, c1l, coupling)
-    z_far, c0h = after((z_far, c0h), c2h)
+    s1, n2, s2 = call(
+        functools.partial(late_sums_kernel, count, local_rows),
+        "late_sums", 2 * 10**9,
+        out_shape=(shape((width, width), f32), shape((half_w, width), f32), shape((width, half_w), f32)),
+        in_specs=[vmem] * 5,
+        out_specs=(vmem,) * 3,
+    )(pt, c1h, c1l, c2h, c2l)
+    z_far, c0h = after((z_far, c0h), s1)
+    z_last = jnp.stack([z_far, z_by, z_bx, z_b])
+    z_last_other = across(z_last)
     s0, u1 = call(
         functools.partial(early_sums_kernel, count, local_rows),
         "early_sums", 2 * 10**9,
@@ -407,15 +416,6 @@
         in_specs=[vmem] * 5,
         out_specs=(vmem,) * 2,
     )(pt, c0h, c0l, p1h, p1l)
-    z_last = jnp.stack([z_far, z_by, z_bx, z_b])
-    z_last_other = across(z_last)
-    s1, n2, s2 = call(
-        functools.partial(late_sums_kernel, count, local_rows),
-        "late_sums", 2 * 10**9,
-        out_shape=(shape((width, width), f32), shape((half_w, width), f32), shape((width, half_w), f32)),
-        in_specs=[vmem] * 5,
-        out_specs=(vmem,) * 3,
-    )(pt, c1h, c1l, c2h, c2l)
     sums = [s0, u1, s1, n2, s2]
     diagonals = call(
         functools.partial(last_kernel, dims, rows),

time: 72.9 us -> 71.8 us (0.985)
  waiting for transfers between devices: 22.7 us -> 21.8 us
    ppermute x19, waiting for transfers between devices: 22.6 us -> 21.3 us  [swap(): return lax.ppermute(value, axis, [(i, i ^ bit) for i in range(parts)])]
  transfers between devices with their start and end apart: 23 -> 23, of which waited for: 11 -> 10; matrix products, arithmetic and copies ran while one was open for 3% -> 3% of each run, Pallas kernels for 15% -> 15%
where the time goes in v11:
time: 71.8 us; the launch traced here: 71.7 us
  starting transfers between devices  24 us (33%)
  waiting for transfers between devices  21.8 us (30%)
  Pallas kernels  21.8 us (30%)
  other arithmetic  2.86 us (4%)
  between operations  1.07 us (1%)
    ppermute x19, starting transfers between devices, swap(): return lax.ppermute(value, axis, [(i, i ^ bit) for i in range(parts)])  23.3 us
    ppermute x19, waiting for transfers between devices, swap(): return lax.ppermute(value, axis, [(i, i ^ bit) for i in range(parts)])  21.3 us
    pallas_call x1, Pallas kernels, replicated_plan(): call(functools.partial(last_kernel, dims, rows), 'other_half', 12 * 10 **...  11.2 us
    pallas_call x1, Pallas kernels, replicated_plan(): call(functools.partial(rows_kernel, dims, supers * part), 'own_half_rows'...  2.96 us
    pallas_call x1, Pallas kernels, replicated_plan(): call(last_rows_kernel, 'last_rows', 2 * 10 ** 9, out_shape=(shape((supers...  2.13 us
    pallas_call x1, Pallas kernels, replicated_plan(): call(functools.partial(place_kernel, (supers, width, rows, span, part)),...  2.02 us
    pallas_call x1, Pallas kernels, replicated_plan(): call(functools.partial(late_sums_kernel, count, local_rows), 'late_sums',...  1.79 us
    pallas_call x1, Pallas kernels, replicated_plan(): call(functools.partial(early_sums_kernel, count, local_rows), 'early_sums...  1.79 us
  transfers between devices with their start and end apart: 23, of which 10 were waited for; matrix products, arithmetic and copies ran while one was open for 3% of the time, Pallas kernels for 15%

profile of v11, /device:TPU:0, one launch (start us, length us, event | category | flops | bytes accessed | tf_op | source)
XLA Modules:
  0.0 71.7 jit_solution(13873980226437256942)
XLA Ops:
  0.6 1.0 %pad_maximum_fusion.5 = bf16[176,640]{1,0:T(8,128)(2,1)S(1)} fusion(bf16[80,640]{1,0:T(8,128)(2,1)} %param.6, bf16[96,640]{1,0:T(8,128)(2,1)} %bitcast.50), kind=kLoop, calls=%fused_computation.10 | loop fusion | flops 450560 | bytes 450560 | tf_op jit(solution)/shard_map/concatenate | solution.py:353
  1.6 3.1 %collective-permute-start.3 = (bf16[176,640]{1,0:T(8,128)(2,1)S(1)}, bf16[176,640]{1,0:T(8,128)(2,1)S(1)}, u32[]{:S(2)}, u32[]{:S(2)}) collective-permute-start(bf16[176,640]{1,0:T(8,128)(2,1)S(1)} %pad_maximum_fusion.5), channel_id=1, source_target_pairs={{0,8},{2,10},{4,12},{6,14},{8,0},{10,2},{12,4},{14,6},{16,24},{18,... | collective-permute-start | bytes 675848 | tf_op jit(solution)/shard_map/ppermute | solution.py:121
  4.7 1.0 %fusion = (bf16[1,176,640]{2,1,0:T(8,128)(2,1)S(1)}, bf16[176,640]{1,0:T(8,128)(2,1)S(1)}) fusion(bf16[80,640]{1,0:T(8,128)(2,1)} %param.6, bf16[96,640]{1,0:T(8,128)(2,1)} %bitcast.51), kind=kLoop, calls=%fused_computation.17 | loop fusion | flops 450560 | bytes 675840 | tf_op jit(solution)/shard_map/stack | solution.py:360
  5.7 1.6 %collective-permute-start = (bf16[176,640]{1,0:T(8,128)(2,1)S(1)}, bf16[176,640]{1,0:T(8,128)(2,1)S(1)}, u32[]{:S(2)}, u32[]{:S(2)}) collective-permute-start(bf16[176,640]{1,0:T(8,128)(2,1)S(1)} %get-tuple-element.69), channel_id=1, source_target_pairs={{0,4},{2,6},{4,0},{6,2},{8,12},{10,14},{12,8},{14,10},{16,20},{18,... | collective-permute-start | bytes 675848 | tf_op jit(solution)/shard_map/ppermute | solution.py:121
  7.3 1.5 %collective-permute-start.2 = (bf16[176,640]{1,0:T(8,128)(2,1)S(1)}, bf16[176,640]{1,0:T(8,128)(2,1)S(1)}, u32[]{:S(2)}, u32[]{:S(2)}) collective-permute-start(bf16[176,640]{1,0:T(8,128)(2,1)S(1)} %get-tuple-element.69), channel_id=1, source_target_pairs={{0,2},{2,0},{4,6},{6,4},{8,10},{10,8},{12,14},{14,12},{16,18},{18,... | collective-permute-start | bytes 675848 | tf_op jit(solution)/shard_map/ppermute | solution.py:121
  8.8 2.6 %collective-permute-start.7 = (bf16[96,640]{1,0:T(8,128)(2,1)}, bf16[96,640]{1,0:T(8,128)(2,1)S(1)}, u32[]{:S(2)}, u32[]{:S(2)}) collective-permute-start(bf16[96,640]{1,0:T(8,128)(2,1)} %bitcast.52), channel_id=1, source_target_pairs={{0,16},{2,18},{4,20},{6,22},{8,24},{10,26},{12,28},{14,30},{16,0},... | collective-permute-start | bytes 368648 | tf_op jit(solution)/shard_map/ppermute | solution.py:121
  11.4 0.2 collective-permute-start.8
  11.6 1.1 %collective-permute-done = bf16[176,640]{1,0:T(8,128)(2,1)S(1)} collective-permute-done((bf16[176,640]{1,0:T(8,128)(2,1)S(1)}, bf16[176,640]{1,0:T(8,128)(2,1)S(1)}, u32[]{:S(2)}, u32[]{:S(2)}) %collective-permute-start) | collective-permute-done | bytes 225312 | tf_op jit(solution)/shard_map/ppermute | solution.py:121
  12.8 1.2 %collective-permute-done.2 = bf16[176,640]{1,0:T(8,128)(2,1)S(1)} collective-permute-done((bf16[176,640]{1,0:T(8,128)(2,1)S(1)}, bf16[176,640]{1,0:T(8,128)(2,1)S(1)}, u32[]{:S(2)}, u32[]{:S(2)}) %collective-permute-start.2) | collective-permute-done | bytes 225312 | tf_op jit(solution)/shard_map/ppermute | solution.py:121
  14.0 1.5 %collective-permute-start.4 = (bf16[176,640]{1,0:T(8,128)(2,1)S(1)}, bf16[176,640]{1,0:T(8,128)(2,1)S(1)}, u32[]{:S(2)}, u32[]{:S(2)}) collective-permute-start(bf16[176,640]{1,0:T(8,128)(2,1)S(1)} %collective-permute-done.3), channel_id=1, source_target_pairs={{0,2},{2,0},{4,6},{6,4},{8,10},{10,8},{12,14},{14,12},{16,18},{18,... | collective-permute-start | bytes 675848 | tf_op jit(solution)/shard_map/ppermute | solution.py:121
  15.5 0.5 collective-permute-start.6
  16.0 0.5 collective-permute-start.1
  16.5 3.9 %collective-permute-done.7 = bf16[96,640]{1,0:T(8,128)(2,1)S(1)} collective-permute-done((bf16[96,640]{1,0:T(8,128)(2,1)}, bf16[96,640]{1,0:T(8,128)(2,1)S(1)}, u32[]{:S(2)}, u32[]{:S(2)}) %collective-permute-start.7) | collective-permute-done | bytes 122912 | tf_op jit(solution)/shard_map/ppermute | solution.py:121
  20.5 0.1 maximum_bitcast_fusion.3
  20.5 1.7 %collective-permute-done.4 = bf16[176,640]{1,0:T(8,128)(2,1)S(1)} collective-permute-done((bf16[176,640]{1,0:T(8,128)(2,1)S(1)}, bf16[176,640]{1,0:T(8,128)(2,1)S(1)}, u32[]{:S(2)}, u32[]{:S(2)}) %collective-permute-start.4) | collective-permute-done | bytes 225312 | tf_op jit(solution)/shard_map/ppermute | solution.py:121
  22.2 2.4 %collective-permute-done.1 = bf16[176,640]{1,0:T(8,128)(2,1)S(1)} collective-permute-done((bf16[176,640]{1,0:T(8,128)(2,1)S(1)}, bf16[176,640]{1,0:T(8,128)(2,1)S(1)}, u32[]{:S(2)}, u32[]{:S(2)}) %collective-permute-start.1) | collective-permute-done | bytes 225312 | tf_op jit(solution)/shard_map/ppermute | solution.py:121
  24.6 1.5 %collective-permute-start.11 = (bf16[2,96,640]{2,1,0:T(8,128)(2,1)S(1)}, bf16[2,96,640]{2,1,0:T(8,128)(2,1)S(1)}, u32[]{:S(2)}, u32[]{:S(2)}) collective-permute-start(bf16[2,96,640]{2,1,0:T(8,128)(2,1)S(1)} %pad_maximum_fusion.3), channel_id=1, source_target_pairs={{0,2},{2,0},{4,6},{6,4},{8,10},{10,8},{12,14},{14,12},{16,18},{18,... | collective-permute-start | bytes 737288 | tf_op jit(solution)/shard_map/ppermute | solution.py:121
  26.1 0.6 collective-permute-start.12
  26.7 2.9 %collective-permute-start.10 = (bf16[80,640]{1,0:T(8,128)(2,1)S(1)}, bf16[80,640]{1,0:T(8,128)(2,1)S(1)}, u32[]{:S(2)}, u32[]{:S(2)}) collective-permute-start(bf16[80,640]{1,0:T(8,128)(2,1)S(1)} %copy-done.4), channel_id=1, source_target_pairs={{0,24},{2,26},{4,28},{6,30},{8,16},{10,18},{12,20},{14,22},{16,8},... | collective-permute-start | bytes 307208 | tf_op jit(solution)/shard_map/ppermute | solution.py:121
  29.6 1.1 %collective-permute-start.5 = (bf16[176,640]{1,0:T(8,128)(2,1)S(1)}, bf16[176,640]{1,0:T(8,128)(2,1)S(1)}, u32[]{:S(2)}, u32[]{:S(2)}) collective-permute-start(bf16[176,640]{1,0:T(8,128)(2,1)S(1)} %collective-permute-done.4), channel_id=1, source_target_pairs={{0,4},{2,6},{4,0},{6,2},{8,12},{10,14},{12,8},{14,10},{16,20},{18,... | collective-permute-start | bytes 675848 | tf_op jit(solution)/shard_map/ppermute | solution.py:121
  30.7 0.1 maximum_bitcast_fusion.1
  30.8 0.1 maximum_bitcast_fusion.2
  30.8 5.7 %collective-permute-done.5 = bf16[176,640]{1,0:T(8,128)(2,1)S(1)} collective-permute-done((bf16[176,640]{1,0:T(8,128)(2,1)S(1)}, bf16[176,640]{1,0:T(8,128)(2,1)S(1)}, u32[]{:S(2)}, u32[]{:S(2)}) %collective-permute-start.5) | collective-permute-done | bytes 225312 | tf_op jit(solution)/shard_map/ppermute | solution.py:121
  36.5 0.1 maximum_bitcast_fusion
  36.6 0.3 pad_maximum_fusion.refs_2_.refs_1_
  36.8 0.0 copy-start.3
  36.9 0.1 collective-permute-start.15
  37.0 0.3 collective-permute-start.13
  37.4 1.2 %collective-permute-start.14 = (bf16[96,640]{1,0:T(8,128)(2,1)S(1)}, bf16[96,640]{1,0:T(8,128)(2,1)S(1)}, u32[]{:S(2)}, u32[]{:S(2)}) collective-permute-start(bf16[96,640]{1,0:T(8,128)(2,1)S(1)} %slice_bitcast_fusion), channel_id=1, source_target_pairs={{0,4},{2,6},{4,0},{6,2},{8,12},{10,14},{12,8},{14,10},{16,20},{18,... | collective-permute-start | bytes 368648 | tf_op jit(solution)/shard_map/ppermute | solution.py:121
  38.6 4.2 %collective-permute-done.13 = bf16[96,640]{1,0:T(8,128)(2,1)S(1)} collective-permute-done((bf16[96,640]{1,0:T(8,128)(2,1)S(1)}, bf16[96,640]{1,0:T(8,128)(2,1)S(1)}, u32[]{:S(2)}, u32[]{:S(2)}) %collective-permute-start.13) | collective-permute-done | bytes 122912 | tf_op jit(solution)/shard_map/ppermute | solution.py:121
  42.8 0.1 collective-permute-done.14
  42.9 0.1 pad_maximum_fusion.1.refs_3_
  43.1 0.1 collective-permute-start.16
  43.2 0.5 collective-permute-start.22
  43.7 1.8 %collective-permute-start.17 = (bf16[2,80,640]{2,1,0:T(8,128)(2,1)S(1)}, bf16[2,80,640]{2,1,0:T(8,128)(2,1)S(1)}, u32[]{:S(2)}, u32[]{:S(2)}) collective-permute-start(bf16[2,80,640]{2,1,0:T(8,128)(2,1)S(1)} %pad_maximum_fusion.6), channel_id=1, source_target_pairs={{0,2},{2,0},{4,6},{6,4},{8,10},{10,8},{12,14},{14,12},{16,18},{18,... | collective-permute-start | bytes 614408 | tf_op jit(solution)/shard_map/ppermute | solution.py:121
  45.5 0.9 %collective-permute-start.18 = (bf16[2,80,640]{2,1,0:T(8,128)(2,1)S(1)}, bf16[2,80,640]{2,1,0:T(8,128)(2,1)S(1)}, u32[]{:S(2)}, u32[]{:S(2)}) collective-permute-start(bf16[2,80,640]{2,1,0:T(8,128)(2,1)S(1)} %pad_maximum_fusion.6), channel_id=1, source_target_pairs={{0,4},{2,6},{4,0},{6,2},{8,12},{10,14},{12,8},{14,10},{16,20},{18,... | collective-permute-start | bytes 614408 | tf_op jit(solution)/shard_map/ppermute | solution.py:121
  46.4 2.0 %place.1.refs_0_ = bf16[3,512,1280]{2,1,0:T(8,128)(2,1)S(1)} custom-call(s32[3,10]{1,0:T(4,128)S(1)} %copy-done.1, s32[3,10]{1,0:T(4,128)S(1)} %copy-done.2, bf16[4,2,176,640]{3,2,1,0:T(8,128)(2,1)S(1)} %pad_maximum_fusion.refs_2_.refs_1_, bf16[4,2,96,640]{3,2,1,0:T(8,128)(2,1)S(1)} %pad_maximum_fusion.1.refs_3_, ...), custom_call_target="tpu_custom_call" | custom-call | flops 2000000000 | bytes 8388608 | tf_op jit(solution)/shard_map/place/pallas_call | solution.py:372
  48.4 3.0 %own_half_rows.1 = (bf16[640,1280]{1,0:T(8,128)(2,1)S(1)}, bf16[640,512]{1,0:T(8,128)(2,1)S(1)}, bf16[640,512]{1,0:T(8,128)(2,1)S(1)}, bf16[640,512]{1,0:T(8,128...) custom-call(bf16[3,512,1280]{2,1,0:T(8,128)(2,1)S(1)} %place.1.refs_0_, ...), custom_call_target="tpu_custom_call" | custom-call | flops 3000000000 | bytes 8388608 | tf_op jit(solution)/shard_map/own_half_rows/pallas_call | solution.py:384
  51.4 0.9 %collective-permute-done.18 = bf16[2,80,640]{2,1,0:T(8,128)(2,1)S(1)} collective-permute-done((bf16[2,80,640]{2,1,0:T(8,128)(2,1)S(1)}, bf16[2,80,640]{2,1,0:T(8,128)(2,1)S(1)}, u32[]{:S(2)}, u32[]{:S(2)}) %collective-permute-start.18) | collective-permute-done | bytes 204832 | tf_op jit(solution)/shard_map/ppermute | solution.py:121
  52.3 0.4 collective-permute-start.19
  52.7 1.1 %collective-permute-start.20 = (bf16[80,640]{1,0:T(8,128)(2,1)S(1)}, bf16[80,640]{1,0:T(8,128)(2,1)S(1)}, u32[]{:S(2)}, u32[]{:S(2)}) collective-permute-start(bf16[80,640]{1,0:T(8,128)(2,1)S(1)} %slice_bitcast_fusion.2), channel_id=1, source_target_pairs={{0,4},{2,6},{4,0},{6,2},{8,12},{10,14},{12,8},{14,10},{16,20},{18,... | collective-permute-start | bytes 307208 | tf_op jit(solution)/shard_map/ppermute | solution.py:121
  53.8 2.1 %last_rows.1 = (f32[3,40,512]{2,1,0:T(8,128)}, bf16[640,256]{1,0:T(8,128)(2,1)S(1)}, bf16[640,256]{1,0:T(8,128)(2,1)S(1)}) custom-call(bf16[3,512,1280]{2,1,0:T(8,128)(2,1)S(1)} %place.1.refs_0_, bf16[640,1280]{1,0:T(8,128)(2,1)S(1)} %get-tuple-element.42.refs_1_, bf16[640,512]{1,0:T(8,128)(2,1)S(1)} %get-tuple-element.61.refs_2_.refs_1_, ...), custom_call_target="tpu_custom_call" | custom-call | flops 2000000000 | bytes 8388608 | tf_op jit(solution)/shard_map/last_rows/pallas_call | solution.py:395
  56.0 1.8 %late_sums.1 = (f32[512,512]{1,0:T(8,128)S(1)}, f32[256,512]{1,0:T(8,128)S(1)}, f32[512,256]{1,0:T(8,128)S(1)}) custom-call(bf16[3,512,1280]{2,1,0:T(8,128)(2,1)S(1)} %place.1.refs_0_, bf16[640,512]{1,0:T(8,128)(2,1)S(1)} %get-tuple-element.52.refs_4_.refs_1_, bf16[640,512]{1,0:T(8,128)(2,1)S(1)} %get-tuple-element.53.refs_5_.refs_2_, ...), custom_call_target="tpu_custom_call" | custom-call | flops 2000000000 | bytes 8388608 | tf_op jit(solution)/shard_map/late_sums/pallas_call | solution.py:402
  57.8 0.1 pad_maximum_fusion.2.refs_1_
  57.9 0.1 collective-permute-start.21
  58.0 1.8 %early_sums.1 = (f32[512,512]{1,0:T(8,128)S(1)}, f32[512,512]{1,0:T(8,128)S(1)}) custom-call(bf16[3,512,1280]{2,1,0:T(8,128)(2,1)S(1)} %place.1.refs_0_, bf16[640,512]{1,0:T(8,128)(2,1)S(1)} %get-tuple-element.61.refs_2_.refs_1_, bf16[640,512]{1,0:T(8,128)(2,1)S(1)} %get-tuple-element.51.refs_3_.refs_2_, bf16[640,512]{1,0:T(8,128)(2,1)S(1)} %get-tuple-element.62.refs_3_, ...), custom_call_target="tpu_custom_call" | custom-call | flops 2000000000 | bytes 8388608 | tf_op jit(solution)/shard_map/early_sums/pallas_call | solution.py:412
  59.8 0.5 collective-permute-done.21.refs_2_
  60.3 11.2 %other_half.1 = f32[3,512,256]{2,1,0:T(8,128)} custom-call(bf16[3,512,1280]{2,1,0:T(8,128)(2,1)S(1)} %place.1.refs_0_, bf16[4,2,80,640]{3,2,1,0:T(8,128)(2,1)S(1)} %pad_maximum_fusion.2.refs_1_, bf16[4,2,80,640]{3,2,1,0:T(8,128)(2,1)S(1)} %collective-permute-done.21.refs_2_, bf16[2,512,512]{2,1,0:T(8,128)(2,1)S(1)} %copy-done, f32[3,512,256]{2,1,0:T(8,128)S(1)} %copy-done.3, ...), custom_call_target="tpu_custom_call" | custom-call | flops 12000000000 | bytes 8388608 | tf_op jit(solution)/shard_map/other_half/pallas_call | solution.py:420
  (31 shorter events, 0.2 us)
Async XLA Ops:
  0.6 26.1 %copy-start.4 = (bf16[80,640]{1,0:T(8,128)(2,1)S(1)}, bf16[80,640]{1,0:T(8,128)(2,1)}, u32[]{:S(2)}) copy-start(bf16[80,640]{1,0:T(8,128)(2,1)} %param.6) | copy-start | bytes 307204
  1.6 10.0 %collective-permute-start.3 = (bf16[176,640]{1,0:T(8,128)(2,1)S(1)}, bf16[176,640]{1,0:T(8,128)(2,1)S(1)}, u32[]{:S(2)}, u32[]{:S(2)}) collective-permute-start(bf16[176,640]{1,0:T(8,128)(2,1)S(1)} %pad_maximum_fusion.5), channel_id=1, source_target_pairs={{0,8},{2,10},{4,12},{6,14},{8,0},{10,2},{12,4},{14,6},{16,24},{18,... | collective-permute-start | bytes 675848 | tf_op jit(solution)/shard_map/ppermute | solution.py:121
  5.7 7.0 %collective-permute-start = (bf16[176,640]{1,0:T(8,128)(2,1)S(1)}, bf16[176,640]{1,0:T(8,128)(2,1)S(1)}, u32[]{:S(2)}, u32[]{:S(2)}) collective-permute-start(bf16[176,640]{1,0:T(8,128)(2,1)S(1)} %get-tuple-element.69), channel_id=1, source_target_pairs={{0,4},{2,6},{4,0},{6,2},{8,12},{10,14},{12,8},{14,10},{16,20},{18,... | collective-permute-start | bytes 675848 | tf_op jit(solution)/shard_map/ppermute | solution.py:121
  7.3 6.7 %collective-permute-start.2 = (bf16[176,640]{1,0:T(8,128)(2,1)S(1)}, bf16[176,640]{1,0:T(8,128)(2,1)S(1)}, u32[]{:S(2)}, u32[]{:S(2)}) collective-permute-start(bf16[176,640]{1,0:T(8,128)(2,1)S(1)} %get-tuple-element.69), channel_id=1, source_target_pairs={{0,2},{2,0},{4,6},{6,4},{8,10},{10,8},{12,14},{14,12},{16,18},{18,... | collective-permute-start | bytes 675848 | tf_op jit(solution)/shard_map/ppermute | solution.py:121
  8.8 11.6 %collective-permute-start.7 = (bf16[96,640]{1,0:T(8,128)(2,1)}, bf16[96,640]{1,0:T(8,128)(2,1)S(1)}, u32[]{:S(2)}, u32[]{:S(2)}) collective-permute-start(bf16[96,640]{1,0:T(8,128)(2,1)} %bitcast.52), channel_id=1, source_target_pairs={{0,16},{2,18},{4,20},{6,22},{8,24},{10,26},{12,28},{14,30},{16,0},... | collective-permute-start | bytes 368648 | tf_op jit(solution)/shard_map/ppermute | solution.py:121
  11.4 9.1 %collective-permute-start.8 = (bf16[96,640]{1,0:T(8,128)(2,1)}, bf16[96,640]{1,0:T(8,128)(2,1)S(1)}, u32[]{:S(2)}, u32[]{:S(2)}) collective-permute-start(bf16[96,640]{1,0:T(8,128)(2,1)} %bitcast.53), channel_id=1, source_target_pairs={{0,24},{2,26},{4,28},{6,30},{8,16},{10,18},{12,20},{14,22},{16,8},... | collective-permute-start | bytes 368648 | tf_op jit(solution)/shard_map/ppermute | solution.py:121
  14.0 8.2 %collective-permute-start.4 = (bf16[176,640]{1,0:T(8,128)(2,1)S(1)}, bf16[176,640]{1,0:T(8,128)(2,1)S(1)}, u32[]{:S(2)}, u32[]{:S(2)}) collective-permute-start(bf16[176,640]{1,0:T(8,128)(2,1)S(1)} %collective-permute-done.3), channel_id=1, source_target_pairs={{0,2},{2,0},{4,6},{6,4},{8,10},{10,8},{12,14},{14,12},{16,18},{18,... | collective-permute-start | bytes 675848 | tf_op jit(solution)/shard_map/ppermute | solution.py:121
  15.5 6.7 %collective-permute-start.6 = (bf16[176,640]{1,0:T(8,128)(2,1)S(1)}, bf16[176,640]{1,0:T(8,128)(2,1)S(1)}, u32[]{:S(2)}, u32[]{:S(2)}) collective-permute-start(bf16[176,640]{1,0:T(8,128)(2,1)S(1)} %collective-permute-done.3), channel_id=1, source_target_pairs={{0,4},{2,6},{4,0},{6,2},{8,12},{10,14},{12,8},{14,10},{16,20},{18,... | collective-permute-start | bytes 675848 | tf_op jit(solution)/shard_map/ppermute | solution.py:121
  16.0 8.6 %collective-permute-start.1 = (bf16[176,640]{1,0:T(8,128)(2,1)S(1)}, bf16[176,640]{1,0:T(8,128)(2,1)S(1)}, u32[]{:S(2)}, u32[]{:S(2)}) collective-permute-start(bf16[176,640]{1,0:T(8,128)(2,1)S(1)} %collective-permute-done), channel_id=1, source_target_pairs={{0,2},{2,0},{4,6},{6,4},{8,10},{10,8},{12,14},{14,12},{16,18},{18,... | collective-permute-start | bytes 675848 | tf_op jit(solution)/shard_map/ppermute | solution.py:121
  24.6 12.4 %collective-permute-start.11 = (bf16[2,96,640]{2,1,0:T(8,128)(2,1)S(1)}, bf16[2,96,640]{2,1,0:T(8,128)(2,1)S(1)}, u32[]{:S(2)}, u32[]{:S(2)}) collective-permute-start(bf16[2,96,640]{2,1,0:T(8,128)(2,1)S(1)} %pad_maximum_fusion.3), channel_id=1, source_target_pairs={{0,2},{2,0},{4,6},{6,4},{8,10},{10,8},{12,14},{14,12},{16,18},{18,... | collective-permute-start | bytes 737288 | tf_op jit(solution)/shard_map/ppermute | solution.py:121
  26.1 10.9 %collective-permute-start.12 = (bf16[2,96,640]{2,1,0:T(8,128)(2,1)S(1)}, bf16[2,96,640]{2,1,0:T(8,128)(2,1)S(1)}, u32[]{:S(2)}, u32[]{:S(2)}) collective-permute-start(bf16[2,96,640]{2,1,0:T(8,128)(2,1)S(1)} %pad_maximum_fusion.3), channel_id=1, source_target_pairs={{0,4},{2,6},{4,0},{6,2},{8,12},{10,14},{12,8},{14,10},{16,20},{18,... | collective-permute-start | bytes 737288 | tf_op jit(solution)/shard_map/ppermute | solution.py:121
  26.7 10.3 %collective-permute-start.10 = (bf16[80,640]{1,0:T(8,128)(2,1)S(1)}, bf16[80,640]{1,0:T(8,128)(2,1)S(1)}, u32[]{:S(2)}, u32[]{:S(2)}) collective-permute-start(bf16[80,640]{1,0:T(8,128)(2,1)S(1)} %copy-done.4), channel_id=1, source_target_pairs={{0,24},{2,26},{4,28},{6,30},{8,16},{10,18},{12,20},{14,22},{16,8},... | collective-permute-start | bytes 307208 | tf_op jit(solution)/shard_map/ppermute | solution.py:121
  29.6 7.4 %collective-permute-start.9 = (bf16[80,640]{1,0:T(8,128)(2,1)S(1)}, bf16[80,640]{1,0:T(8,128)(2,1)S(1)}, u32[]{:S(2)}, u32[]{:S(2)}) collective-permute-start(bf16[80,640]{1,0:T(8,128)(2,1)S(1)} %copy-done.4), channel_id=1, source_target_pairs={{0,16},{2,18},{4,20},{6,22},{8,24},{10,26},{12,28},{14,30},{16,0},... | collective-permute-start | bytes 307208 | tf_op jit(solution)/shard_map/ppermute | solution.py:121
  29.6 6.9 %collective-permute-start.5 = (bf16[176,640]{1,0:T(8,128)(2,1)S(1)}, bf16[176,640]{1,0:T(8,128)(2,1)S(1)}, u32[]{:S(2)}, u32[]{:S(2)}) collective-permute-start(bf16[176,640]{1,0:T(8,128)(2,1)S(1)} %collective-permute-done.4), channel_id=1, source_target_pairs={{0,4},{2,6},{4,0},{6,2},{8,12},{10,14},{12,8},{14,10},{16,20},{18,... | collective-permute-start | bytes 675848 | tf_op jit(solution)/shard_map/ppermute | solution.py:121
  36.8 6.3 %copy-start.3 = (f32[3,512,256]{2,1,0:T(8,128)S(1)}, f32[3,512,256]{2,1,0:T(8,128)}, u32[]{:S(2)}) copy-start(f32[3,512,256]{2,1,0:T(8,128)} %refs_4_.1) | copy-start | bytes 4718596
  36.8 9.5 %copy-start.1 = (s32[3,10]{1,0:T(4,128)S(1)}, s32[3,10]{1,0:T(4,128)}, u32[]{:S(2)}) copy-start(s32[3,10]{1,0:T(4,128)} %refs_0_.1) | copy-start | bytes 364
  36.9 9.5 %copy-start.2 = (s32[3,10]{1,0:T(4,128)S(1)}, s32[3,10]{1,0:T(4,128)}, u32[]{:S(2)}) copy-start(s32[3,10]{1,0:T(4,128)} %refs_1_.1) | copy-start | bytes 364
  36.9 9.5 %collective-permute-start.15 = (bf16[4,2,176,640]{3,2,1,0:T(8,128)(2,1)S(1)}, bf16[4,2,176,640]{3,2,1,0:T(8,128)(2,1)S(1)}, u32[]{:S(2)}, u32[]{:S(2)}) collective-permute-start(bf16[4,2,176,640]{3,2,1,0:T(8,128)(2,1)S(1)} %pad_maximum_fusion.refs_2_.refs_1_), channel_id=1, source_target_pairs={{0,1},{1,0},{2,3},{3,2},{4,5},{5,4},{6,7},{7,6},{8,9},{9,8},{10,11... | collective-permute-start | bytes 5406728 | tf_op jit(solution)/shard_map/ppermute | solution.py:125
  37.0 5.8 %collective-permute-start.13 = (bf16[96,640]{1,0:T(8,128)(2,1)S(1)}, bf16[96,640]{1,0:T(8,128)(2,1)S(1)}, u32[]{:S(2)}, u32[]{:S(2)}) collective-permute-start(bf16[96,640]{1,0:T(8,128)(2,1)S(1)} %slice_bitcast_fusion.1), channel_id=1, source_target_pairs={{0,2},{2,0},{4,6},{6,4},{8,10},{10,8},{12,14},{14,12},{16,18},{18,... | collective-permute-start | bytes 368648 | tf_op jit(solution)/shard_map/ppermute | solution.py:121
  37.4 5.5 %collective-permute-start.14 = (bf16[96,640]{1,0:T(8,128)(2,1)S(1)}, bf16[96,640]{1,0:T(8,128)(2,1)S(1)}, u32[]{:S(2)}, u32[]{:S(2)}) collective-permute-start(bf16[96,640]{1,0:T(8,128)(2,1)S(1)} %slice_bitcast_fusion), channel_id=1, source_target_pairs={{0,4},{2,6},{4,0},{6,2},{8,12},{10,14},{12,8},{14,10},{16,20},{18,... | collective-permute-start | bytes 368648 | tf_op jit(solution)/shard_map/ppermute | solution.py:121
  43.1 3.3 %collective-permute-start.16 = (bf16[4,2,96,640]{3,2,1,0:T(8,128)(2,1)S(1)}, bf16[4,2,96,640]{3,2,1,0:T(8,128)(2,1)S(1)}, u32[]{:S(2)}, u32[]{:S(2)}) collective-permute-start(bf16[4,2,96,640]{3,2,1,0:T(8,128)(2,1)S(1)} %pad_maximum_fusion.1.refs_3_), channel_id=1, source_target_pairs={{0,1},{1,0},{2,3},{3,2},{4,5},{5,4},{6,7},{7,6},{8,9},{9,8},{10,11... | collective-permute-start | bytes 2949128 | tf_op jit(solution)/shard_map/ppermute | solution.py:125
  43.2 16.6 %collective-permute-start.22 = (f32[3,512,256]{2,1,0:T(8,128)S(1)}, f32[3,512,256]{2,1,0:T(8,128)S(1)}, u32[]{:S(2)}, u32[]{:S(2)}) collective-permute-start(f32[3,512,256]{2,1,0:T(8,128)S(1)} %copy-done.3), channel_id=1, source_target_pairs={{0,1},{1,0},{2,3},{3,2},{4,5},{5,4},{6,7},{7,6},{8,9},{9,8},{10,11... | collective-permute-start | bytes 4718600 | tf_op jit(solution)/shard_map/ppermute | solution.py:125
  43.7 4.7 %copy-start = (bf16[2,512,512]{2,1,0:T(8,128)(2,1)S(1)}, bf16[2,512,512]{2,1,0:T(8,128)(2,1)}, u32[]{:S(2)}) copy-start(bf16[2,512,512]{2,1,0:T(8,128)(2,1)} %refs_3_.3) | copy-start | bytes 3145732
  43.7 7.7 %collective-permute-start.17 = (bf16[2,80,640]{2,1,0:T(8,128)(2,1)S(1)}, bf16[2,80,640]{2,1,0:T(8,128)(2,1)S(1)}, u32[]{:S(2)}, u32[]{:S(2)}) collective-permute-start(bf16[2,80,640]{2,1,0:T(8,128)(2,1)S(1)} %pad_maximum_fusion.6), channel_id=1, source_target_pairs={{0,2},{2,0},{4,6},{6,4},{8,10},{10,8},{12,14},{14,12},{16,18},{18,... | collective-permute-start | bytes 614408 | tf_op jit(solution)/shard_map/ppermute | solution.py:121
  45.5 6.8 %collective-permute-start.18 = (bf16[2,80,640]{2,1,0:T(8,128)(2,1)S(1)}, bf16[2,80,640]{2,1,0:T(8,128)(2,1)S(1)}, u32[]{:S(2)}, u32[]{:S(2)}) collective-permute-start(bf16[2,80,640]{2,1,0:T(8,128)(2,1)S(1)} %pad_maximum_fusion.6), channel_id=1, source_target_pairs={{0,4},{2,6},{4,0},{6,2},{8,12},{10,14},{12,8},{14,10},{16,20},{18,... | collective-permute-start | bytes 614408 | tf_op jit(solution)/shard_map/ppermute | solution.py:121
  52.3 5.5 %collective-permute-start.19 = (bf16[80,640]{1,0:T(8,128)(2,1)S(1)}, bf16[80,640]{1,0:T(8,128)(2,1)S(1)}, u32[]{:S(2)}, u32[]{:S(2)}) collective-permute-start(bf16[80,640]{1,0:T(8,128)(2,1)S(1)} %slice_bitcast_fusion.3), channel_id=1, source_target_pairs={{0,2},{2,0},{4,6},{6,4},{8,10},{10,8},{12,14},{14,12},{16,18},{18,... | collective-permute-start | bytes 307208 | tf_op jit(solution)/shard_map/ppermute | solution.py:121
  52.7 5.0 %collective-permute-start.20 = (bf16[80,640]{1,0:T(8,128)(2,1)S(1)}, bf16[80,640]{1,0:T(8,128)(2,1)S(1)}, u32[]{:S(2)}, u32[]{:S(2)}) collective-permute-start(bf16[80,640]{1,0:T(8,128)(2,1)S(1)} %slice_bitcast_fusion.2), channel_id=1, source_target_pairs={{0,4},{2,6},{4,0},{6,2},{8,12},{10,14},{12,8},{14,10},{16,20},{18,... | collective-permute-start | bytes 307208 | tf_op jit(solution)/shard_map/ppermute | solution.py:121
  57.9 2.4 %collective-permute-start.21 = (bf16[4,2,80,640]{3,2,1,0:T(8,128)(2,1)S(1)}, bf16[4,2,80,640]{3,2,1,0:T(8,128)(2,1)S(1)}, u32[]{:S(2)}, u32[]{:S(2)}) collective-permute-start(bf16[4,2,80,640]{3,2,1,0:T(8,128)(2,1)S(1)} %pad_maximum_fusion.2.refs_1_), channel_id=1, source_target_pairs={{0,1},{1,0},{2,3},{3,2},{4,5},{5,4},{6,7},{7,6},{8,9},{9,8},{10,11... | collective-permute-start | bytes 2457608 | tf_op jit(solution)/shard_map/ppermute | solution.py:125
